TPU v7x, 32 devices: a whole 2x2x4 slice. The times are simulated.
32 devices in a mesh: section: 2 (over x), dp: 4 (over z), tensor: 4 (over y, core).
Axes of the slice: x: 2, y: 2, z: 4, core: 2. Of those that a mesh axis runs over, the one named last changes fastest.
Arguments:
- table_input: bfloat16 [8, 1024, 1024], P('dp'), may hold values from -6 to 6
- target_input: bfloat16 [8, 128, 1024], P('dp'), may hold values from -6 to 6
- cotangent: bfloat16 [8, 128, 1024], P('dp'), may hold values from -6 to 6
- table_lengths: int32 [8], P('dp'), may hold values from 51 to 1024, as said below
- target_lengths: int32 [8], P('dp'), may hold values from 16 to 128, as said below
- query_key: bfloat16 [2, 3, 1024, 1024], P('section', None, None, 'tensor'), may hold values from -0.1875 to 0.1875
- value_out: bfloat16 [2, 3, 1024, 1024], P('section', None, None, 'tensor'), may hold values from -0.5 to 0.5
- hidden_in: bfloat16 [2, 1024, 4096], P('section', None, 'tensor'), may hold values from -0.1875 to 0.1875
- hidden_out: bfloat16 [2, 1024, 4096], P('section', None, 'tensor'), may hold values from -0.125 to 0.125
- hidden_bias: float32 [2, 4096], P('section', 'tensor'), may hold values from -3 to 3
- vectors: float32 [2, 11, 1024], P('section'), may hold values from -2 to 2
- cross_bias: float32 [1024], replicated, may hold values from -3 to 3
Outputs:
- decoded: bfloat16 [8, 128, 1024], P('dp', ('section', 'tensor'))
- table_grad: bfloat16 [8, 1024, 1024], P('dp', ('section', 'tensor'))
- target_grad: bfloat16 [8, 128, 1024], P('dp', ('section', 'tensor'))
- query_key_grad: float32 [2, 3, 1024, 1024], P('section', None, None, 'tensor')
- value_out_grad: float32 [2, 3, 1024, 1024], P('section', None, None, 'tensor')
- hidden_in_grad: float32 [2, 1024, 4096], P('section', None, 'tensor')
- hidden_out_grad: float32 [2, 1024, 4096], P('section', None, 'tensor')
- hidden_bias_grad: float32 [2, 4096], P('section', 'tensor')
- vectors_grad: float32 [2, 11, 1024], P('section')
- cross_bias_grad: float32 [1024], replicated
Inputs may be any that keep to these rules, and one draw needn't show every extreme that they name: `table_lengths`: each aligned block of 2 tables (the tables of one index of dp) holds a table of exactly 1024 tokens. `target_lengths`: each aligned block of 2 targets (those of one index of dp) holds one of exactly 128 tokens.
All inputs are finite; a program needn't handle non-finite values.
Results may differ from a plain program's by a relative error of at most 0.034.
Values may be sent and summed in bfloat16 or wider, within the bound.
No kernel may reach another device: no remote copies, remote signals or barrier semaphores. Data moves between devices by JAX's collectives and lax.ppermute only.
A program may use at most 192 MiB of HBM per device.

v0:
```python
import jax
import jax.numpy as jnp
from jax import lax
from jax.sharding import PartitionSpec as P

HEAD = 64
TB = 1
MB = 2


epsilon = 1e-05


def shifted(value, axis, steps):
    count = lax.axis_size(axis)
    initial, last = (max(0, -steps), min(count, count - steps))
    return lax.ppermute(value, axis, [(source, source + steps) for source in range(initial, last)])


def layer_norm(summed, norm_gain, norm_shift):
    centered = summed - jnp.mean(summed, axis=-1, keepdims=True)
    spread = jnp.mean(centered * centered, axis=-1, keepdims=True)
    return centered * lax.rsqrt(spread + epsilon) * norm_gain + norm_shift


def norm_backward(summed, norm_gain, norm_shift, gradient):
    _, pull_back = jax.vjp(layer_norm, summed, norm_gain, norm_shift)
    return pull_back(gradient)


def gelu_exact(before):
    return jax.nn.gelu(before, approximate=False)


def project(inputs, matrix):
    return jnp.einsum("gld,dk->glk", inputs, matrix, preferred_element_type=jnp.float32)


def project_back(inputs, matrix):
    return jnp.einsum("glk,dk->gld", inputs, matrix, preferred_element_type=jnp.float32)


def weight_grad(inputs, gradient):
    return jnp.einsum("gld,glk->dk", inputs, gradient, preferred_element_type=jnp.float32)


def column_sum(gradient):
    return jnp.sum(gradient, axis=(0, 1), dtype=jnp.float32)


def share_sum(gradient):
    return jnp.sum(gradient, axis=(0, 1, 2, 3))


def split_rows(inputs, section_count, tensor_count):
    tables, length_rows, features = inputs.shape
    return inputs.reshape(
        tables, section_count, tensor_count, length_rows // (section_count * tensor_count), features
    )


def share_rows(inputs, section_count, tensor_count, tensor_rank):
    return lax.dynamic_slice_in_dim(
        split_rows(inputs, section_count, tensor_count), tensor_rank, 1, 2
    )


def gather_rows(share_part):
    gathered = lax.all_gather(share_part, "tensor", axis=2, tiled=True)
    return gathered.reshape(gathered.shape[0], -1, gathered.shape[-1])


def reduce_rows(partial_rows, section_count, tensor_count):
    return lax.psum_scatter(
        split_rows(partial_rows, section_count, tensor_count).astype(jnp.bfloat16),
        "tensor",
        scatter_dimension=2,
        tiled=True,
    ).astype(jnp.float32)


def gather_grads(share_part):
    gathered = lax.all_gather(share_part, "tensor", axis=2, tiled=True)
    return gathered.reshape(gathered.shape[0], -1, gathered.shape[-1])


def reduce_grads(partial_rows, section_count, tensor_count):
    return lax.psum_scatter(
        split_rows(partial_rows, section_count, tensor_count).astype(jnp.bfloat16),
        "tensor",
        scatter_dimension=2,
        tiled=True,
    ).astype(jnp.float32)


def send_memory(payload):
    return shifted(payload, "section", 1)


def return_memory(payload):
    return shifted(payload, "section", -1)


def key_mask(key_valid, start_row, block_rows, causal):
    allowed = key_valid[:, None, None, :]
    if causal:
        query_rows = start_row + jnp.arange(block_rows)[:, None]
        key_index = jnp.arange(key_valid.shape[1])[None, :]
        allowed = allowed & (key_index <= query_rows)[None, None]
    return allowed


def attention_forward(queries, key_rows, value_rows, key_valid, causal):
    tables, query_count, features = queries.shape
    head_count = features // HEAD
    block_rows = min(512, query_count)
    scaling = HEAD ** (-0.5)
    query_blocks = queries.reshape(tables, query_count // block_rows, block_rows, head_count, HEAD)
    key_split = key_rows.reshape(tables, -1, head_count, HEAD)
    value_split = value_rows.reshape(tables, -1, head_count, HEAD)

    def one_block(block_index):
        query_part = lax.dynamic_index_in_dim(query_blocks, block_index, 1, keepdims=False)
        scores = (
            jnp.einsum("gqhe,gkhe->ghqk", query_part, key_split, preferred_element_type=jnp.float32)
            * scaling
        )
        scores = jnp.where(
            key_mask(key_valid, block_index * block_rows, block_rows, causal), scores, -1e30
        )
        largest = jnp.max(scores, axis=-1, keepdims=True)
        exponent = jnp.exp(scores - largest)
        denominator = jnp.sum(exponent, axis=-1, keepdims=True)
        weights = (exponent / denominator).astype(jnp.bfloat16)
        output = jnp.einsum(
            "ghqk,gkhe->gqhe", weights, value_split, preferred_element_type=jnp.float32
        )
        return (output, (largest + jnp.log(denominator))[..., 0])

    outputs, log_total = lax.map(one_block, jnp.arange(query_count // block_rows))
    return (jnp.moveaxis(outputs, 0, 1).reshape(tables, query_count, features), log_total)


def attention_backward(queries, key_rows, value_rows, key_valid, causal, log_total, grad_heads):
    tables, query_count, features = queries.shape
    head_count = features // HEAD
    block_rows = min(512, query_count)
    scaling = HEAD ** (-0.5)
    query_blocks = queries.reshape(tables, query_count // block_rows, block_rows, head_count, HEAD)
    grad_blocks = grad_heads.reshape(
        tables, query_count // block_rows, block_rows, head_count, HEAD
    )
    key_split = key_rows.reshape(tables, -1, head_count, HEAD)
    value_split = value_rows.reshape(tables, -1, head_count, HEAD)

    def one_block(running, block_index):
        key_sum, value_sum = running
        query_part = lax.dynamic_index_in_dim(query_blocks, block_index, 1, keepdims=False)
        grad_part = lax.dynamic_index_in_dim(grad_blocks, block_index, 1, keepdims=False)
        scores = (
            jnp.einsum("gqhe,gkhe->ghqk", query_part, key_split, preferred_element_type=jnp.float32)
            * scaling
        )
        scores = jnp.where(
            key_mask(key_valid, block_index * block_rows, block_rows, causal), scores, -1e30
        )
        probability = jnp.exp(scores - log_total[block_index][..., None])
        value_sum = value_sum + jnp.einsum(
            "ghqk,gqhe->gkhe",
            probability.astype(jnp.bfloat16),
            grad_part,
            preferred_element_type=jnp.float32,
        )
        grad_probs = jnp.einsum(
            "gqhe,gkhe->ghqk", grad_part, value_split, preferred_element_type=jnp.float32
        )
        inner_sum = jnp.sum(probability * grad_probs, axis=-1, keepdims=True)
        grad_scores = (probability * (grad_probs - inner_sum)).astype(jnp.bfloat16)
        grad_query = (
            jnp.einsum(
                "ghqk,gkhe->gqhe", grad_scores, key_split, preferred_element_type=jnp.float32
            )
            * scaling
        )
        key_sum = (
            key_sum
            + jnp.einsum(
                "ghqk,gqhe->gkhe", grad_scores, query_part, preferred_element_type=jnp.float32
            )
            * scaling
        )
        return ((key_sum, value_sum), grad_query)

    zero_keys = jnp.zeros(key_split.shape, jnp.float32)
    (key_sum, value_sum), grad_query = lax.scan(
        one_block, (zero_keys, zero_keys), jnp.arange(query_count // block_rows)
    )
    grad_query = jnp.moveaxis(grad_query, 0, 1).reshape(tables, query_count, features)
    return (
        grad_query,
        key_sum.reshape(tables, -1, features),
        value_sum.reshape(tables, -1, features),
    )


def self_forward(
    residual,
    gathered,
    matrices,
    head_shift,
    out_shift,
    key_valid,
    causal,
    section_count,
    tensor_count,
):
    w_query, w_key, w_value, w_output = matrices
    queries = (project(gathered, w_query) + head_shift[0]).astype(jnp.bfloat16)
    key_rows = project(gathered, w_key).astype(jnp.bfloat16)
    value_rows = (project(gathered, w_value) + head_shift[1]).astype(jnp.bfloat16)
    outputs, log_total = attention_forward(queries, key_rows, value_rows, key_valid, causal)
    outputs = outputs.astype(jnp.bfloat16)
    summed = (
        residual
        + reduce_rows(project_back(outputs, w_output), section_count, tensor_count)
        + out_shift
    )
    return (summed, (queries, key_rows, value_rows, outputs, log_total))


def self_backward(
    grad_summed, gathered, kept, matrices, key_valid, causal, section_count, tensor_count
):
    w_query, w_key, w_value, w_output = matrices
    queries, key_rows, value_rows, outputs, log_total = kept
    grad_rows = gather_grads(grad_summed.astype(jnp.bfloat16))
    grad_heads = project(grad_rows, w_output).astype(jnp.bfloat16)
    grad_query, grad_key, grad_value = attention_backward(
        queries, key_rows, value_rows, key_valid, causal, log_total, grad_heads
    )
    grad_query = grad_query.astype(jnp.bfloat16)
    grad_key = grad_key.astype(jnp.bfloat16)
    grad_value = grad_value.astype(jnp.bfloat16)
    partial_rows = (
        project_back(grad_query, w_query)
        + project_back(grad_key, w_key)
        + project_back(grad_value, w_value)
    )
    grad_input = reduce_grads(partial_rows, section_count, tensor_count)
    matrix_grads = (
        weight_grad(gathered, grad_query),
        weight_grad(gathered, grad_key),
        weight_grad(gathered, grad_value),
        weight_grad(grad_rows, outputs),
    )
    shift_grads = (column_sum(grad_query), column_sum(grad_value), share_sum(grad_summed))
    return (grad_input, matrix_grads, shift_grads)


def ffn_forward(
    residual, gathered, weight_in, weight_out, hidden_shift, out_shift, section_count, tensor_count
):
    before = project(gathered, weight_in) + hidden_shift
    hidden = gelu_exact(before).astype(jnp.bfloat16)
    summed = (
        residual
        + reduce_rows(project_back(hidden, weight_out), section_count, tensor_count)
        + out_shift
    )
    return (summed, (before, hidden))


def ffn_backward(grad_summed, gathered, kept, weight_in, weight_out, section_count, tensor_count):
    before, hidden = kept
    grad_rows = gather_grads(grad_summed.astype(jnp.bfloat16))
    grad_hidden = project(grad_rows, weight_out)
    _, pull_back = jax.vjp(gelu_exact, before)
    grad_before = pull_back(grad_hidden)[0].astype(jnp.bfloat16)
    grad_input = reduce_grads(project_back(grad_before, weight_in), section_count, tensor_count)
    matrix_grads = (weight_grad(gathered, grad_before), weight_grad(grad_rows, hidden))
    return (grad_input, matrix_grads, (column_sum(grad_before), share_sum(grad_summed)))


def place_heads(head_rows, other_rows, tensor_rank):
    features = other_rows.shape[1]
    placed = lax.dynamic_update_slice(
        jnp.zeros((3, features), jnp.float32), head_rows, (0, tensor_rank * head_rows.shape[1])
    )
    return jnp.concatenate([placed, other_rows], axis=0)


def encoder_forward(table_share, key_valid, params, section_count, tensor_count):
    query_key, value_out, weight_in, weight_out, hidden_shift, vector_rows, head_shift = params
    matrices = (query_key[0], query_key[1], value_out[0], value_out[1])
    normed = layer_norm(table_share, vector_rows[9], vector_rows[10])
    first_in = gather_rows(normed.astype(jnp.bfloat16))
    summed_one, self_kept = self_forward(
        normed,
        first_in,
        matrices,
        head_shift,
        vector_rows[3],
        key_valid,
        False,
        section_count,
        tensor_count,
    )
    middle = layer_norm(summed_one, vector_rows[5], vector_rows[6])
    second_in = gather_rows(middle.astype(jnp.bfloat16))
    summed_two, ffn_kept = ffn_forward(
        middle,
        second_in,
        weight_in,
        weight_out,
        hidden_shift,
        vector_rows[4],
        section_count,
        tensor_count,
    )
    memory = layer_norm(summed_two, vector_rows[7], vector_rows[8])
    third_in = gather_rows(memory.astype(jnp.bfloat16))
    cross_keys = project(third_in, query_key[2]).astype(jnp.bfloat16)
    cross_values = (project(third_in, value_out[2]) + head_shift[2]).astype(jnp.bfloat16)
    kept = (
        normed,
        first_in,
        summed_one,
        self_kept,
        middle,
        second_in,
        summed_two,
        ffn_kept,
        third_in,
    )
    return (jnp.stack([cross_keys, cross_values]), kept)


def encoder_backward(
    grad_memory_kv, table_share, kept, key_valid, params, tensor_rank, section_count, tensor_count
):
    query_key, value_out, weight_in, weight_out, hidden_shift, vector_rows, head_shift = params
    matrices = (query_key[0], query_key[1], value_out[0], value_out[1])
    normed, first_in, summed_one, self_kept, middle, second_in, summed_two, ffn_kept, third_in = (
        kept
    )
    grad_keys = grad_memory_kv[0]
    grad_values = grad_memory_kv[1]
    partial_rows = project_back(grad_keys, query_key[2]) + project_back(grad_values, value_out[2])
    grad_memory = reduce_grads(partial_rows, section_count, tensor_count)
    grad_two, gain_two, shift_two = norm_backward(
        summed_two, vector_rows[7], vector_rows[8], grad_memory
    )
    grad_middle, ffn_grads, ffn_shifts = ffn_backward(
        grad_two, second_in, ffn_kept, weight_in, weight_out, section_count, tensor_count
    )
    grad_one, gain_one, shift_one = norm_backward(
        summed_one, vector_rows[5], vector_rows[6], grad_two + grad_middle
    )
    grad_normed, self_grads, self_shifts = self_backward(
        grad_one, first_in, self_kept, matrices, key_valid, False, section_count, tensor_count
    )
    grad_input, gain_zero, shift_zero = norm_backward(
        table_share, vector_rows[9], vector_rows[10], grad_one + grad_normed
    )
    head_rows = jnp.stack([self_shifts[0], self_shifts[1], column_sum(grad_values)])
    other_rows = jnp.stack(
        [
            self_shifts[2],
            ffn_shifts[1],
            gain_one,
            shift_one,
            gain_two,
            shift_two,
            gain_zero,
            shift_zero,
        ]
    )
    grads = (
        jnp.stack([self_grads[0], self_grads[1], weight_grad(third_in, grad_keys)]),
        jnp.stack([self_grads[2], self_grads[3], weight_grad(third_in, grad_values)]),
        ffn_grads[0],
        ffn_grads[1],
        ffn_shifts[0],
        place_heads(head_rows, other_rows, tensor_rank),
        jnp.zeros((vector_rows.shape[1],), jnp.float32),
    )
    return (grad_input, grads)


def decoder_forward(
    target_share,
    target_valid,
    table_valid,
    memory_kv,
    params,
    cross_bias,
    section_count,
    tensor_count,
):
    query_key, value_out, weight_in, weight_out, hidden_shift, vector_rows, head_shift = params
    matrices = (query_key[0], query_key[1], value_out[0], value_out[1])
    first_in = gather_rows(target_share.astype(jnp.bfloat16))
    summed_one, self_kept = self_forward(
        target_share,
        first_in,
        matrices,
        head_shift,
        vector_rows[3],
        target_valid,
        True,
        section_count,
        tensor_count,
    )
    middle = layer_norm(summed_one, vector_rows[5], vector_rows[6])
    cross_in = gather_rows(middle.astype(jnp.bfloat16))
    cross_queries = (project(cross_in, query_key[2]) + head_shift[2]).astype(jnp.bfloat16)
    cross_out, cross_log = attention_forward(
        cross_queries, memory_kv[0], memory_kv[1], table_valid, False
    )
    cross_out = cross_out.astype(jnp.bfloat16)
    summed_cross = (
        middle
        + reduce_rows(project_back(cross_out, value_out[2]), section_count, tensor_count)
        + cross_bias
    )
    later = layer_norm(summed_cross, vector_rows[9], vector_rows[10])
    third_in = gather_rows(later.astype(jnp.bfloat16))
    summed_two, ffn_kept = ffn_forward(
        later,
        third_in,
        weight_in,
        weight_out,
        hidden_shift,
        vector_rows[4],
        section_count,
        tensor_count,
    )
    decoded = layer_norm(summed_two, vector_rows[7], vector_rows[8])
    kept = (
        first_in,
        summed_one,
        self_kept,
        cross_in,
        cross_queries,
        cross_out,
        cross_log,
        summed_cross,
        third_in,
        summed_two,
        ffn_kept,
    )
    return (decoded, kept)


def decoder_backward(
    grad_decoded,
    memory_kv,
    kept,
    target_valid,
    table_valid,
    params,
    tensor_rank,
    section_count,
    tensor_count,
):
    query_key, value_out, weight_in, weight_out, hidden_shift, vector_rows, head_shift = params
    matrices = (query_key[0], query_key[1], value_out[0], value_out[1])
    (
        first_in,
        summed_one,
        self_kept,
        cross_in,
        cross_queries,
        cross_out,
        cross_log,
        summed_cross,
        third_in,
        summed_two,
        ffn_kept,
    ) = kept
    grad_two, gain_two, shift_two = norm_backward(
        summed_two, vector_rows[7], vector_rows[8], grad_decoded
    )
    grad_later, ffn_grads, ffn_shifts = ffn_backward(
        grad_two, third_in, ffn_kept, weight_in, weight_out, section_count, tensor_count
    )
    grad_cross, gain_cross, shift_cross = norm_backward(
        summed_cross, vector_rows[9], vector_rows[10], grad_two + grad_later
    )
    grad_rows = gather_grads(grad_cross.astype(jnp.bfloat16))
    grad_cross_heads = project(grad_rows, value_out[2]).astype(jnp.bfloat16)
    grad_cross_query, grad_cross_key, grad_cross_value = attention_backward(
        cross_queries, memory_kv[0], memory_kv[1], table_valid, False, cross_log, grad_cross_heads
    )
    grad_cross_query = grad_cross_query.astype(jnp.bfloat16)
    grad_memory = jnp.stack([grad_cross_key, grad_cross_value]).astype(jnp.bfloat16)
    grad_middle = reduce_grads(
        project_back(grad_cross_query, query_key[2]), section_count, tensor_count
    )
    grad_one, gain_one, shift_one = norm_backward(
        summed_one, vector_rows[5], vector_rows[6], grad_cross + grad_middle
    )
    grad_first, self_grads, self_shifts = self_backward(
        grad_one, first_in, self_kept, matrices, target_valid, True, section_count, tensor_count
    )
    grad_input = grad_one + grad_first
    head_rows = jnp.stack([self_shifts[0], self_shifts[1], column_sum(grad_cross_query)])
    other_rows = jnp.stack(
        [
            self_shifts[2],
            ffn_shifts[1],
            gain_one,
            shift_one,
            gain_two,
            shift_two,
            gain_cross,
            shift_cross,
        ]
    )
    grads = (
        jnp.stack([self_grads[0], self_grads[1], weight_grad(cross_in, grad_cross_query)]),
        jnp.stack([self_grads[2], self_grads[3], weight_grad(grad_rows, cross_out)]),
        ffn_grads[0],
        ffn_grads[1],
        ffn_shifts[0],
        place_heads(head_rows, other_rows, tensor_rank),
        share_sum(grad_cross),
    )
    return (grad_memory, grad_input, grads)


def masked_add(totals, grads, keep_flag):
    return jax.tree.map(
        lambda running, update: running + jnp.where(keep_flag, update, jnp.zeros_like(update)),
        totals,
        grads,
    )


def per_device(
    table_input,
    target_input,
    cotangent,
    table_lengths,
    target_lengths,
    query_key,
    value_out,
    hidden_in,
    hidden_out,
    hidden_bias,
    vectors,
    cross_bias,
):
    section_count = lax.axis_size("section")
    tensor_count = lax.axis_size("tensor")
    tensor_rank = lax.axis_index("tensor")
    section_rank = lax.axis_index("section")
    is_first = section_rank == 0
    not_first = jnp.logical_not(is_first)
    vector_rows = vectors[0]
    features = vector_rows.shape[1]
    head_width = query_key.shape[3]
    head_shift = lax.dynamic_slice_in_dim(vector_rows[0:3], tensor_rank * head_width, head_width, 1)
    params = (
        query_key[0],
        value_out[0],
        hidden_in[0],
        hidden_out[0],
        hidden_bias[0],
        vector_rows,
        head_shift,
    )
    table_slots = table_input.shape[1]
    target_slots = target_input.shape[1]

    def micro_inputs(micro_index):
        lower = micro_index * TB
        table_part = lax.dynamic_slice_in_dim(table_input, lower, TB, 0)
        target_part = lax.dynamic_slice_in_dim(target_input, lower, TB, 0)
        grad_part = lax.dynamic_slice_in_dim(cotangent, lower, TB, 0)
        table_count = lax.dynamic_slice_in_dim(table_lengths, lower, TB, 0)
        target_count = lax.dynamic_slice_in_dim(target_lengths, lower, TB, 0)
        table_share = share_rows(table_part, section_count, tensor_count, tensor_rank).astype(
            jnp.float32
        )
        target_share = share_rows(target_part, section_count, tensor_count, tensor_rank).astype(
            jnp.float32
        )
        grad_share = share_rows(grad_part, section_count, tensor_count, tensor_rank).astype(
            jnp.float32
        )
        table_valid = jnp.arange(table_slots)[None, :] < table_count[:, None]
        target_valid = jnp.arange(target_slots)[None, :] < target_count[:, None]
        return (table_share, target_share, grad_share, table_valid, target_valid)

    grad_zero = (
        jnp.zeros(query_key.shape[1:], jnp.float32),
        jnp.zeros(value_out.shape[1:], jnp.float32),
        jnp.zeros(hidden_in.shape[1:], jnp.float32),
        jnp.zeros(hidden_out.shape[1:], jnp.float32),
        jnp.zeros(hidden_bias.shape[1:], jnp.float32),
        jnp.zeros((11, features), jnp.float32),
        jnp.zeros((features,), jnp.float32),
    )

    def encode(micro_index):
        table_share, _, _, table_valid, _ = micro_inputs(micro_index)
        payload, _ = encoder_forward(table_share, table_valid, params, section_count, tensor_count)
        return payload

    def decode(micro_index, memory_kv):
        _, target_share, _, table_valid, target_valid = micro_inputs(micro_index)
        decoded_share, _ = decoder_forward(
            target_share,
            target_valid,
            table_valid,
            memory_kv,
            params,
            cross_bias,
            section_count,
            tensor_count,
        )
        return decoded_share

    def encode_back(micro_index, grad_memory):
        table_share, _, _, table_valid, _ = micro_inputs(micro_index)
        _, kept = encoder_forward(table_share, table_valid, params, section_count, tensor_count)
        return encoder_backward(
            grad_memory,
            table_share,
            kept,
            table_valid,
            params,
            tensor_rank,
            section_count,
            tensor_count,
        )

    def decode_back(micro_index, memory_kv):
        _, target_share, grad_share, table_valid, target_valid = micro_inputs(micro_index)
        _, kept = decoder_forward(
            target_share,
            target_valid,
            table_valid,
            memory_kv,
            params,
            cross_bias,
            section_count,
            tensor_count,
        )
        return decoder_backward(
            grad_share,
            memory_kv,
            kept,
            target_valid,
            table_valid,
            params,
            tensor_rank,
            section_count,
            tensor_count,
        )

    def forward_step(previous, micro_index):
        arrived_memory = send_memory(encode(micro_index))
        decoded_share = decode(micro_index, arrived_memory)
        return (previous, (arrived_memory, decoded_share))

    _, (memories, decoded_stack) = lax.scan(
        forward_step, jnp.zeros((), jnp.float32), jnp.arange(MB)
    )

    def backward_step(totals, micro_index):
        memory_kv = lax.dynamic_index_in_dim(memories, micro_index, 0, keepdims=False)
        outgoing, target_grad_share, decoder_grads = decode_back(micro_index, memory_kv)
        totals = masked_add(totals, decoder_grads, not_first)
        arrived = return_memory(outgoing)
        table_grad_share, encoder_grads = encode_back(micro_index, arrived)
        totals = masked_add(totals, encoder_grads, is_first)
        return (totals, (table_grad_share, target_grad_share))

    totals, (table_stack, target_stack) = lax.scan(backward_step, grad_zero, jnp.arange(MB))
    table_all = table_stack.reshape((MB * TB,) + table_stack.shape[2:]).astype(jnp.bfloat16)
    target_all = target_stack.reshape((MB * TB,) + target_stack.shape[2:]).astype(jnp.bfloat16)
    decoded_all = decoded_stack.reshape((MB * TB,) + decoded_stack.shape[2:]).astype(jnp.bfloat16)
    summed_grads = (
        lax.psum(totals[0].astype(jnp.bfloat16), "dp").astype(jnp.float32),
        lax.psum(totals[1].astype(jnp.bfloat16), "dp").astype(jnp.float32),
        lax.psum(totals[2].astype(jnp.bfloat16), "dp").astype(jnp.float32),
        lax.psum(totals[3].astype(jnp.bfloat16), "dp").astype(jnp.float32),
        lax.psum(totals[4].astype(jnp.bfloat16), "dp").astype(jnp.float32),
    )
    holder = lax.dynamic_update_slice(
        jnp.zeros((section_count, 11, features), jnp.float32), totals[5][None], (section_rank, 0, 0)
    )
    vector_total, bias_total = lax.psum((holder, totals[6]), ("section", "dp", "tensor"))
    moved_up = shifted(table_all[:, 1, 0], "section", 1)
    moved_down = shifted(jnp.stack([decoded_all[:, 0, 0], target_all[:, 0, 0]]), "section", -1)
    table_out = jnp.where(is_first, table_all[:, 0, 0], moved_up)
    decoded_out = jnp.where(is_first, moved_down[0], decoded_all[:, 1, 0])
    target_out = jnp.where(is_first, moved_down[1], target_all[:, 1, 0])
    vector_out = lax.dynamic_slice_in_dim(vector_total, section_rank, 1, 0)
    return (
        decoded_out,
        table_out,
        target_out,
        summed_grads[0][None],
        summed_grads[1][None],
        summed_grads[2][None],
        summed_grads[3][None],
        summed_grads[4][None],
        vector_out,
        bias_total,
    )


def solution(mesh):
    in_specs = (
        P("dp", None, None),
        P("dp", None, None),
        P("dp", None, None),
        P("dp"),
        P("dp"),
        P("section", None, None, "tensor"),
        P("section", None, None, "tensor"),
        P("section", None, "tensor"),
        P("section", None, "tensor"),
        P("section", "tensor"),
        P("section", None, None),
        P(),
    )
    out_specs = (
        P("dp", ("section", "tensor"), None),
        P("dp", ("section", "tensor"), None),
        P("dp", ("section", "tensor"), None),
        P("section", None, None, "tensor"),
        P("section", None, None, "tensor"),
        P("section", None, "tensor"),
        P("section", None, "tensor"),
        P("section", "tensor"),
        P("section", None, None),
        P(),
    )
    return jax.shard_map(
        per_device, mesh=mesh, in_specs=in_specs, out_specs=out_specs, check_vma=False
    )
```

profile of v0, /device:TPU:0, one launch (start us, length us, event | category | flops | bytes accessed | tf_op | source)
XLA Modules:
  0.0 2600.6 jit_solution(17952282174005019520)
XLA Ops:
  12.0 779.7 %while.151 = (s32[]{:T(128)}, bf16[2,2,1,1024,256]{4,3,1,2,0:T(8,128)(2,1)}, bf16[2,1,2,1,16,1024]{5,4,0,2,3,1:T(8,128)(2,1)}, s32[2]{0:T(128)}, bf16[2,1024,102...) while((s32[]{:T(128)}, ...), condition=%wide.region_26.27_spmd, body=%wide.region_0.26_spmd.sunk | while | flops 9273741312 | bytes 205370064 | solution.py:668
  21.1 23.9 all-gather.9.cloned.1.call-done
  57.7 30.1 %while.155 = (s32[]{:T(128)}, bf16[2,1,512,4,64]{2,4,3,1,0:T(8,128)(2,1)S(1)}, s32[2]{0:T(128)S(1)}, bf16[1,2,512,4,64]{2,4,3,1,0:T(8,128)(2,1)S(1)}, bf16[1,102...) while((s32[]{:T(128)}, ...), condition=%wide.region_6.6_spmd.clone, body=%wide.region_3.5_spmd.clone.sunk | while | flops 549455872 | bytes 18630824 | solution.py:140
  60.9 7.0 fusion.992
  76.0 7.0 fusion.992
  91.8 50.9 %all-reduce.62.cloned.1.call-done = bf16[1,2,4,128,1024]{4,3,2,1,0:T(8,128)(2,1)} async-done(((bf16[1,2,4,128,1024]{4,3,2,1,0:T(8,128)(2,1)}), bf16[1,2,4,128,1024]{4,3,2,1,0:T(8,128)(2,1)}) %all-reduce.62.cloned.1.call-update) | async-done | bytes 2097168 | tf_op jit(solution)/shard_map/while
  164.7 8.5 all-gather.11.cloned.1.call-done
  173.2 13.2 fusion.784
  190.2 55.9 %all-reduce.64.cloned.1.call-done = (bf16[1,2,4,128,1024]{4,3,2,1,0:T(8,128)(2,1)}, bf16[1,2,4,16,1024]{4,3,2,1,0:T(8,128)(2,1)}) async-done(((bf16[1,2,4,128,1024]{4,3,2,1,0:T(8,128)(2,1)}, bf16[1,2,4,16,1024]{4,3,2,1,0:T(8,128)(2,1)}), (bf16[1,2,4,128,1024]{4,3,2,1,0:T(8,128)(2,1)}, bf16[1,2,4,16,1024]{4,3,2,1,0:T(8,128)(2,1)})) %all-reduce.64.cloned.1.call-update) | async-done | bytes 2359312 | tf_op jit(solution)/shard_map/while
  258.9 19.2 all-gather.13.cloned.1.call-done
  288.3 5.8 all_gather.134
  295.5 13.7 collective-permute-done.1
  319.9 33.0 %all-reduce.66.cloned.1.call-done = bf16[1,2,4,16,1024]{4,3,2,1,0:T(8,128)(2,1)} async-done(((bf16[1,2,4,16,1024]{4,3,2,1,0:T(8,128)(2,1)}), bf16[1,2,4,16,1024]{4,3,2,1,0:T(8,128)(2,1)}) %all-reduce.66.cloned.1.call-update) | async-done | bytes 262160 | tf_op jit(solution)/shard_map/while
  366.5 31.1 %all-reduce.68.cloned.1.call-done = bf16[1,2,4,16,1024]{4,3,2,1,0:T(8,128)(2,1)} async-done(((bf16[1,2,4,16,1024]{4,3,2,1,0:T(8,128)(2,1)}), bf16[1,2,4,16,1024]{4,3,2,1,0:T(8,128)(2,1)}) %all-reduce.68.cloned.1.call-update) | async-done | bytes 262160 | tf_op jit(solution)/shard_map/while
  412.3 21.2 all-gather.9.cloned.1.call-done
  446.2 30.1 %while.155 = (s32[]{:T(128)}, bf16[2,1,512,4,64]{2,4,3,1,0:T(8,128)(2,1)S(1)}, s32[2]{0:T(128)S(1)}, bf16[1,2,512,4,64]{2,4,3,1,0:T(8,128)(2,1)S(1)}, bf16[1,102...) while((s32[]{:T(128)}, ...), condition=%wide.region_6.6_spmd.clone, body=%wide.region_3.5_spmd.clone.sunk | while | flops 549455872 | bytes 18630824 | solution.py:140
  449.4 7.0 fusion.992
  464.5 7.0 fusion.992
  480.3 50.9 %all-reduce.62.cloned.1.call-done = bf16[1,2,4,128,1024]{4,3,2,1,0:T(8,128)(2,1)} async-done(((bf16[1,2,4,128,1024]{4,3,2,1,0:T(8,128)(2,1)}), bf16[1,2,4,128,1024]{4,3,2,1,0:T(8,128)(2,1)}) %all-reduce.62.cloned.1.call-update) | async-done | bytes 2097168 | tf_op jit(solution)/shard_map/while
  553.2 8.5 all-gather.11.cloned.1.call-done
  561.7 13.2 fusion.784
  578.7 55.9 %all-reduce.64.cloned.1.call-done = (bf16[1,2,4,128,1024]{4,3,2,1,0:T(8,128)(2,1)}, bf16[1,2,4,16,1024]{4,3,2,1,0:T(8,128)(2,1)}) async-done(((bf16[1,2,4,128,1024]{4,3,2,1,0:T(8,128)(2,1)}, bf16[1,2,4,16,1024]{4,3,2,1,0:T(8,128)(2,1)}), (bf16[1,2,4,128,1024]{4,3,2,1,0:T(8,128)(2,1)}, bf16[1,2,4,16,1024]{4,3,2,1,0:T(8,128)(2,1)})) %all-reduce.64.cloned.1.call-update) | async-done | bytes 2359312 | tf_op jit(solution)/shard_map/while
  647.4 19.2 all-gather.13.cloned.1.call-done
  684.0 13.7 collective-permute-done.1
  708.4 33.0 %all-reduce.66.cloned.1.call-done = bf16[1,2,4,16,1024]{4,3,2,1,0:T(8,128)(2,1)} async-done(((bf16[1,2,4,16,1024]{4,3,2,1,0:T(8,128)(2,1)}), bf16[1,2,4,16,1024]{4,3,2,1,0:T(8,128)(2,1)}) %all-reduce.66.cloned.1.call-update) | async-done | bytes 262160 | tf_op jit(solution)/shard_map/while
  755.0 31.1 %all-reduce.68.cloned.1.call-done = bf16[1,2,4,16,1024]{4,3,2,1,0:T(8,128)(2,1)} async-done(((bf16[1,2,4,16,1024]{4,3,2,1,0:T(8,128)(2,1)}), bf16[1,2,4,16,1024]{4,3,2,1,0:T(8,128)(2,1)}) %all-reduce.68.cloned.1.call-update) | async-done | bytes 262160 | tf_op jit(solution)/shard_map/while
  792.9 1400.6 %while.154 = (s32[]{:T(128)}, f32[3,1024,256]{2,1,0:T(8,128)}, f32[3,1024,256]{2,1,0:T(8,128)}, f32[1024,1024]{1,0:T(8,128)}, f32[1024,1024]{1,0:T(8,128)}, /*in...) while((s32[]{:T(128)}, f32[3,1024,256]{2,1,0:T(8,128)}, ...), condition=%wide.region_101.102_spmd.clone, body=%wide.region_27.101_spmd.clone.sunk | while | flops 26882195456 | bytes 854489600 | solution.py:681
  829.2 21.8 all-reduce.70.cloned.1.call-done
  870.7 32.1 %all-reduce.72.cloned.1.call-done = bf16[1,2,4,16,1024]{4,3,2,1,0:T(8,128)(2,1)} async-done(((bf16[1,2,4,16,1024]{4,3,2,1,0:T(8,128)(2,1)}), bf16[1,2,4,16,1024]{4,3,2,1,0:T(8,128)(2,1)}) %all-reduce.72.cloned.1.call-update) | async-done | bytes 262160 | tf_op jit(solution)/shard_map/while
  919.3 29.8 %all-reduce.74.cloned.1.call-done = bf16[1,2,4,16,1024]{4,3,2,1,0:T(8,128)(2,1)} async-done(((bf16[1,2,4,16,1024]{4,3,2,1,0:T(8,128)(2,1)}), bf16[1,2,4,16,1024]{4,3,2,1,0:T(8,128)(2,1)}) %all-reduce.74.cloned.1.call-update) | async-done | bytes 262160 | tf_op jit(solution)/shard_map/while
  952.1 6.0 all_gather.139
  964.0 9.2 all-gather.15.cloned.1.call-done
  981.9 19.4 while.156
  1007.3 55.3 %all-reduce.76.cloned.1.call-done = (bf16[1,2,4,16,1024]{4,3,2,1,0:T(8,128)(2,1)}, bf16[1,2,4,128,1024]{4,3,2,1,0:T(8,128)(2,1)}) async-done(((bf16[1,2,4,16,1024]{4,3,2,1,0:T(8,128)(2,1)}, bf16[1,2,4,128,1024]{4,3,2,1,0:T(8,128)(2,1)}), (bf16[1,2,4,16,1024]{4,3,2,1,0:T(8,128)(2,1)}, bf16[1,2,4,128,1024]{4,3,2,1,0:T(8,128)(2,1)})) %all-reduce.76.cloned.1.call-update) | async-done | bytes 2359312 | tf_op jit(solution)/shard_map/while
  1090.7 26.0 %collective-permute-done = bf16[2,1,1024,256]{2,3,1,0:T(8,128)(2,1)S(1)} collective-permute-done((bf16[2,1,1024,256]{2,3,1,0:T(8,128)(2,1)S(1)}, bf16[2,1,1024,256]{2,3,1,0:T(8,128)(2,1)S(1)}, u32[]{:S(2)}, u32[]{:S(2)}) %collective-permute-start) | collective-permute-done | bytes 1048608 | tf_op jit(solution)/shard_map/while/body/eval_jaxpr/ppermute | solution.py:17
  1122.2 14.2 multiply_convert_fusion.12
  1140.3 85.0 %all-reduce.78.cloned.1.call-done = (bf16[1,2,4,128,1024]{4,3,2,1,0:T(8,128)(2,1)}, bf16[1,2,4,128,1024]{4,3,2,1,0:T(8,128)(2,1)}) async-done(((bf16[1,2,4,128,1024]{4,3,2,1,0:T(8,128)(2,1)}, bf16[1,2,4,128,1024]{4,3,2,1,0:T(8,128)(2,1)}), (bf16[1,2,4,128,1024]{4,3,2,1,0:T(8,128)(2,1)}, bf16[1,2,4,128,1024]{4,3,2,1,0:T(8,128)(2,1)})) %all-reduce.78.cloned.1.call-update) | async-done | bytes 4194320 | tf_op jit(solution)/shard_map/while
  1256.0 6.8 fusion.963
  1292.0 47.1 %all-reduce.80.cloned.1.call-done = (bf16[1,2,4,16,1024]{4,3,2,1,0:T(8,128)(2,1)}, bf16[1,2,4,128,1024]{4,3,2,1,0:T(8,128)(2,1)}) async-done(((bf16[1,2,4,16,1024]{4,3,2,1,0:T(8,128)(2,1)}, bf16[1,2,4,128,1024]{4,3,2,1,0:T(8,128)(2,1)}), (bf16[1,2,4,16,1024]{4,3,2,1,0:T(8,128)(2,1)}, bf16[1,2,4,128,1024]{4,3,2,1,0:T(8,128)(2,1)})) %all-reduce.80.cloned.1.call-update) | async-done | bytes 2359312 | tf_op jit(solution)/shard_map/while
  1354.7 6.3 all_gather.144
  1383.1 28.1 %while.157 = (s32[]{:T(128)}, f32[1,1024,4,64]{1,3,2,0:T(8,128)S(1)}, f32[1,1024,4,64]{1,3,2,0:T(8,128)}, bf16[2,1,512,4,64]{2,4,3,1,0:T(8,128)(2,1)}, s32[2]{0:...) while((s32[]{:T(128)}, ...), condition=%wide.region_71.71_spmd.clone, body=%wide.region_69.70_spmd.clone.sunk | while | flops 1375075328 | bytes 82899280 | solution.py:195
  1440.1 48.0 %all-reduce.82.cloned.1.call-done = (bf16[1,2,4,128,1024]{4,3,2,1,0:T(8,128)(2,1)}, bf16[1,2,4,16,1024]{4,3,2,1,0:T(8,128)(2,1)}) async-done(((bf16[1,2,4,128,1024]{4,3,2,1,0:T(8,128)(2,1)}, bf16[1,2,4,16,1024]{4,3,2,1,0:T(8,128)(2,1)}), (bf16[1,2,4,128,1024]{4,3,2,1,0:T(8,128)(2,1)}, bf16[1,2,4,16,1024]{4,3,2,1,0:T(8,128)(2,1)})) %all-reduce.82.cloned.1.call-update) | async-done | bytes 2359312 | tf_op jit(solution)/shard_map/while
  1524.7 21.9 all-reduce.70.cloned.1.call-done
  1566.2 32.1 %all-reduce.72.cloned.1.call-done = bf16[1,2,4,16,1024]{4,3,2,1,0:T(8,128)(2,1)} async-done(((bf16[1,2,4,16,1024]{4,3,2,1,0:T(8,128)(2,1)}), bf16[1,2,4,16,1024]{4,3,2,1,0:T(8,128)(2,1)}) %all-reduce.72.cloned.1.call-update) | async-done | bytes 262160 | tf_op jit(solution)/shard_map/while
  1614.9 29.8 %all-reduce.74.cloned.1.call-done = bf16[1,2,4,16,1024]{4,3,2,1,0:T(8,128)(2,1)} async-done(((bf16[1,2,4,16,1024]{4,3,2,1,0:T(8,128)(2,1)}), bf16[1,2,4,16,1024]{4,3,2,1,0:T(8,128)(2,1)}) %all-reduce.74.cloned.1.call-update) | async-done | bytes 262160 | tf_op jit(solution)/shard_map/while
  1647.7 6.2 all_gather.139
  1659.8 9.0 all-gather.15.cloned.1.call-done
  1677.5 19.4 while.156
  1702.9 55.3 %all-reduce.76.cloned.1.call-done = (bf16[1,2,4,16,1024]{4,3,2,1,0:T(8,128)(2,1)}, bf16[1,2,4,128,1024]{4,3,2,1,0:T(8,128)(2,1)}) async-done(((bf16[1,2,4,16,1024]{4,3,2,1,0:T(8,128)(2,1)}, bf16[1,2,4,128,1024]{4,3,2,1,0:T(8,128)(2,1)}), (bf16[1,2,4,16,1024]{4,3,2,1,0:T(8,128)(2,1)}, bf16[1,2,4,128,1024]{4,3,2,1,0:T(8,128)(2,1)})) %all-reduce.76.cloned.1.call-update) | async-done | bytes 2359312 | tf_op jit(solution)/shard_map/while
  1786.0 26.0 %collective-permute-done = bf16[2,1,1024,256]{2,3,1,0:T(8,128)(2,1)S(1)} collective-permute-done((bf16[2,1,1024,256]{2,3,1,0:T(8,128)(2,1)S(1)}, bf16[2,1,1024,256]{2,3,1,0:T(8,128)(2,1)S(1)}, u32[]{:S(2)}, u32[]{:S(2)}) %collective-permute-start) | collective-permute-done | bytes 1048608 | tf_op jit(solution)/shard_map/while/body/eval_jaxpr/ppermute | solution.py:17
  1817.6 14.2 multiply_convert_fusion.12
  1835.7 84.9 %all-reduce.78.cloned.1.call-done = (bf16[1,2,4,128,1024]{4,3,2,1,0:T(8,128)(2,1)}, bf16[1,2,4,128,1024]{4,3,2,1,0:T(8,128)(2,1)}) async-done(((bf16[1,2,4,128,1024]{4,3,2,1,0:T(8,128)(2,1)}, bf16[1,2,4,128,1024]{4,3,2,1,0:T(8,128)(2,1)}), (bf16[1,2,4,128,1024]{4,3,2,1,0:T(8,128)(2,1)}, bf16[1,2,4,128,1024]{4,3,2,1,0:T(8,128)(2,1)})) %all-reduce.78.cloned.1.call-update) | async-done | bytes 4194320 | tf_op jit(solution)/shard_map/while
  1951.3 6.8 fusion.963
  1968.0 6.5 fusion.964
  1989.6 44.8 %all-reduce.80.cloned.1.call-done = (bf16[1,2,4,16,1024]{4,3,2,1,0:T(8,128)(2,1)}, bf16[1,2,4,128,1024]{4,3,2,1,0:T(8,128)(2,1)}) async-done(((bf16[1,2,4,16,1024]{4,3,2,1,0:T(8,128)(2,1)}, bf16[1,2,4,128,1024]{4,3,2,1,0:T(8,128)(2,1)}), (bf16[1,2,4,16,1024]{4,3,2,1,0:T(8,128)(2,1)}, bf16[1,2,4,128,1024]{4,3,2,1,0:T(8,128)(2,1)})) %all-reduce.80.cloned.1.call-update) | async-done | bytes 2359312 | tf_op jit(solution)/shard_map/while
  2050.0 6.1 all_gather.144
  2078.3 28.1 %while.157 = (s32[]{:T(128)}, f32[1,1024,4,64]{1,3,2,0:T(8,128)S(1)}, f32[1,1024,4,64]{1,3,2,0:T(8,128)}, bf16[2,1,512,4,64]{2,4,3,1,0:T(8,128)(2,1)}, s32[2]{0:...) while((s32[]{:T(128)}, ...), condition=%wide.region_71.71_spmd.clone, body=%wide.region_69.70_spmd.clone.sunk | while | flops 1375075328 | bytes 82899280 | solution.py:195
  2129.7 8.7 fusion.960
  2138.5 44.7 %all-reduce.82.cloned.1.call-done = (bf16[1,2,4,128,1024]{4,3,2,1,0:T(8,128)(2,1)}, bf16[1,2,4,16,1024]{4,3,2,1,0:T(8,128)(2,1)}) async-done(((bf16[1,2,4,128,1024]{4,3,2,1,0:T(8,128)(2,1)}, bf16[1,2,4,16,1024]{4,3,2,1,0:T(8,128)(2,1)}), (bf16[1,2,4,128,1024]{4,3,2,1,0:T(8,128)(2,1)}, bf16[1,2,4,16,1024]{4,3,2,1,0:T(8,128)(2,1)})) %all-reduce.82.cloned.1.call-update) | async-done | bytes 2359312 | tf_op jit(solution)/shard_map/while
  2195.9 6.2 convert_bitcast_fusion.5
  2213.0 11.7 psum.53
  2225.3 38.1 %psum.55 = f32[1024]{0:T(1024)} all-reduce(f32[1024]{0:T(1024)S(1)} %copy-done.159), channel_id=1, replica_groups=mesh['section'=2,'dp'=4,'tensor'=4] {'section','dp','tensor'}, use_global_device_ids=true, to_apply=%region_108.109 | all-reduce | flops 1024 | bytes 8192 | tf_op jit(solution)/shard_map/psum | solution.py:695
  2263.4 56.7 %all-reduce.58.cloned.1.call-done = f32[2,11,1024]{2,0,1:T(2,128)} async-done(((f32[2,11,1024]{2,0,1:T(2,128)}), f32[2,11,1024]{2,0,1:T(2,128)}) %all-reduce.58.cloned.1.call-update) | async-done | bytes 90128 | tf_op jit(solution)/shard_map/psum | solution.py:695
  2323.2 258.9 %all-reduce.60.cloned.1.call-done = (bf16[1,3,1024,256]{3,2,1,0:T(8,128)(2,1)}, bf16[1,3,1024,256]{3,2,1,0:T(8,128)(2,1)}, bf16[1,1024,1024]{2,1,0:T(8,128)(2,1)}, bf16[1,1024,1024]{2,1,0:T(8,128)(2,1)}) async-done(((bf16[1,3,1024,256]{3,2,1,0:T(8,128)(2,1)}, bf16[1,3,1024,256]{3,2,1,0:T(8,128)(2,1)}, bf16[1,1024,1024]{2,1,0:T(8,128)(2,1)}, bf16[1,1024,1024]{2,1,0:T(8,128)(2,1)}), ...) | async-done | bytes 7340048 | tf_op jit(solution)/shard_map/psum | solution.py:686
  (1531 shorter events, 852.3 us)
Async XLA Ops:
  12.0 33.0 %all-gather.9.cloned.1.call-start = ((), (), s32[]{:S(2)}) async-start(), calls=%async_computation.2 | async-start | bytes 2621440 | tf_op jit(solution)/shard_map/while/body/eval_jaxpr/all_gather | solution.py:69
  15.5 236.0 %copy-start.72 = (f32[1,1024]{1,0:T(1,128)}, f32[1,1024]{1,0:T(1,128)S(1)}, u32[]{:S(2)}) copy-start(f32[1,1024]{1,0:T(1,128)S(1)} %get-tuple-element.2059) | copy-start | bytes 12292 | tf_op jit(solution)/shard_map/while
  15.5 236.0 %copy-start.74 = (f32[1,1024]{1,0:T(1,128)}, f32[1,1024]{1,0:T(1,128)S(1)}, u32[]{:S(2)}) copy-start(f32[1,1024]{1,0:T(1,128)S(1)} %get-tuple-element.2057) | copy-start | bytes 12292 | tf_op jit(solution)/shard_map/while
  15.5 236.0 %copy-start.103 = (f32[1,1024]{1,0:T(1,128)}, f32[1,1024]{1,0:T(1,128)S(1)}, u32[]{:S(2)}) copy-start(f32[1,1024]{1,0:T(1,128)S(1)} %get-tuple-element.2055) | copy-start | bytes 12292 | tf_op jit(solution)/shard_map/while
  15.5 236.0 %copy-start.105 = (f32[1,1024]{1,0:T(1,128)}, f32[1,1024]{1,0:T(1,128)S(1)}, u32[]{:S(2)}) copy-start(f32[1,1024]{1,0:T(1,128)S(1)} %get-tuple-element.2056) | copy-start | bytes 12292 | tf_op jit(solution)/shard_map/while
  19.6 123.1 %all-reduce.62.cloned.1.call-start = ((), (), s32[]{:S(2)}) async-start(), calls=%async_computation.3 | async-start | bytes 4194304 | tf_op jit(solution)/shard_map/while
  21.1 259.6 %copy-start.167 = (f32[1,256]{1,0:T(1,128)}, f32[1,256]{1,0:T(1,128)S(1)}, u32[]{:S(2)}) copy-start(f32[1,256]{1,0:T(1,128)S(1)} %get-tuple-element.2069) | copy-start | bytes 3076 | tf_op jit(solution)/shard_map/while
  91.1 82.1 %all-gather.11.cloned.1.call-start = ((), (), s32[]{:S(2)}) async-start(), calls=%async_computation.4 | async-start | bytes 2621440 | tf_op jit(solution)/shard_map/while/body/eval_jaxpr/all_gather | solution.py:69
  150.4 95.8 %all-reduce.64.cloned.1.call-start = ((), (), s32[]{:S(2)}) async-start(), calls=%async_computation.5 | async-start | bytes 4718592 | tf_op jit(solution)/shard_map/while
  190.2 87.9 %all-gather.13.cloned.1.call-start = ((), (), s32[]{:S(2)}) async-start(), calls=%async_computation.6 | async-start | bytes 2621440 | tf_op jit(solution)/shard_map/while/body/eval_jaxpr/all_gather | solution.py:69
  255.3 97.5 %all-reduce.66.cloned.1.call-start = ((), (), s32[]{:S(2)}) async-start(), calls=%async_computation.7 | async-start | bytes 524288 | tf_op jit(solution)/shard_map/while
  282.5 26.6 %collective-permute-start.1 = (bf16[2,1,1024,256]{3,2,1,0:T(8,128)(2,1)}, bf16[2,1,1024,256]{3,2,1,0:T(8,128)(2,1)S(1)}, u32[]{:S(2)}, u32[]{:S(2)}) collective-permute-start(bf16[2,1,1024,256]{3,2,1,0:T(8,128)(2,1)} %pad_maximum_fusion.5), channel_id=1, source_target_pairs={{0,16},{1,17},{2,18},{3,19},{4,20},{5,21},{6,22},{7,23},{8,24},{9,... | collective-permute-start | bytes 3145736 | tf_op jit(solution)/shard_map/while/body/eval_jaxpr/ppermute | solution.py:17
  319.8 77.8 %all-reduce.68.cloned.1.call-start = ((), (), s32[]{:S(2)}) async-start(), calls=%async_computation.8 | async-start | bytes 524288 | tf_op jit(solution)/shard_map/while
  403.2 30.3 %all-gather.9.cloned.1.call-start = ((), (), s32[]{:S(2)}) async-start(), calls=%async_computation.2 | async-start | bytes 2621440 | tf_op jit(solution)/shard_map/while/body/eval_jaxpr/all_gather | solution.py:69
  406.7 233.3 %copy-start.72 = (f32[1,1024]{1,0:T(1,128)}, f32[1,1024]{1,0:T(1,128)S(1)}, u32[]{:S(2)}) copy-start(f32[1,1024]{1,0:T(1,128)S(1)} %get-tuple-element.2059) | copy-start | bytes 12292 | tf_op jit(solution)/shard_map/while
  406.7 233.3 %copy-start.74 = (f32[1,1024]{1,0:T(1,128)}, f32[1,1024]{1,0:T(1,128)S(1)}, u32[]{:S(2)}) copy-start(f32[1,1024]{1,0:T(1,128)S(1)} %get-tuple-element.2057) | copy-start | bytes 12292 | tf_op jit(solution)/shard_map/while
  406.7 233.3 %copy-start.103 = (f32[1,1024]{1,0:T(1,128)}, f32[1,1024]{1,0:T(1,128)S(1)}, u32[]{:S(2)}) copy-start(f32[1,1024]{1,0:T(1,128)S(1)} %get-tuple-element.2055) | copy-start | bytes 12292 | tf_op jit(solution)/shard_map/while
  406.7 233.3 %copy-start.105 = (f32[1,1024]{1,0:T(1,128)}, f32[1,1024]{1,0:T(1,128)S(1)}, u32[]{:S(2)}) copy-start(f32[1,1024]{1,0:T(1,128)S(1)} %get-tuple-element.2056) | copy-start | bytes 12292 | tf_op jit(solution)/shard_map/while
  410.8 120.4 %all-reduce.62.cloned.1.call-start = ((), (), s32[]{:S(2)}) async-start(), calls=%async_computation.3 | async-start | bytes 4194304 | tf_op jit(solution)/shard_map/while
  412.3 256.9 %copy-start.167 = (f32[1,256]{1,0:T(1,128)}, f32[1,256]{1,0:T(1,128)S(1)}, u32[]{:S(2)}) copy-start(f32[1,256]{1,0:T(1,128)S(1)} %get-tuple-element.2069) | copy-start | bytes 3076 | tf_op jit(solution)/shard_map/while
  479.6 82.1 %all-gather.11.cloned.1.call-start = ((), (), s32[]{:S(2)}) async-start(), calls=%async_computation.4 | async-start | bytes 2621440 | tf_op jit(solution)/shard_map/while/body/eval_jaxpr/all_gather | solution.py:69
  538.9 95.8 %all-reduce.64.cloned.1.call-start = ((), (), s32[]{:S(2)}) async-start(), calls=%async_computation.5 | async-start | bytes 4718592 | tf_op jit(solution)/shard_map/while
  578.7 87.9 %all-gather.13.cloned.1.call-start = ((), (), s32[]{:S(2)}) async-start(), calls=%async_computation.6 | async-start | bytes 2621440 | tf_op jit(solution)/shard_map/while/body/eval_jaxpr/all_gather | solution.py:69
  643.8 97.5 %all-reduce.66.cloned.1.call-start = ((), (), s32[]{:S(2)}) async-start(), calls=%async_computation.7 | async-start | bytes 524288 | tf_op jit(solution)/shard_map/while
  671.0 26.6 %collective-permute-start.1 = (bf16[2,1,1024,256]{3,2,1,0:T(8,128)(2,1)}, bf16[2,1,1024,256]{3,2,1,0:T(8,128)(2,1)S(1)}, u32[]{:S(2)}, u32[]{:S(2)}) collective-permute-start(bf16[2,1,1024,256]{3,2,1,0:T(8,128)(2,1)} %pad_maximum_fusion.5), channel_id=1, source_target_pairs={{0,16},{1,17},{2,18},{3,19},{4,20},{5,21},{6,22},{7,23},{8,24},{9,... | collective-permute-start | bytes 3145736 | tf_op jit(solution)/shard_map/while/body/eval_jaxpr/ppermute | solution.py:17
  708.3 77.8 %all-reduce.68.cloned.1.call-start = ((), (), s32[]{:S(2)}) async-start(), calls=%async_computation.8 | async-start | bytes 524288 | tf_op jit(solution)/shard_map/while
  799.5 51.5 %all-reduce.70.cloned.1.call-start = ((), (), s32[]{:S(2)}) async-start(), calls=%async_computation.9 | async-start | bytes 524288 | tf_op jit(solution)/shard_map/while
  806.6 96.2 %copy-start.37 = (bf16[1,128,1024]{2,1,0:T(8,128)(2,1)}, bf16[1,128,1024]{2,1,0:T(8,128)(2,1)S(1)}, u32[]{:S(2)}) copy-start(bf16[1,128,1024]{2,1,0:T(8,128)(2,1)S(1)} %constant_dynamic-slice_fusion.22) | copy-start | bytes 786436 | tf_op jit(solution)/shard_map/while
  818.9 83.9 %all-reduce.72.cloned.1.call-start = ((), (), s32[]{:S(2)}) async-start(), calls=%async_computation.10 | async-start | bytes 524288 | tf_op jit(solution)/shard_map/while
  870.6 78.5 %all-reduce.74.cloned.1.call-start = ((), (), s32[]{:S(2)}) async-start(), calls=%async_computation.11 | async-start | bytes 524288 | tf_op jit(solution)/shard_map/while
  904.5 163.4 %copy-start.102 = (f32[2,16]{1,0:T(2,128)}, f32[2,16]{1,0:T(2,128)S(1)}, u32[]{:S(2)}) copy-start(f32[2,16]{1,0:T(2,128)S(1)} %broadcast_multiply_fusion.31) | copy-start | bytes 388 | tf_op jit(solution)/shard_map/while
  904.6 163.2 %copy-start.116 = (f32[2,16]{1,0:T(2,128)}, f32[2,16]{1,0:T(2,128)S(1)}, u32[]{:S(2)}) copy-start(f32[2,16]{1,0:T(2,128)S(1)} %fusion.933) | copy-start | bytes 388 | tf_op jit(solution)/shard_map/while
  917.0 56.2 %all-gather.15.cloned.1.call-start = ((), (), s32[]{:S(2)}) async-start(), calls=%async_computation.12 | async-start | bytes 2621440 | tf_op jit(solution)/shard_map/while/body/eval_jaxpr/all_gather | solution.py:69
  919.2 143.4 %all-reduce.76.cloned.1.call-start = ((), (), s32[]{:S(2)}) async-start(), calls=%async_computation.13 | async-start | bytes 4718592 | tf_op jit(solution)/shard_map/while
  952.0 115.9 %copy-start.130 = (f32[2,16]{1,0:T(2,128)}, f32[2,16]{1,0:T(2,128)S(1)}, u32[]{:S(2)}) copy-start(f32[2,16]{1,0:T(2,128)S(1)} %negate_multiply_fusion.16) | copy-start | bytes 388 | tf_op jit(solution)/shard_map/while
  1006.6 115.6 %all-gather.17.cloned.1.call-start = ((), (), s32[]{:S(2)}) async-start(), calls=%async_computation.14 | async-start | bytes 2621440 | tf_op jit(solution)/shard_map/while/body/eval_jaxpr/all_gather | solution.py:69
  1085.4 139.9 %all-reduce.78.cloned.1.call-start = ((), (), s32[]{:S(2)}) async-start(), calls=%async_computation.15 | async-start | bytes 8388608 | tf_op jit(solution)/shard_map/while
  1089.4 27.3 %collective-permute-start = (bf16[2,1,1024,256]{2,3,1,0:T(8,128)(2,1)S(1)}, bf16[2,1,1024,256]{2,3,1,0:T(8,128)(2,1)S(1)}, u32[]{:S(2)}, u32[]{:S(2)}) collective-permute-start(bf16[2,1,1024,256]{2,3,1,0:T(8,128)(2,1)S(1)} %pad_maximum_fusion.6), channel_id=1, source_target_pairs={{16,0},{17,1},{18,2},{19,3},{20,4},{21,5},{22,6},{23,7},{24,8},{25... | collective-permute-start | bytes 3145736 | tf_op jit(solution)/shard_map/while/body/eval_jaxpr/ppermute | solution.py:17
  1140.2 115.7 %all-gather.19.cloned.1.call-start = ((), (), s32[]{:S(2)}) async-start(), calls=%async_computation.16 | async-start | bytes 2621440 | tf_op jit(solution)/shard_map/while/body/eval_jaxpr/all_gather | solution.py:83
  1233.1 47.1 %all-gather.21.cloned.1.call-start = ((), (), s32[]{:S(2)}) async-start(), calls=%async_computation.18 | async-start | bytes 2621440 | tf_op jit(solution)/shard_map/while/body/eval_jaxpr/all_gather | solution.py:69
  1233.8 105.2 %all-reduce.80.cloned.1.call-start = ((), (), s32[]{:S(2)}) async-start(), calls=%async_computation.17 | async-start | bytes 4718592 | tf_op jit(solution)/shard_map/while
  1272.2 104.7 %all-gather.23.cloned.1.call-start = ((), (), s32[]{:S(2)}) async-start(), calls=%async_computation.19 | async-start | bytes 2621440 | tf_op jit(solution)/shard_map/while/body/eval_jaxpr/all_gather | solution.py:83
  1353.3 134.7 %all-reduce.82.cloned.1.call-start = ((), (), s32[]{:S(2)}) async-start(), calls=%async_computation.20 | async-start | bytes 4718592 | tf_op jit(solution)/shard_map/while
  1495.0 51.6 %all-reduce.70.cloned.1.call-start = ((), (), s32[]{:S(2)}) async-start(), calls=%async_computation.9 | async-start | bytes 524288 | tf_op jit(solution)/shard_map/while
  1502.1 96.2 %copy-start.37 = (bf16[1,128,1024]{2,1,0:T(8,128)(2,1)}, bf16[1,128,1024]{2,1,0:T(8,128)(2,1)S(1)}, u32[]{:S(2)}) copy-start(bf16[1,128,1024]{2,1,0:T(8,128)(2,1)S(1)} %constant_dynamic-slice_fusion.22) | copy-start | bytes 786436 | tf_op jit(solution)/shard_map/while
  1514.4 83.9 %all-reduce.72.cloned.1.call-start = ((), (), s32[]{:S(2)}) async-start(), calls=%async_computation.10 | async-start | bytes 524288 | tf_op jit(solution)/shard_map/while
  1566.2 78.5 %all-reduce.74.cloned.1.call-start = ((), (), s32[]{:S(2)}) async-start(), calls=%async_computation.11 | async-start | bytes 524288 | tf_op jit(solution)/shard_map/while
  1600.0 163.4 %copy-start.102 = (f32[2,16]{1,0:T(2,128)}, f32[2,16]{1,0:T(2,128)S(1)}, u32[]{:S(2)}) copy-start(f32[2,16]{1,0:T(2,128)S(1)} %broadcast_multiply_fusion.31) | copy-start | bytes 388 | tf_op jit(solution)/shard_map/while
  1600.2 163.2 %copy-start.116 = (f32[2,16]{1,0:T(2,128)}, f32[2,16]{1,0:T(2,128)S(1)}, u32[]{:S(2)}) copy-start(f32[2,16]{1,0:T(2,128)S(1)} %fusion.933) | copy-start | bytes 388 | tf_op jit(solution)/shard_map/while
  1612.5 56.2 %all-gather.15.cloned.1.call-start = ((), (), s32[]{:S(2)}) async-start(), calls=%async_computation.12 | async-start | bytes 2621440 | tf_op jit(solution)/shard_map/while/body/eval_jaxpr/all_gather | solution.py:69
  1614.8 143.4 %all-reduce.76.cloned.1.call-start = ((), (), s32[]{:S(2)}) async-start(), calls=%async_computation.13 | async-start | bytes 4718592 | tf_op jit(solution)/shard_map/while
  1647.6 115.9 %copy-start.130 = (f32[2,16]{1,0:T(2,128)}, f32[2,16]{1,0:T(2,128)S(1)}, u32[]{:S(2)}) copy-start(f32[2,16]{1,0:T(2,128)S(1)} %negate_multiply_fusion.16) | copy-start | bytes 388 | tf_op jit(solution)/shard_map/while
  1702.2 115.4 %all-gather.17.cloned.1.call-start = ((), (), s32[]{:S(2)}) async-start(), calls=%async_computation.14 | async-start | bytes 2621440 | tf_op jit(solution)/shard_map/while/body/eval_jaxpr/all_gather | solution.py:69
  1781.0 139.6 %all-reduce.78.cloned.1.call-start = ((), (), s32[]{:S(2)}) async-start(), calls=%async_computation.15 | async-start | bytes 8388608 | tf_op jit(solution)/shard_map/while
  1784.7 27.3 %collective-permute-start = (bf16[2,1,1024,256]{2,3,1,0:T(8,128)(2,1)S(1)}, bf16[2,1,1024,256]{2,3,1,0:T(8,128)(2,1)S(1)}, u32[]{:S(2)}, u32[]{:S(2)}) collective-permute-start(bf16[2,1,1024,256]{2,3,1,0:T(8,128)(2,1)S(1)} %pad_maximum_fusion.6), channel_id=1, source_target_pairs={{16,0},{17,1},{18,2},{19,3},{20,4},{21,5},{22,6},{23,7},{24,8},{25... | collective-permute-start | bytes 3145736 | tf_op jit(solution)/shard_map/while/body/eval_jaxpr/ppermute | solution.py:17
  1835.6 115.7 %all-gather.19.cloned.1.call-start = ((), (), s32[]{:S(2)}) async-start(), calls=%async_computation.16 | async-start | bytes 2621440 | tf_op jit(solution)/shard_map/while/body/eval_jaxpr/all_gather | solution.py:83
  1928.4 47.1 %all-gather.21.cloned.1.call-start = ((), (), s32[]{:S(2)}) async-start(), calls=%async_computation.18 | async-start | bytes 2621440 | tf_op jit(solution)/shard_map/while/body/eval_jaxpr/all_gather | solution.py:69
  1929.2 105.2 %all-reduce.80.cloned.1.call-start = ((), (), s32[]{:S(2)}) async-start(), calls=%async_computation.17 | async-start | bytes 4718592 | tf_op jit(solution)/shard_map/while
  1967.6 104.5 %all-gather.23.cloned.1.call-start = ((), (), s32[]{:S(2)}) async-start(), calls=%async_computation.19 | async-start | bytes 2621440 | tf_op jit(solution)/shard_map/while/body/eval_jaxpr/all_gather | solution.py:83
  2048.7 134.5 %all-reduce.82.cloned.1.call-start = ((), (), s32[]{:S(2)}) async-start(), calls=%async_computation.20 | async-start | bytes 4718592 | tf_op jit(solution)/shard_map/while
  2193.5 126.6 %all-reduce.58.cloned.1.call-start = ((), (), s32[]{:S(2)}) async-start(), calls=%async_computation | async-start | bytes 180224 | tf_op jit(solution)/shard_map/psum | solution.py:695
  2195.9 386.2 %all-reduce.60.cloned.1.call-start = ((), (), s32[]{:S(2)}) async-start(), calls=%async_computation.1 | async-start | bytes 14680064 | tf_op jit(solution)/shard_map/psum | solution.py:686
  2208.2 114.1 %collective-permute-start.3 = (bf16[2,128,1024]{2,1,0:T(8,128)(2,1)S(1)}, bf16[2,128,1024]{2,1,0:T(8,128)(2,1)S(1)}, u32[]{:S(2)}, u32[]{:S(2)}) collective-permute-start(bf16[2,128,1024]{2,1,0:T(8,128)(2,1)S(1)} %slice_bitcast_fusion.3), channel_id=1, source_target_pairs={{0,16},{1,17},{2,18},{3,19},{4,20},{5,21},{6,22},{7,23},{8,24},{9,... | collective-permute-start | bytes 1572872 | tf_op jit(solution)/shard_map/ppermute | solution.py:17
  2211.7 110.0 %collective-permute-start.2 = (bf16[2,2,16,1024]{3,2,1,0:T(8,128)(2,1)S(1)}, bf16[2,2,16,1024]{3,2,1,0:T(8,128)(2,1)S(1)}, u32[]{:S(2)}, u32[]{:S(2)}) collective-permute-start(bf16[2,2,16,1024]{3,2,1,0:T(8,128)(2,1)S(1)} %pad_maximum_fusion.2), channel_id=1, source_target_pairs={{16,0},{17,1},{18,2},{19,3},{20,4},{21,5},{22,6},{23,7},{24,8},{25... | collective-permute-start | bytes 393224 | tf_op jit(solution)/shard_map/ppermute | solution.py:17
  (377 other events, 5130.5 us)
Sparse Core Ops, SparseCore 0:
  19.7 25.2 all-gather.8
  91.2 51.3 all-reduce.61
  150.5 22.6 all-gather.10
  190.3 55.8 all-reduce.63
  255.5 22.6 all-gather.12
  319.9 32.8 all-reduce.65
  365.6 31.9 all-reduce.67
  410.9 22.5 all-gather.8
  479.7 51.3 all-reduce.61
  539.0 22.6 all-gather.10
  578.8 55.8 all-reduce.63
  644.0 22.6 all-gather.12
  708.4 32.8 all-reduce.65
  754.1 31.9 all-reduce.67
  819.0 31.9 all-reduce.69
  870.7 31.9 all-reduce.71
  917.1 31.9 all-reduce.73
  950.5 22.6 all-gather.14
  1006.7 55.8 all-reduce.75
  1085.5 22.6 all-gather.16
  1140.4 84.8 all-reduce.77
  1233.2 22.7 all-gather.18
  1257.6 22.5 all-gather.20
  1283.2 55.8 all-reduce.79
  1353.4 22.6 all-gather.22
  1432.1 55.8 all-reduce.81
  1514.5 32.0 all-reduce.69
  1566.3 31.9 all-reduce.71
  1612.7 31.9 all-reduce.73
  1646.1 22.6 all-gather.14
  1702.3 55.8 all-reduce.75
  1781.1 22.6 all-gather.16
  1835.7 84.8 all-reduce.77
  1928.5 22.7 all-gather.18
  1952.9 22.5 all-gather.20
  1978.5 55.8 all-reduce.79
  2048.8 22.6 all-gather.22
  2127.3 55.8 all-reduce.81
Sparse Core Ops, SparseCore 1:
  2200.1 119.9 all-reduce.57
  2323.2 258.9 all-reduce.59
where the time goes:
time: 2630 us; the launch traced here: 2600 us
  waiting for transfers between devices  1500 us (57%)
  matrix products  465 us (18%)
  other arithmetic  249 us (9%)
  blocking collectives  155 us (6%)
  local copies, waits for them, and re-layouts  151 us (6%)
  loops' own time  46.8 us (2%)
    while x60, waiting for transfers between devices  976 us
    psum x1, waiting for transfers between devices, per_device(): lax.psum(totals[0].astype(jnp.bfloat16), 'dp').astype(jnp.float32)  259 us
    dot_general x50, matrix products, project(): jnp.einsum('gld,dk->glk', inputs, matrix, preferred_element_type=jnp.floa...  149 us
    all_gather x12, waiting for transfers between devices, gather_rows(): gathered = lax.all_gather(share_part, 'tensor', axis=2, tiled=True)  122 us
    dot_general x42, matrix products, project_back(): jnp.einsum('glk,dk->gld', inputs, matrix, preferred_element_type=jnp.floa...  97.8 us
    dot_general x32, matrix products, weight_grad(): jnp.einsum('gld,glk->dk', inputs, gradient, preferred_element_type=jnp.fl...  88.2 us
    ppermute x6, waiting for transfers between devices, shifted(): lax.ppermute(value, axis, [(source, source + steps) for source in range(i...  79.4 us
    all_gather x12, blocking collectives, gather_rows(): gathered = lax.all_gather(share_part, 'tensor', axis=2, tiled=True)  69.5 us
  transfers between devices with their start and end apart: 46, of which 40 were waited for; matrix products, arithmetic and copies ran while one was open for 10% of the time, Pallas kernels for 0%

commit v1 on v0

v1 whole, which is shorter than its diff:
```python
import jax
import jax.numpy as jnp
from jax import lax
from jax.sharding import PartitionSpec as P

HEAD = 64
SCALING = HEAD ** (-0.5)
EPSILON = 1e-05

bf16 = jnp.bfloat16
f32 = jnp.float32


def mm(a, b):
    return lax.dot_general(a, b, (((1,), (0,)), ((), ())), preferred_element_type=f32)


def mm_t(a, b):
    return lax.dot_general(a, b, (((1,), (1,)), ((), ())), preferred_element_type=f32)


def t_mm(a, b):
    return lax.dot_general(a, b, (((0,), (0,)), ((), ())), preferred_element_type=f32)


def norm_stats(summed):
    centered = summed - jnp.mean(summed, axis=-1, keepdims=True)
    spread = jnp.mean(centered * centered, axis=-1, keepdims=True)
    scale = lax.rsqrt(spread + EPSILON)
    return centered * scale, scale


def layer_norm(summed, gain, shift):
    return norm_stats(summed)[0] * gain + shift


def norm_backward(summed, gain, gradient):
    unit, scale = norm_stats(summed)
    scaled = gradient * gain
    inner = scaled - jnp.mean(scaled, axis=-1, keepdims=True)
    inner = inner - unit * jnp.mean(scaled * unit, axis=-1, keepdims=True)
    return (
        inner * scale,
        jnp.sum(gradient * unit, axis=0),
        jnp.sum(gradient, axis=0),
    )


def gelu_pair(before):
    cumulative = 0.5 * (1.0 + lax.erf(before * (0.5 ** 0.5)))
    density = jnp.exp(-0.5 * before * before) * 0.3989422804014327
    return before * cumulative, cumulative + before * density


def flip(value, bit):
    count = lax.axis_size("tensor")
    return lax.ppermute(value, "tensor", [(i, i ^ (1 << bit)) for i in range(count)])


def tensor_bits():
    return lax.axis_size("tensor").bit_length() - 1


def reduce_share(rows):
    bits = tensor_bits()
    for bit in range(bits):
        half = rows.shape[0] // 2
        sent = flip(rows[half:].astype(bf16), bit)
        rows = rows[:half].astype(f32) + sent.astype(f32)
    return rows


def gather_share(share):
    for bit in reversed(range(tensor_bits())):
        share = jnp.concatenate([share, flip(share, bit)], axis=0)
    return share


def reduce_half(rows):
    half = rows[0].astype(f32) + flip(rows[1].astype(bf16), 0).astype(f32)
    for bit in range(1, tensor_bits()):
        half = half.astype(bf16)
        half = half.astype(f32) + flip(half, bit).astype(f32)
    return half


def gather_half(half):
    return jnp.concatenate([half, flip(half, 0)], axis=0)


def to_second(value):
    return lax.ppermute(value, "section", [(0, 1)])


def to_first(value):
    return lax.ppermute(value, "section", [(1, 0)])


def split_heads(value):
    return value.reshape(value.shape[0], value.shape[1], -1, HEAD)


def attention_forward(queries, keys, values, allowed):
    scores = (
        jnp.einsum("gqhe,gkhe->ghqk", split_heads(queries), split_heads(keys), preferred_element_type=f32)
        * SCALING
    )
    scores = jnp.where(allowed[:, None], scores, -1e30)
    largest = jnp.max(scores, axis=-1, keepdims=True)
    exponent = jnp.exp(scores - largest)
    denominator = jnp.sum(exponent, axis=-1, keepdims=True)
    weights = (exponent / denominator).astype(bf16)
    output = jnp.einsum("ghqk,gkhe->gqhe", weights, split_heads(values), preferred_element_type=f32)
    return output.reshape(queries.shape), (largest + jnp.log(denominator))


def attention_backward(queries, keys, values, allowed, log_total, grads):
    q, k, v, g = map(split_heads, (queries, keys, values, grads))
    scores = jnp.einsum("gqhe,gkhe->ghqk", q, k, preferred_element_type=f32) * SCALING
    scores = jnp.where(allowed[:, None], scores, -1e30)
    probability = jnp.exp(scores - log_total)
    grad_value = jnp.einsum("ghqk,gqhe->gkhe", probability.astype(bf16), g, preferred_element_type=f32)
    grad_probs = jnp.einsum("gqhe,gkhe->ghqk", g, v, preferred_element_type=f32)
    inner = jnp.sum(probability * grad_probs, axis=-1, keepdims=True)
    grad_scores = (probability * (grad_probs - inner)).astype(bf16)
    grad_query = jnp.einsum("ghqk,gkhe->gqhe", grad_scores, k, preferred_element_type=f32) * SCALING
    grad_key = jnp.einsum("ghqk,gqhe->gkhe", grad_scores, q, preferred_element_type=f32) * SCALING
    return (
        grad_query.reshape(queries.shape).astype(bf16),
        grad_key.reshape(keys.shape).astype(bf16),
        grad_value.reshape(values.shape).astype(bf16),
    )


def per_device(
    table_input,
    target_input,
    cotangent,
    table_lengths,
    target_lengths,
    query_key,
    value_out,
    hidden_in,
    hidden_out,
    hidden_bias,
    vectors,
    cross_bias,
):
    sections = lax.axis_size("section")
    count = lax.axis_size("tensor")
    bits = tensor_bits()
    rank = lax.axis_index("tensor")
    section = lax.axis_index("section")
    is_first = section == 0
    tables, slots, width = table_input.shape
    targets = target_input.shape[1]
    columns = query_key.shape[3]
    rows = vectors[0]
    head_rows = lax.dynamic_slice_in_dim(rows[0:3], rank * columns, columns, 1)
    w_query, w_key, w_third_q = query_key[0, 0], query_key[0, 1], query_key[0, 2]
    w_value, w_out, w_third_v = value_out[0, 0], value_out[0, 1], value_out[0, 2]
    w_in, w_hidden_out, b_hidden = hidden_in[0], hidden_out[0], hidden_bias[0]
    w_cross_key, w_cross_value, b_cross_value = to_second(w_third_q), to_second(w_third_v), to_second(head_rows[2])

    masks = [int(format(p, f"0{bits}b")[::-1], 2) for p in range(count)]
    owners = rank ^ jnp.array(masks, jnp.int32)
    short = slots // (sections * count)
    row_index = (
        jnp.arange(sections)[None, :, None] * (count * short)
        + owners[:, None, None] * short
        + jnp.arange(short)[None, None, :]
    ).reshape(-1)
    table_rows = jnp.take(table_input.reshape(tables, sections, count, short, width), owners, axis=2)
    table_rows = jnp.swapaxes(table_rows, 1, 2).reshape(tables, slots, width)
    share = sections * short
    table_valid = row_index[None, :] < table_lengths[:, None]

    cores = 2
    small = targets // (sections * count)
    core_order = (rank % cores) ^ jnp.arange(cores)
    half = targets // cores

    def target_frame(value):
        split = value.reshape(tables, sections, count // cores, cores, small, width)
        split = jnp.take(split, core_order, axis=3)
        return jnp.transpose(split, (3, 0, 2, 1, 4, 5)).reshape(cores, tables * half, width)

    target_index = (
        jnp.arange(sections)[None, None, :, None] * (count * small)
        + jnp.arange(count // cores)[None, :, None, None] * (cores * small)
        + core_order[:, None, None, None] * small
        + jnp.arange(small)[None, None, None, :]
    ).reshape(-1)
    target_rows = target_frame(target_input)
    grad_rows_half = target_frame(cotangent)[0].astype(f32)
    target_valid = target_index[None, :] < target_lengths[:, None]
    causal = (target_index[None, :] <= target_index[:, None])[None] & target_valid[:, None, :]

    def per_table(value):
        return jnp.swapaxes(value.reshape(cores, tables, half, -1), 0, 1).reshape(tables, targets, -1)

    def in_frame(value):
        return jnp.swapaxes(value.reshape(tables, cores, half, -1), 0, 1).reshape(cores, tables * half, -1)

    def flat(value):
        return value.reshape(-1, value.shape[-1])

    def ffn_forward(inputs):
        hidden, slope = gelu_pair(mm(inputs, w_in) + b_hidden)
        hidden, slope = hidden.astype(bf16), slope.astype(bf16)
        return hidden, slope, mm_t(hidden, w_hidden_out).astype(bf16)

    def ffn_backward(grads, slope):
        grad_before = (mm(grads, w_hidden_out) * slope.astype(f32)).astype(bf16)
        return grad_before, mm_t(grad_before, w_in).astype(bf16)

    def encode(table):
        summed_zero = table_rows[table].astype(f32)
        normed = layer_norm(summed_zero, rows[9], rows[10])
        first_in = normed.astype(bf16)
        queries = (mm(first_in, w_query) + head_rows[0]).astype(bf16)
        keys = mm(first_in, w_key).astype(bf16)
        values = (mm(first_in, w_value) + head_rows[1]).astype(bf16)
        heads, log_total = attention_forward(queries[None], keys[None], values[None], table_valid[table][None, None])
        heads = heads[0].astype(bf16)
        summed_one = normed[:share] + reduce_share(mm_t(heads, w_out)) + rows[3]
        middle = layer_norm(summed_one, rows[5], rows[6])
        second_in = gather_share(middle.astype(bf16))
        hidden, slope, partial = ffn_forward(second_in)
        summed_two = middle + reduce_share(partial) + rows[4]
        memory = layer_norm(summed_two, rows[7], rows[8]).astype(bf16)
        kept = (summed_zero[:share], first_in, queries, keys, values, heads, log_total, summed_one, second_in, hidden, slope, summed_two)
        return memory, kept

    memories, kept_tables = zip(*[encode(table) for table in range(tables)])

    dec_first = flat(target_rows)
    dec_q = (mm(dec_first, w_query) + head_rows[0]).astype(bf16)
    dec_k = mm(dec_first, w_key).astype(bf16)
    dec_v = (mm(dec_first, w_value) + head_rows[1]).astype(bf16)
    dec_heads, dec_log = attention_forward(per_table(dec_q), per_table(dec_k), per_table(dec_v), causal)
    dec_heads = in_frame(dec_heads.astype(bf16))
    dec_one = (
        target_rows[0].astype(f32)
        + reduce_half(mm_t(flat(dec_heads), w_out).reshape(cores, -1, width))
        + rows[3]
    )
    dec_middle = layer_norm(dec_one, rows[5], rows[6])
    cross_in = gather_half(dec_middle.astype(bf16))
    cross_q = (mm(cross_in, w_third_q) + head_rows[2]).astype(bf16)

    memory_rows = jnp.stack([gather_share(to_second(memory)) for memory in memories])
    cross_k = mm(flat(memory_rows), w_cross_key).astype(bf16).reshape(tables, slots, columns)
    cross_v = (mm(flat(memory_rows), w_cross_value) + b_cross_value).astype(bf16).reshape(tables, slots, columns)
    cross_heads, cross_log = attention_forward(per_table(cross_q), cross_k, cross_v, table_valid[:, None])
    cross_heads = flat(in_frame(cross_heads.astype(bf16)))
    dec_three = dec_middle + reduce_half(mm_t(cross_heads, w_third_v).reshape(cores, -1, width)) + cross_bias
    dec_later = layer_norm(dec_three, rows[9], rows[10])
    third_in = gather_half(dec_later.astype(bf16))
    dec_hidden, dec_slope, partial = ffn_forward(third_in)
    dec_two = dec_later + reduce_half(partial.reshape(cores, -1, width)) + rows[4]
    decoded = layer_norm(dec_two, rows[7], rows[8]).astype(bf16)

    grad_two, dec_gain_two, dec_shift_two = norm_backward(dec_two, rows[7], grad_rows_half)
    grad_two_rows = gather_half(grad_two.astype(bf16))
    dec_before_grad, partial = ffn_backward(grad_two_rows, dec_slope)
    grad_later = reduce_half(partial.reshape(cores, -1, width))
    grad_three, dec_gain_three, dec_shift_three = norm_backward(dec_three, rows[9], grad_two + grad_later)
    grad_three_rows = gather_half(grad_three.astype(bf16))
    grad_cross_heads = mm(grad_three_rows, w_third_v).astype(bf16)
    grad_cross_q, grad_cross_k, grad_cross_v = attention_backward(
        per_table(cross_q), cross_k, cross_v, table_valid[:, None], cross_log, per_table(grad_cross_heads)
    )
    grad_memory = []
    for table in range(tables):
        partial = mm_t(grad_cross_k[table], w_cross_key) + mm_t(grad_cross_v[table], w_cross_value)
        grad_memory.append(to_first(reduce_share(partial).astype(bf16)).astype(f32))
    third_q_grad = to_first(t_mm(flat(memory_rows), flat(grad_cross_k)).astype(bf16))
    third_v_grad = to_first(t_mm(flat(memory_rows), flat(grad_cross_v)).astype(bf16))
    third_bias_grad = to_first(jnp.sum(flat(grad_cross_v).astype(f32), axis=0))

    grad_cross_q = flat(in_frame(grad_cross_q))
    grad_middle = reduce_half(mm_t(grad_cross_q, w_third_q).reshape(cores, -1, width))
    grad_one, dec_gain_one, dec_shift_one = norm_backward(dec_one, rows[5], grad_three + grad_middle)
    grad_one_rows = gather_half(grad_one.astype(bf16))
    grad_heads = mm(grad_one_rows, w_out).astype(bf16)
    grad_q, grad_k, grad_v = attention_backward(
        per_table(dec_q), per_table(dec_k), per_table(dec_v), causal, dec_log, per_table(grad_heads)
    )
    grad_q, grad_k, grad_v = (flat(in_frame(value)) for value in (grad_q, grad_k, grad_v))
    partial = mm_t(grad_q, w_query) + mm_t(grad_k, w_key) + mm_t(grad_v, w_value)
    target_grad = (grad_one + reduce_half(partial.reshape(cores, -1, width))).astype(bf16)
    dec_matrix = (
        t_mm(dec_first, grad_q),
        t_mm(dec_first, grad_k),
        t_mm(cross_in, grad_cross_q),
        t_mm(dec_first, grad_v),
        t_mm(grad_one_rows, flat(dec_heads)),
        t_mm(grad_three_rows, cross_heads),
        t_mm(third_in, dec_before_grad),
        t_mm(grad_two_rows, dec_hidden),
    )
    dec_head_rows = [jnp.sum(value.astype(f32), axis=0) for value in (grad_q, grad_v, grad_cross_q)]
    dec_bias = jnp.sum(dec_before_grad.astype(f32), axis=0)
    doubled = cores / count
    dec_rows = [
        value * doubled
        for value in (
            jnp.sum(grad_one, axis=0),
            jnp.sum(grad_two, axis=0),
            dec_gain_one,
            dec_shift_one,
            dec_gain_two,
            dec_shift_two,
            dec_gain_three,
            dec_shift_three,
            jnp.sum(grad_three, axis=0),
        )
    ]

    def encode_back(table):
        (summed_zero, first_in, queries, keys, values, heads, log_total, summed_one, second_in, hidden, slope, summed_two) = (
            kept_tables[table]
        )
        grad_two, gain_two, shift_two = norm_backward(summed_two, rows[7], grad_memory[table])
        grad_two_rows = gather_share(grad_two.astype(bf16))
        grad_before, partial = ffn_backward(grad_two_rows, slope)
        grad_middle = reduce_share(partial)
        grad_one, gain_one, shift_one = norm_backward(summed_one, rows[5], grad_two + grad_middle)
        grad_one_rows = gather_share(grad_one.astype(bf16))
        grad_heads = mm(grad_one_rows, w_out).astype(bf16)
        grad_q, grad_k, grad_v = (
            value[0]
            for value in attention_backward(
                queries[None], keys[None], values[None], table_valid[table][None, None], log_total, grad_heads[None]
            )
        )
        partial = mm_t(grad_q, w_query) + mm_t(grad_k, w_key) + mm_t(grad_v, w_value)
        grad_normed = reduce_share(partial)
        table_grad, gain_zero, shift_zero = norm_backward(summed_zero, rows[9], grad_one + grad_normed)
        sums = (
            jnp.sum(grad_one, axis=0),
            jnp.sum(grad_two, axis=0),
            gain_one,
            shift_one,
            gain_two,
            shift_two,
            gain_zero,
            shift_zero,
        )
        pairs = (first_in, grad_q, grad_k, grad_v, grad_one_rows, heads, second_in, grad_before, grad_two_rows, hidden)
        return table_grad.astype(bf16), sums, pairs

    table_grads, sums, pairs = zip(*[encode_back(table) for table in range(tables)])
    enc_rows = [sum(values) for values in zip(*sums)]
    (first_in, grad_q, grad_k, grad_v, grad_one_rows, heads, second_in, grad_before, grad_two_rows, hidden) = (
        jnp.concatenate(values) for values in zip(*pairs)
    )
    enc_matrix = (
        t_mm(first_in, grad_q),
        t_mm(first_in, grad_k),
        third_q_grad,
        t_mm(first_in, grad_v),
        t_mm(grad_one_rows, heads),
        third_v_grad,
        t_mm(second_in, grad_before),
        t_mm(grad_two_rows, hidden),
    )
    enc_head_rows = [jnp.sum(grad_q.astype(f32), axis=0), jnp.sum(grad_v.astype(f32), axis=0), third_bias_grad]
    enc_bias = jnp.sum(grad_before.astype(f32), axis=0)

    matrix = [
        lax.psum(jnp.where(is_first, own.astype(bf16), other.astype(bf16)), "dp").astype(f32)
        for own, other in zip(enc_matrix, dec_matrix)
    ]
    query_key_grad = jnp.stack(matrix[0:3])
    value_out_grad = jnp.stack(matrix[3:6])

    head_sums = jnp.where(is_first, jnp.stack(enc_head_rows), jnp.stack(dec_head_rows))
    placed = lax.dynamic_update_slice(jnp.zeros((3, width), f32), head_sums, (0, rank * columns))
    other_rows = jnp.where(is_first, jnp.stack(enc_rows), jnp.stack(dec_rows[:8]))
    cross_row = jnp.where(is_first, 0.0, dec_rows[8])
    bias_sum = lax.psum(jnp.where(is_first, enc_bias, dec_bias), "dp")
    vector_total = lax.psum(jnp.concatenate([placed, other_rows]), ("dp", "tensor"))
    cross_total = lax.psum(cross_row, ("section", "dp", "tensor"))

    table_grads = jnp.stack(table_grads).reshape(tables, sections, short, width)
    moved_up = lax.ppermute(table_grads[:, 1], "section", [(0, 1)])
    table_out = jnp.where(is_first, table_grads[:, 0], moved_up)
    own = lax.dynamic_slice_in_dim(
        jnp.stack([decoded, target_grad]).reshape(2, tables, count // cores, sections, small, width),
        rank // cores,
        1,
        2,
    )[:, :, 0]
    moved_down = lax.ppermute(own[:, :, 0], "section", [(1, 0)])
    small_out = jnp.where(is_first, moved_down, own[:, :, 1])
    return (
        small_out[0],
        table_out,
        small_out[1],
        query_key_grad[None],
        value_out_grad[None],
        matrix[6][None],
        matrix[7][None],
        bias_sum[None],
        vector_total[None],
        cross_total,
    )


def solution(mesh):
    in_specs = (
        P("dp", None, None),
        P("dp", None, None),
        P("dp", None, None),
        P("dp"),
        P("dp"),
        P("section", None, None, "tensor"),
        P("section", None, None, "tensor"),
        P("section", None, "tensor"),
        P("section", None, "tensor"),
        P("section", "tensor"),
        P("section", None, None),
        P(),
    )
    out_specs = (
        P("dp", ("section", "tensor"), None),
        P("dp", ("section", "tensor"), None),
        P("dp", ("section", "tensor"), None),
        P("section", None, None, "tensor"),
        P("section", None, None, "tensor"),
        P("section", None, "tensor"),
        P("section", None, "tensor"),
        P("section", "tensor"),
        P("section", None, None),
        P(),
    )
    return jax.shard_map(
        per_device, mesh=mesh, in_specs=in_specs, out_specs=out_specs, check_vma=False
    )
```

time: 2630 us -> 1000 us (0.38)
  waiting for transfers between devices: 1500 us -> 290 us
  matrix products: 465 us -> 215 us
  other arithmetic: 249 us -> 154 us
  starting transfers between devices: 17.6 us -> 72.2 us
  loops' own time: 46.8 us -> 0 us
  local copies, waits for them, and re-layouts: 151 us -> 117 us
  blocking collectives: 155 us -> 124 us
    while x60 -> x0, waiting for transfers between devices: 976 us -> none
    dot_general x184 -> x86, matrix products: 430 us -> 215 us  [the longest x22 49.1 us: mm(): lax.dot_general(a, b, (((1,), (0,)), ((), ())), preferred_element_type=f32)]
    psum x2 -> x1, waiting for transfers between devices: 316 us -> 136 us  [per_device(): lax.psum(jnp.where(is_first, own.astype(bf16), other.astype(bf16)), 'dp')]
    all_gather x16 -> x0, waiting for transfers between devices: 129 us -> none  [the longest x12 122 us: gather_rows(): gathered = lax.all_gather(share_part, 'tensor', axis=2, tiled=True)]
    all_gather x18 -> x0, blocking collectives: 106 us -> none  [the longest x12 69.5 us: gather_rows(): gathered = lax.all_gather(share_part, 'tensor', axis=2, tiled=True)]
    reduce_sum x88 -> x43, other arithmetic: 129 us -> 51.6 us  [the longest x4 17.2 us: attention_forward(): denominator = jnp.sum(exponent, axis=-1, keepdims=True)]
    ppermute x6 -> x65, waiting for transfers between devices: 79.4 us -> 154 us  [the longest x53 122 us: flip(): lax.ppermute(value, 'tensor', [(i, i ^ 1 << bit) for i in range(count)])]
    psum x2 -> x3, blocking collectives: 49.8 us -> 124 us  [the longest x1 67.6 us: per_device(): lax.psum(jnp.concatenate([placed, other_rows]), ('dp', 'tensor'))]
  transfers between devices with their start and end apart: 46 -> 66, of which waited for: 40 -> 29; matrix products, arithmetic and copies ran while one was open for 10% -> 41% of each run, Pallas kernels for 0% -> 0%
where the time goes in v1:
time: 1000 us; the launch traced here: 991 us
  waiting for transfers between devices  290 us (29%)
  matrix products  215 us (22%)
  other arithmetic  154 us (15%)
  blocking collectives  124 us (12%)
  local copies, waits for them, and re-layouts  117 us (12%)
  starting transfers between devices  72.2 us (7%)
  between operations  18.7 us (2%)
    psum x1, waiting for transfers between devices, per_device(): lax.psum(jnp.where(is_first, own.astype(bf16), other.astype(bf16)), 'dp')  136 us
    ppermute x53, waiting for transfers between devices, flip(): lax.ppermute(value, 'tensor', [(i, i ^ 1 << bit) for i in range(count)])  122 us
    psum x1, blocking collectives, per_device(): lax.psum(jnp.concatenate([placed, other_rows]), ('dp', 'tensor'))  67.6 us
    dot_general x22, matrix products, mm(): lax.dot_general(a, b, (((1,), (0,)), ((), ())), preferred_element_type=f32)  49.1 us
    psum x1, blocking collectives, per_device(): cross_total = lax.psum(cross_row, ('section', 'dp', 'tensor'))  41.9 us
    ppermute x53, starting transfers between devices, flip(): lax.ppermute(value, 'tensor', [(i, i ^ 1 << bit) for i in range(count)])  40.7 us
    dot_general x16, matrix products, t_mm(): lax.dot_general(a, b, (((0,), (0,)), ((), ())), preferred_element_type=f32)  38.2 us
    dot_general x24, matrix products, mm_t(): lax.dot_general(a, b, (((1,), (1,)), ((), ())), preferred_element_type=f32)  35.2 us
  transfers between devices with their start and end apart: 66, of which 29 were waited for; matrix products, arithmetic and copies ran while one was open for 41% of the time, Pallas kernels for 0%

profile of v1, /device:TPU:0, one launch (start us, length us, event | category | flops | bytes accessed | tf_op | source)
XLA Modules:
  0.0 991.0 jit_solution(2012666126393319136)
XLA Ops:
  8.7 5.4 collective-permute-start.21
  17.8 5.0 gather_fusion
  22.8 2.7 select_bitcast_fusion
  27.6 2.6 add_convert_fusion
  32.6 7.5 fusion.348
  40.2 8.0 fusion.1
  48.2 7.6 fusion.154
  62.2 7.4 fusion.349
  69.6 8.0 fusion
  77.6 7.4 fusion.155
  98.9 3.4 fusion.316
  102.4 7.3 collective-permute-done.12
  109.7 10.3 %collective-permute-done.3 = bf16[256,1024]{1,0:T(8,128)(2,1)S(1)} collective-permute-done((bf16[256,1024]{1,0:T(8,128)(2,1)S(1)}, bf16[256,1024]{1,0:T(8,128)(2,1)S(1)}, u32[]{:S(2)}, u32[]{:S(2)}) %collective-permute-start.3) | collective-permute-done | bytes 524320 | tf_op jit(solution)/shard_map/ppermute | solution.py:57
  131.4 4.5 collective-permute-done.4
  146.6 9.7 collective-permute-done.13
  174.5 3.9 fusion.44
  178.5 8.0 multiply_convert_fusion.6
  192.1 3.0 slice_convert_fusion.7
  201.2 9.3 collective-permute-done.7
  210.5 11.2 %collective-permute-done.16 = bf16[256,1024]{1,0:T(8,128)(2,1)S(1)} collective-permute-done((bf16[256,1024]{1,0:T(8,128)(2,1)S(1)}, bf16[256,1024]{1,0:T(8,128)(2,1)S(1)}, u32[]{:S(2)}, u32[]{:S(2)}) %collective-permute-start.16) | collective-permute-done | bytes 524320 | tf_op jit(solution)/shard_map/ppermute | solution.py:57
  227.8 9.7 collective-permute-done.8
  239.0 7.3 collective-permute-done.17
  249.1 8.8 collective-permute-done.18
  262.0 5.2 collective-permute-start.23
  278.2 3.3 convolution_convert_fusion
  281.5 4.7 reshape.1308
  286.2 4.1 copy.184
  290.2 4.6 fusion.35
  294.8 4.4 reshape.1307
  299.2 4.1 copy.185
  318.5 6.0 collective-permute-done.25
  336.9 4.4 collective-permute-done.28
  356.0 5.7 collective-permute-done.31
  364.4 41.9 %psum.87 = f32[1024]{0:T(1024)} all-reduce(f32[1024]{0:T(1024)S(1)} %multiply_select_fusion.3), channel_id=1, replica_groups=mesh['section'=2,'dp'=4,'tensor'=4] {'section','dp','tensor'}, use_global_device_ids=true, to_apply=%region_95.97 | all-reduce | flops 1024 | bytes 8192 | tf_op jit(solution)/shard_map/psum | solution.py:385
  410.4 4.9 convert_reduce_fusion.3
  422.7 4.8 fusion.153
  447.2 3.8 convolution_add_fusion.2
  454.7 2.6 collective-permute-start.34
  458.8 2.7 slice.759
  487.7 7.9 collective-permute-done.40
  514.6 12.0 %collective-permute-done.52 = bf16[256,1024]{1,0:T(8,128)(2,1)S(1)} collective-permute-done((bf16[256,1024]{1,0:T(8,128)(2,1)S(1)}, bf16[256,1024]{1,0:T(8,128)(2,1)S(1)}, u32[]{:S(2)}, u32[]{:S(2)}) %collective-permute-start.52) | collective-permute-done | bytes 524320 | tf_op jit(solution)/shard_map/ppermute | solution.py:96
  526.7 2.8 fusion.323
  532.8 9.0 collective-permute-done.42
  559.4 4.9 multiply_convert_fusion.3
  567.4 5.0 collective-permute-done.53
  581.4 6.0 multiply_convert_fusion.2
  590.0 3.0 collective-permute-done.45
  593.7 5.2 fusion.34
  602.2 9.7 collective-permute-done.56
  616.3 7.3 fusion.22
  634.8 9.4 multiply_reduce_fusion.1
  644.2 8.1 multiply_convert_fusion.1
  652.3 3.5 fusion.149
  659.9 10.2 %fusion.123 = bf16[4,64,1024]{2,1,0:T(8,128)(2,1)} fusion(bf16[1024,4,64]{0,2,1:T(8,128)(2,1)S(1)} %bitcast.592, f32[4,1024,1024]{1,2,0:T(8,128)} %get-tuple-element.164, f32[4,1024]{1,0:T(4,128)S(1)} %copy-done.151), kind=kOutput, calls=%fused_computation.199 | convolution fusion | flops 545521664 | bytes 17842176 | tf_op jit(solution)/shard_map/ghqk,gqhe->gkhe/dot_general | solution.py:122
  675.3 3.5 fusion.126
  678.8 11.2 %multiply_reduce_fusion = (f32[4,1024]{1,0:T(4,128)}, f32[4,1024,1024]{1,2,0:T(8,128)}) fusion(f32[4,1024,1024]{1,2,0:T(8,128)S(1)} %bitcast.551, f32[4,1024]{1,0:T(4,128)S(1)} %copy-done.150, bf16[1024,4,64]{0,2,1:T(8,128)(2,1)} %bitcast.594, bf16[1024,4,64]{0,2,1:T(8,128)(2,1)} %bitcast.618), kind=kOutput, calls=%fused_computation.4 | convolution fusion | flops 549449728 | bytes 34635776 | tf_op jit(solution)/shard_map/gqhe,gkhe->ghqk/dot_general | solution.py:123
  690.0 8.2 multiply_convert_fusion
  698.1 2.7 fusion.151
  731.2 14.1 %psum.85 = f32[1,1024]{1,0:T(1,128)} all-reduce(f32[1,1024]{1,0:T(1,128)S(1)} %bitcast.715), channel_id=1, replica_groups=mesh['section'=2,'dp'=4,'tensor'=4] {'dp'}, use_global_device_ids=true, to_apply=%region_62.64 | all-reduce | flops 1024 | bytes 8192 | tf_op jit(solution)/shard_map/psum | solution.py:383
  751.6 5.5 collective-permute-done.60
  759.4 7.6 collective-permute-start.61
  768.1 67.6 %psum.86 = f32[1,11,1024]{2,0,1:T(1,128)} all-reduce(f32[1,11,1024]{2,0,1:T(1,128)S(1)} %broadcast_in_dim.223), channel_id=1, replica_groups=mesh['section'=2,'dp'=4,'tensor'=4] {'dp','tensor'}, use_global_device_ids=true, to_apply=%region_93.95 | all-reduce | flops 11264 | bytes 90112 | tf_op jit(solution)/shard_map/psum | solution.py:384
  837.6 135.5 %all-reduce.3.cloned.1.call-done = (bf16[1,1024,256]{2,1,0:T(8,128)(2,1)}, bf16[1,1024,256]{2,1,0:T(8,128)(2,1)}, bf16[1,1024,256]{2,1,0:T(8,128)(2,1)}, bf16[1,...) async-done(((bf16[1,1024,256]{2,1,0:T(8,128)(2,1)}, ...) | async-done | bytes 7340048 | tf_op jit(solution)/shard_map/psum | solution.py:373
  973.1 4.2 broadcast_in_dim.218
  (995 shorter events, 342.9 us)
Async XLA Ops:
  7.2 965.9 %all-reduce.3.cloned.1.call-start = ((), (), s32[]{:S(2)}) async-start(), calls=%async_computation | async-start | bytes 14680064 | tf_op jit(solution)/shard_map/psum | solution.py:373
  8.7 281.5 %collective-permute-start.21 = (f32[256]{0:T(256)}, f32[256]{0:T(256)}, u32[]{:S(2)}, u32[]{:S(2)}) collective-permute-start(f32[256]{0:T(256)} %bitcast.60), channel_id=1, source_target_pairs={{0,16},{1,17},{2,18},{3,19},{4,20},{5,21},{6,22},{7,23},{8,24},{9,... | collective-permute-start | bytes 3080 | tf_op jit(solution)/shard_map/ppermute | solution.py:92
  59.8 32.8 %collective-permute-start.11 = (bf16[512,1024]{1,0:T(8,128)(2,1)}, bf16[512,1024]{1,0:T(8,128)(2,1)S(1)}, u32[]{:S(2)}, u32[]{:S(2)}) collective-permute-start(bf16[512,1024]{1,0:T(8,128)(2,1)} %slice.760), channel_id=1, source_target_pairs={{0,1},{1,0},{2,3},{3,2},{4,5},{5,4},{6,7},{7,6},{8,9},{9,8},{10,11... | collective-permute-start | bytes 3145736 | tf_op jit(solution)/shard_map/ppermute | solution.py:57
  88.9 7.5 collective-permute-start.2
  90.3 199.9 %collective-permute-start.20 = (bf16[1024,256]{1,0:T(8,128)(2,1)}, bf16[1024,256]{1,0:T(8,128)(2,1)}, u32[]{:S(2)}, u32[]{:S(2)}) collective-permute-start(bf16[1024,256]{1,0:T(8,128)(2,1)} %slice_bitcast_fusion.1), channel_id=1, source_target_pairs={{0,16},{1,17},{2,18},{3,19},{4,20},{5,21},{6,22},{7,23},{8,24},{9,... | collective-permute-start | bytes 1572872 | tf_op jit(solution)/shard_map/ppermute | solution.py:92
  94.8 14.9 %collective-permute-start.12 = (bf16[256,1024]{1,0:T(8,128)(2,1)S(1)}, bf16[256,1024]{1,0:T(8,128)(2,1)S(1)}, u32[]{:S(2)}, u32[]{:S(2)}) collective-permute-start(bf16[256,1024]{1,0:T(8,128)(2,1)S(1)} %slice.769), channel_id=1, source_target_pairs={{0,2},{1,3},{2,0},{3,1},{4,6},{5,7},{6,4},{7,5},{8,10},{9,11},{10,... | collective-permute-start | bytes 1572872 | tf_op jit(solution)/shard_map/ppermute | solution.py:57
  98.1 21.9 %collective-permute-start.3 = (bf16[256,1024]{1,0:T(8,128)(2,1)S(1)}, bf16[256,1024]{1,0:T(8,128)(2,1)S(1)}, u32[]{:S(2)}, u32[]{:S(2)}) collective-permute-start(bf16[256,1024]{1,0:T(8,128)(2,1)S(1)} %slice.771), channel_id=1, source_target_pairs={{0,2},{1,3},{2,0},{3,1},{4,6},{5,7},{6,4},{7,5},{8,10},{9,11},{10,... | collective-permute-start | bytes 1572872 | tf_op jit(solution)/shard_map/ppermute | solution.py:57
  122.6 13.3 %collective-permute-start.4 = (bf16[256,1024]{1,0:T(8,128)(2,1)}, bf16[256,1024]{1,0:T(8,128)(2,1)}, u32[]{:S(2)}, u32[]{:S(2)}) collective-permute-start(bf16[256,1024]{1,0:T(8,128)(2,1)} %get-tuple-element.82), channel_id=1, source_target_pairs={{0,2},{1,3},{2,0},{3,1},{4,6},{5,7},{6,4},{7,5},{8,10},{9,11},{10,... | collective-permute-start | bytes 1572872 | tf_op jit(solution)/shard_map/ppermute | solution.py:57
  137.2 2.7 collective-permute-start.5
  142.1 14.3 %collective-permute-start.13 = (bf16[256,1024]{1,0:T(8,128)(2,1)S(1)}, bf16[256,1024]{1,0:T(8,128)(2,1)S(1)}, u32[]{:S(2)}, u32[]{:S(2)}) collective-permute-start(bf16[256,1024]{1,0:T(8,128)(2,1)S(1)} %get-tuple-element.80), channel_id=1, source_target_pairs={{0,2},{1,3},{2,0},{3,1},{4,6},{5,7},{6,4},{7,5},{8,10},{9,11},{10,... | collective-permute-start | bytes 1572872 | tf_op jit(solution)/shard_map/ppermute | solution.py:57
  157.5 16.9 %collective-permute-start.14 = (bf16[512,1024]{1,0:T(8,128)(2,1)}, bf16[512,1024]{1,0:T(8,128)(2,1)}, u32[]{:S(2)}, u32[]{:S(2)}) collective-permute-start(bf16[512,1024]{1,0:T(8,128)(2,1)} %pad_maximum_fusion.9), channel_id=1, source_target_pairs={{0,1},{1,0},{2,3},{3,2},{4,5},{5,4},{6,7},{7,6},{8,9},{9,8},{10,11... | collective-permute-start | bytes 3145736 | tf_op jit(solution)/shard_map/ppermute | solution.py:57
  172.7 26.8 %collective-permute-start = (bf16[128,1024]{1,0:T(8,128)(2,1)S(1)}, bf16[128,1024]{1,0:T(8,128)(2,1)S(1)}, u32[]{:S(2)}, u32[]{:S(2)}) collective-permute-start(bf16[128,1024]{1,0:T(8,128)(2,1)S(1)} %slice.775), channel_id=1, source_target_pairs={{0,1},{1,0},{2,3},{3,2},{4,5},{5,4},{6,7},{7,6},{8,9},{9,8},{10,11... | collective-permute-start | bytes 786440 | tf_op jit(solution)/shard_map/ppermute | solution.py:57
  189.0 6.2 collective-permute-start.6
  191.5 5.7 collective-permute-start.15
  195.7 14.8 %collective-permute-start.7 = (bf16[256,1024]{1,0:T(8,128)(2,1)S(1)}, bf16[256,1024]{1,0:T(8,128)(2,1)S(1)}, u32[]{:S(2)}, u32[]{:S(2)}) collective-permute-start(bf16[256,1024]{1,0:T(8,128)(2,1)S(1)} %slice.770), channel_id=1, source_target_pairs={{0,2},{1,3},{2,0},{3,1},{4,6},{5,7},{6,4},{7,5},{8,10},{9,11},{10,... | collective-permute-start | bytes 1572872 | tf_op jit(solution)/shard_map/ppermute | solution.py:57
  197.8 24.0 %collective-permute-start.16 = (bf16[256,1024]{1,0:T(8,128)(2,1)S(1)}, bf16[256,1024]{1,0:T(8,128)(2,1)S(1)}, u32[]{:S(2)}, u32[]{:S(2)}) collective-permute-start(bf16[256,1024]{1,0:T(8,128)(2,1)S(1)} %slice.768), channel_id=1, source_target_pairs={{0,2},{1,3},{2,0},{3,1},{4,6},{5,7},{6,4},{7,5},{8,10},{9,11},{10,... | collective-permute-start | bytes 1572872 | tf_op jit(solution)/shard_map/ppermute | solution.py:57
  199.6 27.9 %collective-permute-start.1 = (bf16[128,1024]{1,0:T(8,128)(2,1)S(1)}, bf16[128,1024]{1,0:T(8,128)(2,1)S(1)}, u32[]{:S(2)}, u32[]{:S(2)}) collective-permute-start(bf16[128,1024]{1,0:T(8,128)(2,1)S(1)} %fusion.222), channel_id=1, source_target_pairs={{0,2},{1,3},{2,0},{3,1},{4,6},{5,7},{6,4},{7,5},{8,10},{9,11},{10,... | collective-permute-start | bytes 786440 | tf_op jit(solution)/shard_map/ppermute | solution.py:57
  223.8 13.7 %collective-permute-start.8 = (bf16[256,1024]{1,0:T(8,128)(2,1)S(1)}, bf16[256,1024]{1,0:T(8,128)(2,1)S(1)}, u32[]{:S(2)}, u32[]{:S(2)}) collective-permute-start(bf16[256,1024]{1,0:T(8,128)(2,1)S(1)} %get-tuple-element.143), channel_id=1, source_target_pairs={{0,16},{1,17},{2,18},{3,19},{4,20},{5,21},{6,22},{7,23},{8,24},{9,... | collective-permute-start | bytes 1572872 | tf_op jit(solution)/shard_map/ppermute | solution.py:92
  225.2 21.1 %collective-permute-start.17 = (bf16[256,1024]{1,0:T(8,128)(2,1)S(1)}, bf16[256,1024]{1,0:T(8,128)(2,1)S(1)}, u32[]{:S(2)}, u32[]{:S(2)}) collective-permute-start(bf16[256,1024]{1,0:T(8,128)(2,1)S(1)} %get-tuple-element.144), channel_id=1, source_target_pairs={{0,16},{1,17},{2,18},{3,19},{4,20},{5,21},{6,22},{7,23},{8,24},{9,... | collective-permute-start | bytes 1572872 | tf_op jit(solution)/shard_map/ppermute | solution.py:92
  237.4 10.5 %collective-permute-start.9 = (bf16[256,1024]{1,0:T(8,128)(2,1)S(1)}, bf16[256,1024]{1,0:T(8,128)(2,1)S(1)}, u32[]{:S(2)}, u32[]{:S(2)}) collective-permute-start(bf16[256,1024]{1,0:T(8,128)(2,1)S(1)} %collective-permute-done.8), channel_id=1, source_target_pairs={{0,2},{1,3},{2,0},{3,1},{4,6},{5,7},{6,4},{7,5},{8,10},{9,11},{10,... | collective-permute-start | bytes 1572872 | tf_op jit(solution)/shard_map/ppermute | solution.py:57
  246.2 11.6 %collective-permute-start.18 = (bf16[256,1024]{1,0:T(8,128)(2,1)S(1)}, bf16[256,1024]{1,0:T(8,128)(2,1)S(1)}, u32[]{:S(2)}, u32[]{:S(2)}) collective-permute-start(bf16[256,1024]{1,0:T(8,128)(2,1)S(1)} %collective-permute-done.17), channel_id=1, source_target_pairs={{0,2},{1,3},{2,0},{3,1},{4,6},{5,7},{6,4},{7,5},{8,10},{9,11},{10,... | collective-permute-start | bytes 1572872 | tf_op jit(solution)/shard_map/ppermute | solution.py:57
  249.1 21.3 %collective-permute-start.10 = (bf16[512,1024]{1,0:T(8,128)(2,1)}, bf16[512,1024]{1,0:T(8,128)(2,1)}, u32[]{:S(2)}, u32[]{:S(2)}) collective-permute-start(bf16[512,1024]{1,0:T(8,128)(2,1)} %pad_maximum_fusion.8), channel_id=1, source_target_pairs={{0,1},{1,0},{2,3},{3,2},{4,5},{5,4},{6,7},{7,6},{8,9},{9,8},{10,11... | collective-permute-start | bytes 3145736 | tf_op jit(solution)/shard_map/ppermute | solution.py:57
  259.0 13.1 %collective-permute-start.19 = (bf16[512,1024]{1,0:T(8,128)(2,1)}, bf16[512,1024]{1,0:T(8,128)(2,1)}, u32[]{:S(2)}, u32[]{:S(2)}) collective-permute-start(bf16[512,1024]{1,0:T(8,128)(2,1)} %pad_maximum_fusion.10), channel_id=1, source_target_pairs={{0,1},{1,0},{2,3},{3,2},{4,5},{5,4},{6,7},{7,6},{8,9},{9,8},{10,11... | collective-permute-start | bytes 3145736 | tf_op jit(solution)/shard_map/ppermute | solution.py:57
  259.2 2.9 collective-permute-start.22
  262.0 16.2 %collective-permute-start.23 = (bf16[1024,256]{1,0:T(8,128)(2,1)}, bf16[1024,256]{1,0:T(8,128)(2,1)}, u32[]{:S(2)}, u32[]{:S(2)}) collective-permute-start(bf16[1024,256]{1,0:T(8,128)(2,1)} %slice_bitcast_fusion), channel_id=1, source_target_pairs={{0,16},{1,17},{2,18},{3,19},{4,20},{5,21},{6,22},{7,23},{8,24},{9,... | collective-permute-start | bytes 1572872 | tf_op jit(solution)/shard_map/ppermute | solution.py:92
  312.8 2.9 collective-permute-start.24
  315.7 8.8 collective-permute-start.25
  330.0 1.7 collective-permute-start.27
  332.4 8.9 collective-permute-start.28
  350.5 2.7 collective-permute-start.30
  353.3 8.4 collective-permute-start.31
  364.4 42.5 %collective-permute-start.32 = (bf16[128,1024]{1,0:T(8,128)(2,1)}, bf16[128,1024]{1,0:T(8,128)(2,1)}, u32[]{:S(2)}, u32[]{:S(2)}) collective-permute-start(bf16[128,1024]{1,0:T(8,128)(2,1)} %convert_element_type.828), channel_id=1, source_target_pairs={{0,1},{1,0},{2,3},{3,2},{4,5},{5,4},{6,7},{7,6},{8,9},{9,8},{10,11... | collective-permute-start | bytes 786440 | tf_op jit(solution)/shard_map/ppermute | solution.py:57
  421.3 345.9 %collective-permute-start.64 = (f32[256]{0:T(256)}, f32[256]{0:T(256)}, u32[]{:S(2)}, u32[]{:S(2)}) collective-permute-start(f32[256]{0:T(256)} %reduce_sum.840), channel_id=1, source_target_pairs={{16,0},{17,1},{18,2},{19,3},{20,4},{21,5},{22,6},{23,7},{24,8},{25... | collective-permute-start | bytes 3080 | tf_op jit(solution)/shard_map/ppermute | solution.py:96
  427.5 38.8 %collective-permute-start.63 = (bf16[1024,256]{1,0:T(8,128)(2,1)}, bf16[1024,256]{1,0:T(8,128)(2,1)}, u32[]{:S(2)}, u32[]{:S(2)}) collective-permute-start(bf16[1024,256]{1,0:T(8,128)(2,1)} %fusion.153), channel_id=1, source_target_pairs={{16,0},{17,1},{18,2},{19,3},{20,4},{21,5},{22,6},{23,7},{24,8},{25... | collective-permute-start | bytes 1572872 | tf_op jit(solution)/shard_map/ppermute | solution.py:96
  435.0 35.1 %collective-permute-start.62 = (bf16[1024,256]{1,0:T(8,128)(2,1)}, bf16[1024,256]{1,0:T(8,128)(2,1)}, u32[]{:S(2)}, u32[]{:S(2)}) collective-permute-start(bf16[1024,256]{1,0:T(8,128)(2,1)} %fusion.152), channel_id=1, source_target_pairs={{16,0},{17,1},{18,2},{19,3},{20,4},{21,5},{22,6},{23,7},{24,8},{25... | collective-permute-start | bytes 1572872 | tf_op jit(solution)/shard_map/ppermute | solution.py:96
  438.9 14.7 %collective-permute-start.33 = (bf16[128,1024]{1,0:T(8,128)(2,1)}, bf16[128,1024]{1,0:T(8,128)(2,1)}, u32[]{:S(2)}, u32[]{:S(2)}) collective-permute-start(bf16[128,1024]{1,0:T(8,128)(2,1)} %slice.773), channel_id=1, source_target_pairs={{0,1},{1,0},{2,3},{3,2},{4,5},{5,4},{6,7},{7,6},{8,9},{9,8},{10,11... | collective-permute-start | bytes 786440 | tf_op jit(solution)/shard_map/ppermute | solution.py:57
  444.2 39.2 %collective-permute-start.50 = (bf16[512,1024]{1,0:T(8,128)(2,1)}, bf16[512,1024]{1,0:T(8,128)(2,1)}, u32[]{:S(2)}, u32[]{:S(2)}) collective-permute-start(bf16[512,1024]{1,0:T(8,128)(2,1)} %slice.757), channel_id=1, source_target_pairs={{0,1},{1,0},{2,3},{3,2},{4,5},{5,4},{6,7},{7,6},{8,9},{9,8},{10,11... | collective-permute-start | bytes 3145736 | tf_op jit(solution)/shard_map/ppermute | solution.py:57
  454.7 9.3 collective-permute-start.34
  464.1 14.2 %collective-permute-start.39 = (bf16[512,1024]{1,0:T(8,128)(2,1)}, bf16[512,1024]{1,0:T(8,128)(2,1)}, u32[]{:S(2)}, u32[]{:S(2)}) collective-permute-start(bf16[512,1024]{1,0:T(8,128)(2,1)} %slice.759), channel_id=1, source_target_pairs={{0,1},{1,0},{2,3},{3,2},{4,5},{5,4},{6,7},{7,6},{8,9},{9,8},{10,11... | collective-permute-start | bytes 3145736 | tf_op jit(solution)/shard_map/ppermute | solution.py:57
  466.3 5.7 collective-permute-start.35
  480.7 14.9 %collective-permute-start.40 = (bf16[256,1024]{1,0:T(8,128)(2,1)S(1)}, bf16[256,1024]{1,0:T(8,128)(2,1)S(1)}, u32[]{:S(2)}, u32[]{:S(2)}) collective-permute-start(bf16[256,1024]{1,0:T(8,128)(2,1)S(1)} %slice.767), channel_id=1, source_target_pairs={{0,2},{1,3},{2,0},{3,1},{4,6},{5,7},{6,4},{7,5},{8,10},{9,11},{10,... | collective-permute-start | bytes 1572872 | tf_op jit(solution)/shard_map/ppermute | solution.py:57
  487.4 21.4 %collective-permute-start.51 = (bf16[256,1024]{1,0:T(8,128)(2,1)}, bf16[256,1024]{1,0:T(8,128)(2,1)}, u32[]{:S(2)}, u32[]{:S(2)}) collective-permute-start(bf16[256,1024]{1,0:T(8,128)(2,1)} %slice.764), channel_id=1, source_target_pairs={{0,2},{1,3},{2,0},{3,1},{4,6},{5,7},{6,4},{7,5},{8,10},{9,11},{10,... | collective-permute-start | bytes 1572872 | tf_op jit(solution)/shard_map/ppermute | solution.py:57
  496.5 15.6 %collective-permute-start.41 = (bf16[256,1024]{1,0:T(8,128)(2,1)}, bf16[256,1024]{1,0:T(8,128)(2,1)}, u32[]{:S(2)}, u32[]{:S(2)}) collective-permute-start(bf16[256,1024]{1,0:T(8,128)(2,1)} %fusion.196), channel_id=1, source_target_pairs={{16,0},{17,1},{18,2},{19,3},{20,4},{21,5},{22,6},{23,7},{24,8},{25... | collective-permute-start | bytes 1572872 | tf_op jit(solution)/shard_map/ppermute | solution.py:96
  510.4 16.2 %collective-permute-start.52 = (bf16[256,1024]{1,0:T(8,128)(2,1)S(1)}, bf16[256,1024]{1,0:T(8,128)(2,1)S(1)}, u32[]{:S(2)}, u32[]{:S(2)}) collective-permute-start(bf16[256,1024]{1,0:T(8,128)(2,1)S(1)} %fusion.193), channel_id=1, source_target_pairs={{16,0},{17,1},{18,2},{19,3},{20,4},{21,5},{22,6},{23,7},{24,8},{25... | collective-permute-start | bytes 1572872 | tf_op jit(solution)/shard_map/ppermute | solution.py:96
  530.3 11.4 %collective-permute-start.42 = (bf16[256,1024]{1,0:T(8,128)(2,1)S(1)}, bf16[256,1024]{1,0:T(8,128)(2,1)S(1)}, u32[]{:S(2)}, u32[]{:S(2)}) collective-permute-start(bf16[256,1024]{1,0:T(8,128)(2,1)S(1)} %get-tuple-element.78), channel_id=1, source_target_pairs={{0,2},{1,3},{2,0},{3,1},{4,6},{5,7},{6,4},{7,5},{8,10},{9,11},{10,... | collective-permute-start | bytes 1572872 | tf_op jit(solution)/shard_map/ppermute | solution.py:57
  542.9 11.6 %collective-permute-start.43 = (bf16[512,1024]{1,0:T(8,128)(2,1)}, bf16[512,1024]{1,0:T(8,128)(2,1)}, u32[]{:S(2)}, u32[]{:S(2)}) collective-permute-start(bf16[512,1024]{1,0:T(8,128)(2,1)} %pad_maximum_fusion.11), channel_id=1, source_target_pairs={{0,1},{1,0},{2,3},{3,2},{4,5},{5,4},{6,7},{7,6},{8,9},{9,8},{10,11... | collective-permute-start | bytes 3145736 | tf_op jit(solution)/shard_map/ppermute | solution.py:57
  547.7 19.3 %collective-permute-start.36 = (bf16[128,1024]{1,0:T(8,128)(2,1)S(1)}, bf16[128,1024]{1,0:T(8,128)(2,1)S(1)}, u32[]{:S(2)}, u32[]{:S(2)}) collective-permute-start(bf16[128,1024]{1,0:T(8,128)(2,1)S(1)} %slice.772), channel_id=1, source_target_pairs={{0,1},{1,0},{2,3},{3,2},{4,5},{5,4},{6,7},{7,6},{8,9},{9,8},{10,11... | collective-permute-start | bytes 786440 | tf_op jit(solution)/shard_map/ppermute | solution.py:57
  557.7 14.7 %collective-permute-start.53 = (bf16[256,1024]{1,0:T(8,128)(2,1)S(1)}, bf16[256,1024]{1,0:T(8,128)(2,1)S(1)}, u32[]{:S(2)}, u32[]{:S(2)}) collective-permute-start(bf16[256,1024]{1,0:T(8,128)(2,1)S(1)} %get-tuple-element.76), channel_id=1, source_target_pairs={{0,2},{1,3},{2,0},{3,1},{4,6},{5,7},{6,4},{7,5},{8,10},{9,11},{10,... | collective-permute-start | bytes 1572872 | tf_op jit(solution)/shard_map/ppermute | solution.py:57
  566.9 12.2 %collective-permute-start.44 = (bf16[512,1024]{1,0:T(8,128)(2,1)S(1)}, bf16[512,1024]{1,0:T(8,128)(2,1)S(1)}, u32[]{:S(2)}, u32[]{:S(2)}) collective-permute-start(bf16[512,1024]{1,0:T(8,128)(2,1)S(1)} %slice.504), channel_id=1, source_target_pairs={{0,1},{1,0},{2,3},{3,2},{4,5},{5,4},{6,7},{7,6},{8,9},{9,8},{10,11... | collective-permute-start | bytes 3145736 | tf_op jit(solution)/shard_map/ppermute | solution.py:57
  567.1 10.4 %collective-permute-start.37 = (bf16[128,1024]{1,0:T(8,128)(2,1)S(1)}, bf16[128,1024]{1,0:T(8,128)(2,1)S(1)}, u32[]{:S(2)}, u32[]{:S(2)}) collective-permute-start(bf16[128,1024]{1,0:T(8,128)(2,1)S(1)} %fusion.219), channel_id=1, source_target_pairs={{0,2},{1,3},{2,0},{3,1},{4,6},{5,7},{6,4},{7,5},{8,10},{9,11},{10,... | collective-permute-start | bytes 786440 | tf_op jit(solution)/shard_map/ppermute | solution.py:57
  572.5 8.9 collective-permute-start.54
  579.6 13.4 %collective-permute-start.45 = (bf16[256,1024]{1,0:T(8,128)(2,1)S(1)}, bf16[256,1024]{1,0:T(8,128)(2,1)S(1)}, u32[]{:S(2)}, u32[]{:S(2)}) collective-permute-start(bf16[256,1024]{1,0:T(8,128)(2,1)S(1)} %slice.766), channel_id=1, source_target_pairs={{0,2},{1,3},{2,0},{3,1},{4,6},{5,7},{6,4},{7,5},{8,10},{9,11},{10,... | collective-permute-start | bytes 1572872 | tf_op jit(solution)/shard_map/ppermute | solution.py:57
  589.9 9.0 collective-permute-start.55
  599.4 12.5 %collective-permute-start.56 = (bf16[256,1024]{1,0:T(8,128)(2,1)S(1)}, bf16[256,1024]{1,0:T(8,128)(2,1)S(1)}, u32[]{:S(2)}, u32[]{:S(2)}) collective-permute-start(bf16[256,1024]{1,0:T(8,128)(2,1)S(1)} %slice.763), channel_id=1, source_target_pairs={{0,2},{1,3},{2,0},{3,1},{4,6},{5,7},{6,4},{7,5},{8,10},{9,11},{10,... | collective-permute-start | bytes 1572872 | tf_op jit(solution)/shard_map/ppermute | solution.py:57
  614.5 11.5 %collective-permute-start.46 = (bf16[256,1024]{1,0:T(8,128)(2,1)S(1)}, bf16[256,1024]{1,0:T(8,128)(2,1)S(1)}, u32[]{:S(2)}, u32[]{:S(2)}) collective-permute-start(bf16[256,1024]{1,0:T(8,128)(2,1)S(1)} %get-tuple-element.86), channel_id=1, source_target_pairs={{0,2},{1,3},{2,0},{3,1},{4,6},{5,7},{6,4},{7,5},{8,10},{9,11},{10,... | collective-permute-start | bytes 1572872 | tf_op jit(solution)/shard_map/ppermute | solution.py:57
  626.1 3.2 collective-permute-start.47
  631.2 24.6 %collective-permute-start.57 = (bf16[256,1024]{1,0:T(8,128)(2,1)}, bf16[256,1024]{1,0:T(8,128)(2,1)}, u32[]{:S(2)}, u32[]{:S(2)}) collective-permute-start(bf16[256,1024]{1,0:T(8,128)(2,1)} %get-tuple-element.84), channel_id=1, source_target_pairs={{0,2},{1,3},{2,0},{3,1},{4,6},{5,7},{6,4},{7,5},{8,10},{9,11},{10,... | collective-permute-start | bytes 1572872 | tf_op jit(solution)/shard_map/ppermute | solution.py:57
  658.1 13.9 %collective-permute-start.58 = (bf16[512,1024]{1,0:T(8,128)(2,1)}, bf16[512,1024]{1,0:T(8,128)(2,1)}, u32[]{:S(2)}, u32[]{:S(2)}) collective-permute-start(bf16[512,1024]{1,0:T(8,128)(2,1)} %pad_maximum_fusion.14), channel_id=1, source_target_pairs={{0,1},{1,0},{2,3},{3,2},{4,5},{5,4},{6,7},{7,6},{8,9},{9,8},{10,11... | collective-permute-start | bytes 3145736 | tf_op jit(solution)/shard_map/ppermute | solution.py:57
  716.6 9.6 collective-permute-start.38
  722.1 6.8 collective-permute-start.48
  726.0 19.4 %collective-permute-start.59 = (bf16[512,1024]{1,0:T(8,128)(2,1)}, bf16[512,1024]{1,0:T(8,128)(2,1)}, u32[]{:S(2)}, u32[]{:S(2)}) collective-permute-start(bf16[512,1024]{1,0:T(8,128)(2,1)} %slice.756), channel_id=1, source_target_pairs={{0,1},{1,0},{2,3},{3,2},{4,5},{5,4},{6,7},{7,6},{8,9},{9,8},{10,11... | collective-permute-start | bytes 3145736 | tf_op jit(solution)/shard_map/ppermute | solution.py:57
  730.7 18.8 %collective-permute-start.49 = (bf16[256,1024]{1,0:T(8,128)(2,1)}, bf16[256,1024]{1,0:T(8,128)(2,1)}, u32[]{:S(2)}, u32[]{:S(2)}) collective-permute-start(bf16[256,1024]{1,0:T(8,128)(2,1)} %slice.765), channel_id=1, source_target_pairs={{0,2},{1,3},{2,0},{3,1},{4,6},{5,7},{6,4},{7,5},{8,10},{9,11},{10,... | collective-permute-start | bytes 1572872 | tf_op jit(solution)/shard_map/ppermute | solution.py:57
  747.9 9.2 collective-permute-start.60
  759.4 76.3 %collective-permute-start.61 = (bf16[2,128,1024]{2,1,0:T(8,128)(2,1)}, bf16[2,128,1024]{2,1,0:T(8,128)(2,1)S(1)}, u32[]{:S(2)}, u32[]{:S(2)}) collective-permute-start(bf16[2,128,1024]{2,1,0:T(8,128)(2,1)} %fusion.218), channel_id=1, source_target_pairs={{0,16},{1,17},{2,18},{3,19},{4,20},{5,21},{6,22},{7,23},{8,24},{9,... | collective-permute-start | bytes 1572872 | tf_op jit(solution)/shard_map/ppermute | solution.py:388
  (276 other events, 3568.0 us)
Sparse Core Ops, SparseCore 0:
  714.9 258.2 all-reduce.2

commit v2 on v1

v2 whole, which is shorter than its diff:
```python
import jax
import jax.numpy as jnp
from jax import lax
from jax.experimental import pallas as pl
from jax.experimental.pallas import tpu as pltpu
from jax.sharding import PartitionSpec as P

HEAD = 64
SCALING = HEAD ** (-0.5)
EPSILON = 1e-05

bf16 = jnp.bfloat16
f32 = jnp.float32


def mm(a, b):
    return lax.dot_general(a, b, (((1,), (0,)), ((), ())), preferred_element_type=f32)


def mm_t(a, b):
    return lax.dot_general(a, b, (((1,), (1,)), ((), ())), preferred_element_type=f32)


def t_mm(a, b):
    return lax.dot_general(a, b, (((0,), (0,)), ((), ())), preferred_element_type=f32)


def norm_stats(summed):
    centered = summed - jnp.mean(summed, axis=-1, keepdims=True)
    spread = jnp.mean(centered * centered, axis=-1, keepdims=True)
    scale = lax.rsqrt(spread + EPSILON)
    return centered * scale, scale


def gelu_pair(before):
    cumulative = 0.5 * (1.0 + lax.erf(before * (0.5 ** 0.5)))
    density = jnp.exp(-0.5 * before * before) * 0.3989422804014327
    return before * cumulative, cumulative + before * density


def shaped(rows, width, dtype=bf16):
    return jax.ShapeDtypeStruct((rows, width), dtype)


def full(shape):
    return pl.BlockSpec(shape, lambda *_: (0,) * len(shape))


def turned(steps):
    return lambda i, *_: ((i + steps // 2) % steps, 0)


def low_high(rows, width, steps):
    return [
        pl.BlockSpec((rows, width), lambda i, *_: (jnp.maximum(i - steps // 2, 0), 0)),
        pl.BlockSpec((rows, width), lambda i, *_: (jnp.minimum(i, steps // 2 - 1), 0)),
    ]


def put_low_high(value, low, high):
    first = pl.program_id(0) < pl.num_programs(0) // 2

    @pl.when(first)
    def _():
        high[...] = value

    @pl.when(jnp.logical_not(first))
    def _():
        low[...] = value


def pick_block(parts, held):
    steps = len(parts)
    at = (pl.program_id(0) + steps // 2) % steps
    for index, part in enumerate(parts):
        @pl.when(at == index)
        def _(part=part):
            held[...] = part[...]
    return held[...]


def cost(flops, moved, exps=0):
    return pl.CostEstimate(flops=int(flops), bytes_accessed=int(moved), transcendentals=int(exps))


class Order:
    def __init__(self):
        self.last = None


order = Order()


def call(kernel, grid, in_specs, out_specs, out_shape, scratch, estimate, *args, prefetch=()):
    count = len(prefetch) + len(args)
    after = [] if order.last is None else [order.last]

    def ordered(*refs):
        kernel(*refs[:count], *refs[count + len(after) :])

    grid_spec = pltpu.PrefetchScalarGridSpec(
        num_scalar_prefetch=len(prefetch),
        grid=grid,
        in_specs=list(in_specs) + [pl.BlockSpec(memory_space=pl.ANY)] * len(after),
        out_specs=out_specs,
        scratch_shapes=scratch,
    )
    results = pl.pallas_call(
        ordered,
        grid_spec=grid_spec,
        out_shape=out_shape,
        compiler_params=pltpu.CompilerParams(vmem_limit_bytes=48 * 1024 * 1024),
        cost_estimate=estimate,
        name=kernel.__qualname__.split(".")[0],
    )(*prefetch, *args, *after)
    order.last = min(results, key=lambda result: result.size) if isinstance(results, (list, tuple)) else results
    return results


def gate(*values, behind=()):
    count = len(values)
    after = ([] if order.last is None else [order.last]) + list(behind)
    results = pl.pallas_call(
        lambda *refs: None,
        in_specs=[pl.BlockSpec(memory_space=pl.ANY)] * (count + len(after)),
        out_specs=[pl.BlockSpec(memory_space=pl.ANY)] * count,
        out_shape=[jax.ShapeDtypeStruct(value.shape, value.dtype) for value in values],
        input_output_aliases={index: index for index in range(count)},
        cost_estimate=cost(0, 0),
        name="gate",
    )(*values, *after)
    order.last = results[0]
    return results if count > 1 else results[0]


def norm_kernel(residual, keep, sent, bias, gain, shift, summed_out, wide_out, out):
    summed = residual[...] + (keep[...].astype(f32) + sent[...].astype(f32)) + bias[...]
    normed = norm_stats(summed)[0] * gain[...] + shift[...]
    summed_out[...] = summed
    wide_out[...] = normed
    out[...] = normed.astype(bf16)


def norm_forward(residual, parts, bias, gain, shift):
    rows, width = residual.shape
    block, row = full((rows, width)), full((1, width))
    return call(
        norm_kernel, (1,), [block] * 3 + [row] * 3, [block] * 3,
        [shaped(rows, width, f32)] * 2 + [shaped(rows, width)], [],
        cost(12 * rows * width, 18 * rows * width),
        residual, *parts, bias, gain, shift,
    )


def norm_back_kernel(count, *refs):
    grads, (summed, gain, wide_out, out, sums) = refs[:count], refs[count:]
    gradient = grads[0][...].astype(f32)
    for grad in grads[1:]:
        gradient = gradient + grad[...].astype(f32)
    unit, scale = norm_stats(summed[...].astype(f32))
    scaled = gradient * gain[...]
    inner = scaled - jnp.mean(scaled, axis=-1, keepdims=True)
    inner = (inner - unit * jnp.mean(scaled * unit, axis=-1, keepdims=True)) * scale
    wide_out[...] = inner
    out[...] = inner.astype(bf16)
    sums[...] = jnp.concatenate(
        [
            jnp.sum(gradient * unit, axis=0, keepdims=True),
            jnp.sum(gradient, axis=0, keepdims=True),
            jnp.sum(inner, axis=0, keepdims=True),
            jnp.zeros((5, inner.shape[1]), f32),
        ]
    )


def norm_backward(summed, gain, grads):
    rows, width = summed.shape
    block, row = full((rows, width)), full((1, width))

    def kernel(*refs):
        norm_back_kernel(len(grads), *refs)

    return call(
        kernel, (1,), [block] * (len(grads) + 1) + [row], [block] * 2 + [full((8, width))],
        [shaped(rows, width, f32), shaped(rows, width), shaped(8, width, f32)], [],
        cost(20 * rows * width, 18 * rows * width),
        *grads, summed, gain,
    )


def qkv_kernel(sections, owners, *refs):
    parts = refs[:sections]
    gain, shift, w_q, w_k, w_v, bias, x_out, q_out, k_out, v_out, own_norm, own_raw = refs[sections:]
    raw = jnp.concatenate([part[...] for part in parts], axis=0)
    normed = norm_stats(raw.astype(f32))[0] * gain[...] + shift[...]
    x = normed.astype(bf16)
    x_out[...] = x
    q_out[...] = (mm(x, w_q[...]) + bias[0:1]).astype(bf16)
    k_out[...] = mm(x, w_k[...]).astype(bf16)
    v_out[...] = (mm(x, w_v[...]) + bias[1:2]).astype(bf16)

    @pl.when(pl.program_id(0) == 0)
    def _():
        own_norm[...] = normed
        own_raw[...] = raw


def encoder_qkv(table_rows, table, owners, gain, shift, w_q, w_k, w_v, bias, sections):
    slots, width = table_rows.shape[1:]
    count = owners.shape[0]
    short = slots // (sections * count)
    share = sections * short
    columns = w_q.shape[1]

    def part_spec(s):
        return pl.BlockSpec((None, short, width), lambda i, order: (table, s * count + order[i], 0))

    def block(columns):
        return pl.BlockSpec((share, columns), lambda i, order: (i, 0))

    def kernel(*refs):
        qkv_kernel(sections, *refs)

    return call(
        kernel, (count,),
        [part_spec(s) for s in range(sections)] + [full((1, width))] * 2 + [full((width, columns))] * 3 + [full(bias.shape)],
        [block(width)] + [block(columns)] * 3 + [full((share, width))] * 2,
        [shaped(slots, width)] + [shaped(slots, columns)] * 3 + [shaped(share, width, f32), shaped(share, width)],
        [],
        cost(6 * slots * width * columns, 8 * slots * width),
        *([table_rows] * sections), gain, shift, w_q, w_k, w_v, bias,
        prefetch=[owners],
    )


def pair_mask(head):
    return (lax.broadcasted_iota(jnp.int32, (1, 128), 1) // HEAD) == head


def attention_rows(q_all, k_all, v_all, mask):
    rows, columns = q_all.shape
    lanes = lax.broadcasted_iota(jnp.int32, (rows, 128), 1)
    logs = jnp.zeros((rows, 128), f32)
    parts = []
    for pair in range(columns // 128):
        at = slice(pair * 128, pair * 128 + 128)
        q = q_all[:, at] * jnp.asarray(SCALING, bf16)
        k, v = k_all[:, at], v_all[:, at]
        outs = []
        for head in range(2):
            scores = mm_t(jnp.where(pair_mask(head), q, jnp.zeros_like(q)), k) + mask
            largest = jnp.max(scores, axis=-1, keepdims=True)
            exponent = jnp.exp(scores - largest)
            total = jnp.sum(exponent, axis=-1, keepdims=True)
            outs.append(mm(exponent.astype(bf16), v) / total)
            logs = jnp.where(lanes == pair * 2 + head, largest + jnp.log(total), logs)
        parts.append(jnp.where(pair_mask(0), outs[0], outs[1]))
    return jnp.concatenate(parts, axis=1), jnp.transpose(logs)


def attention_kernel(q_ref, k_ref, v_ref, mask_ref, w_out, heads_out, wide_out, log_out, low, high):
    wide, logs = attention_rows(q_ref[...], k_ref, v_ref, mask_ref[...])
    heads = wide.astype(bf16)
    wide_out[...] = wide
    heads_out[...] = heads
    log_out[...] = logs[: log_out.shape[0]]
    put_low_high(mm_t(heads, w_out[...]).astype(bf16), low, high)


def encoder_attention(queries, keys, values, mask, w_out, steps):
    slots, columns = queries.shape
    width = w_out.shape[0]
    rows = slots // steps
    block = pl.BlockSpec((rows, columns), turned(steps))
    return call(
        attention_kernel, (steps,),
        [block, full((slots, columns)), full((slots, columns)), full((1, slots)), full((width, columns))],
        [block, block, pl.BlockSpec((8, rows), lambda i: (0, (i + steps // 2) % steps))] + low_high(rows, width, steps),
        [shaped(slots, columns), shaped(slots, columns, f32), shaped(8, slots, f32)] + [shaped(slots // 2, width)] * 2,
        [],
        cost(8 * slots * slots * columns, 8 * slots * columns + 2 * slots * width, slots * slots * columns // HEAD),
        queries, keys, values, mask, w_out,
    )


def attention_back_rows(grads, wide, logs, q_all, k_all, v_all, mask, add):
    inner = jnp.transpose(grads.astype(f32) * wide)
    sub = lax.broadcasted_iota(jnp.int32, (128, 1), 0) // HEAD
    parts = []
    for pair in range(grads.shape[1] // 128):
        at = slice(pair * 128, pair * 128 + 128)
        q = q_all[:, at] * jnp.asarray(SCALING, bf16)
        k, v, g = k_all[:, at], v_all[:, at], grads[:, at]
        dk, dv, dq = 0.0, 0.0, []
        for head in range(2):
            keep = pair_mask(head)
            q_one = jnp.where(keep, q, jnp.zeros_like(q))
            g_one = jnp.where(keep, g, jnp.zeros_like(g))
            at_head = pair * 2 + head
            probability = jnp.exp((mm_t(k, q_one) + mask) - logs[at_head : at_head + 1, :])
            dv = dv + mm(probability.astype(bf16), g_one)
            delta = jnp.sum(inner[at_head * HEAD : (at_head + 1) * HEAD], axis=0, keepdims=True)
            scores_grad = (probability * (mm_t(v, g_one) - delta)).astype(bf16)
            dk = dk + mm(scores_grad, q_one)
            dq.append(t_mm(k, scores_grad))
        add(at, dk, dv)
        parts.append(jnp.transpose(jnp.where(sub == 0, dq[0], dq[1]) * SCALING))
    return jnp.concatenate(parts, axis=1).astype(bf16)


def attention_back_kernel(steps, *refs):
    parts = refs[:steps]
    (wide_ref, log_ref, q_ref, k_ref, v_ref, mask_ref, w_out, rows_out, dq_out, dk_out, dv_out, q_sum, v_sum, held, dk_sum, dv_sum) = refs[steps:]
    step = pl.program_id(0)
    grad_rows = pick_block(parts, held)
    rows_out[...] = grad_rows
    grads = mm(grad_rows, w_out[...]).astype(bf16)

    @pl.when(step == 0)
    def _():
        dk_sum[...] = jnp.zeros_like(dk_sum)
        dv_sum[...] = jnp.zeros_like(dv_sum)
        q_sum[...] = jnp.zeros_like(q_sum)

    def add(at, dk, dv):
        dk_sum[:, at] += dk
        dv_sum[:, at] += dv

    dq = attention_back_rows(grads, wide_ref[...], log_ref, q_ref[...], k_ref, v_ref, mask_ref[...], add)
    dq_out[...] = dq
    q_sum[...] += jnp.sum(dq.astype(f32), axis=0, keepdims=True)

    @pl.when(step == steps - 1)
    def _():
        dk_out[...] = dk_sum[...].astype(bf16)
        dv = dv_sum[...].astype(bf16)
        dv_out[...] = dv
        v_sum[...] = jnp.sum(dv.astype(f32), axis=0, keepdims=True)


def encoder_attention_back(grad_parts, wide, logs, queries, keys, values, mask, w_out):
    slots, columns = queries.shape
    width = w_out.shape[0]
    steps = len(grad_parts)
    rows = slots // steps
    whole, row = full((slots, columns)), full((1, columns))
    block = pl.BlockSpec((rows, columns), turned(steps))

    def kernel(*refs):
        attention_back_kernel(steps, *refs)

    return call(
        kernel, (steps,),
        [full((rows, width))] * steps
        + [block, pl.BlockSpec((8, rows), lambda i: (0, (i + steps // 2) % steps)), block, whole, whole, full((slots, 1)), full((width, columns))],
        [pl.BlockSpec((rows, width), turned(steps)), block, whole, whole, row, row],
        [shaped(slots, width)] + [shaped(slots, columns)] * 3 + [shaped(1, columns, f32)] * 2,
        [pltpu.VMEM((rows, width), bf16)] + [pltpu.VMEM((slots, columns), f32)] * 2,
        cost(20 * slots * slots * columns, 16 * slots * columns + 2 * slots * width, slots * slots * columns // HEAD),
        *grad_parts, wide, logs, queries, keys, values, mask, w_out,
    )


def ffn_kernel(steps, *refs):
    parts, (w_in, bias, w_out, x_out, hidden_out, slope_out, low, high, held) = refs[:steps], refs[steps:]
    x = pick_block(parts, held)
    x_out[...] = x
    hidden, slope = gelu_pair(mm(x, w_in[...]) + bias[...])
    hidden = hidden.astype(bf16)
    hidden_out[...] = hidden
    slope_out[...] = slope.astype(bf16)
    put_low_high(mm_t(hidden, w_out[...]).astype(bf16), low, high)


def ffn_forward(parts, w_in, bias, w_out):
    steps = len(parts)
    rows, width = parts[0].shape
    slots = rows * steps
    units = w_in.shape[1]
    block = pl.BlockSpec((rows, units), turned(steps))

    def kernel(*refs):
        ffn_kernel(steps, *refs)

    return call(
        kernel, (steps,),
        [full((rows, width))] * steps + [full((width, units)), full((1, units)), full((width, units))],
        [pl.BlockSpec((rows, width), turned(steps)), block, block] + low_high(rows, width, steps),
        [shaped(slots, width)] + [shaped(slots, units)] * 2 + [shaped(slots // 2, width)] * 2,
        [pltpu.VMEM((rows, width), bf16)],
        cost(4 * slots * width * units, 8 * slots * units + 4 * units * width, 2 * slots * units),
        *parts, w_in, bias, w_out,
    )


def ffn_back_kernel(steps, *refs):
    parts, (slope, w_in, w_out, x_out, before_out, low, high, bias_out, held) = refs[:steps], refs[steps:]
    x = pick_block(parts, held)
    x_out[...] = x
    before = (mm(x, w_out[...]) * slope[...].astype(f32)).astype(bf16)
    before_out[...] = before

    @pl.when(pl.program_id(0) == 0)
    def _():
        bias_out[...] = jnp.zeros_like(bias_out)

    bias_out[...] += jnp.sum(before.astype(f32), axis=0, keepdims=True)
    put_low_high(mm_t(before, w_in[...]).astype(bf16), low, high)


def ffn_backward(parts, slope, w_in, w_out):
    steps = len(parts)
    rows, width = parts[0].shape
    slots = rows * steps
    units = w_in.shape[1]
    block = pl.BlockSpec((rows, units), turned(steps))

    def kernel(*refs):
        ffn_back_kernel(steps, *refs)

    return call(
        kernel, (steps,),
        [full((rows, width))] * steps + [block, full((width, units)), full((width, units))],
        [pl.BlockSpec((rows, width), turned(steps)), block] + low_high(rows, width, steps) + [full((1, units))],
        [shaped(slots, width), shaped(slots, units)] + [shaped(slots // 2, width)] * 2 + [shaped(1, units, f32)],
        [pltpu.VMEM((rows, width), bf16)],
        cost(4 * slots * width * units, 6 * slots * units + 4 * units * width),
        *parts, slope, w_in, w_out,
    )


def back_sum(values, matrices, steps):
    slots, columns = values[0].shape
    width = matrices[0].shape[0]
    rows = slots // steps
    count = len(values)

    def kernel(*refs):
        total = 0.0
        for value, matrix in zip(refs[:count], refs[count : 2 * count]):
            total = total + mm_t(value[...], matrix[...])
        put_low_high(total.astype(bf16), *refs[2 * count :])

    return call(
        kernel, (steps,),
        [pl.BlockSpec((rows, columns), turned(steps))] * count + [full((width, columns))] * count,
        low_high(rows, width, steps),
        [shaped(slots // 2, width)] * 2, [],
        cost(2 * count * slots * width * columns, 2 * slots * width),
        *values, *matrices,
    )


def project_parts(parts, matrices, biases):
    steps = len(parts)
    rows, width = parts[0].shape
    slots = rows * steps
    columns = matrices[0].shape[1]
    count = len(matrices)

    def kernel(*refs):
        held = refs[-1]
        x = pick_block(refs[:steps], held)
        inner = refs[steps:-1]
        inner[2 * count][...] = x
        for index in range(count):
            inner[2 * count + 1 + index][...] = (mm(x, inner[index][...]) + inner[count + index][...]).astype(bf16)

    return call(
        kernel, (steps,),
        [full((rows, width))] * steps + [full((width, columns))] * count + [full((1, columns))] * count,
        [pl.BlockSpec((rows, width), turned(steps))] + [pl.BlockSpec((rows, columns), turned(steps))] * count,
        [shaped(slots, width)] + [shaped(slots, columns)] * count,
        [pltpu.VMEM((rows, width), bf16)],
        cost(2 * count * slots * width * columns, 4 * slots * width),
        *parts, *matrices, *biases,
    )


CHUNKS = 4


MASKS = (0, 2, 1, 3)


def weight_grad(section, order_ref, enc_pairs, dec_pairs):
    width = dec_pairs[0][0].shape[1]
    chunk = width // CHUNKS
    tables, count = len(enc_pairs), len(dec_pairs)
    total_columns = sum(g.shape[1] for _, g in dec_pairs)
    flat = [pair for pairs in (*enc_pairs, dec_pairs) for pair in pairs]

    def kernel(at, order_at, *refs):
        ins, (low, high) = refs[: 2 * len(flat)], refs[2 * len(flat) :]

        def product(index):
            return jnp.concatenate(
                [t_mm(ins[2 * (index * count + one)][...], ins[2 * (index * count + one) + 1][...]) for one in range(count)], axis=1
            )

        @pl.when(at[0] == 0)
        def _():
            total = 0.0
            for table in range(tables):
                total = total + product(table)
            put_low_high(total.astype(bf16), low, high)

        @pl.when(at[0] != 0)
        def _():
            put_low_high(product(tables).astype(bf16), low, high)

    in_specs, args = [], []
    for x, g in flat:
        in_specs += [pl.BlockSpec((x.shape[0], chunk), lambda i, s, at: (0, at[i])), full(g.shape)]
        args += [x, g]
    rows = sum(x.shape[0] for x, _ in flat) // count
    half = jax.ShapeDtypeStruct((2, chunk, total_columns), bf16)
    return call(
        kernel, (CHUNKS,), in_specs,
        [
            pl.BlockSpec((None, chunk, total_columns), lambda i, *_: (jnp.maximum(i - 2, 0), 0, 0)),
            pl.BlockSpec((None, chunk, total_columns), lambda i, *_: (jnp.minimum(i, 1), 0, 0)),
        ],
        [half] * 2, [],
        cost(2 * rows * width * total_columns, 2 * rows * (width + total_columns)),
        *args,
        prefetch=[section, order_ref],
    )


def sum_places(low, high, parts):
    chunk, columns = low.shape[1:]
    if lax.axis_size("dp") != CHUNKS:
        low, high = lax.psum((low, high), "dp")
        parts.extend([low[0], low[1], high[0], high[1]])
        return
    sent = flip(high, 0, "dp")
    yield "made"

    def add_pair(low_ref, sent_ref, own, far):
        own[...] = (low_ref[0].astype(f32) + sent_ref[0].astype(f32)).astype(bf16)
        far[...] = (low_ref[1].astype(f32) + sent_ref[1].astype(f32)).astype(bf16)

    whole = pl.BlockSpec(low.shape, lambda *_: (0, 0, 0))
    own, far = call(
        add_pair, (1,), [whole] * 2, [full((chunk, columns))] * 2, [shaped(chunk, columns)] * 2, [], cost(0, 6 * low.size), low, sent
    )
    sent = flip(far, 1, "dp")
    yield "one"
    total = add_rows(own, sent)
    second = flip(total, 1, "dp")
    third = flip(total, 0, "dp")
    yield "two"
    second = gate(second)
    fourth = flip(second, 0, "dp")
    parts.extend([total, second, third, fourth])
    yield "three"


def put_chunk(place, parts, put):
    other = place[0] ^ pl.program_id(0)
    for part, mask in zip(parts, MASKS):
        @pl.when(other == mask)
        def _(part=part):
            put(part)


def unite_one(place, parts):
    chunk, columns = parts[0].shape

    def kernel(place_at, *refs):
        def put(part):
            refs[-1][...] = part[...].astype(f32)

        put_chunk(place_at, refs[:-1], put)

    return call(
        kernel, (CHUNKS,), [full((chunk, columns))] * CHUNKS, pl.BlockSpec((chunk, columns), lambda i, *_: (i, 0)),
        shaped(CHUNKS * chunk, columns, f32), [], cost(0, 24 * chunk * columns), *parts,
        prefetch=[place],
    )


def pick_third(section, place, arrived, own):
    width, columns = own[0].shape
    rows = width // CHUNKS

    def kernel(at, place_at, *refs):
        turn = (pl.program_id(0) - place_at[0]) % CHUNKS
        first = at[0] == 0
        value = jnp.concatenate([jnp.where(first, a[...], b[...]) for a, b in zip(refs[:2], refs[2:4])], axis=1)
        for index in range(CHUNKS):
            @pl.when(turn == index)
            def _(index=index):
                refs[4 + index][...] = value

    block = pl.BlockSpec((rows, columns), lambda i, *_: (i, 0))
    return call(
        kernel, (CHUNKS,), [block] * 4, [full((rows, 2 * columns))] * CHUNKS, [shaped(rows, 2 * columns)] * CHUNKS, [],
        cost(0, 8 * width * columns), *arrived, *own,
        prefetch=[section, place],
    )


def send_chunks(chunks):
    return [lax.ppermute(chunk, "dp", [(i, (i + s + 1) % CHUNKS) for i in range(CHUNKS)]) for s, chunk in enumerate(chunks)]


def sum_chunks(own, sent):
    def kernel(*refs):
        total = refs[0][...].astype(f32)
        for ref in refs[1:-1]:
            total = total + ref[...].astype(f32)
        refs[-1][...] = total.astype(bf16)

    return call(
        kernel, (1,), [full(own.shape)] * CHUNKS, full(own.shape), shaped(*own.shape), [], cost(0, 10 * own.size), own, *sent
    )


def unite(place, qk, vo, thirds):
    rows, columns = qk[0].shape[0], qk[0].shape[1] // 2

    def kernel(place_at, *refs):
        qk, vo, chunks, (first, second) = refs[:CHUNKS], refs[CHUNKS : 2 * CHUNKS], refs[2 * CHUNKS : 3 * CHUNKS], refs[3 * CHUNKS :]
        for parts, out in ((qk, first), (vo, second)):
            def put(part, out=out):
                out[0] = part[:, :columns].astype(f32)
                out[1] = part[:, columns:].astype(f32)

            put_chunk(place_at, parts, put)
        turn = (place_at[0] - pl.program_id(0)) % CHUNKS
        for index in range(CHUNKS):
            @pl.when(turn == index)
            def _(index=index):
                first[2] = chunks[index][:, :columns].astype(f32)
                second[2] = chunks[index][:, columns:].astype(f32)

    stacked = pl.BlockSpec((3, rows, columns), lambda i, *_: (0, i, 0))
    return call(
        kernel, (CHUNKS,), [full((rows, 2 * columns))] * (3 * CHUNKS), [stacked] * 2,
        [jax.ShapeDtypeStruct((3, CHUNKS * rows, columns), f32)] * 2, [],
        cost(0, 36 * CHUNKS * rows * columns), *qk, *vo, *thirds,
        prefetch=[place],
    )


def weight_sum(xs, gs):
    count = len(xs)
    width, columns = xs[0].shape[1], gs[0].shape[1]

    def kernel(*refs):
        total = t_mm(refs[0][...], refs[count][...])
        for index in range(1, count):
            total = total + t_mm(refs[index][...], refs[count + index][...])
        refs[-1][...] = total.astype(bf16)

    rows = sum(x.shape[0] for x in xs)
    return call(
        kernel, (1,), [full(value.shape) for value in (*xs, *gs)], full((width, columns)), shaped(width, columns), [],
        cost(2 * rows * width * columns, 2 * rows * (width + columns)),
        *xs, *gs,
    )


def add_halves(low, sent):
    rows, width = low.shape[0] // 2, low.shape[1]

    def kernel(low_ref, sent_ref, low_out, high_out):
        total = (low_ref[...].astype(f32) + sent_ref[...].astype(f32)).astype(bf16)
        low_out[...] = total[:rows]
        high_out[...] = total[rows:]

    return call(
        kernel, (1,), [full((2 * rows, width))] * 2, [full((rows, width))] * 2, [shaped(rows, width)] * 2, [],
        cost(2 * rows * width, 12 * rows * width), low, sent,
    )


def add_rows(low, sent):
    rows, width = low.shape

    def kernel(low_ref, sent_ref, out):
        out[...] = (low_ref[...].astype(f32) + sent_ref[...].astype(f32)).astype(bf16)

    return call(
        kernel, (1,), [full((rows, width))] * 2, full((rows, width)), shaped(rows, width), [],
        cost(rows * width, 6 * rows * width), low, sent,
    )


def flip(value, bit, axis="tensor"):
    count = lax.axis_size(axis)
    return lax.ppermute(value, axis, [(i, i ^ (1 << bit)) for i in range(count)])


def axis_bits(axis):
    return lax.axis_size(axis).bit_length() - 1


def reduce_rest(low, sent):
    for bit in range(1, axis_bits("tensor")):
        low, high = add_halves(low, sent)
        sent = flip(high, bit)
    return low, sent


def gather_share(share):
    parts = [share]
    for bit in reversed(range(axis_bits("tensor"))):
        parts = parts + [flip(part, bit) for part in parts]
    return parts


def half_rest(low, sent):
    for bit in range(1, axis_bits("tensor")):
        low = add_rows(low, sent)
        sent = flip(low, bit)
    return low, sent


def gather_half(half):
    return [half, flip(half, 0)]


def to_second(value):
    return lax.ppermute(value, "section", [(0, 1)])


def to_first(value):
    return lax.ppermute(value, "section", [(1, 0)])


def sum_over(value, axis):
    for bit in range(axis_bits(axis)):
        value = value + flip(value, bit, axis)
    return value


def table_rows_of(value, table, tables, half):
    return jnp.concatenate([value[(core * tables + table) * half : (core * tables + table + 1) * half] for core in range(2)], axis=0)


def in_frame(values, half):
    return jnp.concatenate([value[core * half : (core + 1) * half] for core in range(2) for value in values], axis=0)


def decoder_attend(q, keys, values, masks, w_out, outs):
    heads_out, wide_out, log_out, low, high = outs
    tables = len(keys)
    half = q.shape[0] // (2 * tables)
    wides = []
    for table in range(tables):
        wide, logs = attention_rows(table_rows_of(q, table, tables, half), keys[table], values[table], masks[table])
        wides.append(wide)
        log_out[table * 8 : table * 8 + 8] = logs[:8]
    wide = in_frame(wides, half)
    heads = wide.astype(bf16)
    wide_out[...] = wide
    heads_out[...] = heads
    partial = mm_t(heads, w_out).astype(bf16)
    low[...] = partial[: tables * half]
    high[...] = partial[tables * half :]


def attend_shapes(rows, columns, width, tables):
    shapes = [(rows, columns, bf16), (rows, columns, f32), (8 * tables, rows // tables, f32), (rows // 2, width, bf16), (rows // 2, width, bf16)]
    return [full(shape[:2]) for shape in shapes], [shaped(*shape) for shape in shapes]


def decoder_self(parts, w_q, w_k, w_v, bias, masks, w_out):
    tables = masks.shape[0]
    rows, width = 2 * parts[0].shape[0], parts[0].shape[1]
    half = rows // (2 * tables)
    columns = w_q.shape[1]

    def kernel(own, other, w_q, w_k, w_v, bias, masks, w_out, x_out, q_out, k_out, v_out, *outs):
        x = jnp.concatenate([own[...], other[...]], axis=0)
        x_out[...] = x
        q = (mm(x, w_q[...]) + bias[0:1]).astype(bf16)
        k = mm(x, w_k[...]).astype(bf16)
        v = (mm(x, w_v[...]) + bias[1:2]).astype(bf16)
        q_out[...], k_out[...], v_out[...] = q, k, v
        keys, values = ([table_rows_of(value, table, tables, half) for table in range(tables)] for value in (k, v))
        decoder_attend(q, keys, values, [masks[table] for table in range(tables)], w_out[...], outs)

    specs, shapes = attend_shapes(rows, columns, width, tables)
    return call(
        kernel, (1,),
        [full(value.shape) for value in (*parts, w_q, w_k, w_v, bias, masks, w_out)],
        [full((rows, width))] + [full((rows, columns))] * 3 + specs,
        [shaped(rows, width)] + [shaped(rows, columns)] * 3 + shapes, [],
        cost(8 * rows * width * columns, 8 * width * columns),
        *parts, w_q, w_k, w_v, bias, masks, w_out,
    )


def decoder_cross(parts, w_q, bias, keys, values, masks, w_out):
    tables = len(keys)
    rows, width = 2 * parts[0].shape[0], parts[0].shape[1]
    columns = w_q.shape[1]

    def kernel(own, other, w_q, bias, masks, w_out, *refs):
        keys, values, (x_out, q_out), outs = refs[:tables], refs[tables : 2 * tables], refs[2 * tables : 2 * tables + 2], refs[2 * tables + 2 :]
        x = jnp.concatenate([own[...], other[...]], axis=0)
        x_out[...] = x
        q = (mm(x, w_q[...]) + bias[...]).astype(bf16)
        q_out[...] = q
        decoder_attend(q, keys, values, [masks[table : table + 1] for table in range(tables)], w_out[...], outs)

    specs, shapes = attend_shapes(rows, columns, width, tables)
    return call(
        kernel, (1,),
        [full(value.shape) for value in (*parts, w_q, bias, masks, w_out, *keys, *values)],
        [full((rows, width)), full((rows, columns))] + specs,
        [shaped(rows, width), shaped(rows, columns)] + shapes, [],
        cost(4 * rows * width * columns + 4 * rows * keys[0].shape[0] * columns, 8 * width * columns),
        *parts, w_q, bias, masks, w_out, *keys, *values,
    )


def decoder_attend_back(grads, wide, logs, q, keys, values, masks):
    tables = len(keys)
    half = q.shape[0] // (2 * tables)
    dqs, dks, dvs = [], [], []
    for table in range(tables):
        dk_parts, dv_parts = [], []

        def add(at, dk, dv):
            dk_parts.append(dk.astype(bf16))
            dv_parts.append(dv.astype(bf16))

        g, w, q_rows = (table_rows_of(value, table, tables, half) for value in (grads, wide, q))
        dqs.append(attention_back_rows(g, w, logs[table * 8 : table * 8 + 8], q_rows, keys[table], values[table], masks[table], add))
        dks.append(jnp.concatenate(dk_parts, axis=1))
        dvs.append(jnp.concatenate(dv_parts, axis=1))
    return in_frame(dqs, half), dks, dvs


def rows_sum(value):
    return jnp.sum(value.astype(f32), axis=0, keepdims=True)


def decoder_cross_back(parts, w_out, wide, logs, q, keys, values, masks, w_q):
    tables = len(keys)
    rows, width = 2 * parts[0].shape[0], parts[0].shape[1]
    columns = w_q.shape[1]
    slots = keys[0].shape[0]

    def kernel(own, other, w_out, wide, logs, q, masks, w_q, *refs):
        keys, values, outs = refs[:tables], refs[tables : 2 * tables], refs[2 * tables :]
        x = jnp.concatenate([own[...], other[...]], axis=0)
        outs[0][...] = x
        grads = mm(x, w_out[...]).astype(bf16)
        columns_of = [masks[:, table : table + 1] for table in range(tables)]
        dq, dks, dvs = decoder_attend_back(grads, wide[...], logs[...], q[...], keys, values, columns_of)
        outs[1][...] = dq
        outs[2][...] = rows_sum(dq)
        partial = mm_t(dq, w_q[...]).astype(bf16)
        outs[3][...] = partial[: rows // 2]
        outs[4][...] = partial[rows // 2 :]
        total = 0.0
        for table in range(tables):
            outs[6 + table][...] = dks[table]
            outs[6 + tables + table][...] = dvs[table]
            total = total + rows_sum(dvs[table])
        outs[5][...] = total

    shapes = [(rows, width, bf16), (rows, columns, bf16), (1, columns, f32), (rows // 2, width, bf16), (rows // 2, width, bf16), (1, columns, f32)]
    shapes += [(slots, columns, bf16)] * (2 * tables)
    return call(
        kernel, (1,),
        [full(value.shape) for value in (*parts, w_out, wide, logs, q, masks, w_q, *keys, *values)],
        [full(shape[:2]) for shape in shapes], [shaped(*shape) for shape in shapes], [],
        cost(4 * rows * width * columns + 10 * rows * slots * columns, 8 * width * columns),
        *parts, w_out, wide, logs, q, masks, w_q, *keys, *values,
    )


def decoder_self_back(parts, w_out, wide, logs, q, k, v, masks, w_q, w_k, w_v):
    tables = masks.shape[0]
    rows, width = 2 * parts[0].shape[0], parts[0].shape[1]
    half = rows // (2 * tables)
    columns = w_q.shape[1]

    def kernel(own, other, w_out, wide, logs, q, k, v, masks, w_q, w_k, w_v, x_out, q_out, k_out, v_out, q_sum, v_sum, low, high):
        x = jnp.concatenate([own[...], other[...]], axis=0)
        x_out[...] = x
        grads = mm(x, w_out[...]).astype(bf16)
        keys, values = ([table_rows_of(value[...], table, tables, half) for table in range(tables)] for value in (k, v))
        dq, dks, dvs = decoder_attend_back(grads, wide[...], logs[...], q[...], keys, values, [masks[table] for table in range(tables)])
        dk, dv = in_frame(dks, half), in_frame(dvs, half)
        q_out[...], k_out[...], v_out[...] = dq, dk, dv
        q_sum[...], v_sum[...] = rows_sum(dq), rows_sum(dv)
        partial = (mm_t(dq, w_q[...]) + mm_t(dk, w_k[...]) + mm_t(dv, w_v[...])).astype(bf16)
        low[...] = partial[: rows // 2]
        high[...] = partial[rows // 2 :]

    shapes = [(rows, width, bf16)] + [(rows, columns, bf16)] * 3 + [(1, columns, f32)] * 2 + [(rows // 2, width, bf16)] * 2
    return call(
        kernel, (1,),
        [full(value.shape) for value in (*parts, w_out, wide, logs, q, k, v, masks, w_q, w_k, w_v)],
        [full(shape[:2]) for shape in shapes], [shaped(*shape) for shape in shapes], [],
        cost(12 * rows * width * columns, 8 * width * columns),
        *parts, w_out, wide, logs, q, k, v, masks, w_q, w_k, w_v,
    )


def per_device(
    table_input,
    target_input,
    cotangent,
    table_lengths,
    target_lengths,
    query_key,
    value_out,
    hidden_in,
    hidden_out,
    hidden_bias,
    vectors,
    cross_bias,
):
    sections = lax.axis_size("section")
    count = lax.axis_size("tensor")
    bits = axis_bits("tensor")
    rank = lax.axis_index("tensor")
    section = lax.axis_index("section")
    is_first = section == 0
    section_ref = section.reshape(1).astype(jnp.int32)
    in_line = lax.axis_size("dp") == CHUNKS
    order_ref = jnp.where(in_line, lax.axis_index("dp"), 0).astype(jnp.int32) ^ jnp.array(MASKS[2:] + MASKS[:2], jnp.int32)
    place_ref = jnp.where(in_line, lax.axis_index("dp"), 0).reshape(1).astype(jnp.int32)
    tables, slots, width = table_input.shape
    targets = target_input.shape[1]
    columns = query_key.shape[3]
    rows = vectors[0]
    row = [rows[index : index + 1] for index in range(rows.shape[0])]
    head_rows = lax.dynamic_slice_in_dim(rows[0:3], rank * columns, columns, 1)
    no_bias = jnp.zeros((1, columns), f32)
    w_query, w_key, w_third_q = query_key[0, 0], query_key[0, 1], query_key[0, 2]
    w_value, w_out, w_third_v = value_out[0, 0], value_out[0, 1], value_out[0, 2]
    w_in, w_hidden_out = hidden_in[0], hidden_out[0]
    w_cross_key, w_cross_value, b_cross_value = to_second(w_third_q), to_second(w_third_v), to_second(head_rows[2:3])

    masks = [int(format(p, f"0{bits}b")[::-1], 2) for p in range(count)]
    owners = rank.astype(jnp.int32) ^ jnp.array(masks, jnp.int32)
    short = slots // (sections * count)
    row_index = (
        jnp.arange(sections)[None, :, None] * (count * short)
        + owners[:, None, None] * short
        + jnp.arange(short)[None, None, :]
    ).reshape(-1)
    table_valid = row_index[None, :] < table_lengths[:, None]
    table_mask = jnp.where(table_valid, 0.0, -1e30).astype(f32)

    cores = 2
    small = targets // (sections * count)
    core_order = (rank % cores) ^ jnp.arange(cores)
    half = targets // cores

    def target_frame(value):
        split = value.reshape(tables, sections, count // cores, cores, small, width)
        split = jnp.take(split, core_order, axis=3)
        return jnp.transpose(split, (3, 0, 2, 1, 4, 5)).reshape(cores, tables * half, width)

    target_index = (
        jnp.arange(sections)[None, None, :, None] * (count * small)
        + jnp.arange(count // cores)[None, :, None, None] * (cores * small)
        + core_order[:, None, None, None] * small
        + jnp.arange(small)[None, None, None, :]
    ).reshape(-1)
    target_rows = target_frame(target_input)
    grad_rows_half = target_frame(cotangent)[0]
    target_valid = target_index[None, :] < target_lengths[:, None]
    causal = (target_index[None, :] <= target_index[:, None])[None] & target_valid[:, None, :]

    causal_mask = jnp.where(causal, 0.0, -1e30).astype(f32)
    causal_back = jnp.swapaxes(causal_mask, 1, 2)

    encoder_kept, encoder_out = {}, {}
    cross, dec, grad_memory = {}, {}, {}
    order.last = None

    def encode(table):
        first_in, queries, keys, values, normed, raw = encoder_qkv(
            table_input, table, owners, row[9], row[10], w_query, w_key, w_value, head_rows[0:2], sections
        )
        yield "qkv"
        heads, wide, logs, low, high = encoder_attention(queries, keys, values, table_mask[table][None], w_out, count)
        sent = flip(high, 0)
        yield "attention"
        parts = reduce_rest(low, sent)
        yield "reduce"
        summed_one, middle, sent = norm_forward(normed, parts, row[3], row[5], row[6])
        parts = gather_share(sent)
        yield "norm"
        yield "gather"
        second_in, hidden, slope, low, high = ffn_forward(parts, w_in, hidden_bias, w_hidden_out)
        sent = flip(high, 0)
        yield "ffn"
        parts = reduce_rest(low, sent)
        yield "reduce two"
        summed_two, _, memory = norm_forward(middle, parts, row[4], row[7], row[8])
        encoder_kept[table] = (raw, first_in, queries, keys, values, heads, wide, logs, summed_one, second_in, hidden, slope, summed_two)
        memory = to_second(memory)
        yield "memory"
        parts = gather_share(memory)
        yield "moved"
        yield "gather two"
        cross[table] = project_parts(parts, [w_cross_key, w_cross_value], [no_bias, b_cross_value])
        yield "cross"

    def decode():
        dec["first"], q, k, v, heads, wide, logs, low, high = decoder_self(
            [target_rows[0], target_rows[1]], w_query, w_key, w_value, head_rows[0:2], causal_mask, w_out
        )
        dec["self"] = (q, k, v, heads, wide, logs)
        sent = flip(high, 0)
        yield "self"
        parts = half_rest(low, sent)
        yield "reduce"
        dec["one"], middle, sent = norm_forward(target_rows[0].astype(f32), parts, row[3], row[5], row[6])
        sent = gather_half(sent)
        yield "norm"
        keys, values = [cross[table][1] for table in range(tables)], [cross[table][2] for table in range(tables)]
        cross_in, q, heads, wide, logs, low, high = decoder_cross(
            sent, w_third_q, head_rows[2:3], keys, values, table_mask, w_third_v
        )
        parts = half_rest(low, flip(high, 0))
        three, later, sent = norm_forward(middle, parts, cross_bias[None], row[9], row[10])
        third_in, hidden, slope, low, high = ffn_forward(gather_half(sent), w_in, hidden_bias, w_hidden_out)
        parts = half_rest(low, flip(high, 0))
        two, _, dec["out"] = norm_forward(later, parts, row[4], row[7], row[8])
        grad_two, sent, dec["sums_two"] = norm_backward(two, row[7], [grad_rows_half])
        grad_two_rows, before_grad, low, high, dec["bias"] = ffn_backward(gather_half(sent), slope, w_in, w_hidden_out)
        parts = half_rest(low, flip(high, 0))
        grad_three, sent, dec["sums_three"] = norm_backward(three, row[9], [grad_two, *parts])
        grad_three_rows, dq, dec["third_sum"], low, high, third_bias, *rest = decoder_cross_back(
            gather_half(sent), w_third_v, wide, logs, q, keys, values, jnp.swapaxes(table_mask, 0, 1), w_third_q
        )
        dec["cross_rows"] = low, high
        dks, dvs = rest[:tables], rest[tables:]
        for table in range(tables):
            low, high = back_sum([dks[table], dvs[table]], [w_cross_key, w_cross_value], count)
            dec["memory", table] = low, flip(high, 0)
        dec["grad_three"] = grad_three
        dec["pairs"] = {"in": [(third_in, before_grad)], "out": [(grad_two_rows, hidden)]}
        yield "back"
        memory_rows = [cross[table][0] for table in range(tables)]
        arrived = weight_sum(memory_rows, dks), weight_sum(memory_rows, dvs)
        own = weight_sum([cross_in], [dq]), weight_sum([grad_three_rows], [heads])
        yield "thirds"
        arrived = [to_first(value) for value in gate(*arrived)]
        dec["third_bias"] = to_first(third_bias)
        yield "third send"
        first, *rest = pick_third(section_ref, place_ref, arrived, own)
        if in_line:
            sent = send_chunks(rest)
        yield "third pick"
        if in_line:
            total = sum_chunks(first, sent)
            sent = send_chunks([total] * (CHUNKS - 1))
            dec["thirds"] = [total, *sent]
        else:
            totals = lax.psum([first, *rest], "dp")
            dec["thirds"] = totals[:1] + totals[:0:-1]
        yield "third sum"

    def memory_back(table):
        keep, sent = reduce_rest(*dec["memory", table])
        yield "reduce"
        grad_memory[table] = to_first(add_rows(keep, sent))
        yield "moved"

    def decode_rest():
        low, high = gate(*dec["cross_rows"])
        sent = flip(high, 0)
        yield "start"
        parts = half_rest(low, sent)
        yield "reduce"
        grad_one, sent, dec["sums_one"] = norm_backward(dec["one"], row[5], [dec["grad_three"], *parts])
        sent = gather_half(sent)
        yield "norm"
        q, k, v, heads, wide, logs = dec["self"]
        grad_one_rows, grad_q, grad_k, grad_v, dec["sum_q"], dec["sum_v"], low, high = decoder_self_back(
            sent, w_out, wide, logs, q, k, v, causal_back, w_query, w_key, w_value
        )
        first = dec["first"]
        dec["pairs"].update({"qk": [(first, grad_q), (first, grad_k)], "vo": [(first, grad_v), (grad_one_rows, heads)]})
        sent = flip(high, 0)
        yield "self"
        keep, sent = half_rest(low, sent)
        yield "reduce two"
        dec["target_grad"] = (grad_one + keep.astype(f32) + sent.astype(f32)).astype(bf16)

    def encode_back(table):
        (raw, first_in, queries, keys, values, heads, wide, logs, summed_one, second_in, hidden, slope, summed_two) = encoder_kept[table]
        grad_two, sent, sums_two = norm_backward(summed_two, row[7], [grad_memory[table]])
        parts = gather_share(sent)
        yield "norm two"
        yield "gather two"
        grad_two_rows, grad_before, low, high, bias = ffn_backward(parts, slope, w_in, w_hidden_out)
        pairs = {"in": [(second_in, grad_before)], "out": [(grad_two_rows, hidden)]}
        encoder_out[table] = pairs
        sent = flip(high, 0)
        yield "ffn"
        parts = reduce_rest(low, sent)
        yield "reduce two"
        grad_one, sent, sums_one = norm_backward(summed_one, row[5], [grad_two, *parts])
        parts = gather_share(sent)
        yield "norm one"
        yield "gather one"
        grad_one_rows, grad_q, grad_k, grad_v, sum_q, sum_v = encoder_attention_back(
            parts, wide, logs, queries, keys, values, table_mask[table][:, None], w_out
        )
        pairs.update({"qk": [(first_in, grad_q), (first_in, grad_k)], "vo": [(first_in, grad_v), (grad_one_rows, heads)]})
        yield "attention"
        low, high = back_sum([grad_q, grad_k, grad_v], [w_query, w_key, w_value], count)
        sent = flip(high, 0)
        yield "back"
        parts = reduce_rest(low, sent)
        yield "reduce one"
        _, pairs["table_grad"], sums_zero = norm_backward(raw, row[9], [grad_one, *parts])
        sums = [sums_one[2], sums_two[2], sums_one[0], sums_one[1], sums_two[0], sums_two[1], sums_zero[0], sums_zero[1]]
        pairs["sums"] = (jnp.stack(sums), sum_q[0], sum_v[0], bias)
        yield "norm zero"

    totals = {}

    def weights(name):
        totals[name] = []
        low, high = weight_grad(section_ref, order_ref, [encoder_out[table][name] for table in range(tables)], dec["pairs"][name])
        return sum_places(low, high, totals[name])

    def to(part, *labels):
        for label in labels:
            for said in part:
                if said == label:
                    break

    def each(parts, *labels):
        for label in labels:
            for part in parts:
                to(part, label)

    ahead, *behind = forward = [encode(table) for table in range(tables)]
    decoder = decode()
    to(ahead, "qkv", "attention")
    w_cross_key, w_cross_value, b_cross_value = gate(w_cross_key, w_cross_value, b_cross_value)
    each(behind, "qkv")
    to(ahead, "reduce")
    each(behind, "attention")
    to(ahead, "norm")
    each(behind, "reduce")
    to(decoder, "self", "reduce")
    to(ahead, "ffn")
    each(behind, "norm")
    to(decoder, "norm")
    to(ahead, "reduce two")
    each(behind, "ffn")
    to(ahead, "memory")
    each(behind, "reduce two", "memory")
    each(forward, "cross")

    to(decoder, "back")
    returned = [memory_back(table) for table in range(tables)]
    each(returned, "reduce")
    to(decoder, "thirds")
    each(returned, "moved")
    rest = decode_rest()

    ahead, *behind = backward = [encode_back(table) for table in range(tables)]
    to(ahead, "norm two")
    each(behind, "norm two")
    to(rest, "start")
    to(decoder, "third send")
    to(ahead, "ffn")
    to(rest, "reduce")
    to(ahead, "reduce two")
    to(decoder, "third pick")
    each(behind, "ffn")
    to(ahead, "norm one")
    each(behind, "reduce two")
    out_sum = weights("out")
    to(out_sum, "made")
    to(decoder, "third sum")
    in_sum = weights("in")
    to(in_sum, "made")
    to(rest, "norm")
    to(ahead, "attention")
    to(out_sum, "one")
    each(behind, "norm one")
    to(rest, "self")
    to(ahead, "back")
    to(in_sum, "one")
    to(rest, "reduce two")
    to(ahead, "reduce one")
    to(out_sum, "two")
    each(behind, "attention")
    to(in_sum, "two")
    qk_sum = weights("qk")
    to(qk_sum, "made")
    vo_sum = weights("vo")
    to(vo_sum, "made")
    to(out_sum, "three")
    each(behind, "back")
    to(ahead, "norm zero")
    to(in_sum, "three")
    to(qk_sum, "one")
    each(behind, "reduce one")
    to(vo_sum, "one")
    to(qk_sum, "two")
    each(behind, "norm zero")
    to(vo_sum, "two")
    to(qk_sum, "three")
    to(vo_sum, "three")
    for part in (rest, decoder, out_sum, in_sum, qk_sum, vo_sum, *backward, *forward):
        to(part, "end")

    table_grads = [encoder_out[table]["table_grad"] for table in range(tables)]
    enc_rows, enc_sum_q, enc_sum_v, enc_bias = (sum(values) for values in zip(*[encoder_out[table]["sums"] for table in range(tables)]))
    decoded, target_grad = dec["out"], dec["target_grad"]
    sums_one, sums_two, sums_three = dec["sums_one"], dec["sums_two"], dec["sums_three"]
    dec_rows = jnp.stack(
        [sums_one[2], sums_two[2], sums_one[0], sums_one[1], sums_two[0], sums_two[1], sums_three[0], sums_three[1], sums_three[2]]
    ) * (cores / count)
    dec_head_rows = [dec["sum_q"][0], dec["sum_v"][0], dec["third_sum"][0]]
    dec_bias = dec["bias"]
    third_bias_grad = dec["third_bias"][0]

    total_out, total_in = unite_one(place_ref, totals["out"]), unite_one(place_ref, totals["in"])
    query_key_grad, value_out_grad = unite(place_ref, totals["qk"], totals["vo"], dec["thirds"])

    head_sums = jnp.where(is_first, jnp.stack([enc_sum_q, enc_sum_v, third_bias_grad]), jnp.stack(dec_head_rows))
    placed = lax.dynamic_update_slice(jnp.zeros((3, width), f32), head_sums, (0, rank * columns))
    other_rows = jnp.where(is_first, jnp.pad(enc_rows, ((0, 1), (0, 0))), dec_rows)
    bias_row = jnp.pad(jnp.where(is_first, enc_bias, dec_bias), ((0, 0), (0, width - enc_bias.shape[1])))
    bundle = sum_over(jnp.concatenate([placed, other_rows, bias_row]), "dp")
    bias_sum = bundle[12:13, : enc_bias.shape[1]]
    bundle = sum_over(bundle[:12], "tensor")
    vector_total = bundle[:11]
    cross_total = bundle[11] + lax.ppermute(bundle[11], "section", [(0, 1), (1, 0)])

    table_grads = jnp.stack(table_grads).reshape(tables, sections, short, width)
    moved_up = lax.ppermute(table_grads[:, 1], "section", [(0, 1)])
    table_out = jnp.where(is_first, table_grads[:, 0], moved_up)
    own = lax.dynamic_slice_in_dim(
        jnp.stack([decoded, target_grad]).reshape(2, tables, count // cores, sections, small, width),
        rank // cores,
        1,
        2,
    )[:, :, 0]
    moved_down = lax.ppermute(own[:, :, 0], "section", [(1, 0)])
    small_out = jnp.where(is_first, moved_down, own[:, :, 1])
    return (
        small_out[0],
        table_out,
        small_out[1],
        query_key_grad[None],
        value_out_grad[None],
        total_in[None],
        total_out[None],
        bias_sum,
        vector_total[None],
        cross_total,
    )


def solution(mesh):
    in_specs = (
        P("dp", None, None),
        P("dp", None, None),
        P("dp", None, None),
        P("dp"),
        P("dp"),
        P("section", None, None, "tensor"),
        P("section", None, None, "tensor"),
        P("section", None, "tensor"),
        P("section", None, "tensor"),
        P("section", "tensor"),
        P("section", None, None),
        P(),
    )
    out_specs = (
        P("dp", ("section", "tensor"), None),
        P("dp", ("section", "tensor"), None),
        P("dp", ("section", "tensor"), None),
        P("section", None, None, "tensor"),
        P("section", None, None, "tensor"),
        P("section", None, "tensor"),
        P("section", None, "tensor"),
        P("section", "tensor"),
        P("section", None, None),
        P(),
    )
    return jax.shard_map(
        per_device, mesh=mesh, in_specs=in_specs, out_specs=out_specs, check_vma=False
    )
```

time: 1000 us -> 747 us (0.75)
  Pallas kernels: 0 us -> 249 us
  matrix products: 215 us -> 0 us
  other arithmetic: 154 us -> 8.91 us
  blocking collectives: 124 us -> 0 us
  local copies, waits for them, and re-layouts: 117 us -> 82 us
  starting transfers between devices: 72.2 us -> 101 us
  between operations: 18.7 us -> 3.63 us
    pallas_call x0 -> x84, Pallas kernels: none -> 249 us  [the longest x77 249 us: call(): pl.pallas_call(ordered, grid_spec=grid_spec, out_shape=out_shape, compile...]
    dot_general x86 -> x0, matrix products: 215 us -> none  [the longest x22 49.1 us: mm(): lax.dot_general(a, b, (((1,), (0,)), ((), ())), preferred_element_type=f32)]
    ppermute x53 -> x92, waiting for transfers between devices: 122 us -> 262 us  [the longest x85 261 us: flip(): return lax.ppermute(value, axis, [(i, i ^ 1 << bit) for i in range(count)])]
    psum x1 -> x0, waiting for transfers between devices: 136 us -> none  [per_device(): lax.psum(jnp.where(is_first, own.astype(bf16), other.astype(bf16)), 'dp')]
    psum x3 -> x0, blocking collectives: 124 us -> none  [the longest x1 67.6 us: per_device(): lax.psum(jnp.concatenate([placed, other_rows]), ('dp', 'tensor'))]
    reduce_sum x43 -> x0, other arithmetic: 51.6 us -> none  [the longest x4 17.2 us: attention_forward(): denominator = jnp.sum(exponent, axis=-1, keepdims=True)]
    convert_element_type x25 -> x2, other arithmetic: 36.6 us -> 1.31 us  [the longest x1 1.26 us: decode_rest(): (grad_one + keep.astype(f32) + sent.astype(f32)).astype(bf16)]
    ppermute x53 -> x92, starting transfers between devices: 40.7 us -> 75.9 us  [the longest x85 64.7 us: flip(): return lax.ppermute(value, axis, [(i, i ^ 1 << bit) for i in range(count)])]
  transfers between devices with their start and end apart: 66 -> 104, of which waited for: 29 -> 45; matrix products, arithmetic and copies ran while one was open for 41% -> 5% of each run, Pallas kernels for 0% -> 25%
where the time goes in v2:
time: 747 us; the launch traced here: 734 us
  waiting for transfers between devices  290 us (39%)
  Pallas kernels  249 us (33%)
  starting transfers between devices  101 us (14%)
  local copies, waits for them, and re-layouts  82 us (11%)
  other arithmetic  8.91 us (1%)
    ppermute x85, waiting for transfers between devices, flip(): return lax.ppermute(value, axis, [(i, i ^ 1 << bit) for i in range(count)])  261 us
    pallas_call x77, Pallas kernels, call(): pl.pallas_call(ordered, grid_spec=grid_spec, out_shape=out_shape, compile...  249 us
    ppermute x85, starting transfers between devices, flip(): return lax.ppermute(value, axis, [(i, i ^ 1 << bit) for i in range(count)])  64.7 us
    unnamed x496, local copies, waits for them, and re-layouts  54.6 us
    ppermute x5, waiting for transfers between devices, to_first(): return lax.ppermute(value, 'section', [(1, 0)])  15.7 us
  transfers between devices with their start and end apart: 104, of which 45 were waited for; matrix products, arithmetic and copies ran while one was open for 5% of the time, Pallas kernels for 25%

profile of v2, /device:TPU:0, one launch (start us, length us, event | category | flops | bytes accessed | tf_op | source)
XLA Modules:
  0.0 734.3 jit_solution(9584044741078603226)
XLA Ops:
  3.6 5.6 collective-permute-start
  14.7 6.4 encoder_qkv.2
  22.8 10.4 %attention_kernel.2 = (bf16[1024,256]{1,0:T(8,128)(2,1)S(1)}, f32[1024,256]{1,0:T(8,128)S(1)}, f32[8,1024]{1,0:T(8,128)S(1)}, bf16[512,1024]{1,0:T(8,128)(2,1)S(1)}, bf16[512,1024]{1,0:T(8,128)(2,1)}) custom-call(bf16[1024,256]{1,0:T(8,128)(2,1)S(1)} %get-tuple-element.215.refs_0_.refs_5_.refs_6_, bf16[1024,256]{1,0:T(8,128)(2,1)S(1)} %get-tuple-element.216.refs_1_.refs_7_, ...), custom_call_target="tpu_custom_call" | custom-call | flops 2147483648 | bytes 4194304 | tf_op jit(solution)/shard_map/attention_kernel/pallas_call | solution.py:108
  42.4 6.4 encoder_qkv.3
  53.6 10.3 %attention_kernel.3 = (bf16[1024,256]{1,0:T(8,128)(2,1)S(1)}, f32[1024,256]{1,0:T(8,128)S(1)}, f32[8,1024]{1,0:T(8,128)S(1)}, bf16[512,1024]{1,0:T(8,128)(2,1)S(1)}, bf16[512,1024]{1,0:T(8,128)(2,1)}) custom-call(bf16[1024,256]{1,0:T(8,128)(2,1)S(1)} %get-tuple-element.220.refs_2_.refs_0_.refs_6_, bf16[1024,256]{1,0:T(8,128)(2,1)S(1)} %get-tuple-element.221.refs_1_.refs_7_, ...), custom_call_target="tpu_custom_call" | custom-call | flops 2147483648 | bytes 4194304 | tf_op jit(solution)/shard_map/attention_kernel/pallas_call | solution.py:108
  72.4 11.6 %collective-permute-done.9.refs_1_ = bf16[256,1024]{1,0:T(8,128)(2,1)} collective-permute-done((bf16[256,1024]{1,0:T(8,128)(2,1)}, bf16[256,1024]{1,0:T(8,128)(2,1)}, u32[]{:S(2)}, u32[]{:S(2)}) %collective-permute-start.9) | collective-permute-done | bytes 524320 | tf_op jit(solution)/shard_map/ppermute | solution.py:694
  95.6 10.7 %ffn_forward.3 = (bf16[1024,1024]{1,0:T(8,128)(2,1)}, bf16[1024,1024]{1,0:T(8,128)(2,1)}, bf16[1024,1024]{1,0:T(8,128)(2,1)}, bf16[512,1024]{1,0:T(8,128)(2,1)S(1)}, bf16[512,1024]{1,0:T(8,128)(2,1)S(1)}) custom-call(bf16[256,1024]{1,0:T(8,128)(2,1)} %get-tuple-element.238.refs_0_, bf16[256,1024]{1,0:T(8,128)(2,1)} %collective-permute-done.9.refs_1_, ...), custom_call_target="tpu_custom_call" | custom-call | flops 4294967296 | bytes 12582912 | tf_op jit(solution)/shard_map/ffn_forward/pallas_call | solution.py:108
  109.9 12.0 %collective-permute-done.15.refs_1_ = bf16[256,1024]{1,0:T(8,128)(2,1)S(1)} collective-permute-done((bf16[256,1024]{1,0:T(8,128)(2,1)S(1)}, bf16[256,1024]{1,0:T(8,128)(2,1)S(1)}, u32[]{:S(2)}, u32[]{:S(2)}) %collective-permute-start.15) | collective-permute-done | bytes 524320 | tf_op jit(solution)/shard_map/ppermute | solution.py:694
  123.0 7.6 %collective-permute-done.7.refs_2_ = bf16[128,1024]{1,0:T(8,128)(2,1)S(1)} collective-permute-done((bf16[128,1024]{1,0:T(8,128)(2,1)S(1)}, bf16[128,1024]{1,0:T(8,128)(2,1)S(1)}, u32[]{:S(2)}, u32[]{:S(2)}) %collective-permute-start.7) | collective-permute-done | bytes 262176 | tf_op jit(solution)/shard_map/ppermute | solution.py:694
  131.7 10.1 %ffn_forward.4 = (bf16[1024,1024]{1,0:T(8,128)(2,1)}, bf16[1024,1024]{1,0:T(8,128)(2,1)}, bf16[1024,1024]{1,0:T(8,128)(2,1)}, bf16[512,1024]{1,0:T(8,128)(2,1)S(1)}, bf16[512,1024]{1,0:T(8,128)(2,1)S(1)}) custom-call(bf16[256,1024]{1,0:T(8,128)(2,1)S(1)} %get-tuple-element.248.refs_0_, bf16[256,1024]{1,0:T(8,128)(2,1)S(1)} %collective-permute-done.15.refs_1_, ...), custom_call_target="tpu_custom_call" | custom-call | flops 4294967296 | bytes 12582912 | tf_op jit(solution)/shard_map/ffn_forward/pallas_call | solution.py:108
  142.9 13.2 %collective-permute-done.14.refs_2_ = bf16[256,1024]{1,0:T(8,128)(2,1)S(1)} collective-permute-done((bf16[256,1024]{1,0:T(8,128)(2,1)S(1)}, bf16[256,1024]{1,0:T(8,128)(2,1)S(1)}, u32[]{:S(2)}, u32[]{:S(2)}) %collective-permute-start.14) | collective-permute-done | bytes 524320 | tf_op jit(solution)/shard_map/ppermute | solution.py:694
  160.4 11.1 %collective-permute-done.23.refs_2_ = bf16[256,1024]{1,0:T(8,128)(2,1)S(1)} collective-permute-done((bf16[256,1024]{1,0:T(8,128)(2,1)S(1)}, bf16[256,1024]{1,0:T(8,128)(2,1)S(1)}, u32[]{:S(2)}, u32[]{:S(2)}) %collective-permute-start.23) | collective-permute-done | bytes 524320 | tf_op jit(solution)/shard_map/ppermute | solution.py:694
  175.5 9.2 %collective-permute-done.24.refs_0_ = bf16[256,1024]{1,0:T(8,128)(2,1)S(1)} collective-permute-done((bf16[256,1024]{1,0:T(8,128)(2,1)S(1)}, bf16[256,1024]{1,0:T(8,128)(2,1)S(1)}, u32[]{:S(2)}, u32[]{:S(2)}) %collective-permute-start.24) | collective-permute-done | bytes 524320 | tf_op jit(solution)/shard_map/ppermute | solution.py:727
  189.0 9.3 %collective-permute-done.25.refs_1_ = bf16[256,1024]{1,0:T(8,128)(2,1)S(1)} collective-permute-done((bf16[256,1024]{1,0:T(8,128)(2,1)S(1)}, bf16[256,1024]{1,0:T(8,128)(2,1)S(1)}, u32[]{:S(2)}, u32[]{:S(2)}) %collective-permute-start.25) | collective-permute-done | bytes 524320 | tf_op jit(solution)/shard_map/ppermute | solution.py:694
  198.8 4.0 project_parts.2
  202.8 4.3 project_parts.3
  207.1 3.7 decoder_cross.1
  213.7 7.3 collective-permute-done.29.refs_2_
  222.9 4.2 ffn_forward.5
  229.9 7.2 collective-permute-done.32.refs_2_
  240.3 4.5 ffn_backward.3
  248.5 7.3 collective-permute-done.35.refs_2_
  257.9 5.4 decoder_cross_back.1
  265.3 3.6 back_sum.4
  269.1 3.3 back_sum.5
  276.6 3.8 weight_sum.4.refs_4_.refs_0_
  280.3 3.1 weight_sum.5.refs_2_.refs_1_
  284.2 3.8 collective-permute-done.40.refs_1_
  289.4 9.0 %collective-permute-done.39.refs_1_ = bf16[256,1024]{1,0:T(8,128)(2,1)S(1)} collective-permute-done((bf16[256,1024]{1,0:T(8,128)(2,1)S(1)}, bf16[256,1024]{1,0:T(8,128)(2,1)S(1)}, u32[]{:S(2)}, u32[]{:S(2)}) %collective-permute-start.39) | collective-permute-done | bytes 524320 | tf_op jit(solution)/shard_map/ppermute | solution.py:694
  298.6 3.8 collective-permute-done.42.refs_0_
  306.8 8.8 %collective-permute-done.44.refs_1_ = bf16[256,1024]{1,0:T(8,128)(2,1)} collective-permute-done((bf16[256,1024]{1,0:T(8,128)(2,1)S(1)}, bf16[256,1024]{1,0:T(8,128)(2,1)}, u32[]{:S(2)}, u32[]{:S(2)}) %collective-permute-start.44) | collective-permute-done | bytes 524320 | tf_op jit(solution)/shard_map/ppermute | solution.py:694
  322.5 10.9 %ffn_backward.4 = (bf16[1024,1024]{1,0:T(8,128)(2,1)}, bf16[1024,1024]{1,0:T(8,128)(2,1)}, bf16[512,1024]{1,0:T(8,128)(2,1)S(1)}, bf16[512,1024]{1,0:T(8,128)(2,1)}, f32[1,1024]{1,0:T(1,128)S(1)}) custom-call(bf16[256,1024]{1,0:T(8,128)(2,1)S(1)} %copy-done.224, bf16[256,1024]{1,0:T(8,128)(2,1)} %collective-permute-done.44.refs_1_, ...), custom_call_target="tpu_custom_call" | custom-call | flops 4294967296 | bytes 10485760 | tf_op jit(solution)/shard_map/ffn_backward/pallas_call | solution.py:108
  339.1 9.9 %collective-permute-done.48.refs_1_ = bf16[256,1024]{1,0:T(8,128)(2,1)} collective-permute-done((bf16[256,1024]{1,0:T(8,128)(2,1)}, bf16[256,1024]{1,0:T(8,128)(2,1)}, u32[]{:S(2)}, u32[]{:S(2)}) %collective-permute-start.48) | collective-permute-done | bytes 524320 | tf_op jit(solution)/shard_map/ppermute | solution.py:694
  353.7 9.3 %collective-permute-done.52.refs_3_ = bf16[1024,256]{1,0:T(8,128)(2,1)} collective-permute-done((bf16[1024,256]{1,0:T(8,128)(2,1)S(1)}, bf16[1024,256]{1,0:T(8,128)(2,1)}, u32[]{:S(2)}, u32[]{:S(2)}) %collective-permute-start.52) | collective-permute-done | bytes 524320 | tf_op jit(solution)/shard_map/ppermute | solution.py:731
  366.1 10.9 %ffn_backward.5 = (bf16[1024,1024]{1,0:T(8,128)(2,1)}, bf16[1024,1024]{1,0:T(8,128)(2,1)}, bf16[512,1024]{1,0:T(8,128)(2,1)S(1)}, bf16[512,1024]{1,0:T(8,128)(2,1)S(1)}, f32[1,1024]{1,0:T(1,128)S(1)}) custom-call(bf16[256,1024]{1,0:T(8,128)(2,1)} %get-tuple-element.318.refs_0_, bf16[256,1024]{1,0:T(8,128)(2,1)} %collective-permute-done.48.refs_1_, ...), custom_call_target="tpu_custom_call" | custom-call | flops 4294967296 | bytes 10485760 | tf_op jit(solution)/shard_map/ffn_backward/pallas_call | solution.py:108
  378.2 13.2 %collective-permute-done.58.refs_2_ = bf16[256,1024]{1,0:T(8,128)(2,1)S(1)} collective-permute-done((bf16[256,1024]{1,0:T(8,128)(2,1)S(1)}, bf16[256,1024]{1,0:T(8,128)(2,1)S(1)}, u32[]{:S(2)}, u32[]{:S(2)}) %collective-permute-start.58) | collective-permute-done | bytes 524320 | tf_op jit(solution)/shard_map/ppermute | solution.py:694
  402.2 9.6 %weight_grad.4 = (bf16[2,256,1024]{2,1,0:T(8,128)(2,1)S(1)}, bf16[2,256,1024]{2,1,0:T(8,128)(2,1)}) custom-call(s32[1]{0:T(128)} %bitcast.31.refs_0_, s32[4]{0:T(128)S(1)} %broadcast_xor_fusion.refs_1_, bf16[1024,1024]{1,0:T(8,128)(2,1)S(1)} %copy-done.230, bf16[1024,1024]{1,0:T(8,128)(2,1)} %get-tuple-element.332.refs_3_, ...), custom_call_target="tpu_custom_call" | custom-call | flops 4831838208 | bytes 9437184 | tf_op jit(solution)/shard_map/weight_grad/pallas_call | solution.py:108
  423.1 8.7 %weight_grad.5 = (bf16[2,256,1024]{2,1,0:T(8,128)(2,1)S(1)}, bf16[2,256,1024]{2,1,0:T(8,128)(2,1)S(1)}) custom-call(s32[1]{0:T(128)} %bitcast.31.refs_0_, s32[4]{0:T(128)S(1)} %copy-done.190, bf16[1024,1024]{1,0:T(8,128)(2,1)S(1)} %copy-done.233, bf16[1024,1024]{1,0:T(8,128)(2,1)} %get-tuple-element.316.refs_3_, ...), custom_call_target="tpu_custom_call" | custom-call | flops 4831838208 | bytes 9437184 | tf_op jit(solution)/shard_map/weight_grad/pallas_call | solution.py:108
  432.5 5.1 collective-permute-start.66
  437.6 16.6 %encoder_attention_back.2 = (bf16[1024,1024]{1,0:T(8,128)(2,1)}, bf16[1024,256]{1,0:T(8,128)(2,1)S(1)}, bf16[1024,256]{1,0:T(8,128)(2,1)S(1)}, bf16[1024,256]{1,...) custom-call(bf16[256,1024]{1,0:T(8,128)(2,1)} %get-tuple-element.355.refs_0_, ...), custom_call_target="tpu_custom_call" | custom-call | flops 5368709120 | bytes 6291456 | tf_op jit(solution)/shard_map/encoder_attention_back/pallas_call | solution.py:108
  463.5 3.7 back_sum.6
  471.2 10.8 %collective-permute-done.71.refs_1_ = bf16[256,1024]{1,0:T(8,128)(2,1)} collective-permute-done((bf16[256,1024]{1,0:T(8,128)(2,1)}, bf16[256,1024]{1,0:T(8,128)(2,1)}, u32[]{:S(2)}, u32[]{:S(2)}) %collective-permute-start.71) | collective-permute-done | bytes 524320 | tf_op jit(solution)/shard_map/ppermute | solution.py:694
  493.5 13.0 %collective-permute-done.74.refs_1_ = bf16[256,1024]{1,0:T(8,128)(2,1)} collective-permute-done((bf16[256,1024]{1,0:T(8,128)(2,1)}, bf16[256,1024]{1,0:T(8,128)(2,1)}, u32[]{:S(2)}, u32[]{:S(2)}) %collective-permute-start.74) | collective-permute-done | bytes 524320 | tf_op jit(solution)/shard_map/ppermute | solution.py:694
  508.6 16.7 %encoder_attention_back.3 = (bf16[1024,1024]{1,0:T(8,128)(2,1)}, bf16[1024,256]{1,0:T(8,128)(2,1)S(1)}, bf16[1024,256]{1,0:T(8,128)(2,1)S(1)}, bf16[1024,256]{1,...) custom-call(bf16[256,1024]{1,0:T(8,128)(2,1)} %get-tuple-element.375.refs_0_, ...), custom_call_target="tpu_custom_call" | custom-call | flops 5368709120 | bytes 6291456 | tf_op jit(solution)/shard_map/encoder_attention_back/pallas_call | solution.py:108
  525.4 3.6 collective-permute-done.76.refs_1_
  530.3 7.2 weight_grad.6
  537.6 7.2 weight_grad.7
  548.7 3.6 back_sum.7
  553.4 3.9 collective-permute-start.78
  557.3 9.3 %collective-permute-done.70.refs_2_ = bf16[256,1024]{1,0:T(8,128)(2,1)S(1)} collective-permute-done((bf16[256,1024]{1,0:T(8,128)(2,1)S(1)}, bf16[256,1024]{1,0:T(8,128)(2,1)S(1)}, u32[]{:S(2)}, u32[]{:S(2)}) %collective-permute-start.70) | collective-permute-done | bytes 524320 | tf_op jit(solution)/shard_map/ppermute | solution.py:694
  569.1 10.5 %collective-permute-done.79.refs_0_ = bf16[256,1024]{1,0:T(8,128)(2,1)S(1)} collective-permute-done((bf16[256,1024]{1,0:T(8,128)(2,1)S(1)}, bf16[256,1024]{1,0:T(8,128)(2,1)S(1)}, u32[]{:S(2)}, u32[]{:S(2)}) %collective-permute-start.79) | collective-permute-done | bytes 524320 | tf_op jit(solution)/shard_map/ppermute | solution.py:694
  609.8 9.9 %collective-permute-done.81.refs_1_ = bf16[256,512]{1,0:T(8,128)(2,1)S(1)} collective-permute-done((bf16[256,512]{1,0:T(8,128)(2,1)}, bf16[256,512]{1,0:T(8,128)(2,1)S(1)}, u32[]{:S(2)}, u32[]{:S(2)}) %collective-permute-start.81) | collective-permute-done | bytes 262176 | tf_op jit(solution)/shard_map/ppermute | solution.py:694
  635.7 9.4 %collective-permute-done.100 = f32[13,1024]{1,0:T(8,128)S(1)} collective-permute-done((f32[13,1024]{1,0:T(8,128)S(1)}, f32[13,1024]{1,0:T(8,128)S(1)}, u32[]{:S(2)}, u32[]{:S(2)}) %collective-permute-start.100) | collective-permute-done | bytes 53280 | tf_op jit(solution)/shard_map/ppermute | solution.py:694
  646.5 3.4 collective-permute-start.85
  650.1 3.4 collective-permute-done.68
  657.5 4.0 collective-permute-done.85.refs_1_
  661.4 5.6 collective-permute-start.83
  667.3 28.3 %collective-permute-done.88.refs_0_ = bf16[256,512]{1,0:T(8,128)(2,1)S(1)} collective-permute-done((bf16[256,512]{1,0:T(8,128)(2,1)S(1)}, bf16[256,512]{1,0:T(8,128)(2,1)S(1)}, u32[]{:S(2)}, u32[]{:S(2)}) %collective-permute-start.88) | collective-permute-done | bytes 262176 | tf_op jit(solution)/shard_map/ppermute | solution.py:694
  706.1 4.0 unite_one.2.refs_5_
  710.2 3.6 unite_one.3.refs_13_
  714.6 5.6 collective-permute-done.87.refs_4_
  720.3 5.6 collective-permute-done.89.refs_7_
  725.9 4.0 collective-permute-done.90.refs_8_
  729.9 4.2 unite.1
  (801 shorter events, 235.3 us)
Async XLA Ops:
  3.6 38.2 %collective-permute-start = (bf16[1024,256]{1,0:T(8,128)(2,1)S(1)}, bf16[1024,256]{1,0:T(8,128)(2,1)}, u32[]{:S(2)}, u32[]{:S(2)}) collective-permute-start(bf16[1024,256]{1,0:T(8,128)(2,1)S(1)} %get-tuple-element.475.refs_2_.refs_7_), channel_id=1, source_target_pairs={{0,16},{1,17},{2,18},{3,19},{4,20},{5,21},{6,22},{7,23},{8,24},{9,... | collective-permute-start | bytes 1572872 | tf_op jit(solution)/shard_map/ppermute | solution.py:727
  9.2 32.6 %collective-permute-start.1 = (bf16[1024,256]{1,0:T(8,128)(2,1)S(1)}, bf16[1024,256]{1,0:T(8,128)(2,1)}, u32[]{:S(2)}, u32[]{:S(2)}) collective-permute-start(bf16[1024,256]{1,0:T(8,128)(2,1)S(1)} %get-tuple-element.439.refs_5_.refs_2_), channel_id=1, source_target_pairs={{0,16},{1,17},{2,18},{3,19},{4,20},{5,21},{6,22},{7,23},{8,24},{9,... | collective-permute-start | bytes 1572872 | tf_op jit(solution)/shard_map/ppermute | solution.py:727
  11.3 30.5 %collective-permute-start.2 = (f32[1,256]{1,0:T(1,128)S(1)}, f32[1,256]{1,0:T(1,128)S(1)}, u32[]{:S(2)}, u32[]{:S(2)}) collective-permute-start(f32[1,256]{1,0:T(1,128)S(1)} %fusion.7.refs_3_), channel_id=1, source_target_pairs={{0,16},{1,17},{2,18},{3,19},{4,20},{5,21},{6,22},{7,23},{8,24},{9,... | collective-permute-start | bytes 3080 | tf_op jit(solution)/shard_map/ppermute | solution.py:727
  52.0 14.4 %collective-permute-start.5 = (bf16[256,1024]{1,0:T(8,128)(2,1)S(1)}, bf16[256,1024]{1,0:T(8,128)(2,1)S(1)}, u32[]{:S(2)}, u32[]{:S(2)}) collective-permute-start(bf16[256,1024]{1,0:T(8,128)(2,1)S(1)} %get-tuple-element.229), channel_id=1, source_target_pairs={{0,2},{1,3},{2,0},{3,1},{4,6},{5,7},{6,4},{7,5},{8,10},{9,11},{10,... | collective-permute-start | bytes 1572872 | tf_op jit(solution)/shard_map/ppermute | solution.py:694
  65.9 18.2 %collective-permute-start.4 = (bf16[512,1024]{1,0:T(8,128)(2,1)}, bf16[512,1024]{1,0:T(8,128)(2,1)}, u32[]{:S(2)}, u32[]{:S(2)}) collective-permute-start(bf16[512,1024]{1,0:T(8,128)(2,1)} %get-tuple-element.227), channel_id=1, source_target_pairs={{0,1},{1,0},{2,3},{3,2},{4,5},{5,4},{6,7},{7,6},{8,9},{9,8},{10,11... | collective-permute-start | bytes 3145736 | tf_op jit(solution)/shard_map/ppermute | solution.py:694
  72.3 23.2 %collective-permute-start.10 = (bf16[256,1024]{1,0:T(8,128)(2,1)}, bf16[256,1024]{1,0:T(8,128)(2,1)S(1)}, u32[]{:S(2)}, u32[]{:S(2)}) collective-permute-start(bf16[256,1024]{1,0:T(8,128)(2,1)} %get-tuple-element.238.refs_0_), channel_id=1, source_target_pairs={{0,1},{1,0},{2,3},{3,2},{4,5},{5,4},{6,7},{7,6},{8,9},{9,8},{10,11... | collective-permute-start | bytes 1572872 | tf_op jit(solution)/shard_map/ppermute | solution.py:694
  106.4 24.5 %collective-permute-start.13 = (bf16[512,1024]{1,0:T(8,128)(2,1)S(1)}, bf16[512,1024]{1,0:T(8,128)(2,1)S(1)}, u32[]{:S(2)}, u32[]{:S(2)}) collective-permute-start(bf16[512,1024]{1,0:T(8,128)(2,1)S(1)} %get-tuple-element.244), channel_id=1, source_target_pairs={{0,1},{1,0},{2,3},{3,2},{4,5},{5,4},{6,7},{7,6},{8,9},{9,8},{10,11... | collective-permute-start | bytes 3145736 | tf_op jit(solution)/shard_map/ppermute | solution.py:694
  109.9 21.3 %collective-permute-start.16 = (bf16[256,1024]{1,0:T(8,128)(2,1)S(1)}, bf16[256,1024]{1,0:T(8,128)(2,1)S(1)}, u32[]{:S(2)}, u32[]{:S(2)}) collective-permute-start(bf16[256,1024]{1,0:T(8,128)(2,1)S(1)} %get-tuple-element.248.refs_0_), channel_id=1, source_target_pairs={{0,1},{1,0},{2,3},{3,2},{4,5},{5,4},{6,7},{7,6},{8,9},{9,8},{10,11... | collective-permute-start | bytes 1572872 | tf_op jit(solution)/shard_map/ppermute | solution.py:694
  141.8 15.8 %collective-permute-start.22 = (bf16[512,1024]{1,0:T(8,128)(2,1)S(1)}, bf16[512,1024]{1,0:T(8,128)(2,1)S(1)}, u32[]{:S(2)}, u32[]{:S(2)}) collective-permute-start(bf16[512,1024]{1,0:T(8,128)(2,1)S(1)} %get-tuple-element.254), channel_id=1, source_target_pairs={{0,1},{1,0},{2,3},{3,2},{4,5},{5,4},{6,7},{7,6},{8,9},{9,8},{10,11... | collective-permute-start | bytes 3145736 | tf_op jit(solution)/shard_map/ppermute | solution.py:694
  141.8 14.3 %collective-permute-start.14 = (bf16[256,1024]{1,0:T(8,128)(2,1)S(1)}, bf16[256,1024]{1,0:T(8,128)(2,1)S(1)}, u32[]{:S(2)}, u32[]{:S(2)}) collective-permute-start(bf16[256,1024]{1,0:T(8,128)(2,1)S(1)} %get-tuple-element.247), channel_id=1, source_target_pairs={{0,2},{1,3},{2,0},{3,1},{4,6},{5,7},{6,4},{7,5},{8,10},{9,11},{10,... | collective-permute-start | bytes 1572872 | tf_op jit(solution)/shard_map/ppermute | solution.py:694
  159.0 15.3 %collective-permute-start.18 = (bf16[256,1024]{1,0:T(8,128)(2,1)S(1)}, bf16[256,1024]{1,0:T(8,128)(2,1)S(1)}, u32[]{:S(2)}, u32[]{:S(2)}) collective-permute-start(bf16[256,1024]{1,0:T(8,128)(2,1)S(1)} %get-tuple-element.250), channel_id=1, source_target_pairs={{0,16},{1,17},{2,18},{3,19},{4,20},{5,21},{6,22},{7,23},{8,24},{9,... | collective-permute-start | bytes 1572872 | tf_op jit(solution)/shard_map/ppermute | solution.py:727
  273.2 14.8 %collective-permute-start.40 = (bf16[256,1024]{1,0:T(8,128)(2,1)S(1)}, bf16[256,1024]{1,0:T(8,128)(2,1)S(1)}, u32[]{:S(2)}, u32[]{:S(2)}) collective-permute-start(bf16[256,1024]{1,0:T(8,128)(2,1)S(1)} %get-tuple-element.300), channel_id=1, source_target_pairs={{0,2},{1,3},{2,0},{3,1},{4,6},{5,7},{6,4},{7,5},{8,10},{9,11},{10,... | collective-permute-start | bytes 1572872 | tf_op jit(solution)/shard_map/ppermute | solution.py:694
  275.4 23.0 %collective-permute-start.39 = (bf16[256,1024]{1,0:T(8,128)(2,1)S(1)}, bf16[256,1024]{1,0:T(8,128)(2,1)S(1)}, u32[]{:S(2)}, u32[]{:S(2)}) collective-permute-start(bf16[256,1024]{1,0:T(8,128)(2,1)S(1)} %get-tuple-element.299), channel_id=1, source_target_pairs={{0,2},{1,3},{2,0},{3,1},{4,6},{5,7},{6,4},{7,5},{8,10},{9,11},{10,... | collective-permute-start | bytes 1572872 | tf_op jit(solution)/shard_map/ppermute | solution.py:694
  306.7 14.7 %collective-permute-start.45 = (bf16[256,1024]{1,0:T(8,128)(2,1)S(1)}, bf16[256,1024]{1,0:T(8,128)(2,1)}, u32[]{:S(2)}, u32[]{:S(2)}) collective-permute-start(bf16[256,1024]{1,0:T(8,128)(2,1)S(1)} %get-tuple-element.311.refs_0_), channel_id=1, source_target_pairs={{0,1},{1,0},{2,3},{3,2},{4,5},{5,4},{6,7},{7,6},{8,9},{9,8},{10,11... | collective-permute-start | bytes 1572872 | tf_op jit(solution)/shard_map/ppermute | solution.py:694
  334.3 16.7 %collective-permute-start.53 = (bf16[512,1024]{1,0:T(8,128)(2,1)}, bf16[512,1024]{1,0:T(8,128)(2,1)}, u32[]{:S(2)}, u32[]{:S(2)}) collective-permute-start(bf16[512,1024]{1,0:T(8,128)(2,1)} %get-tuple-element.322), channel_id=1, source_target_pairs={{0,1},{1,0},{2,3},{3,2},{4,5},{5,4},{6,7},{7,6},{8,9},{9,8},{10,11... | collective-permute-start | bytes 3145736 | tf_op jit(solution)/shard_map/ppermute | solution.py:694
  334.3 14.7 %collective-permute-start.48 = (bf16[256,1024]{1,0:T(8,128)(2,1)}, bf16[256,1024]{1,0:T(8,128)(2,1)}, u32[]{:S(2)}, u32[]{:S(2)}) collective-permute-start(bf16[256,1024]{1,0:T(8,128)(2,1)} %get-tuple-element.318.refs_0_), channel_id=1, source_target_pairs={{0,2},{1,3},{2,0},{3,1},{4,6},{5,7},{6,4},{7,5},{8,10},{9,11},{10,... | collective-permute-start | bytes 1572872 | tf_op jit(solution)/shard_map/ppermute | solution.py:694
  335.5 18.2 %collective-permute-start.51 = (bf16[1024,256]{1,0:T(8,128)(2,1)}, bf16[1024,256]{1,0:T(8,128)(2,1)}, u32[]{:S(2)}, u32[]{:S(2)}) collective-permute-start(bf16[1024,256]{1,0:T(8,128)(2,1)} %get-tuple-element.313.refs_7_), channel_id=1, source_target_pairs={{16,0},{17,1},{18,2},{19,3},{20,4},{21,5},{22,6},{23,7},{24,8},{25... | collective-permute-start | bytes 1572872 | tf_op jit(solution)/shard_map/ppermute | solution.py:731
  336.8 26.2 %collective-permute-start.52 = (bf16[1024,256]{1,0:T(8,128)(2,1)S(1)}, bf16[1024,256]{1,0:T(8,128)(2,1)}, u32[]{:S(2)}, u32[]{:S(2)}) collective-permute-start(bf16[1024,256]{1,0:T(8,128)(2,1)S(1)} %copy-done.6), channel_id=1, source_target_pairs={{16,0},{17,1},{18,2},{19,3},{20,4},{21,5},{22,6},{23,7},{24,8},{25... | collective-permute-start | bytes 1572872 | tf_op jit(solution)/shard_map/ppermute | solution.py:731
  338.8 27.3 %collective-permute-start.49 = (bf16[256,1024]{1,0:T(8,128)(2,1)}, bf16[256,1024]{1,0:T(8,128)(2,1)}, u32[]{:S(2)}, u32[]{:S(2)}) collective-permute-start(bf16[256,1024]{1,0:T(8,128)(2,1)} %get-tuple-element.318.refs_0_), channel_id=1, source_target_pairs={{0,1},{1,0},{2,3},{3,2},{4,5},{5,4},{6,7},{7,6},{8,9},{9,8},{10,11... | collective-permute-start | bytes 1572872 | tf_op jit(solution)/shard_map/ppermute | solution.py:694
  349.0 17.1 %collective-permute-start.50 = (bf16[256,1024]{1,0:T(8,128)(2,1)}, bf16[256,1024]{1,0:T(8,128)(2,1)}, u32[]{:S(2)}, u32[]{:S(2)}) collective-permute-start(bf16[256,1024]{1,0:T(8,128)(2,1)} %collective-permute-done.48.refs_1_), channel_id=1, source_target_pairs={{0,1},{1,0},{2,3},{3,2},{4,5},{5,4},{6,7},{7,6},{8,9},{9,8},{10,11... | collective-permute-start | bytes 1572872 | tf_op jit(solution)/shard_map/ppermute | solution.py:694
  377.0 24.1 %collective-permute-start.57 = (bf16[512,1024]{1,0:T(8,128)(2,1)S(1)}, bf16[512,1024]{1,0:T(8,128)(2,1)S(1)}, u32[]{:S(2)}, u32[]{:S(2)}) collective-permute-start(bf16[512,1024]{1,0:T(8,128)(2,1)S(1)} %get-tuple-element.338), channel_id=1, source_target_pairs={{0,1},{1,0},{2,3},{3,2},{4,5},{5,4},{6,7},{7,6},{8,9},{9,8},{10,11... | collective-permute-start | bytes 3145736 | tf_op jit(solution)/shard_map/ppermute | solution.py:694
  377.1 14.3 %collective-permute-start.58 = (bf16[256,1024]{1,0:T(8,128)(2,1)S(1)}, bf16[256,1024]{1,0:T(8,128)(2,1)S(1)}, u32[]{:S(2)}, u32[]{:S(2)}) collective-permute-start(bf16[256,1024]{1,0:T(8,128)(2,1)S(1)} %get-tuple-element.340), channel_id=1, source_target_pairs={{0,2},{1,3},{2,0},{3,1},{4,6},{5,7},{6,4},{7,5},{8,10},{9,11},{10,... | collective-permute-start | bytes 1572872 | tf_op jit(solution)/shard_map/ppermute | solution.py:694
  394.1 19.1 %collective-permute-start.62 = (bf16[256,1024]{1,0:T(8,128)(2,1)}, bf16[256,1024]{1,0:T(8,128)(2,1)}, u32[]{:S(2)}, u32[]{:S(2)}) collective-permute-start(bf16[256,1024]{1,0:T(8,128)(2,1)} %get-tuple-element.355.refs_0_), channel_id=1, source_target_pairs={{0,2},{1,3},{2,0},{3,1},{4,6},{5,7},{6,4},{7,5},{8,10},{9,11},{10,... | collective-permute-start | bytes 1572872 | tf_op jit(solution)/shard_map/ppermute | solution.py:694
  395.2 17.3 %collective-permute-start.54 = (bf16[256,512]{1,0:T(8,128)(2,1)S(1)}, bf16[256,512]{1,0:T(8,128)(2,1)S(1)}, u32[]{:S(2)}, u32[]{:S(2)}) collective-permute-start(bf16[256,512]{1,0:T(8,128)(2,1)S(1)} %get-tuple-element.328), channel_id=1, source_target_pairs={{0,4},{4,8},{8,12},{12,0},{1,5},{5,9},{9,13},{13,1},{2,6},{6,10},{... | collective-permute-start | bytes 786440 | tf_op jit(solution)/shard_map/ppermute | solution.py:606
  396.8 19.4 %collective-permute-start.55 = (bf16[256,512]{1,0:T(8,128)(2,1)}, bf16[256,512]{1,0:T(8,128)(2,1)}, u32[]{:S(2)}, u32[]{:S(2)}) collective-permute-start(bf16[256,512]{1,0:T(8,128)(2,1)} %get-tuple-element.329), channel_id=1, source_target_pairs={{0,8},{4,12},{8,0},{12,4},{1,9},{5,13},{9,1},{13,5},{2,10},{6,14},... | collective-permute-start | bytes 786440 | tf_op jit(solution)/shard_map/ppermute | solution.py:606
  399.4 17.7 %collective-permute-start.56 = (bf16[256,512]{1,0:T(8,128)(2,1)}, bf16[256,512]{1,0:T(8,128)(2,1)}, u32[]{:S(2)}, u32[]{:S(2)}) collective-permute-start(bf16[256,512]{1,0:T(8,128)(2,1)} %get-tuple-element.330), channel_id=1, source_target_pairs={{0,12},{4,0},{8,4},{12,8},{1,13},{5,1},{9,5},{13,9},{2,14},{6,2},{... | collective-permute-start | bytes 786440 | tf_op jit(solution)/shard_map/ppermute | solution.py:606
  411.8 42.5 %collective-permute-start.61 = (bf16[2,256,1024]{2,1,0:T(8,128)(2,1)}, bf16[2,256,1024]{2,1,0:T(8,128)(2,1)}, u32[]{:S(2)}, u32[]{:S(2)}) collective-permute-start(bf16[2,256,1024]{2,1,0:T(8,128)(2,1)} %get-tuple-element.354), channel_id=1, source_target_pairs={{0,4},{4,0},{8,12},{12,8},{1,5},{5,1},{9,13},{13,9},{2,6},{6,2},{1... | collective-permute-start | bytes 3145736 | tf_op jit(solution)/shard_map/ppermute | solution.py:694
  413.2 19.3 %collective-permute-start.63 = (bf16[256,1024]{1,0:T(8,128)(2,1)}, bf16[256,1024]{1,0:T(8,128)(2,1)}, u32[]{:S(2)}, u32[]{:S(2)}) collective-permute-start(bf16[256,1024]{1,0:T(8,128)(2,1)} %get-tuple-element.355.refs_0_), channel_id=1, source_target_pairs={{0,1},{1,0},{2,3},{3,2},{4,5},{5,4},{6,7},{7,6},{8,9},{9,8},{10,11... | collective-permute-start | bytes 1572872 | tf_op jit(solution)/shard_map/ppermute | solution.py:694
  413.2 24.4 %collective-permute-start.64 = (bf16[256,1024]{1,0:T(8,128)(2,1)}, bf16[256,1024]{1,0:T(8,128)(2,1)}, u32[]{:S(2)}, u32[]{:S(2)}) collective-permute-start(bf16[256,1024]{1,0:T(8,128)(2,1)} %collective-permute-done.62.refs_1_), channel_id=1, source_target_pairs={{0,1},{1,0},{2,3},{3,2},{4,5},{5,4},{6,7},{7,6},{8,9},{9,8},{10,11... | collective-permute-start | bytes 1572872 | tf_op jit(solution)/shard_map/ppermute | solution.py:694
  416.2 15.7 %collective-permute-start.47 = (bf16[128,1024]{1,0:T(8,128)(2,1)S(1)}, bf16[128,1024]{1,0:T(8,128)(2,1)S(1)}, u32[]{:S(2)}, u32[]{:S(2)}) collective-permute-start(bf16[128,1024]{1,0:T(8,128)(2,1)S(1)} %add_rows.18.refs_2_.refs_1_), channel_id=1, source_target_pairs={{0,2},{1,3},{2,0},{3,1},{4,6},{5,7},{6,4},{7,5},{8,10},{9,11},{10,... | collective-permute-start | bytes 786440 | tf_op jit(solution)/shard_map/ppermute | solution.py:694
  417.1 40.0 %collective-permute-start.60 = (bf16[256,1024]{1,0:T(8,128)(2,1)}, bf16[256,1024]{1,0:T(8,128)(2,1)S(1)}, u32[]{:S(2)}, u32[]{:S(2)}) collective-permute-start(bf16[256,1024]{1,0:T(8,128)(2,1)} %copy-done.220), channel_id=1, source_target_pairs={{0,2},{1,3},{2,0},{3,1},{4,6},{5,7},{6,4},{7,5},{8,10},{9,11},{10,... | collective-permute-start | bytes 1572872 | tf_op jit(solution)/shard_map/ppermute | solution.py:694
  432.4 26.5 %collective-permute-start.59 = (bf16[128,1024]{1,0:T(8,128)(2,1)S(1)}, bf16[128,1024]{1,0:T(8,128)(2,1)S(1)}, u32[]{:S(2)}, u32[]{:S(2)}) collective-permute-start(bf16[128,1024]{1,0:T(8,128)(2,1)S(1)} %get-tuple-element.347.refs_0_), channel_id=1, source_target_pairs={{0,1},{1,0},{2,3},{3,2},{4,5},{5,4},{6,7},{7,6},{8,9},{9,8},{10,11... | collective-permute-start | bytes 786440 | tf_op jit(solution)/shard_map/ppermute | solution.py:694
  432.5 49.5 %collective-permute-start.66 = (bf16[2,256,1024]{2,1,0:T(8,128)(2,1)S(1)}, bf16[2,256,1024]{2,1,0:T(8,128)(2,1)S(1)}, u32[]{:S(2)}, u32[]{:S(2)}) collective-permute-start(bf16[2,256,1024]{2,1,0:T(8,128)(2,1)S(1)} %get-tuple-element.363), channel_id=1, source_target_pairs={{0,4},{4,0},{8,12},{12,8},{1,5},{5,1},{9,13},{13,9},{2,6},{6,2},{1... | collective-permute-start | bytes 3145736 | tf_op jit(solution)/shard_map/ppermute | solution.py:694
  467.3 24.6 %collective-permute-start.69 = (bf16[512,1024]{1,0:T(8,128)(2,1)}, bf16[512,1024]{1,0:T(8,128)(2,1)}, u32[]{:S(2)}, u32[]{:S(2)}) collective-permute-start(bf16[512,1024]{1,0:T(8,128)(2,1)} %get-tuple-element.371), channel_id=1, source_target_pairs={{0,1},{1,0},{2,3},{3,2},{4,5},{5,4},{6,7},{7,6},{8,9},{9,8},{10,11... | collective-permute-start | bytes 3145736 | tf_op jit(solution)/shard_map/ppermute | solution.py:694
  467.5 14.5 %collective-permute-start.71 = (bf16[256,1024]{1,0:T(8,128)(2,1)}, bf16[256,1024]{1,0:T(8,128)(2,1)}, u32[]{:S(2)}, u32[]{:S(2)}) collective-permute-start(bf16[256,1024]{1,0:T(8,128)(2,1)} %get-tuple-element.375.refs_0_), channel_id=1, source_target_pairs={{0,2},{1,3},{2,0},{3,1},{4,6},{5,7},{6,4},{7,5},{8,10},{9,11},{10,... | collective-permute-start | bytes 1572872 | tf_op jit(solution)/shard_map/ppermute | solution.py:694
  468.6 37.9 %collective-permute-start.74 = (bf16[256,1024]{1,0:T(8,128)(2,1)}, bf16[256,1024]{1,0:T(8,128)(2,1)}, u32[]{:S(2)}, u32[]{:S(2)}) collective-permute-start(bf16[256,1024]{1,0:T(8,128)(2,1)} %get-tuple-element.377), channel_id=1, source_target_pairs={{0,8},{4,12},{8,0},{12,4},{1,9},{5,13},{9,1},{13,5},{2,10},{6,14},... | collective-permute-start | bytes 1572872 | tf_op jit(solution)/shard_map/ppermute | solution.py:694
  471.2 37.3 %collective-permute-start.72 = (bf16[256,1024]{1,0:T(8,128)(2,1)}, bf16[256,1024]{1,0:T(8,128)(2,1)}, u32[]{:S(2)}, u32[]{:S(2)}) collective-permute-start(bf16[256,1024]{1,0:T(8,128)(2,1)} %get-tuple-element.375.refs_0_), channel_id=1, source_target_pairs={{0,1},{1,0},{2,3},{3,2},{4,5},{5,4},{6,7},{7,6},{8,9},{9,8},{10,11... | collective-permute-start | bytes 1572872 | tf_op jit(solution)/shard_map/ppermute | solution.py:694
  482.0 26.5 %collective-permute-start.73 = (bf16[256,1024]{1,0:T(8,128)(2,1)}, bf16[256,1024]{1,0:T(8,128)(2,1)}, u32[]{:S(2)}, u32[]{:S(2)}) collective-permute-start(bf16[256,1024]{1,0:T(8,128)(2,1)} %collective-permute-done.71.refs_1_), channel_id=1, source_target_pairs={{0,1},{1,0},{2,3},{3,2},{4,5},{5,4},{6,7},{7,6},{8,9},{9,8},{10,11... | collective-permute-start | bytes 1572872 | tf_op jit(solution)/shard_map/ppermute | solution.py:694
  485.0 44.0 %collective-permute-start.76 = (bf16[256,1024]{1,0:T(8,128)(2,1)}, bf16[256,1024]{1,0:T(8,128)(2,1)}, u32[]{:S(2)}, u32[]{:S(2)}) collective-permute-start(bf16[256,1024]{1,0:T(8,128)(2,1)} %get-tuple-element.393), channel_id=1, source_target_pairs={{0,8},{4,12},{8,0},{12,4},{1,9},{5,13},{9,1},{13,5},{2,10},{6,14},... | collective-permute-start | bytes 1572872 | tf_op jit(solution)/shard_map/ppermute | solution.py:694
  508.5 37.1 %collective-permute-start.75 = (bf16[256,1024]{1,0:T(8,128)(2,1)}, bf16[256,1024]{1,0:T(8,128)(2,1)}, u32[]{:S(2)}, u32[]{:S(2)}) collective-permute-start(bf16[256,1024]{1,0:T(8,128)(2,1)} %add_rows.20.refs_11_.refs_1_), channel_id=1, source_target_pairs={{0,8},{4,12},{8,0},{12,4},{1,9},{5,13},{9,1},{13,5},{2,10},{6,14},... | collective-permute-start | bytes 1572872 | tf_op jit(solution)/shard_map/ppermute | solution.py:694
  552.3 30.9 %collective-permute-start.77 = (bf16[512,1024]{1,0:T(8,128)(2,1)}, bf16[512,1024]{1,0:T(8,128)(2,1)}, u32[]{:S(2)}, u32[]{:S(2)}) collective-permute-start(bf16[512,1024]{1,0:T(8,128)(2,1)} %get-tuple-element.400), channel_id=1, source_target_pairs={{0,1},{1,0},{2,3},{3,2},{4,5},{5,4},{6,7},{7,6},{8,9},{9,8},{10,11... | collective-permute-start | bytes 3145736 | tf_op jit(solution)/shard_map/ppermute | solution.py:694
  552.3 14.3 %collective-permute-start.70 = (bf16[256,1024]{1,0:T(8,128)(2,1)S(1)}, bf16[256,1024]{1,0:T(8,128)(2,1)S(1)}, u32[]{:S(2)}, u32[]{:S(2)}) collective-permute-start(bf16[256,1024]{1,0:T(8,128)(2,1)S(1)} %copy-done.222), channel_id=1, source_target_pairs={{0,2},{1,3},{2,0},{3,1},{4,6},{5,7},{6,4},{7,5},{8,10},{9,11},{10,... | collective-permute-start | bytes 1572872 | tf_op jit(solution)/shard_map/ppermute | solution.py:694
  553.4 26.2 %collective-permute-start.79 = (bf16[256,1024]{1,0:T(8,128)(2,1)S(1)}, bf16[256,1024]{1,0:T(8,128)(2,1)S(1)}, u32[]{:S(2)}, u32[]{:S(2)}) collective-permute-start(bf16[256,1024]{1,0:T(8,128)(2,1)S(1)} %add_rows.21.refs_14_.refs_1_), channel_id=1, source_target_pairs={{0,8},{4,12},{8,0},{12,4},{1,9},{5,13},{9,1},{13,5},{2,10},{6,14},... | collective-permute-start | bytes 1572872 | tf_op jit(solution)/shard_map/ppermute | solution.py:694
  553.4 27.4 %collective-permute-start.78 = (bf16[2,256,512]{2,1,0:T(8,128)(2,1)}, bf16[2,256,512]{2,1,0:T(8,128)(2,1)}, u32[]{:S(2)}, u32[]{:S(2)}) collective-permute-start(bf16[2,256,512]{2,1,0:T(8,128)(2,1)} %get-tuple-element.401), channel_id=1, source_target_pairs={{0,4},{4,0},{8,12},{12,8},{1,5},{5,1},{9,13},{13,9},{2,6},{6,2},{1... | collective-permute-start | bytes 1572872 | tf_op jit(solution)/shard_map/ppermute | solution.py:694
  557.3 50.2 %collective-permute-start.82 = (bf16[2,256,512]{2,1,0:T(8,128)(2,1)}, bf16[2,256,512]{2,1,0:T(8,128)(2,1)}, u32[]{:S(2)}, u32[]{:S(2)}) collective-permute-start(bf16[2,256,512]{2,1,0:T(8,128)(2,1)} %get-tuple-element.408), channel_id=1, source_target_pairs={{0,4},{4,0},{8,12},{12,8},{1,5},{5,1},{9,13},{13,9},{2,6},{6,2},{1... | collective-permute-start | bytes 1572872 | tf_op jit(solution)/shard_map/ppermute | solution.py:694
  585.5 34.2 %collective-permute-start.80 = (bf16[256,1024]{1,0:T(8,128)(2,1)}, bf16[256,1024]{1,0:T(8,128)(2,1)S(1)}, u32[]{:S(2)}, u32[]{:S(2)}) collective-permute-start(bf16[256,1024]{1,0:T(8,128)(2,1)} %get-tuple-element.405), channel_id=1, source_target_pairs={{0,2},{1,3},{2,0},{3,1},{4,6},{5,7},{6,4},{7,5},{8,10},{9,11},{10,... | collective-permute-start | bytes 1572872 | tf_op jit(solution)/shard_map/ppermute | solution.py:694
  589.9 15.4 %collective-permute-start.98 = (f32[1,256]{1,0:T(1,128)S(1)}, f32[1,256]{1,0:T(1,128)}, u32[]{:S(2)}, u32[]{:S(2)}) collective-permute-start(f32[1,256]{1,0:T(1,128)S(1)} %copy-done.229), channel_id=1, source_target_pairs={{16,0},{17,1},{18,2},{19,3},{20,4},{21,5},{22,6},{23,7},{24,8},{25... | collective-permute-start | bytes 3080 | tf_op jit(solution)/shard_map/ppermute | solution.py:731
  595.4 24.2 %collective-permute-start.81 = (bf16[256,512]{1,0:T(8,128)(2,1)}, bf16[256,512]{1,0:T(8,128)(2,1)S(1)}, u32[]{:S(2)}, u32[]{:S(2)}) collective-permute-start(bf16[256,512]{1,0:T(8,128)(2,1)} %copy-done.225), channel_id=1, source_target_pairs={{0,8},{4,12},{8,0},{12,4},{1,9},{5,13},{9,1},{13,5},{2,10},{6,14},... | collective-permute-start | bytes 786440 | tf_op jit(solution)/shard_map/ppermute | solution.py:694
  598.1 47.1 %collective-permute-start.91 = (bf16[256,512]{1,0:T(8,128)(2,1)}, bf16[256,512]{1,0:T(8,128)(2,1)}, u32[]{:S(2)}, u32[]{:S(2)}) collective-permute-start(bf16[256,512]{1,0:T(8,128)(2,1)} %copy-done.75), channel_id=1, source_target_pairs={{0,4},{4,8},{8,12},{12,0},{1,5},{5,9},{9,13},{13,1},{2,6},{6,10},{... | collective-permute-start | bytes 786440 | tf_op jit(solution)/shard_map/ppermute | solution.py:606
  605.2 44.8 %collective-permute-start.92 = (bf16[256,512]{1,0:T(8,128)(2,1)}, bf16[256,512]{1,0:T(8,128)(2,1)}, u32[]{:S(2)}, u32[]{:S(2)}) collective-permute-start(bf16[256,512]{1,0:T(8,128)(2,1)} %copy-done.75), channel_id=1, source_target_pairs={{0,8},{4,12},{8,0},{12,4},{1,9},{5,13},{9,1},{13,5},{2,10},{6,14},... | collective-permute-start | bytes 786440 | tf_op jit(solution)/shard_map/ppermute | solution.py:606
  607.5 20.5 %collective-permute-start.67 = (bf16[128,1024]{1,0:T(8,128)(2,1)S(1)}, bf16[128,1024]{1,0:T(8,128)(2,1)}, u32[]{:S(2)}, u32[]{:S(2)}) collective-permute-start(bf16[128,1024]{1,0:T(8,128)(2,1)S(1)} %add_rows.19.refs_2_), channel_id=1, source_target_pairs={{0,2},{1,3},{2,0},{3,1},{4,6},{5,7},{6,4},{7,5},{8,10},{9,11},{10,... | collective-permute-start | bytes 786440 | tf_op jit(solution)/shard_map/ppermute | solution.py:694
  629.2 24.4 %collective-permute-start.94 = (bf16[256,1024]{1,0:T(8,128)(2,1)S(1)}, bf16[256,1024]{1,0:T(8,128)(2,1)S(1)}, u32[]{:S(2)}, u32[]{:S(2)}) collective-permute-start(bf16[256,1024]{1,0:T(8,128)(2,1)S(1)} %add_rows.21.refs_14_.refs_1_), channel_id=1, source_target_pairs={{0,4},{4,0},{8,12},{12,8},{1,5},{5,1},{9,13},{13,9},{2,6},{6,2},{1... | collective-permute-start | bytes 1572872 | tf_op jit(solution)/shard_map/ppermute | solution.py:694
  632.7 22.8 %collective-permute-start.84 = (bf16[256,512]{1,0:T(8,128)(2,1)S(1)}, bf16[256,512]{1,0:T(8,128)(2,1)S(1)}, u32[]{:S(2)}, u32[]{:S(2)}) collective-permute-start(bf16[256,512]{1,0:T(8,128)(2,1)S(1)} %add_rows.22.refs_5_.refs_1_), channel_id=1, source_target_pairs={{0,8},{4,12},{8,0},{12,4},{1,9},{5,13},{9,1},{13,5},{2,10},{6,14},... | collective-permute-start | bytes 786440 | tf_op jit(solution)/shard_map/ppermute | solution.py:694
  646.5 14.9 %collective-permute-start.85 = (bf16[256,512]{1,0:T(8,128)(2,1)S(1)}, bf16[256,512]{1,0:T(8,128)(2,1)S(1)}, u32[]{:S(2)}, u32[]{:S(2)}) collective-permute-start(bf16[256,512]{1,0:T(8,128)(2,1)S(1)} %copy-done.227), channel_id=1, source_target_pairs={{0,8},{4,12},{8,0},{12,4},{1,9},{5,13},{9,1},{13,5},{2,10},{6,14},... | collective-permute-start | bytes 786440 | tf_op jit(solution)/shard_map/ppermute | solution.py:694
  650.0 49.7 %collective-permute-start.96 = (bf16[256,1024]{1,0:T(8,128)(2,1)}, bf16[256,1024]{1,0:T(8,128)(2,1)}, u32[]{:S(2)}, u32[]{:S(2)}) collective-permute-start(bf16[256,1024]{1,0:T(8,128)(2,1)} %add_rows.20.refs_11_.refs_1_), channel_id=1, source_target_pairs={{0,4},{4,0},{8,12},{12,8},{1,5},{5,1},{9,13},{13,9},{2,6},{6,2},{1... | collective-permute-start | bytes 1572872 | tf_op jit(solution)/shard_map/ppermute | solution.py:694
  653.5 46.3 %collective-permute-start.95 = (bf16[256,1024]{1,0:T(8,128)(2,1)S(1)}, bf16[256,1024]{1,0:T(8,128)(2,1)}, u32[]{:S(2)}, u32[]{:S(2)}) collective-permute-start(bf16[256,1024]{1,0:T(8,128)(2,1)S(1)} %copy-done.15), channel_id=1, source_target_pairs={{0,4},{4,0},{8,12},{12,8},{1,5},{5,1},{9,13},{13,9},{2,6},{6,2},{1... | collective-permute-start | bytes 1572872 | tf_op jit(solution)/shard_map/ppermute | solution.py:694
  653.6 48.2 %collective-permute-start.97 = (bf16[256,1024]{1,0:T(8,128)(2,1)}, bf16[256,1024]{1,0:T(8,128)(2,1)}, u32[]{:S(2)}, u32[]{:S(2)}) collective-permute-start(bf16[256,1024]{1,0:T(8,128)(2,1)} %gate.10.refs_6_.refs_2_), channel_id=1, source_target_pairs={{0,4},{4,0},{8,12},{12,8},{1,5},{5,1},{9,13},{13,9},{2,6},{6,2},{1... | collective-permute-start | bytes 1572872 | tf_op jit(solution)/shard_map/ppermute | solution.py:694
  661.4 42.4 %collective-permute-start.83 = (bf16[2,128,1024]{2,1,0:T(8,128)(2,1)}, bf16[2,128,1024]{2,1,0:T(8,128)(2,1)}, u32[]{:S(2)}, u32[]{:S(2)}) collective-permute-start(bf16[2,128,1024]{2,1,0:T(8,128)(2,1)} %fusion.3), channel_id=1, source_target_pairs={{0,16},{1,17},{2,18},{3,19},{4,20},{5,21},{6,22},{7,23},{8,24},{9,... | collective-permute-start | bytes 1572872 | tf_op jit(solution)/shard_map/ppermute | solution.py:1245
  667.2 28.4 %collective-permute-start.88 = (bf16[256,512]{1,0:T(8,128)(2,1)S(1)}, bf16[256,512]{1,0:T(8,128)(2,1)S(1)}, u32[]{:S(2)}, u32[]{:S(2)}) collective-permute-start(bf16[256,512]{1,0:T(8,128)(2,1)S(1)} %add_rows.23.refs_1_.refs_5_), channel_id=1, source_target_pairs={{0,8},{4,12},{8,0},{12,4},{1,9},{5,13},{9,1},{13,5},{2,10},{6,14},... | collective-permute-start | bytes 786440 | tf_op jit(solution)/shard_map/ppermute | solution.py:694
  699.7 14.9 %collective-permute-start.93 = (bf16[256,512]{1,0:T(8,128)(2,1)S(1)}, bf16[256,512]{1,0:T(8,128)(2,1)S(1)}, u32[]{:S(2)}, u32[]{:S(2)}) collective-permute-start(bf16[256,512]{1,0:T(8,128)(2,1)S(1)} %copy-done.76), channel_id=1, source_target_pairs={{0,12},{4,0},{8,4},{12,8},{1,13},{5,1},{9,5},{13,9},{2,14},{6,2},{... | collective-permute-start | bytes 786440 | tf_op jit(solution)/shard_map/ppermute | solution.py:606
  699.8 14.8 %collective-permute-start.86 = (bf16[256,512]{1,0:T(8,128)(2,1)S(1)}, bf16[256,512]{1,0:T(8,128)(2,1)S(1)}, u32[]{:S(2)}, u32[]{:S(2)}) collective-permute-start(bf16[256,512]{1,0:T(8,128)(2,1)S(1)} %add_rows.22.refs_5_.refs_1_), channel_id=1, source_target_pairs={{0,4},{4,0},{8,12},{12,8},{1,5},{5,1},{9,13},{13,9},{2,6},{6,2},{1... | collective-permute-start | bytes 786440 | tf_op jit(solution)/shard_map/ppermute | solution.py:694
  701.8 18.4 %collective-permute-start.87 = (bf16[256,512]{1,0:T(8,128)(2,1)}, bf16[256,512]{1,0:T(8,128)(2,1)S(1)}, u32[]{:S(2)}, u32[]{:S(2)}) collective-permute-start(bf16[256,512]{1,0:T(8,128)(2,1)} %gate.12.refs_1_.refs_2_), channel_id=1, source_target_pairs={{0,4},{4,0},{8,12},{12,8},{1,5},{5,1},{9,13},{13,9},{2,6},{6,2},{1... | collective-permute-start | bytes 786440 | tf_op jit(solution)/shard_map/ppermute | solution.py:694
  701.9 24.0 %collective-permute-start.89 = (bf16[256,512]{1,0:T(8,128)(2,1)}, bf16[256,512]{1,0:T(8,128)(2,1)S(1)}, u32[]{:S(2)}, u32[]{:S(2)}) collective-permute-start(bf16[256,512]{1,0:T(8,128)(2,1)} %copy-done.25), channel_id=1, source_target_pairs={{0,4},{4,0},{8,12},{12,8},{1,5},{5,1},{9,13},{13,9},{2,6},{6,2},{1... | collective-permute-start | bytes 786440 | tf_op jit(solution)/shard_map/ppermute | solution.py:694
  703.8 26.0 %collective-permute-start.90 = (bf16[256,512]{1,0:T(8,128)(2,1)}, bf16[256,512]{1,0:T(8,128)(2,1)S(1)}, u32[]{:S(2)}, u32[]{:S(2)}) collective-permute-start(bf16[256,512]{1,0:T(8,128)(2,1)} %gate.13.refs_5_.refs_6_), channel_id=1, source_target_pairs={{0,4},{4,0},{8,12},{12,8},{1,5},{5,1},{9,13},{13,9},{2,6},{6,2},{1... | collective-permute-start | bytes 786440 | tf_op jit(solution)/shard_map/ppermute | solution.py:694
  (287 other events, 2803.0 us)

commit v3 on v2

--- a/solution.py
+++ b/solution.py
@@ -81,6 +81,80 @@
 
 def cost(flops, moved, exps=0):
     return pl.CostEstimate(flops=int(flops), bytes_accessed=int(moved), transcendentals=int(exps))
+
+
+ORDER = (
+    ("g", "send"),
+    ("e0", "qkv"),
+    ("e0", "attention"),
+    ("g", "gate"),
+    ("e1", "qkv"),
+    ("e0", "reduce"),
+    ("e1", "attention"),
+    ("e0", "norm"),
+    ("e1", "reduce"),
+    ("d", "self"),
+    ("d", "reduce"),
+    ("e0", "ffn"),
+    ("e1", "norm"),
+    ("d", "norm"),
+    ("e0", "reduce two"),
+    ("e1", "ffn"),
+    ("e0", "memory"),
+    ("e1", "reduce two"),
+    ("e1", "memory"),
+    ("e0", "cross"),
+    ("e1", "cross"),
+    ("d", "back"),
+    ("m0", "reduce"),
+    ("m1", "reduce"),
+    ("d", "thirds"),
+    ("m0", "moved"),
+    ("m1", "moved"),
+    ("b0", "norm two"),
+    ("b1", "norm two"),
+    ("r", "start"),
+    ("d", "third send"),
+    ("b0", "ffn"),
+    ("r", "reduce"),
+    ("b0", "reduce two"),
+    ("d", "third pick"),
+    ("b1", "ffn"),
+    ("b0", "norm one"),
+    ("b1", "reduce two"),
+    ("out", "made"),
+    ("d", "third sum"),
+    ("in", "made"),
+    ("r", "norm"),
+    ("b0", "attention"),
+    ("b1", "norm one"),
+    ("r", "self"),
+    ("b0", "back"),
+    ("r", "reduce two"),
+    ("b0", "reduce one"),
+    ("out", "one"),
+    ("b1", "attention"),
+    ("out", "two"),
+    ("qk", "made"),
+    ("vo", "made"),
+    ("in", "one"),
+    ("b1", "back"),
+    ("d", "third end"),
+    ("b0", "norm zero"),
+    ("out", "three"),
+    ("b1", "reduce one"),
+    ("in", "two"),
+    ("b1", "norm zero"),
+    ("qk", "one"),
+    ("vo", "one"),
+    ("in", "three"),
+    ("out", "four"),
+    ("qk", "two"),
+    ("vo", "two"),
+    ("in", "four"),
+    ("qk", "three"),
+    ("vo", "three"),
+)
 
 
 class Order:
@@ -480,104 +554,115 @@
 CHUNKS = 4
 
 
-MASKS = (0, 2, 1, 3)
-
-
 def weight_grad(section, order_ref, enc_pairs, dec_pairs):
-    width = dec_pairs[0][0].shape[1]
+    pairs = [(x if isinstance(x, tuple) else (x,), g) for one in (*enc_pairs, dec_pairs) for x, g in one]
+    width = pairs[0][0][0].shape[1]
     chunk = width // CHUNKS
     tables, count = len(enc_pairs), len(dec_pairs)
     total_columns = sum(g.shape[1] for _, g in dec_pairs)
-    flat = [pair for pairs in (*enc_pairs, dec_pairs) for pair in pairs]
+    starts, in_specs, args = [], [], []
+    for x, g in pairs:
+        starts.append(len(args))
+        in_specs += [pl.BlockSpec((part.shape[0], chunk), lambda i, s, at: (0, at[i])) for part in x] + [full(g.shape)]
+        args += [*x, g]
 
     def kernel(at, order_at, *refs):
-        ins, (low, high) = refs[: 2 * len(flat)], refs[2 * len(flat) :]
+        out = refs[-1]
+
+        def one_product(index):
+            start, blocks = starts[index], len(pairs[index][0])
+            x = jnp.concatenate([ref[...] for ref in refs[start : start + blocks]], axis=0) if blocks > 1 else refs[start][...]
+            return t_mm(x, refs[start + blocks][...])
 
         def product(index):
-            return jnp.concatenate(
-                [t_mm(ins[2 * (index * count + one)][...], ins[2 * (index * count + one) + 1][...]) for one in range(count)], axis=1
-            )
+            return jnp.concatenate([one_product(index * count + one) for one in range(count)], axis=1)
 
         @pl.when(at[0] == 0)
         def _():
             total = 0.0
             for table in range(tables):
                 total = total + product(table)
-            put_low_high(total.astype(bf16), low, high)
+            out[...] = total.astype(bf16)
 
         @pl.when(at[0] != 0)
         def _():
-            put_low_high(product(tables).astype(bf16), low, high)
-
-    in_specs, args = [], []
-    for x, g in flat:
-        in_specs += [pl.BlockSpec((x.shape[0], chunk), lambda i, s, at: (0, at[i])), full(g.shape)]
-        args += [x, g]
-    rows = sum(x.shape[0] for x, _ in flat) // count
-    half = jax.ShapeDtypeStruct((2, chunk, total_columns), bf16)
+            out[...] = product(tables).astype(bf16)
+
+    rows = sum(g.shape[0] for _, g in pairs) // count
     return call(
         kernel, (CHUNKS,), in_specs,
-        [
-            pl.BlockSpec((None, chunk, total_columns), lambda i, *_: (jnp.maximum(i - 2, 0), 0, 0)),
-            pl.BlockSpec((None, chunk, total_columns), lambda i, *_: (jnp.minimum(i, 1), 0, 0)),
-        ],
-        [half] * 2, [],
+        pl.BlockSpec((None, chunk, total_columns), lambda i, *_: (i, 0, 0)),
+        jax.ShapeDtypeStruct((CHUNKS, chunk, total_columns), bf16), [],
         cost(2 * rows * width * total_columns, 2 * rows * (width + total_columns)),
         *args,
         prefetch=[section, order_ref],
     )
 
 
-def sum_places(low, high, parts):
-    chunk, columns = low.shape[1:]
+def sum_line(rows, parts):
+    half = (CHUNKS // 2, *rows.shape[1:])
     if lax.axis_size("dp") != CHUNKS:
-        low, high = lax.psum((low, high), "dp")
-        parts.extend([low[0], low[1], high[0], high[1]])
+        rows = lax.psum(rows, "dp")
+        parts.extend([rows[: CHUNKS // 2], rows[CHUNKS // 2 :]] * 2)
         return
-    sent = flip(high, 0, "dp")
+    inward, across, outward = [(0, 1), (3, 2)], [(1, 2), (2, 1)], [(1, 0), (2, 3)]
+    sent = lax.ppermute(rows, "dp", inward)
     yield "made"
 
-    def add_pair(low_ref, sent_ref, own, far):
-        own[...] = (low_ref[0].astype(f32) + sent_ref[0].astype(f32)).astype(bf16)
-        far[...] = (low_ref[1].astype(f32) + sent_ref[1].astype(f32)).astype(bf16)
-
-    whole = pl.BlockSpec(low.shape, lambda *_: (0, 0, 0))
-    own, far = call(
-        add_pair, (1,), [whole] * 2, [full((chunk, columns))] * 2, [shaped(chunk, columns)] * 2, [], cost(0, 6 * low.size), low, sent
-    )
-    sent = flip(far, 1, "dp")
+    def block(shape):
+        return pl.BlockSpec(shape, lambda *_: (0, 0, 0))
+
+    def add_side(rows_ref, sent_ref, own, other):
+        for index in range(CHUNKS):
+            total = (rows_ref[index].astype(f32) + sent_ref[index].astype(f32)).astype(bf16)
+            (own if index < CHUNKS // 2 else other)[index % (CHUNKS // 2)] = total
+
+    own, other = call(
+        add_side, (1,), [block(rows.shape)] * 2, [block(half)] * 2, [jax.ShapeDtypeStruct(half, bf16)] * 2, [],
+        cost(0, 6 * rows.size), rows, sent,
+    )
+    sent = lax.ppermute(other, "dp", across)
     yield "one"
-    total = add_rows(own, sent)
-    second = flip(total, 1, "dp")
-    third = flip(total, 0, "dp")
+
+    def add_across(own_ref, sent_ref, out):
+        for index in range(CHUNKS // 2):
+            out[index] = (own_ref[index].astype(f32) + sent_ref[index].astype(f32)).astype(bf16)
+
+    total = call(
+        add_across, (1,), [block(half)] * 2, block(half), jax.ShapeDtypeStruct(half, bf16), [], cost(0, 3 * rows.size), own, sent
+    )
+    crossed = lax.ppermute(total, "dp", across)
+    first = lax.ppermute(total, "dp", outward)
     yield "two"
-    second = gate(second)
-    fourth = flip(second, 0, "dp")
-    parts.extend([total, second, third, fourth])
+    crossed, first = gate(crossed, first)
+    second = lax.ppermute(crossed, "dp", outward)
+    parts.extend([total, crossed, first, second])
     yield "three"
 
 
-def put_chunk(place, parts, put):
-    other = place[0] ^ pl.program_id(0)
-    for part, mask in zip(parts, MASKS):
-        @pl.when(other == mask)
+def put_chunk(line, parts, put):
+    step = pl.program_id(0)
+    other = (step // (CHUNKS // 2)) ^ line[0]
+    for index, part in enumerate(parts):
+        @pl.when(jnp.logical_and(other == index % 2, line[1] == 1 - index // 2))
         def _(part=part):
-            put(part)
-
-
-def unite_one(place, parts):
-    chunk, columns = parts[0].shape
-
-    def kernel(place_at, *refs):
-        def put(part):
-            refs[-1][...] = part[...].astype(f32)
-
-        put_chunk(place_at, refs[:-1], put)
-
-    return call(
-        kernel, (CHUNKS,), [full((chunk, columns))] * CHUNKS, pl.BlockSpec((chunk, columns), lambda i, *_: (i, 0)),
+            put(part[step % (CHUNKS // 2)])
+
+
+def unite_one(line, parts):
+    half, chunk, columns = parts[0].shape
+
+    def kernel(line_at, *refs):
+        def put(value):
+            refs[-1][...] = value.astype(f32)
+
+        put_chunk(line_at, refs[:-1], put)
+
+    return call(
+        kernel, (CHUNKS,), [pl.BlockSpec(parts[0].shape, lambda *_: (0, 0, 0))] * 4,
+        pl.BlockSpec((chunk, columns), lambda i, *_: (i, 0)),
         shaped(CHUNKS * chunk, columns, f32), [], cost(0, 24 * chunk * columns), *parts,
-        prefetch=[place],
+        prefetch=[line],
     )
 
 
@@ -618,17 +703,17 @@
     )
 
 
-def unite(place, qk, vo, thirds):
-    rows, columns = qk[0].shape[0], qk[0].shape[1] // 2
-
-    def kernel(place_at, *refs):
-        qk, vo, chunks, (first, second) = refs[:CHUNKS], refs[CHUNKS : 2 * CHUNKS], refs[2 * CHUNKS : 3 * CHUNKS], refs[3 * CHUNKS :]
+def unite(place, line, qk, vo, thirds):
+    rows, columns = qk[0].shape[1], qk[0].shape[2] // 2
+
+    def kernel(place_at, line_at, *refs):
+        qk, vo, chunks, (first, second) = refs[:4], refs[4:8], refs[8 : 8 + CHUNKS], refs[8 + CHUNKS :]
         for parts, out in ((qk, first), (vo, second)):
-            def put(part, out=out):
-                out[0] = part[:, :columns].astype(f32)
-                out[1] = part[:, columns:].astype(f32)
-
-            put_chunk(place_at, parts, put)
+            def put(value, out=out):
+                out[0] = value[:, :columns].astype(f32)
+                out[1] = value[:, columns:].astype(f32)
+
+            put_chunk(line_at, parts, put)
         turn = (place_at[0] - pl.program_id(0)) % CHUNKS
         for index in range(CHUNKS):
             @pl.when(turn == index)
@@ -638,10 +723,49 @@
 
     stacked = pl.BlockSpec((3, rows, columns), lambda i, *_: (0, i, 0))
     return call(
-        kernel, (CHUNKS,), [full((rows, 2 * columns))] * (3 * CHUNKS), [stacked] * 2,
+        kernel, (CHUNKS,),
+        [pl.BlockSpec(qk[0].shape, lambda *_: (0, 0, 0))] * 8 + [full((rows, 2 * columns))] * CHUNKS, [stacked] * 2,
         [jax.ShapeDtypeStruct((3, CHUNKS * rows, columns), f32)] * 2, [],
         cost(0, 36 * CHUNKS * rows * columns), *qk, *vo, *thirds,
-        prefetch=[place],
+        prefetch=[place, line],
+    )
+
+
+def vector_rows(section, rank, encoder, third_bias, decoder, factor):
+    width = decoder[0].shape[1]
+    columns, units = decoder[3].shape[1], decoder[6].shape[1]
+    args = [value for one in encoder for value in one] + [third_bias, *decoder]
+    tables, each = len(encoder), len(encoder[0])
+
+    def kernel(at, rank_at, *refs):
+        out = refs[-1]
+        out[...] = jnp.zeros_like(out)
+
+        def put(one, two, last, heads, bias, scale):
+            picked = [one[2:3], two[2:3], one[0:1], one[1:2], two[0:1], two[1:2], last[0:1], last[1:2]]
+            for index, value in enumerate(picked):
+                out[3 + index : 4 + index, :] = value * scale
+            out[12:13, :units] = bias
+            for place in range(width // columns):
+                @pl.when(rank_at[0] == place)
+                def _(place=place):
+                    for index, value in enumerate(heads):
+                        out[index : index + 1, place * columns : (place + 1) * columns] = value
+
+        @pl.when(at[0] == 0)
+        def _():
+            one, two, last, q, v, bias = (sum(refs[table * each + index][...] for table in range(tables)) for index in range(each))
+            put(one, two, last, (q, v, refs[tables * each][...]), bias, 1.0)
+
+        @pl.when(at[0] != 0)
+        def _():
+            one, two, last, q, v, third, bias = (ref[...] for ref in refs[tables * each + 1 : -1])
+            put(one, two, last, (q, v, third), bias, factor)
+            out[11:12, :] = last[2:3] * factor
+
+    return call(
+        kernel, (1,), [full(value.shape) for value in args], full((16, width)), shaped(16, width, f32), [], cost(0, 200 * width),
+        *args, prefetch=[section, rank],
     )
 
 
@@ -705,10 +829,14 @@
     return low, sent
 
 
-def gather_share(share):
-    parts = [share]
-    for bit in reversed(range(axis_bits("tensor"))):
-        parts = parts + [flip(part, bit) for part in parts]
+def gather_start(share):
+    return [share] + [flip(share, bit) for bit in reversed(range(axis_bits("tensor")))]
+
+
+def gather_rest(started):
+    parts, first = [started[0]], started[1:]
+    for index, bit in enumerate(reversed(range(axis_bits("tensor")))):
+        parts = parts + [first[index]] + [flip(part, bit) for part in parts[1:]]
     return parts
 
 
@@ -928,7 +1056,11 @@
     is_first = section == 0
     section_ref = section.reshape(1).astype(jnp.int32)
     in_line = lax.axis_size("dp") == CHUNKS
-    order_ref = jnp.where(in_line, lax.axis_index("dp"), 0).astype(jnp.int32) ^ jnp.array(MASKS[2:] + MASKS[:2], jnp.int32)
+    place = lax.axis_index("dp")
+    beyond = jnp.logical_and(in_line, place >= CHUNKS // 2).astype(jnp.int32)
+    inner = jnp.where(in_line, ((place == 1) | (place == 2)).astype(jnp.int32), 1)
+    line_ref = jnp.stack([beyond, inner])
+    order_ref = (jnp.arange(CHUNKS, dtype=jnp.int32) + beyond * (CHUNKS // 2)) % CHUNKS
     place_ref = jnp.where(in_line, lax.axis_index("dp"), 0).reshape(1).astype(jnp.int32)
     tables, slots, width = table_input.shape
     targets = target_input.shape[1]
@@ -940,7 +1072,6 @@
     w_query, w_key, w_third_q = query_key[0, 0], query_key[0, 1], query_key[0, 2]
     w_value, w_out, w_third_v = value_out[0, 0], value_out[0, 1], value_out[0, 2]
     w_in, w_hidden_out = hidden_in[0], hidden_out[0]
-    w_cross_key, w_cross_value, b_cross_value = to_second(w_third_q), to_second(w_third_v), to_second(head_rows[2:3])
 
     masks = [int(format(p, f"0{bits}b")[::-1], 2) for p in range(count)]
     owners = rank.astype(jnp.int32) ^ jnp.array(masks, jnp.int32)
@@ -979,6 +1110,7 @@
 
     encoder_kept, encoder_out = {}, {}
     cross, dec, grad_memory = {}, {}, {}
+    w_cross_key = w_cross_value = b_cross_value = None
     order.last = None
 
     def encode(table):
@@ -992,8 +1124,9 @@
         parts = reduce_rest(low, sent)
         yield "reduce"
         summed_one, middle, sent = norm_forward(normed, parts, row[3], row[5], row[6])
-        parts = gather_share(sent)
+        started = gather_start(sent)
         yield "norm"
+        parts = gather_rest(started)
         yield "gather"
         second_in, hidden, slope, low, high = ffn_forward(parts, w_in, hidden_bias, w_hidden_out)
         sent = flip(high, 0)
@@ -1004,10 +1137,10 @@
         encoder_kept[table] = (raw, first_in, queries, keys, values, heads, wide, logs, summed_one, second_in, hidden, slope, summed_two)
         memory = to_second(memory)
         yield "memory"
-        parts = gather_share(memory)
+        started = gather_start(memory)
         yield "moved"
         yield "gather two"
-        cross[table] = project_parts(parts, [w_cross_key, w_cross_value], [no_bias, b_cross_value])
+        cross[table] = project_parts(gather_rest(started), [w_cross_key, w_cross_value], [no_bias, b_cross_value])
         yield "cross"
 
     def decode():
@@ -1065,6 +1198,8 @@
             totals = lax.psum([first, *rest], "dp")
             dec["thirds"] = totals[:1] + totals[:0:-1]
         yield "third sum"
+        dec["thirds"] = gate(*dec["thirds"])
+        yield "third end"
 
     def memory_back(table):
         keep, sent = reduce_rest(*dec["memory", table])
@@ -1096,22 +1231,23 @@
     def encode_back(table):
         (raw, first_in, queries, keys, values, heads, wide, logs, summed_one, second_in, hidden, slope, summed_two) = encoder_kept[table]
         grad_two, sent, sums_two = norm_backward(summed_two, row[7], [grad_memory[table]])
-        parts = gather_share(sent)
+        started = gather_start(sent)
         yield "norm two"
+        parts = gather_rest(started)
+        pairs = encoder_out[table] = {"out": [(tuple(parts), hidden)]}
         yield "gather two"
-        grad_two_rows, grad_before, low, high, bias = ffn_backward(parts, slope, w_in, w_hidden_out)
-        pairs = {"in": [(second_in, grad_before)], "out": [(grad_two_rows, hidden)]}
-        encoder_out[table] = pairs
+        _, grad_before, low, high, bias = ffn_backward(parts, slope, w_in, w_hidden_out)
+        pairs["in"] = [(second_in, grad_before)]
         sent = flip(high, 0)
         yield "ffn"
         parts = reduce_rest(low, sent)
         yield "reduce two"
         grad_one, sent, sums_one = norm_backward(summed_one, row[5], [grad_two, *parts])
-        parts = gather_share(sent)
+        started = gather_start(sent)
         yield "norm one"
         yield "gather one"
         grad_one_rows, grad_q, grad_k, grad_v, sum_q, sum_v = encoder_attention_back(
-            parts, wide, logs, queries, keys, values, table_mask[table][:, None], w_out
+            gather_rest(started), wide, logs, queries, keys, values, table_mask[table][:, None], w_out
         )
         pairs.update({"qk": [(first_in, grad_q), (first_in, grad_k)], "vo": [(first_in, grad_v), (grad_one_rows, heads)]})
         yield "attention"
@@ -1121,123 +1257,58 @@
         parts = reduce_rest(low, sent)
         yield "reduce one"
         _, pairs["table_grad"], sums_zero = norm_backward(raw, row[9], [grad_one, *parts])
-        sums = [sums_one[2], sums_two[2], sums_one[0], sums_one[1], sums_two[0], sums_two[1], sums_zero[0], sums_zero[1]]
-        pairs["sums"] = (jnp.stack(sums), sum_q[0], sum_v[0], bias)
+        pairs["sums"] = (sums_one, sums_two, sums_zero, sum_q, sum_v, bias)
         yield "norm zero"
 
     totals = {}
 
     def weights(name):
         totals[name] = []
-        low, high = weight_grad(section_ref, order_ref, [encoder_out[table][name] for table in range(tables)], dec["pairs"][name])
-        return sum_places(low, high, totals[name])
-
-    def to(part, *labels):
-        for label in labels:
-            for said in part:
-                if said == label:
-                    break
-
-    def each(parts, *labels):
-        for label in labels:
-            for part in parts:
-                to(part, label)
-
-    ahead, *behind = forward = [encode(table) for table in range(tables)]
-    decoder = decode()
-    to(ahead, "qkv", "attention")
-    w_cross_key, w_cross_value, b_cross_value = gate(w_cross_key, w_cross_value, b_cross_value)
-    each(behind, "qkv")
-    to(ahead, "reduce")
-    each(behind, "attention")
-    to(ahead, "norm")
-    each(behind, "reduce")
-    to(decoder, "self", "reduce")
-    to(ahead, "ffn")
-    each(behind, "norm")
-    to(decoder, "norm")
-    to(ahead, "reduce two")
-    each(behind, "ffn")
-    to(ahead, "memory")
-    each(behind, "reduce two", "memory")
-    each(forward, "cross")
-
-    to(decoder, "back")
-    returned = [memory_back(table) for table in range(tables)]
-    each(returned, "reduce")
-    to(decoder, "thirds")
-    each(returned, "moved")
-    rest = decode_rest()
-
-    ahead, *behind = backward = [encode_back(table) for table in range(tables)]
-    to(ahead, "norm two")
-    each(behind, "norm two")
-    to(rest, "start")
-    to(decoder, "third send")
-    to(ahead, "ffn")
-    to(rest, "reduce")
-    to(ahead, "reduce two")
-    to(decoder, "third pick")
-    each(behind, "ffn")
-    to(ahead, "norm one")
-    each(behind, "reduce two")
-    out_sum = weights("out")
-    to(out_sum, "made")
-    to(decoder, "third sum")
-    in_sum = weights("in")
-    to(in_sum, "made")
-    to(rest, "norm")
-    to(ahead, "attention")
-    to(out_sum, "one")
-    each(behind, "norm one")
-    to(rest, "self")
-    to(ahead, "back")
-    to(in_sum, "one")
-    to(rest, "reduce two")
-    to(ahead, "reduce one")
-    to(out_sum, "two")
-    each(behind, "attention")
-    to(in_sum, "two")
-    qk_sum = weights("qk")
-    to(qk_sum, "made")
-    vo_sum = weights("vo")
-    to(vo_sum, "made")
-    to(out_sum, "three")
-    each(behind, "back")
-    to(ahead, "norm zero")
-    to(in_sum, "three")
-    to(qk_sum, "one")
-    each(behind, "reduce one")
-    to(vo_sum, "one")
-    to(qk_sum, "two")
-    each(behind, "norm zero")
-    to(vo_sum, "two")
-    to(qk_sum, "three")
-    to(vo_sum, "three")
-    for part in (rest, decoder, out_sum, in_sum, qk_sum, vo_sum, *backward, *forward):
-        to(part, "end")
+        rows = weight_grad(section_ref, order_ref, [encoder_out[table][name] for table in range(tables)], dec["pairs"][name])
+        yield from sum_line(rows, totals[name])
+        if name in ("out", "in"):
+            totals[name] = unite_one(line_ref, totals[name])
+            yield "four"
+
+    def cross_weights():
+        nonlocal w_cross_key, w_cross_value, b_cross_value
+        sent = gate(w_third_q, w_third_v, head_rows[2:3])
+        w_cross_key, w_cross_value, b_cross_value = (to_second(value) for value in sent)
+        yield "send"
+        w_cross_key, w_cross_value, b_cross_value = gate(w_cross_key, w_cross_value, b_cross_value)
+        yield "gate"
+
+    parts = {"d": decode(), "g": cross_weights(), "r": decode_rest()}
+    for table in range(tables):
+        parts[f"e{table}"] = encode(table)
+        parts[f"m{table}"] = memory_back(table)
+        parts[f"b{table}"] = encode_back(table)
+    for name in ("out", "in", "qk", "vo"):
+        parts[name] = weights(name)
+    for name, label in ORDER:
+        for said in parts[name]:
+            if said == label:
+                break
+    for part in parts.values():
+        for _ in part:
+            pass
 
     table_grads = [encoder_out[table]["table_grad"] for table in range(tables)]
-    enc_rows, enc_sum_q, enc_sum_v, enc_bias = (sum(values) for values in zip(*[encoder_out[table]["sums"] for table in range(tables)]))
     decoded, target_grad = dec["out"], dec["target_grad"]
-    sums_one, sums_two, sums_three = dec["sums_one"], dec["sums_two"], dec["sums_three"]
-    dec_rows = jnp.stack(
-        [sums_one[2], sums_two[2], sums_one[0], sums_one[1], sums_two[0], sums_two[1], sums_three[0], sums_three[1], sums_three[2]]
-    ) * (cores / count)
-    dec_head_rows = [dec["sum_q"][0], dec["sum_v"][0], dec["third_sum"][0]]
-    dec_bias = dec["bias"]
-    third_bias_grad = dec["third_bias"][0]
-
-    total_out, total_in = unite_one(place_ref, totals["out"]), unite_one(place_ref, totals["in"])
-    query_key_grad, value_out_grad = unite(place_ref, totals["qk"], totals["vo"], dec["thirds"])
-
-    head_sums = jnp.where(is_first, jnp.stack([enc_sum_q, enc_sum_v, third_bias_grad]), jnp.stack(dec_head_rows))
-    placed = lax.dynamic_update_slice(jnp.zeros((3, width), f32), head_sums, (0, rank * columns))
-    other_rows = jnp.where(is_first, jnp.pad(enc_rows, ((0, 1), (0, 0))), dec_rows)
-    bias_row = jnp.pad(jnp.where(is_first, enc_bias, dec_bias), ((0, 0), (0, width - enc_bias.shape[1])))
-    bundle = sum_over(jnp.concatenate([placed, other_rows, bias_row]), "dp")
-    bias_sum = bundle[12:13, : enc_bias.shape[1]]
-    bundle = sum_over(bundle[:12], "tensor")
+    total_out, total_in = totals["out"], totals["in"]
+
+    bundle = vector_rows(
+        section_ref,
+        rank.reshape(1).astype(jnp.int32),
+        [encoder_out[table]["sums"] for table in range(tables)],
+        dec["third_bias"],
+        [dec[name] for name in ("sums_one", "sums_two", "sums_three", "sum_q", "sum_v", "third_sum", "bias")],
+        cores / count,
+    )
+    bundle = sum_over(bundle, "dp")
+    query_key_grad, value_out_grad = unite(place_ref, line_ref, totals["qk"], totals["vo"], dec["thirds"])
+    bias_sum = bundle[12:13, : w_in.shape[1]]
+    bundle = sum_over(bundle, "tensor")
     vector_total = bundle[:11]
     cross_total = bundle[11] + lax.ppermute(bundle[11], "section", [(0, 1), (1, 0)])
 

time: 747 us -> 743 us (level)
  waiting for transfers between devices: 290 us -> 259 us
  starting transfers between devices: 101 us -> 125 us
    ppermute x85 -> x65, waiting for transfers between devices: 261 us -> 171 us  [flip(): return lax.ppermute(value, axis, [(i, i ^ 1 << bit) for i in range(count)])]
    ppermute x0 -> x20, starting transfers between devices: none -> 58.1 us  [the longest x4 40.6 us: sum_line(): sent = lax.ppermute(rows, 'dp', inward)]
    ppermute x0 -> x20, waiting for transfers between devices: none -> 50.1 us  [the longest x4 29.9 us: sum_line(): second = lax.ppermute(crossed, 'dp', outward)]
    ppermute x85 -> x65, starting transfers between devices: 64.7 us -> 36.2 us  [flip(): return lax.ppermute(value, axis, [(i, i ^ 1 << bit) for i in range(count)])]
    slice x17 -> x2, local copies, waits for them, and re-layouts: 13.5 us -> 0.6 us  [the longest x1 0.6 us: per_device(): bias_sum = bundle[12:13, :w_in.shape[1]]]
    ppermute x6, waiting for transfers between devices: 0.76 us -> 11.4 us  [send_chunks(): lax.ppermute(chunk, 'dp', [(i, (i + s + 1) % CHUNKS) for i in range(CHUNK...]
    unnamed x496 -> x493, local copies, waits for them, and re-layouts: 54.6 us -> 63.5 us
    pallas_call x77 -> x78, Pallas kernels: 249 us -> 254 us  [call(): pl.pallas_call(ordered, grid_spec=grid_spec, out_shape=out_shape, compile...]
  transfers between devices with their start and end apart: 104 -> 104, of which waited for: 45 -> 45; matrix products, arithmetic and copies ran while one was open for 5% -> 3% of each run, Pallas kernels for 25% -> 28%
where the time goes in v3:
time: 743 us; the launch traced here: 731 us
  waiting for transfers between devices  259 us (35%)
  Pallas kernels  254 us (34%)
  starting transfers between devices  125 us (17%)
  local copies, waits for them, and re-layouts  77.8 us (10%)
  other arithmetic  10.6 us (1%)
    pallas_call x78, Pallas kernels, call(): pl.pallas_call(ordered, grid_spec=grid_spec, out_shape=out_shape, compile...  254 us
    ppermute x65, waiting for transfers between devices, flip(): return lax.ppermute(value, axis, [(i, i ^ 1 << bit) for i in range(count)])  171 us
    unnamed x493, local copies, waits for them, and re-layouts  63.5 us
    ppermute x4, starting transfers between devices, sum_line(): sent = lax.ppermute(rows, 'dp', inward)  40.6 us
    ppermute x65, starting transfers between devices, flip(): return lax.ppermute(value, axis, [(i, i ^ 1 << bit) for i in range(count)])  36.2 us
    ppermute x4, waiting for transfers between devices, sum_line(): second = lax.ppermute(crossed, 'dp', outward)  29.9 us
    ppermute x5, waiting for transfers between devices, to_first(): return lax.ppermute(value, 'section', [(1, 0)])  15.1 us
  transfers between devices with their start and end apart: 104, of which 45 were waited for; matrix products, arithmetic and copies ran while one was open for 3% of the time, Pallas kernels for 28%

profile of v3, /device:TPU:0, one launch (start us, length us, event | category | flops | bytes accessed | tf_op | source)
XLA Modules:
  0.0 730.8 jit_solution(16566199896533746340)
XLA Ops:
  1.4 2.8 slice_bitcast_fusion
  7.0 5.6 collective-permute-start
  19.1 6.4 encoder_qkv.2
  27.2 10.2 %attention_kernel.2 = (bf16[1024,256]{1,0:T(8,128)(2,1)S(1)}, f32[1024,256]{1,0:T(8,128)S(1)}, f32[8,1024]{1,0:T(8,128)S(1)}, bf16[512,1024]{1,0:T(8,128)(2,1)S(1)}, bf16[512,1024]{1,0:T(8,128)(2,1)}) custom-call(bf16[1024,256]{1,0:T(8,128)(2,1)S(1)} %get-tuple-element.223.refs_0_.refs_5_.refs_6_, bf16[1024,256]{1,0:T(8,128)(2,1)S(1)} %get-tuple-element.224.refs_1_.refs_7_, ...), custom_call_target="tpu_custom_call" | custom-call | flops 2147483648 | bytes 4194304 | tf_op jit(solution)/shard_map/attention_kernel/pallas_call | solution.py:182
  48.2 6.4 encoder_qkv.3
  60.1 10.3 %attention_kernel.3 = (bf16[1024,256]{1,0:T(8,128)(2,1)S(1)}, f32[1024,256]{1,0:T(8,128)S(1)}, f32[8,1024]{1,0:T(8,128)S(1)}, bf16[512,1024]{1,0:T(8,128)(2,1)S(1)}, bf16[512,1024]{1,0:T(8,128)(2,1)}) custom-call(bf16[1024,256]{1,0:T(8,128)(2,1)S(1)} %get-tuple-element.228.refs_2_.refs_0_.refs_6_, bf16[1024,256]{1,0:T(8,128)(2,1)S(1)} %get-tuple-element.229.refs_1_.refs_7_, ...), custom_call_target="tpu_custom_call" | custom-call | flops 2147483648 | bytes 4194304 | tf_op jit(solution)/shard_map/attention_kernel/pallas_call | solution.py:182
  78.9 11.5 %collective-permute-done.9.refs_1_ = bf16[256,1024]{1,0:T(8,128)(2,1)} collective-permute-done((bf16[256,1024]{1,0:T(8,128)(2,1)}, bf16[256,1024]{1,0:T(8,128)(2,1)}, u32[]{:S(2)}, u32[]{:S(2)}) %collective-permute-start.9) | collective-permute-done | bytes 524320 | tf_op jit(solution)/shard_map/ppermute | solution.py:818
  100.7 10.7 %ffn_forward.3 = (bf16[1024,1024]{1,0:T(8,128)(2,1)}, bf16[1024,1024]{1,0:T(8,128)(2,1)}, bf16[1024,1024]{1,0:T(8,128)(2,1)}, bf16[512,1024]{1,0:T(8,128)(2,1)S(1)}, bf16[512,1024]{1,0:T(8,128)(2,1)S(1)}) custom-call(bf16[256,1024]{1,0:T(8,128)(2,1)} %get-tuple-element.246.refs_0_, bf16[256,1024]{1,0:T(8,128)(2,1)} %collective-permute-done.9.refs_1_, ...), custom_call_target="tpu_custom_call" | custom-call | flops 4294967296 | bytes 12582912 | tf_op jit(solution)/shard_map/ffn_forward/pallas_call | solution.py:182
  115.0 11.8 %collective-permute-done.15.refs_1_ = bf16[256,1024]{1,0:T(8,128)(2,1)S(1)} collective-permute-done((bf16[256,1024]{1,0:T(8,128)(2,1)S(1)}, bf16[256,1024]{1,0:T(8,128)(2,1)S(1)}, u32[]{:S(2)}, u32[]{:S(2)}) %collective-permute-start.15) | collective-permute-done | bytes 524320 | tf_op jit(solution)/shard_map/ppermute | solution.py:818
  128.1 7.4 %collective-permute-done.7.refs_2_ = bf16[128,1024]{1,0:T(8,128)(2,1)S(1)} collective-permute-done((bf16[128,1024]{1,0:T(8,128)(2,1)S(1)}, bf16[128,1024]{1,0:T(8,128)(2,1)S(1)}, u32[]{:S(2)}, u32[]{:S(2)}) %collective-permute-start.7) | collective-permute-done | bytes 262176 | tf_op jit(solution)/shard_map/ppermute | solution.py:818
  136.2 10.1 %ffn_forward.4 = (bf16[1024,1024]{1,0:T(8,128)(2,1)}, bf16[1024,1024]{1,0:T(8,128)(2,1)}, bf16[1024,1024]{1,0:T(8,128)(2,1)}, bf16[512,1024]{1,0:T(8,128)(2,1)S(1)}, bf16[512,1024]{1,0:T(8,128)(2,1)S(1)}) custom-call(bf16[256,1024]{1,0:T(8,128)(2,1)S(1)} %get-tuple-element.256.refs_0_, bf16[256,1024]{1,0:T(8,128)(2,1)S(1)} %collective-permute-done.15.refs_1_, ...), custom_call_target="tpu_custom_call" | custom-call | flops 4294967296 | bytes 12582912 | tf_op jit(solution)/shard_map/ffn_forward/pallas_call | solution.py:182
  147.6 13.1 %collective-permute-done.14.refs_2_ = bf16[256,1024]{1,0:T(8,128)(2,1)S(1)} collective-permute-done((bf16[256,1024]{1,0:T(8,128)(2,1)S(1)}, bf16[256,1024]{1,0:T(8,128)(2,1)S(1)}, u32[]{:S(2)}, u32[]{:S(2)}) %collective-permute-start.14) | collective-permute-done | bytes 524320 | tf_op jit(solution)/shard_map/ppermute | solution.py:818
  165.1 10.9 %collective-permute-done.23.refs_2_ = bf16[256,1024]{1,0:T(8,128)(2,1)S(1)} collective-permute-done((bf16[256,1024]{1,0:T(8,128)(2,1)S(1)}, bf16[256,1024]{1,0:T(8,128)(2,1)S(1)}, u32[]{:S(2)}, u32[]{:S(2)}) %collective-permute-start.23) | collective-permute-done | bytes 524320 | tf_op jit(solution)/shard_map/ppermute | solution.py:818
  180.1 9.0 %collective-permute-done.24.refs_0_ = bf16[256,1024]{1,0:T(8,128)(2,1)S(1)} collective-permute-done((bf16[256,1024]{1,0:T(8,128)(2,1)S(1)}, bf16[256,1024]{1,0:T(8,128)(2,1)S(1)}, u32[]{:S(2)}, u32[]{:S(2)}) %collective-permute-start.24) | collective-permute-done | bytes 524320 | tf_op jit(solution)/shard_map/ppermute | solution.py:855
  193.5 9.2 %collective-permute-done.25.refs_1_ = bf16[256,1024]{1,0:T(8,128)(2,1)S(1)} collective-permute-done((bf16[256,1024]{1,0:T(8,128)(2,1)S(1)}, bf16[256,1024]{1,0:T(8,128)(2,1)S(1)}, u32[]{:S(2)}, u32[]{:S(2)}) %collective-permute-start.25) | collective-permute-done | bytes 524320 | tf_op jit(solution)/shard_map/ppermute | solution.py:818
  203.2 3.9 project_parts.2
  207.2 4.2 project_parts.3
  211.5 3.6 decoder_cross.1
  218.1 7.1 collective-permute-done.29.refs_2_
  227.2 4.1 ffn_forward.5
  234.4 7.1 collective-permute-done.32.refs_2_
  244.6 4.5 ffn_backward.3
  252.9 7.1 collective-permute-done.35.refs_2_
  262.2 5.4 decoder_cross_back.1
  269.0 3.3 back_sum.4
  272.5 3.3 back_sum.5
  280.2 3.8 weight_sum.4.refs_4_.refs_0_
  283.9 3.0 weight_sum.5.refs_2_.refs_1_
  287.7 3.7 collective-permute-done.40.refs_1_
  292.9 9.0 %collective-permute-done.39.refs_1_ = bf16[256,1024]{1,0:T(8,128)(2,1)S(1)} collective-permute-done((bf16[256,1024]{1,0:T(8,128)(2,1)S(1)}, bf16[256,1024]{1,0:T(8,128)(2,1)S(1)}, u32[]{:S(2)}, u32[]{:S(2)}) %collective-permute-start.39) | collective-permute-done | bytes 524320 | tf_op jit(solution)/shard_map/ppermute | solution.py:818
  302.0 3.8 collective-permute-done.42.refs_0_
  309.5 8.7 %collective-permute-done.44.refs_1_.refs_3_ = bf16[256,1024]{1,0:T(8,128)(2,1)} collective-permute-done((bf16[256,1024]{1,0:T(8,128)(2,1)S(1)}, bf16[256,1024]{1,0:T(8,128)(2,1)}, u32[]{:S(2)}, u32[]{:S(2)}) %collective-permute-start.44) | collective-permute-done | bytes 524320 | tf_op jit(solution)/shard_map/ppermute | solution.py:818
  318.2 2.7 collective-permute-done.41.refs_0_
  325.1 10.8 %ffn_backward.4 = (bf16[1024,1024]{1,0:T(8,128)(2,1)}, bf16[1024,1024]{1,0:T(8,128)(2,1)}, bf16[512,1024]{1,0:T(8,128)(2,1)S(1)}, bf16[512,1024]{1,0:T(8,128)(2,1)}, f32[1,1024]{1,0:T(1,128)S(1)}) custom-call(bf16[256,1024]{1,0:T(8,128)(2,1)S(1)} %copy-done.219, bf16[256,1024]{1,0:T(8,128)(2,1)} %collective-permute-done.44.refs_1_.refs_3_, ...), custom_call_target="tpu_custom_call" | custom-call | flops 4294967296 | bytes 10485760 | tf_op jit(solution)/shard_map/ffn_backward/pallas_call | solution.py:182
  341.6 10.0 %collective-permute-done.48.refs_1_.refs_8_ = bf16[256,1024]{1,0:T(8,128)(2,1)} collective-permute-done((bf16[256,1024]{1,0:T(8,128)(2,1)}, bf16[256,1024]{1,0:T(8,128)(2,1)}, u32[]{:S(2)}, u32[]{:S(2)}) %collective-permute-start.48) | collective-permute-done | bytes 524320 | tf_op jit(solution)/shard_map/ppermute | solution.py:818
  357.0 8.6 %collective-permute-done.52.refs_3_ = bf16[1024,256]{1,0:T(8,128)(2,1)} collective-permute-done((bf16[1024,256]{1,0:T(8,128)(2,1)S(1)}, bf16[1024,256]{1,0:T(8,128)(2,1)}, u32[]{:S(2)}, u32[]{:S(2)}) %collective-permute-start.52) | collective-permute-done | bytes 524320 | tf_op jit(solution)/shard_map/ppermute | solution.py:859
  369.9 11.1 %ffn_backward.5 = (bf16[1024,1024]{1,0:T(8,128)(2,1)}, bf16[1024,1024]{1,0:T(8,128)(2,1)}, bf16[512,1024]{1,0:T(8,128)(2,1)S(1)}, bf16[512,1024]{1,0:T(8,128)(2,1)}, f32[1,1024]{1,0:T(1,128)S(1)}) custom-call(bf16[256,1024]{1,0:T(8,128)(2,1)} %get-tuple-element.326.refs_0_.refs_7_, bf16[256,1024]{1,0:T(8,128)(2,1)} %collective-permute-done.48.refs_1_.refs_8_, ...), custom_call_target="tpu_custom_call" | custom-call | flops 4294967296 | bytes 10485760 | tf_op jit(solution)/shard_map/ffn_backward/pallas_call | solution.py:182
  391.7 6.7 collective-permute-done.61.refs_1_
  400.6 9.8 %weight_grad.4.refs_4_.refs_0_ = bf16[4,256,1024]{2,1,0:T(8,128)(2,1)} custom-call(s32[1]{0:T(128)} %bitcast.31.refs_0_, s32[4]{0:T(128)S(1)} %and_select_fusion.2.refs_1_, bf16[256,1024]{1,0:T(8,128)(2,1)S(1)} %copy-done.220, bf16[256,1024]{1,0:T(8,128)(2,1)} %collective-permute-done.44.refs_1_.refs_3_, ...), custom_call_target="tpu_custom_call" | custom-call | flops 4831838208 | bytes 9437184 | tf_op jit(solution)/shard_map/weight_grad/pallas_call | solution.py:182
  412.5 5.2 collective-permute-start.75
  421.2 9.3 %weight_grad.5.refs_5_.refs_0_ = bf16[4,256,1024]{2,1,0:T(8,128)(2,1)} custom-call(s32[1]{0:T(128)} %bitcast.31.refs_0_, s32[4]{0:T(128)S(1)} %and_select_fusion.2.refs_1_, bf16[1024,1024]{1,0:T(8,128)(2,1)S(1)} %copy-done.228, bf16[1024,1024]{1,0:T(8,128)(2,1)} %get-tuple-element.324.refs_3_, bf16[1024,1024]{1,0:T(8,128)(2,1)} %get-tuple-element.325.refs_4_, ...), custom_call_target="tpu_custom_call" | custom-call | flops 4831838208 | bytes 9437184 | tf_op jit(solution)/shard_map/weight_grad/pallas_call | solution.py:182
  433.1 16.5 %encoder_attention_back.2 = (bf16[1024,1024]{1,0:T(8,128)(2,1)}, bf16[1024,256]{1,0:T(8,128)(2,1)S(1)}, bf16[1024,256]{1,0:T(8,128)(2,1)S(1)}, bf16[1024,256]{1,...) custom-call(bf16[256,1024]{1,0:T(8,128)(2,1)} %get-tuple-element.358.refs_0_, ...), custom_call_target="tpu_custom_call" | custom-call | flops 5368709120 | bytes 6291456 | tf_op jit(solution)/shard_map/encoder_attention_back/pallas_call | solution.py:182
  465.3 2.8 sum_line.8
  470.0 4.8 collective-permute-done.72.refs_1_
  476.0 3.0 collective-permute-start.70
  483.3 16.6 %encoder_attention_back.3 = (bf16[1024,1024]{1,0:T(8,128)(2,1)}, bf16[1024,256]{1,0:T(8,128)(2,1)S(1)}, bf16[1024,256]{1,0:T(8,128)(2,1)S(1)}, bf16[1024,256]{1,...) custom-call(bf16[256,1024]{1,0:T(8,128)(2,1)} %get-tuple-element.375.refs_0_, ...), custom_call_target="tpu_custom_call" | custom-call | flops 5368709120 | bytes 6291456 | tf_op jit(solution)/shard_map/encoder_attention_back/pallas_call | solution.py:182
  503.3 7.3 weight_grad.6.refs_14_.refs_0_
  510.6 7.1 weight_grad.7.refs_2_.refs_0_
  517.8 3.4 sum_line.10
  522.2 3.6 back_sum.7
  529.5 11.4 %collective-permute-done.71.refs_3_ = bf16[256,512]{1,0:T(8,128)(2,1)S(1)} collective-permute-done((bf16[256,512]{1,0:T(8,128)(2,1)S(1)}, bf16[256,512]{1,0:T(8,128)(2,1)S(1)}, u32[]{:S(2)}, u32[]{:S(2)}) %collective-permute-start.71) | collective-permute-done | bytes 262176 | tf_op jit(solution)/shard_map/ppermute | solution.py:691
  542.2 12.4 %collective-permute-done.68.refs_2_ = bf16[256,1024]{1,0:T(8,128)(2,1)S(1)} collective-permute-done((bf16[256,1024]{1,0:T(8,128)(2,1)}, bf16[256,1024]{1,0:T(8,128)(2,1)S(1)}, u32[]{:S(2)}, u32[]{:S(2)}) %collective-permute-start.68) | collective-permute-done | bytes 524320 | tf_op jit(solution)/shard_map/ppermute | solution.py:818
  555.3 30.4 %collective-permute-start.84 = (bf16[4,256,512]{2,1,0:T(8,128)(2,1)}, bf16[4,256,512]{2,1,0:T(8,128)(2,1)}, u32[]{:S(2)}, u32[]{:S(2)}) collective-permute-start(bf16[4,256,512]{2,1,0:T(8,128)(2,1)} %weight_grad.6.refs_14_.refs_0_), channel_id=1, source_target_pairs={{0,4},{12,8},{1,5},{13,9},{2,6},{14,10},{3,7},{15,11},{16,20},{28,... | collective-permute-start | bytes 3145736 | tf_op jit(solution)/shard_map/ppermute | solution.py:609
  603.2 10.5 %collective-permute-done.81.refs_2_ = bf16[256,1024]{1,0:T(8,128)(2,1)S(1)} collective-permute-done((bf16[256,1024]{1,0:T(8,128)(2,1)S(1)}, bf16[256,1024]{1,0:T(8,128)(2,1)S(1)}, u32[]{:S(2)}, u32[]{:S(2)}) %collective-permute-start.81) | collective-permute-done | bytes 524320 | tf_op jit(solution)/shard_map/ppermute | solution.py:818
  619.7 8.6 %collective-permute-done.89.refs_1_ = bf16[4,256,512]{2,1,0:T(8,128)(2,1)} collective-permute-done((bf16[4,256,512]{2,1,0:T(8,128)(2,1)}, bf16[4,256,512]{2,1,0:T(8,128)(2,1)}, u32[]{:S(2)}, u32[]{:S(2)}) %collective-permute-start.89) | collective-permute-done | bytes 1048608 | tf_op jit(solution)/shard_map/ppermute | solution.py:609
  637.0 14.3 %collective-permute-done.86.refs_4_ = bf16[2,256,1024]{2,1,0:T(8,128)(2,1)} collective-permute-done((bf16[2,256,1024]{2,1,0:T(8,128)(2,1)S(1)}, bf16[2,256,1024]{2,1,0:T(8,128)(2,1)}, u32[]{:S(2)}, u32[]{:S(2)}) %collective-permute-start.86) | collective-permute-done | bytes 1048608 | tf_op jit(solution)/shard_map/ppermute | solution.py:638
  652.4 4.8 unite_one.2.refs_2_
  667.1 6.6 collective-permute-done.92.refs_4_
  675.7 4.2 unite_one.3.refs_2_
  681.5 3.4 collective-permute-done.91.refs_1_
  684.9 8.1 %collective-permute-done.96.refs_1_ = bf16[2,256,512]{2,1,0:T(8,128)(2,1)} collective-permute-done((bf16[2,256,512]{2,1,0:T(8,128)(2,1)S(1)}, bf16[2,256,512]{2,1,0:T(8,128)(2,1)}, u32[]{:S(2)}, u32[]{:S(2)}) %collective-permute-start.96) | collective-permute-done | bytes 524320 | tf_op jit(solution)/shard_map/ppermute | solution.py:635
  712.2 2.8 collective-permute-done.103
  717.4 7.2 collective-permute-done.97.refs_9_
  725.6 4.9 unite.1
  (776 shorter events, 236.6 us)
Async XLA Ops:
  7.0 40.6 %collective-permute-start = (bf16[1024,256]{1,0:T(8,128)(2,1)}, bf16[1024,256]{1,0:T(8,128)(2,1)}, u32[]{:S(2)}, u32[]{:S(2)}) collective-permute-start(bf16[1024,256]{1,0:T(8,128)(2,1)} %get-tuple-element.220.refs_9_), channel_id=1, source_target_pairs={{0,16},{1,17},{2,18},{3,19},{4,20},{5,21},{6,22},{7,23},{8,24},{9,... | collective-permute-start | bytes 1572872 | tf_op jit(solution)/shard_map/ppermute | solution.py:855
  12.6 35.0 %collective-permute-start.1 = (bf16[1024,256]{1,0:T(8,128)(2,1)}, bf16[1024,256]{1,0:T(8,128)(2,1)}, u32[]{:S(2)}, u32[]{:S(2)}) collective-permute-start(bf16[1024,256]{1,0:T(8,128)(2,1)} %get-tuple-element.221), channel_id=1, source_target_pairs={{0,16},{1,17},{2,18},{3,19},{4,20},{5,21},{6,22},{7,23},{8,24},{9,... | collective-permute-start | bytes 1572872 | tf_op jit(solution)/shard_map/ppermute | solution.py:855
  14.7 32.9 %collective-permute-start.2 = (f32[1,256]{1,0:T(1,128)}, f32[1,256]{1,0:T(1,128)S(1)}, u32[]{:S(2)}, u32[]{:S(2)}) collective-permute-start(f32[1,256]{1,0:T(1,128)} %get-tuple-element.222), channel_id=1, source_target_pairs={{0,16},{1,17},{2,18},{3,19},{4,20},{5,21},{6,22},{7,23},{8,24},{9,... | collective-permute-start | bytes 3080 | tf_op jit(solution)/shard_map/ppermute | solution.py:855
  40.8 15.6 %collective-permute-start.3 = (bf16[512,1024]{1,0:T(8,128)(2,1)}, bf16[512,1024]{1,0:T(8,128)(2,1)}, u32[]{:S(2)}, u32[]{:S(2)}) collective-permute-start(bf16[512,1024]{1,0:T(8,128)(2,1)} %get-tuple-element.232), channel_id=1, source_target_pairs={{0,1},{1,0},{2,3},{3,2},{4,5},{5,4},{6,7},{7,6},{8,9},{9,8},{10,11... | collective-permute-start | bytes 3145736 | tf_op jit(solution)/shard_map/ppermute | solution.py:818
  58.5 14.4 %collective-permute-start.5 = (bf16[256,1024]{1,0:T(8,128)(2,1)S(1)}, bf16[256,1024]{1,0:T(8,128)(2,1)S(1)}, u32[]{:S(2)}, u32[]{:S(2)}) collective-permute-start(bf16[256,1024]{1,0:T(8,128)(2,1)S(1)} %get-tuple-element.237), channel_id=1, source_target_pairs={{0,2},{1,3},{2,0},{3,1},{4,6},{5,7},{6,4},{7,5},{8,10},{9,11},{10,... | collective-permute-start | bytes 1572872 | tf_op jit(solution)/shard_map/ppermute | solution.py:818
  72.3 18.2 %collective-permute-start.4 = (bf16[512,1024]{1,0:T(8,128)(2,1)}, bf16[512,1024]{1,0:T(8,128)(2,1)}, u32[]{:S(2)}, u32[]{:S(2)}) collective-permute-start(bf16[512,1024]{1,0:T(8,128)(2,1)} %get-tuple-element.235), channel_id=1, source_target_pairs={{0,1},{1,0},{2,3},{3,2},{4,5},{5,4},{6,7},{7,6},{8,9},{9,8},{10,11... | collective-permute-start | bytes 3145736 | tf_op jit(solution)/shard_map/ppermute | solution.py:818
  76.2 14.2 %collective-permute-start.9 = (bf16[256,1024]{1,0:T(8,128)(2,1)}, bf16[256,1024]{1,0:T(8,128)(2,1)}, u32[]{:S(2)}, u32[]{:S(2)}) collective-permute-start(bf16[256,1024]{1,0:T(8,128)(2,1)} %get-tuple-element.246.refs_0_), channel_id=1, source_target_pairs={{0,2},{1,3},{2,0},{3,1},{4,6},{5,7},{6,4},{7,5},{8,10},{9,11},{10,... | collective-permute-start | bytes 1572872 | tf_op jit(solution)/shard_map/ppermute | solution.py:818
  78.8 21.8 %collective-permute-start.10 = (bf16[256,1024]{1,0:T(8,128)(2,1)}, bf16[256,1024]{1,0:T(8,128)(2,1)S(1)}, u32[]{:S(2)}, u32[]{:S(2)}) collective-permute-start(bf16[256,1024]{1,0:T(8,128)(2,1)} %get-tuple-element.246.refs_0_), channel_id=1, source_target_pairs={{0,1},{1,0},{2,3},{3,2},{4,5},{5,4},{6,7},{7,6},{8,9},{9,8},{10,11... | collective-permute-start | bytes 1572872 | tf_op jit(solution)/shard_map/ppermute | solution.py:818
  99.3 13.9 %collective-permute-start.8 = (bf16[256,1024]{1,0:T(8,128)(2,1)S(1)}, bf16[256,1024]{1,0:T(8,128)(2,1)S(1)}, u32[]{:S(2)}, u32[]{:S(2)}) collective-permute-start(bf16[256,1024]{1,0:T(8,128)(2,1)S(1)} %get-tuple-element.245), channel_id=1, source_target_pairs={{0,2},{1,3},{2,0},{3,1},{4,6},{5,7},{6,4},{7,5},{8,10},{9,11},{10,... | collective-permute-start | bytes 1572872 | tf_op jit(solution)/shard_map/ppermute | solution.py:818
  111.4 24.5 %collective-permute-start.13 = (bf16[512,1024]{1,0:T(8,128)(2,1)S(1)}, bf16[512,1024]{1,0:T(8,128)(2,1)S(1)}, u32[]{:S(2)}, u32[]{:S(2)}) collective-permute-start(bf16[512,1024]{1,0:T(8,128)(2,1)S(1)} %get-tuple-element.252), channel_id=1, source_target_pairs={{0,1},{1,0},{2,3},{3,2},{4,5},{5,4},{6,7},{7,6},{8,9},{9,8},{10,11... | collective-permute-start | bytes 3145736 | tf_op jit(solution)/shard_map/ppermute | solution.py:818
  115.0 21.2 %collective-permute-start.16 = (bf16[256,1024]{1,0:T(8,128)(2,1)S(1)}, bf16[256,1024]{1,0:T(8,128)(2,1)S(1)}, u32[]{:S(2)}, u32[]{:S(2)}) collective-permute-start(bf16[256,1024]{1,0:T(8,128)(2,1)S(1)} %get-tuple-element.256.refs_0_), channel_id=1, source_target_pairs={{0,1},{1,0},{2,3},{3,2},{4,5},{5,4},{6,7},{7,6},{8,9},{9,8},{10,11... | collective-permute-start | bytes 1572872 | tf_op jit(solution)/shard_map/ppermute | solution.py:818
  146.3 15.8 %collective-permute-start.22 = (bf16[512,1024]{1,0:T(8,128)(2,1)S(1)}, bf16[512,1024]{1,0:T(8,128)(2,1)S(1)}, u32[]{:S(2)}, u32[]{:S(2)}) collective-permute-start(bf16[512,1024]{1,0:T(8,128)(2,1)S(1)} %get-tuple-element.262), channel_id=1, source_target_pairs={{0,1},{1,0},{2,3},{3,2},{4,5},{5,4},{6,7},{7,6},{8,9},{9,8},{10,11... | collective-permute-start | bytes 3145736 | tf_op jit(solution)/shard_map/ppermute | solution.py:818
  146.3 14.3 %collective-permute-start.14 = (bf16[256,1024]{1,0:T(8,128)(2,1)S(1)}, bf16[256,1024]{1,0:T(8,128)(2,1)S(1)}, u32[]{:S(2)}, u32[]{:S(2)}) collective-permute-start(bf16[256,1024]{1,0:T(8,128)(2,1)S(1)} %get-tuple-element.255), channel_id=1, source_target_pairs={{0,2},{1,3},{2,0},{3,1},{4,6},{5,7},{6,4},{7,5},{8,10},{9,11},{10,... | collective-permute-start | bytes 1572872 | tf_op jit(solution)/shard_map/ppermute | solution.py:818
  163.7 15.1 %collective-permute-start.18 = (bf16[256,1024]{1,0:T(8,128)(2,1)S(1)}, bf16[256,1024]{1,0:T(8,128)(2,1)S(1)}, u32[]{:S(2)}, u32[]{:S(2)}) collective-permute-start(bf16[256,1024]{1,0:T(8,128)(2,1)S(1)} %get-tuple-element.258), channel_id=1, source_target_pairs={{0,16},{1,17},{2,18},{3,19},{4,20},{5,21},{6,22},{7,23},{8,24},{9,... | collective-permute-start | bytes 1572872 | tf_op jit(solution)/shard_map/ppermute | solution.py:855
  178.8 14.2 %collective-permute-start.19 = (bf16[256,1024]{1,0:T(8,128)(2,1)S(1)}, bf16[256,1024]{1,0:T(8,128)(2,1)S(1)}, u32[]{:S(2)}, u32[]{:S(2)}) collective-permute-start(bf16[256,1024]{1,0:T(8,128)(2,1)S(1)} %collective-permute-done.18.refs_0_), channel_id=1, source_target_pairs={{0,2},{1,3},{2,0},{3,1},{4,6},{5,7},{6,4},{7,5},{8,10},{9,11},{10,... | collective-permute-start | bytes 1572872 | tf_op jit(solution)/shard_map/ppermute | solution.py:818
  193.0 14.1 %collective-permute-start.26 = (bf16[256,1024]{1,0:T(8,128)(2,1)S(1)}, bf16[256,1024]{1,0:T(8,128)(2,1)S(1)}, u32[]{:S(2)}, u32[]{:S(2)}) collective-permute-start(bf16[256,1024]{1,0:T(8,128)(2,1)S(1)} %collective-permute-done.24.refs_0_), channel_id=1, source_target_pairs={{0,1},{1,0},{2,3},{3,2},{4,5},{5,4},{6,7},{7,6},{8,9},{9,8},{10,11... | collective-permute-start | bytes 1572872 | tf_op jit(solution)/shard_map/ppermute | solution.py:818
  276.6 14.8 %collective-permute-start.40 = (bf16[256,1024]{1,0:T(8,128)(2,1)S(1)}, bf16[256,1024]{1,0:T(8,128)(2,1)S(1)}, u32[]{:S(2)}, u32[]{:S(2)}) collective-permute-start(bf16[256,1024]{1,0:T(8,128)(2,1)S(1)} %get-tuple-element.308), channel_id=1, source_target_pairs={{0,2},{1,3},{2,0},{3,1},{4,6},{5,7},{6,4},{7,5},{8,10},{9,11},{10,... | collective-permute-start | bytes 1572872 | tf_op jit(solution)/shard_map/ppermute | solution.py:818
  278.9 23.0 %collective-permute-start.39 = (bf16[256,1024]{1,0:T(8,128)(2,1)S(1)}, bf16[256,1024]{1,0:T(8,128)(2,1)S(1)}, u32[]{:S(2)}, u32[]{:S(2)}) collective-permute-start(bf16[256,1024]{1,0:T(8,128)(2,1)S(1)} %get-tuple-element.307), channel_id=1, source_target_pairs={{0,2},{1,3},{2,0},{3,1},{4,6},{5,7},{6,4},{7,5},{8,10},{9,11},{10,... | collective-permute-start | bytes 1572872 | tf_op jit(solution)/shard_map/ppermute | solution.py:818
  291.6 14.2 %collective-permute-start.42 = (bf16[256,1024]{1,0:T(8,128)(2,1)S(1)}, bf16[256,1024]{1,0:T(8,128)(2,1)S(1)}, u32[]{:S(2)}, u32[]{:S(2)}) collective-permute-start(bf16[256,1024]{1,0:T(8,128)(2,1)S(1)} %add_rows.12.refs_2_), channel_id=1, source_target_pairs={{16,0},{17,1},{18,2},{19,3},{20,4},{21,5},{22,6},{23,7},{24,8},{25... | collective-permute-start | bytes 1572872 | tf_op jit(solution)/shard_map/ppermute | solution.py:859
  309.4 14.7 %collective-permute-start.45 = (bf16[256,1024]{1,0:T(8,128)(2,1)S(1)}, bf16[256,1024]{1,0:T(8,128)(2,1)}, u32[]{:S(2)}, u32[]{:S(2)}) collective-permute-start(bf16[256,1024]{1,0:T(8,128)(2,1)S(1)} %get-tuple-element.319.refs_0_.refs_2_), channel_id=1, source_target_pairs={{0,1},{1,0},{2,3},{3,2},{4,5},{5,4},{6,7},{7,6},{8,9},{9,8},{10,11... | collective-permute-start | bytes 1572872 | tf_op jit(solution)/shard_map/ppermute | solution.py:818
  337.0 16.4 %collective-permute-start.53 = (bf16[512,1024]{1,0:T(8,128)(2,1)}, bf16[512,1024]{1,0:T(8,128)(2,1)}, u32[]{:S(2)}, u32[]{:S(2)}) collective-permute-start(bf16[512,1024]{1,0:T(8,128)(2,1)} %get-tuple-element.330), channel_id=1, source_target_pairs={{0,1},{1,0},{2,3},{3,2},{4,5},{5,4},{6,7},{7,6},{8,9},{9,8},{10,11... | collective-permute-start | bytes 3145736 | tf_op jit(solution)/shard_map/ppermute | solution.py:818
  337.0 14.7 %collective-permute-start.48 = (bf16[256,1024]{1,0:T(8,128)(2,1)}, bf16[256,1024]{1,0:T(8,128)(2,1)}, u32[]{:S(2)}, u32[]{:S(2)}) collective-permute-start(bf16[256,1024]{1,0:T(8,128)(2,1)} %get-tuple-element.326.refs_0_.refs_7_), channel_id=1, source_target_pairs={{0,2},{1,3},{2,0},{3,1},{4,6},{5,7},{6,4},{7,5},{8,10},{9,11},{10,... | collective-permute-start | bytes 1572872 | tf_op jit(solution)/shard_map/ppermute | solution.py:818
  338.0 19.0 %collective-permute-start.51 = (bf16[1024,256]{1,0:T(8,128)(2,1)}, bf16[1024,256]{1,0:T(8,128)(2,1)}, u32[]{:S(2)}, u32[]{:S(2)}) collective-permute-start(bf16[1024,256]{1,0:T(8,128)(2,1)} %get-tuple-element.321.refs_7_), channel_id=1, source_target_pairs={{16,0},{17,1},{18,2},{19,3},{20,4},{21,5},{22,6},{23,7},{24,8},{25... | collective-permute-start | bytes 1572872 | tf_op jit(solution)/shard_map/ppermute | solution.py:859
  339.3 26.2 %collective-permute-start.52 = (bf16[1024,256]{1,0:T(8,128)(2,1)S(1)}, bf16[1024,256]{1,0:T(8,128)(2,1)}, u32[]{:S(2)}, u32[]{:S(2)}) collective-permute-start(bf16[1024,256]{1,0:T(8,128)(2,1)S(1)} %copy-done.20), channel_id=1, source_target_pairs={{16,0},{17,1},{18,2},{19,3},{20,4},{21,5},{22,6},{23,7},{24,8},{25... | collective-permute-start | bytes 1572872 | tf_op jit(solution)/shard_map/ppermute | solution.py:859
  341.3 28.6 %collective-permute-start.49 = (bf16[256,1024]{1,0:T(8,128)(2,1)}, bf16[256,1024]{1,0:T(8,128)(2,1)}, u32[]{:S(2)}, u32[]{:S(2)}) collective-permute-start(bf16[256,1024]{1,0:T(8,128)(2,1)} %get-tuple-element.326.refs_0_.refs_7_), channel_id=1, source_target_pairs={{0,1},{1,0},{2,3},{3,2},{4,5},{5,4},{6,7},{7,6},{8,9},{9,8},{10,11... | collective-permute-start | bytes 1572872 | tf_op jit(solution)/shard_map/ppermute | solution.py:818
  351.6 18.3 %collective-permute-start.50 = (bf16[256,1024]{1,0:T(8,128)(2,1)}, bf16[256,1024]{1,0:T(8,128)(2,1)}, u32[]{:S(2)}, u32[]{:S(2)}) collective-permute-start(bf16[256,1024]{1,0:T(8,128)(2,1)} %collective-permute-done.48.refs_1_.refs_8_), channel_id=1, source_target_pairs={{0,1},{1,0},{2,3},{3,2},{4,5},{5,4},{6,7},{7,6},{8,9},{9,8},{10,11... | collective-permute-start | bytes 1572872 | tf_op jit(solution)/shard_map/ppermute | solution.py:818
  356.1 25.0 %collective-permute-start.58 = (bf16[256,1024]{1,0:T(8,128)(2,1)S(1)}, bf16[256,1024]{1,0:T(8,128)(2,1)S(1)}, u32[]{:S(2)}, u32[]{:S(2)}) collective-permute-start(bf16[256,1024]{1,0:T(8,128)(2,1)S(1)} %get-tuple-element.346), channel_id=1, source_target_pairs={{0,2},{1,3},{2,0},{3,1},{4,6},{5,7},{6,4},{7,5},{8,10},{9,11},{10,... | collective-permute-start | bytes 1572872 | tf_op jit(solution)/shard_map/ppermute | solution.py:818
  383.8 14.6 %collective-permute-start.61 = (bf16[256,1024]{1,0:T(8,128)(2,1)}, bf16[256,1024]{1,0:T(8,128)(2,1)}, u32[]{:S(2)}, u32[]{:S(2)}) collective-permute-start(bf16[256,1024]{1,0:T(8,128)(2,1)} %get-tuple-element.358.refs_0_), channel_id=1, source_target_pairs={{0,2},{1,3},{2,0},{3,1},{4,6},{5,7},{6,4},{7,5},{8,10},{9,11},{10,... | collective-permute-start | bytes 1572872 | tf_op jit(solution)/shard_map/ppermute | solution.py:818
  386.1 24.3 %collective-permute-start.54 = (bf16[256,512]{1,0:T(8,128)(2,1)}, bf16[256,512]{1,0:T(8,128)(2,1)S(1)}, u32[]{:S(2)}, u32[]{:S(2)}) collective-permute-start(bf16[256,512]{1,0:T(8,128)(2,1)} %copy-done.225), channel_id=1, source_target_pairs={{0,4},{4,8},{8,12},{12,0},{1,5},{5,9},{9,13},{13,1},{2,6},{6,10},{... | collective-permute-start | bytes 786440 | tf_op jit(solution)/shard_map/ppermute | solution.py:691
  387.7 24.0 %collective-permute-start.55 = (bf16[256,512]{1,0:T(8,128)(2,1)}, bf16[256,512]{1,0:T(8,128)(2,1)S(1)}, u32[]{:S(2)}, u32[]{:S(2)}) collective-permute-start(bf16[256,512]{1,0:T(8,128)(2,1)} %copy-done.224), channel_id=1, source_target_pairs={{0,8},{4,12},{8,0},{12,4},{1,9},{5,13},{9,1},{13,5},{2,10},{6,14},... | collective-permute-start | bytes 786440 | tf_op jit(solution)/shard_map/ppermute | solution.py:691
  390.3 22.2 %collective-permute-start.56 = (bf16[256,512]{1,0:T(8,128)(2,1)}, bf16[256,512]{1,0:T(8,128)(2,1)S(1)}, u32[]{:S(2)}, u32[]{:S(2)}) collective-permute-start(bf16[256,512]{1,0:T(8,128)(2,1)} %copy-done.223), channel_id=1, source_target_pairs={{0,12},{4,0},{8,4},{12,8},{1,13},{5,1},{9,5},{13,9},{2,14},{6,2},{... | collective-permute-start | bytes 786440 | tf_op jit(solution)/shard_map/ppermute | solution.py:691
  391.7 41.4 %collective-permute-start.62 = (bf16[256,1024]{1,0:T(8,128)(2,1)}, bf16[256,1024]{1,0:T(8,128)(2,1)S(1)}, u32[]{:S(2)}, u32[]{:S(2)}) collective-permute-start(bf16[256,1024]{1,0:T(8,128)(2,1)} %get-tuple-element.358.refs_0_), channel_id=1, source_target_pairs={{0,1},{1,0},{2,3},{3,2},{4,5},{5,4},{6,7},{7,6},{8,9},{9,8},{10,11... | collective-permute-start | bytes 1572872 | tf_op jit(solution)/shard_map/ppermute | solution.py:818
  398.4 34.6 %collective-permute-start.63 = (bf16[256,1024]{1,0:T(8,128)(2,1)}, bf16[256,1024]{1,0:T(8,128)(2,1)S(1)}, u32[]{:S(2)}, u32[]{:S(2)}) collective-permute-start(bf16[256,1024]{1,0:T(8,128)(2,1)} %collective-permute-done.61.refs_1_), channel_id=1, source_target_pairs={{0,1},{1,0},{2,3},{3,2},{4,5},{5,4},{6,7},{7,6},{8,9},{9,8},{10,11... | collective-permute-start | bytes 1572872 | tf_op jit(solution)/shard_map/ppermute | solution.py:818
  410.4 20.2 %collective-permute-start.47 = (bf16[128,1024]{1,0:T(8,128)(2,1)}, bf16[128,1024]{1,0:T(8,128)(2,1)S(1)}, u32[]{:S(2)}, u32[]{:S(2)}) collective-permute-start(bf16[128,1024]{1,0:T(8,128)(2,1)} %add_rows.14.refs_2_.refs_1_), channel_id=1, source_target_pairs={{0,2},{1,3},{2,0},{3,1},{4,6},{5,7},{6,4},{7,5},{8,10},{9,11},{10,... | collective-permute-start | bytes 786440 | tf_op jit(solution)/shard_map/ppermute | solution.py:818
  411.7 38.6 %collective-permute-start.60 = (bf16[256,1024]{1,0:T(8,128)(2,1)}, bf16[256,1024]{1,0:T(8,128)(2,1)S(1)}, u32[]{:S(2)}, u32[]{:S(2)}) collective-permute-start(bf16[256,1024]{1,0:T(8,128)(2,1)} %get-tuple-element.357), channel_id=1, source_target_pairs={{0,2},{1,3},{2,0},{3,1},{4,6},{5,7},{6,4},{7,5},{8,10},{9,11},{10,... | collective-permute-start | bytes 1572872 | tf_op jit(solution)/shard_map/ppermute | solution.py:818
  412.5 51.9 %collective-permute-start.75 = (bf16[4,256,1024]{2,1,0:T(8,128)(2,1)}, bf16[4,256,1024]{2,1,0:T(8,128)(2,1)}, u32[]{:S(2)}, u32[]{:S(2)}) collective-permute-start(bf16[4,256,1024]{2,1,0:T(8,128)(2,1)} %weight_grad.4.refs_4_.refs_0_), channel_id=1, source_target_pairs={{0,4},{12,8},{1,5},{13,9},{2,6},{14,10},{3,7},{15,11},{16,20},{28,... | collective-permute-start | bytes 6291464 | tf_op jit(solution)/shard_map/ppermute | solution.py:609
  433.0 19.0 %collective-permute-start.59 = (bf16[128,1024]{1,0:T(8,128)(2,1)S(1)}, bf16[128,1024]{1,0:T(8,128)(2,1)S(1)}, u32[]{:S(2)}, u32[]{:S(2)}) collective-permute-start(bf16[128,1024]{1,0:T(8,128)(2,1)S(1)} %get-tuple-element.351.refs_0_), channel_id=1, source_target_pairs={{0,1},{1,0},{2,3},{3,2},{4,5},{5,4},{6,7},{7,6},{8,9},{9,8},{10,11... | collective-permute-start | bytes 786440 | tf_op jit(solution)/shard_map/ppermute | solution.py:818
  457.9 59.8 %collective-permute-start.76 = (bf16[4,256,1024]{2,1,0:T(8,128)(2,1)}, bf16[4,256,1024]{2,1,0:T(8,128)(2,1)}, u32[]{:S(2)}, u32[]{:S(2)}) collective-permute-start(bf16[4,256,1024]{2,1,0:T(8,128)(2,1)} %weight_grad.5.refs_5_.refs_0_), channel_id=1, source_target_pairs={{0,4},{12,8},{1,5},{13,9},{2,6},{14,10},{3,7},{15,11},{16,20},{28,... | collective-permute-start | bytes 6291464 | tf_op jit(solution)/shard_map/ppermute | solution.py:609
  460.6 14.2 %collective-permute-start.72 = (bf16[256,1024]{1,0:T(8,128)(2,1)}, bf16[256,1024]{1,0:T(8,128)(2,1)}, u32[]{:S(2)}, u32[]{:S(2)}) collective-permute-start(bf16[256,1024]{1,0:T(8,128)(2,1)} %get-tuple-element.375.refs_0_), channel_id=1, source_target_pairs={{0,2},{1,3},{2,0},{3,1},{4,6},{5,7},{6,4},{7,5},{8,10},{9,11},{10,... | collective-permute-start | bytes 1572872 | tf_op jit(solution)/shard_map/ppermute | solution.py:818
  469.1 30.8 %collective-permute-start.77 = (bf16[2,256,1024]{2,1,0:T(8,128)(2,1)}, bf16[2,256,1024]{2,1,0:T(8,128)(2,1)S(1)}, u32[]{:S(2)}, u32[]{:S(2)}) collective-permute-start(bf16[2,256,1024]{2,1,0:T(8,128)(2,1)} %get-tuple-element.393), channel_id=1, source_target_pairs={{4,8},{8,4},{5,9},{9,5},{6,10},{10,6},{7,11},{11,7},{20,24},{24,20... | collective-permute-start | bytes 3145736 | tf_op jit(solution)/shard_map/ppermute | solution.py:624
  475.9 50.9 %collective-permute-start.69 = (bf16[256,512]{1,0:T(8,128)(2,1)S(1)}, bf16[256,512]{1,0:T(8,128)(2,1)S(1)}, u32[]{:S(2)}, u32[]{:S(2)}) collective-permute-start(bf16[256,512]{1,0:T(8,128)(2,1)S(1)} %sum_chunks.1.refs_8_.refs_0_), channel_id=1, source_target_pairs={{0,4},{4,8},{8,12},{12,0},{1,5},{5,9},{9,13},{13,1},{2,6},{6,10},{... | collective-permute-start | bytes 786440 | tf_op jit(solution)/shard_map/ppermute | solution.py:691
  476.0 52.5 %collective-permute-start.70 = (bf16[256,512]{1,0:T(8,128)(2,1)S(1)}, bf16[256,512]{1,0:T(8,128)(2,1)S(1)}, u32[]{:S(2)}, u32[]{:S(2)}) collective-permute-start(bf16[256,512]{1,0:T(8,128)(2,1)S(1)} %sum_chunks.1.refs_8_.refs_0_), channel_id=1, source_target_pairs={{0,8},{4,12},{8,0},{12,4},{1,9},{5,13},{9,1},{13,5},{2,10},{6,14},... | collective-permute-start | bytes 786440 | tf_op jit(solution)/shard_map/ppermute | solution.py:691
  501.2 91.2 %collective-permute-start.79 = (bf16[2,256,1024]{2,1,0:T(8,128)(2,1)}, bf16[2,256,1024]{2,1,0:T(8,128)(2,1)S(1)}, u32[]{:S(2)}, u32[]{:S(2)}) collective-permute-start(bf16[2,256,1024]{2,1,0:T(8,128)(2,1)} %sum_line.9.refs_14_.refs_1_), channel_id=1, source_target_pairs={{4,8},{8,4},{5,9},{9,5},{6,10},{10,6},{7,11},{11,7},{20,24},{24,20... | collective-permute-start | bytes 3145736 | tf_op jit(solution)/shard_map/ppermute | solution.py:634
  501.9 93.6 %collective-permute-start.80 = (bf16[2,256,1024]{2,1,0:T(8,128)(2,1)}, bf16[2,256,1024]{2,1,0:T(8,128)(2,1)}, u32[]{:S(2)}, u32[]{:S(2)}) collective-permute-start(bf16[2,256,1024]{2,1,0:T(8,128)(2,1)} %sum_line.9.refs_14_.refs_1_), channel_id=1, source_target_pairs={{4,0},{8,12},{5,1},{9,13},{6,2},{10,14},{7,3},{11,15},{20,16},{24,... | collective-permute-start | bytes 3145736 | tf_op jit(solution)/shard_map/ppermute | solution.py:635
  526.7 68.7 %collective-permute-start.78 = (bf16[512,1024]{1,0:T(8,128)(2,1)}, bf16[512,1024]{1,0:T(8,128)(2,1)}, u32[]{:S(2)}, u32[]{:S(2)}) collective-permute-start(bf16[512,1024]{1,0:T(8,128)(2,1)} %get-tuple-element.400), channel_id=1, source_target_pairs={{0,1},{1,0},{2,3},{3,2},{4,5},{5,4},{6,7},{7,6},{8,9},{9,8},{10,11... | collective-permute-start | bytes 3145736 | tf_op jit(solution)/shard_map/ppermute | solution.py:818
  526.7 71.5 %collective-permute-start.82 = (bf16[2,256,1024]{2,1,0:T(8,128)(2,1)}, bf16[2,256,1024]{2,1,0:T(8,128)(2,1)}, u32[]{:S(2)}, u32[]{:S(2)}) collective-permute-start(bf16[2,256,1024]{2,1,0:T(8,128)(2,1)} %get-tuple-element.406), channel_id=1, source_target_pairs={{4,8},{8,4},{5,9},{9,5},{6,10},{10,6},{7,11},{11,7},{20,24},{24,20... | collective-permute-start | bytes 3145736 | tf_op jit(solution)/shard_map/ppermute | solution.py:624
  540.9 13.7 %collective-permute-start.68 = (bf16[256,1024]{1,0:T(8,128)(2,1)}, bf16[256,1024]{1,0:T(8,128)(2,1)S(1)}, u32[]{:S(2)}, u32[]{:S(2)}) collective-permute-start(bf16[256,1024]{1,0:T(8,128)(2,1)} %get-tuple-element.373), channel_id=1, source_target_pairs={{0,2},{1,3},{2,0},{3,1},{4,6},{5,7},{6,4},{7,5},{8,10},{9,11},{10,... | collective-permute-start | bytes 1572872 | tf_op jit(solution)/shard_map/ppermute | solution.py:818
  555.3 61.6 %collective-permute-start.84 = (bf16[4,256,512]{2,1,0:T(8,128)(2,1)}, bf16[4,256,512]{2,1,0:T(8,128)(2,1)}, u32[]{:S(2)}, u32[]{:S(2)}) collective-permute-start(bf16[4,256,512]{2,1,0:T(8,128)(2,1)} %weight_grad.6.refs_14_.refs_0_), channel_id=1, source_target_pairs={{0,4},{12,8},{1,5},{13,9},{2,6},{14,10},{3,7},{15,11},{16,20},{28,... | collective-permute-start | bytes 3145736 | tf_op jit(solution)/shard_map/ppermute | solution.py:609
  593.2 35.2 %collective-permute-start.89 = (bf16[4,256,512]{2,1,0:T(8,128)(2,1)}, bf16[4,256,512]{2,1,0:T(8,128)(2,1)}, u32[]{:S(2)}, u32[]{:S(2)}) collective-permute-start(bf16[4,256,512]{2,1,0:T(8,128)(2,1)} %weight_grad.7.refs_2_.refs_0_), channel_id=1, source_target_pairs={{0,4},{12,8},{1,5},{13,9},{2,6},{14,10},{3,7},{15,11},{16,20},{28,... | collective-permute-start | bytes 3145736 | tf_op jit(solution)/shard_map/ppermute | solution.py:609
  599.9 31.0 %collective-permute-start.87 = (bf16[2,256,1024]{2,1,0:T(8,128)(2,1)S(1)}, bf16[2,256,1024]{2,1,0:T(8,128)(2,1)S(1)}, u32[]{:S(2)}, u32[]{:S(2)}) collective-permute-start(bf16[2,256,1024]{2,1,0:T(8,128)(2,1)S(1)} %sum_line.11.refs_5_.refs_1_), channel_id=1, source_target_pairs={{4,8},{8,4},{5,9},{9,5},{6,10},{10,6},{7,11},{11,7},{20,24},{24,20... | collective-permute-start | bytes 3145736 | tf_op jit(solution)/shard_map/ppermute | solution.py:634
  600.7 30.3 %collective-permute-start.88 = (bf16[2,256,1024]{2,1,0:T(8,128)(2,1)S(1)}, bf16[2,256,1024]{2,1,0:T(8,128)(2,1)S(1)}, u32[]{:S(2)}, u32[]{:S(2)}) collective-permute-start(bf16[2,256,1024]{2,1,0:T(8,128)(2,1)S(1)} %sum_line.11.refs_5_.refs_1_), channel_id=1, source_target_pairs={{4,0},{8,12},{5,1},{9,13},{6,2},{10,14},{7,3},{11,15},{20,16},{24,... | collective-permute-start | bytes 3145736 | tf_op jit(solution)/shard_map/ppermute | solution.py:635
  613.7 37.5 %collective-permute-start.86 = (bf16[2,256,1024]{2,1,0:T(8,128)(2,1)S(1)}, bf16[2,256,1024]{2,1,0:T(8,128)(2,1)}, u32[]{:S(2)}, u32[]{:S(2)}) collective-permute-start(bf16[2,256,1024]{2,1,0:T(8,128)(2,1)S(1)} %copy-done.5), channel_id=1, source_target_pairs={{4,0},{8,12},{5,1},{9,13},{6,2},{10,14},{7,3},{11,15},{20,16},{24,... | collective-permute-start | bytes 3145736 | tf_op jit(solution)/shard_map/ppermute | solution.py:638
  632.7 41.0 %collective-permute-start.92 = (bf16[2,256,1024]{2,1,0:T(8,128)(2,1)}, bf16[2,256,1024]{2,1,0:T(8,128)(2,1)}, u32[]{:S(2)}, u32[]{:S(2)}) collective-permute-start(bf16[2,256,1024]{2,1,0:T(8,128)(2,1)} %get-tuple-element.413.refs_5_.refs_2_), channel_id=1, source_target_pairs={{4,0},{8,12},{5,1},{9,13},{6,2},{10,14},{7,3},{11,15},{20,16},{24,... | collective-permute-start | bytes 3145736 | tf_op jit(solution)/shard_map/ppermute | solution.py:638
  634.0 23.3 %collective-permute-start.85 = (bf16[2,256,512]{2,1,0:T(8,128)(2,1)}, bf16[2,256,512]{2,1,0:T(8,128)(2,1)S(1)}, u32[]{:S(2)}, u32[]{:S(2)}) collective-permute-start(bf16[2,256,512]{2,1,0:T(8,128)(2,1)} %copy-done.222), channel_id=1, source_target_pairs={{4,8},{8,4},{5,9},{9,5},{6,10},{10,6},{7,11},{11,7},{20,24},{24,20... | collective-permute-start | bytes 1572872 | tf_op jit(solution)/shard_map/ppermute | solution.py:624
  634.9 28.9 %collective-permute-start.93 = (bf16[2,256,512]{2,1,0:T(8,128)(2,1)}, bf16[2,256,512]{2,1,0:T(8,128)(2,1)S(1)}, u32[]{:S(2)}, u32[]{:S(2)}) collective-permute-start(bf16[2,256,512]{2,1,0:T(8,128)(2,1)} %copy-done.221), channel_id=1, source_target_pairs={{4,8},{8,4},{5,9},{9,5},{6,10},{10,6},{7,11},{11,7},{20,24},{24,20... | collective-permute-start | bytes 1572872 | tf_op jit(solution)/shard_map/ppermute | solution.py:624
  635.6 29.0 %collective-permute-start.65 = (bf16[128,1024]{1,0:T(8,128)(2,1)S(1)}, bf16[128,1024]{1,0:T(8,128)(2,1)}, u32[]{:S(2)}, u32[]{:S(2)}) collective-permute-start(bf16[128,1024]{1,0:T(8,128)(2,1)S(1)} %copy-done.41), channel_id=1, source_target_pairs={{0,2},{1,3},{2,0},{3,1},{4,6},{5,7},{6,4},{7,5},{8,10},{9,11},{10,... | collective-permute-start | bytes 786440 | tf_op jit(solution)/shard_map/ppermute | solution.py:818
  661.5 18.5 %collective-permute-start.90 = (bf16[2,256,512]{2,1,0:T(8,128)(2,1)S(1)}, bf16[2,256,512]{2,1,0:T(8,128)(2,1)S(1)}, u32[]{:S(2)}, u32[]{:S(2)}) collective-permute-start(bf16[2,256,512]{2,1,0:T(8,128)(2,1)S(1)} %sum_line.14.refs_2_), channel_id=1, source_target_pairs={{4,8},{8,4},{5,9},{9,5},{6,10},{10,6},{7,11},{11,7},{20,24},{24,20... | collective-permute-start | bytes 1572872 | tf_op jit(solution)/shard_map/ppermute | solution.py:634
  662.3 22.6 %collective-permute-start.91 = (bf16[2,256,512]{2,1,0:T(8,128)(2,1)S(1)}, bf16[2,256,512]{2,1,0:T(8,128)(2,1)}, u32[]{:S(2)}, u32[]{:S(2)}) collective-permute-start(bf16[2,256,512]{2,1,0:T(8,128)(2,1)S(1)} %sum_line.14.refs_2_), channel_id=1, source_target_pairs={{4,0},{8,12},{5,1},{9,13},{6,2},{10,14},{7,3},{11,15},{20,16},{24,... | collective-permute-start | bytes 1572872 | tf_op jit(solution)/shard_map/ppermute | solution.py:635
  663.9 21.0 %collective-permute-start.95 = (bf16[2,256,512]{2,1,0:T(8,128)(2,1)S(1)}, bf16[2,256,512]{2,1,0:T(8,128)(2,1)S(1)}, u32[]{:S(2)}, u32[]{:S(2)}) collective-permute-start(bf16[2,256,512]{2,1,0:T(8,128)(2,1)S(1)} %sum_line.15.refs_5_.refs_6_), channel_id=1, source_target_pairs={{4,8},{8,4},{5,9},{9,5},{6,10},{10,6},{7,11},{11,7},{20,24},{24,20... | collective-permute-start | bytes 1572872 | tf_op jit(solution)/shard_map/ppermute | solution.py:634
  664.6 28.4 %collective-permute-start.96 = (bf16[2,256,512]{2,1,0:T(8,128)(2,1)S(1)}, bf16[2,256,512]{2,1,0:T(8,128)(2,1)}, u32[]{:S(2)}, u32[]{:S(2)}) collective-permute-start(bf16[2,256,512]{2,1,0:T(8,128)(2,1)S(1)} %sum_line.15.refs_5_.refs_6_), channel_id=1, source_target_pairs={{4,0},{8,12},{5,1},{9,13},{6,2},{10,14},{7,3},{11,15},{20,16},{24,... | collective-permute-start | bytes 1572872 | tf_op jit(solution)/shard_map/ppermute | solution.py:635
  673.7 19.3 %collective-permute-start.98 = (f32[1,256]{1,0:T(1,128)S(1)}, f32[1,256]{1,0:T(1,128)S(1)}, u32[]{:S(2)}, u32[]{:S(2)}) collective-permute-start(f32[1,256]{1,0:T(1,128)S(1)} %copy-done.227), channel_id=1, source_target_pairs={{16,0},{17,1},{18,2},{19,3},{20,4},{21,5},{22,6},{23,7},{24,8},{25... | collective-permute-start | bytes 3080 | tf_op jit(solution)/shard_map/ppermute | solution.py:859
  680.0 19.6 %collective-permute-start.66 = (bf16[2,2,16,1024]{3,2,1,0:T(8,128)(2,1)}, bf16[2,2,16,1024]{3,2,1,0:T(8,128)(2,1)}, u32[]{:S(2)}, u32[]{:S(2)}) collective-permute-start(bf16[2,2,16,1024]{3,2,1,0:T(8,128)(2,1)} %slice_bitcast_fusion.7), channel_id=1, source_target_pairs={{16,0},{17,1},{18,2},{19,3},{20,4},{21,5},{22,6},{23,7},{24,8},{25... | collective-permute-start | bytes 393224 | tf_op jit(solution)/shard_map/ppermute | solution.py:1324
  700.7 16.8 %collective-permute-start.94 = (bf16[2,256,512]{2,1,0:T(8,128)(2,1)S(1)}, bf16[2,256,512]{2,1,0:T(8,128)(2,1)S(1)}, u32[]{:S(2)}, u32[]{:S(2)}) collective-permute-start(bf16[2,256,512]{2,1,0:T(8,128)(2,1)S(1)} %copy-done.15), channel_id=1, source_target_pairs={{4,0},{8,12},{5,1},{9,13},{6,2},{10,14},{7,3},{11,15},{20,16},{24,... | collective-permute-start | bytes 1572872 | tf_op jit(solution)/shard_map/ppermute | solution.py:638
  702.0 22.6 %collective-permute-start.97 = (bf16[2,256,512]{2,1,0:T(8,128)(2,1)S(1)}, bf16[2,256,512]{2,1,0:T(8,128)(2,1)S(1)}, u32[]{:S(2)}, u32[]{:S(2)}) collective-permute-start(bf16[2,256,512]{2,1,0:T(8,128)(2,1)S(1)} %copy-done.18), channel_id=1, source_target_pairs={{4,0},{8,12},{5,1},{9,13},{6,2},{10,14},{7,3},{11,15},{20,16},{24,... | collective-permute-start | bytes 1572872 | tf_op jit(solution)/shard_map/ppermute | solution.py:638
  (284 other events, 2390.5 us)

commit v4 on v3

--- a/solution.py
+++ b/solution.py
@@ -139,12 +139,12 @@
     ("vo", "made"),
     ("in", "one"),
     ("b1", "back"),
-    ("d", "third end"),
     ("b0", "norm zero"),
     ("out", "three"),
     ("b1", "reduce one"),
     ("in", "two"),
     ("b1", "norm zero"),
+    ("d", "third end"),
     ("qk", "one"),
     ("vo", "one"),
     ("in", "three"),

time: 743 us -> 720 us (0.969)
  waiting for transfers between devices: 259 us -> 249 us
  starting transfers between devices: 125 us -> 116 us
    ppermute x4, starting transfers between devices: 40.6 us -> 23 us  [sum_line(): sent = lax.ppermute(rows, 'dp', inward)]
    ppermute x6, waiting for transfers between devices: 11.4 us -> 0.02 us  [send_chunks(): lax.ppermute(chunk, 'dp', [(i, (i + s + 1) % CHUNKS) for i in range(CHUNK...]
    unnamed x493 -> x489, local copies, waits for them, and re-layouts: 63.5 us -> 65 us
  transfers between devices with their start and end apart: 104 -> 104, of which waited for: 45 -> 44; matrix products, arithmetic and copies ran while one was open for 3% -> 3% of each run, Pallas kernels for 28% -> 28%
where the time goes in v4:
time: 720 us; the launch traced here: 709 us
  Pallas kernels  250 us (35%)
  waiting for transfers between devices  249 us (35%)
  starting transfers between devices  116 us (16%)
  local copies, waits for them, and re-layouts  79.4 us (11%)
  other arithmetic  9.7 us (1%)
    pallas_call x78, Pallas kernels, call(): pl.pallas_call(ordered, grid_spec=grid_spec, out_shape=out_shape, compile...  250 us
    ppermute x65, waiting for transfers between devices, flip(): return lax.ppermute(value, axis, [(i, i ^ 1 << bit) for i in range(count)])  171 us
    unnamed x489, local copies, waits for them, and re-layouts  65 us
    ppermute x65, starting transfers between devices, flip(): return lax.ppermute(value, axis, [(i, i ^ 1 << bit) for i in range(count)])  41.4 us
    ppermute x4, waiting for transfers between devices, sum_line(): second = lax.ppermute(crossed, 'dp', outward)  27.7 us
    ppermute x4, starting transfers between devices, sum_line(): sent = lax.ppermute(rows, 'dp', inward)  23 us
    ppermute x5, waiting for transfers between devices, to_first(): return lax.ppermute(value, 'section', [(1, 0)])  15.1 us
  transfers between devices with their start and end apart: 104, of which 44 were waited for; matrix products, arithmetic and copies ran while one was open for 3% of the time, Pallas kernels for 28%

profile of v4, /device:TPU:0, one launch (start us, length us, event | category | flops | bytes accessed | tf_op | source)
XLA Modules:
  0.0 708.5 jit_solution(17037343063094383370)
XLA Ops:
  1.4 2.8 slice_bitcast_fusion
  7.1 5.7 collective-permute-start
  19.2 6.4 encoder_qkv.2
  27.3 10.2 %attention_kernel.2 = (bf16[1024,256]{1,0:T(8,128)(2,1)S(1)}, f32[1024,256]{1,0:T(8,128)S(1)}, f32[8,1024]{1,0:T(8,128)S(1)}, bf16[512,1024]{1,0:T(8,128)(2,1)S(1)}, bf16[512,1024]{1,0:T(8,128)(2,1)}) custom-call(bf16[1024,256]{1,0:T(8,128)(2,1)S(1)} %get-tuple-element.223.refs_0_.refs_5_.refs_6_, bf16[1024,256]{1,0:T(8,128)(2,1)S(1)} %get-tuple-element.224.refs_1_.refs_7_, ...), custom_call_target="tpu_custom_call" | custom-call | flops 2147483648 | bytes 4194304 | tf_op jit(solution)/shard_map/attention_kernel/pallas_call | solution.py:182
  48.3 6.4 encoder_qkv.3
  60.2 10.3 %attention_kernel.3 = (bf16[1024,256]{1,0:T(8,128)(2,1)S(1)}, f32[1024,256]{1,0:T(8,128)S(1)}, f32[8,1024]{1,0:T(8,128)S(1)}, bf16[512,1024]{1,0:T(8,128)(2,1)S(1)}, bf16[512,1024]{1,0:T(8,128)(2,1)}) custom-call(bf16[1024,256]{1,0:T(8,128)(2,1)S(1)} %get-tuple-element.228.refs_2_.refs_0_.refs_6_, bf16[1024,256]{1,0:T(8,128)(2,1)S(1)} %get-tuple-element.229.refs_1_.refs_7_, ...), custom_call_target="tpu_custom_call" | custom-call | flops 2147483648 | bytes 4194304 | tf_op jit(solution)/shard_map/attention_kernel/pallas_call | solution.py:182
  79.0 11.5 %collective-permute-done.9.refs_1_ = bf16[256,1024]{1,0:T(8,128)(2,1)} collective-permute-done((bf16[256,1024]{1,0:T(8,128)(2,1)}, bf16[256,1024]{1,0:T(8,128)(2,1)}, u32[]{:S(2)}, u32[]{:S(2)}) %collective-permute-start.9) | collective-permute-done | bytes 524320 | tf_op jit(solution)/shard_map/ppermute | solution.py:818
  100.8 10.7 %ffn_forward.3 = (bf16[1024,1024]{1,0:T(8,128)(2,1)}, bf16[1024,1024]{1,0:T(8,128)(2,1)}, bf16[1024,1024]{1,0:T(8,128)(2,1)}, bf16[512,1024]{1,0:T(8,128)(2,1)S(1)}, bf16[512,1024]{1,0:T(8,128)(2,1)S(1)}) custom-call(bf16[256,1024]{1,0:T(8,128)(2,1)} %get-tuple-element.246.refs_0_, bf16[256,1024]{1,0:T(8,128)(2,1)} %collective-permute-done.9.refs_1_, ...), custom_call_target="tpu_custom_call" | custom-call | flops 4294967296 | bytes 12582912 | tf_op jit(solution)/shard_map/ffn_forward/pallas_call | solution.py:182
  115.1 11.8 %collective-permute-done.15.refs_1_ = bf16[256,1024]{1,0:T(8,128)(2,1)S(1)} collective-permute-done((bf16[256,1024]{1,0:T(8,128)(2,1)S(1)}, bf16[256,1024]{1,0:T(8,128)(2,1)S(1)}, u32[]{:S(2)}, u32[]{:S(2)}) %collective-permute-start.15) | collective-permute-done | bytes 524320 | tf_op jit(solution)/shard_map/ppermute | solution.py:818
  128.3 7.4 %collective-permute-done.7.refs_2_ = bf16[128,1024]{1,0:T(8,128)(2,1)S(1)} collective-permute-done((bf16[128,1024]{1,0:T(8,128)(2,1)S(1)}, bf16[128,1024]{1,0:T(8,128)(2,1)S(1)}, u32[]{:S(2)}, u32[]{:S(2)}) %collective-permute-start.7) | collective-permute-done | bytes 262176 | tf_op jit(solution)/shard_map/ppermute | solution.py:818
  136.3 10.1 %ffn_forward.4 = (bf16[1024,1024]{1,0:T(8,128)(2,1)}, bf16[1024,1024]{1,0:T(8,128)(2,1)}, bf16[1024,1024]{1,0:T(8,128)(2,1)}, bf16[512,1024]{1,0:T(8,128)(2,1)S(1)}, bf16[512,1024]{1,0:T(8,128)(2,1)S(1)}) custom-call(bf16[256,1024]{1,0:T(8,128)(2,1)S(1)} %get-tuple-element.256.refs_0_, bf16[256,1024]{1,0:T(8,128)(2,1)S(1)} %collective-permute-done.15.refs_1_, ...), custom_call_target="tpu_custom_call" | custom-call | flops 4294967296 | bytes 12582912 | tf_op jit(solution)/shard_map/ffn_forward/pallas_call | solution.py:182
  147.7 13.0 %collective-permute-done.14.refs_2_ = bf16[256,1024]{1,0:T(8,128)(2,1)S(1)} collective-permute-done((bf16[256,1024]{1,0:T(8,128)(2,1)S(1)}, bf16[256,1024]{1,0:T(8,128)(2,1)S(1)}, u32[]{:S(2)}, u32[]{:S(2)}) %collective-permute-start.14) | collective-permute-done | bytes 524320 | tf_op jit(solution)/shard_map/ppermute | solution.py:818
  165.2 10.9 %collective-permute-done.23.refs_2_ = bf16[256,1024]{1,0:T(8,128)(2,1)S(1)} collective-permute-done((bf16[256,1024]{1,0:T(8,128)(2,1)S(1)}, bf16[256,1024]{1,0:T(8,128)(2,1)S(1)}, u32[]{:S(2)}, u32[]{:S(2)}) %collective-permute-start.23) | collective-permute-done | bytes 524320 | tf_op jit(solution)/shard_map/ppermute | solution.py:818
  180.2 9.0 %collective-permute-done.24.refs_0_ = bf16[256,1024]{1,0:T(8,128)(2,1)S(1)} collective-permute-done((bf16[256,1024]{1,0:T(8,128)(2,1)S(1)}, bf16[256,1024]{1,0:T(8,128)(2,1)S(1)}, u32[]{:S(2)}, u32[]{:S(2)}) %collective-permute-start.24) | collective-permute-done | bytes 524320 | tf_op jit(solution)/shard_map/ppermute | solution.py:855
  193.7 9.2 %collective-permute-done.25.refs_1_ = bf16[256,1024]{1,0:T(8,128)(2,1)S(1)} collective-permute-done((bf16[256,1024]{1,0:T(8,128)(2,1)S(1)}, bf16[256,1024]{1,0:T(8,128)(2,1)S(1)}, u32[]{:S(2)}, u32[]{:S(2)}) %collective-permute-start.25) | collective-permute-done | bytes 524320 | tf_op jit(solution)/shard_map/ppermute | solution.py:818
  203.4 3.9 project_parts.2
  207.3 4.3 project_parts.3
  211.6 3.6 decoder_cross.1
  218.3 7.1 %collective-permute-done.29.refs_2_ = bf16[128,1024]{1,0:T(8,128)(2,1)S(1)} collective-permute-done((bf16[128,1024]{1,0:T(8,128)(2,1)S(1)}, bf16[128,1024]{1,0:T(8,128)(2,1)S(1)}, u32[]{:S(2)}, u32[]{:S(2)}) %collective-permute-start.29) | collective-permute-done | bytes 262176 | tf_op jit(solution)/shard_map/ppermute | solution.py:818
  227.3 4.1 ffn_forward.5
  234.5 7.1 collective-permute-done.32.refs_2_
  244.8 4.5 ffn_backward.3
  253.1 7.1 %collective-permute-done.35.refs_2_ = bf16[128,1024]{1,0:T(8,128)(2,1)S(1)} collective-permute-done((bf16[128,1024]{1,0:T(8,128)(2,1)S(1)}, bf16[128,1024]{1,0:T(8,128)(2,1)S(1)}, u32[]{:S(2)}, u32[]{:S(2)}) %collective-permute-start.35) | collective-permute-done | bytes 262176 | tf_op jit(solution)/shard_map/ppermute | solution.py:818
  262.3 5.4 decoder_cross_back.1
  269.1 3.3 back_sum.4
  272.7 3.3 back_sum.5
  280.3 3.8 weight_sum.4.refs_4_.refs_0_
  284.1 3.0 weight_sum.5.refs_2_.refs_1_
  287.9 3.7 collective-permute-done.40.refs_1_
  293.0 9.0 %collective-permute-done.39.refs_1_ = bf16[256,1024]{1,0:T(8,128)(2,1)S(1)} collective-permute-done((bf16[256,1024]{1,0:T(8,128)(2,1)S(1)}, bf16[256,1024]{1,0:T(8,128)(2,1)S(1)}, u32[]{:S(2)}, u32[]{:S(2)}) %collective-permute-start.39) | collective-permute-done | bytes 524320 | tf_op jit(solution)/shard_map/ppermute | solution.py:818
  302.1 3.8 collective-permute-done.42.refs_0_
  309.6 8.7 %collective-permute-done.44.refs_1_.refs_3_ = bf16[256,1024]{1,0:T(8,128)(2,1)} collective-permute-done((bf16[256,1024]{1,0:T(8,128)(2,1)S(1)}, bf16[256,1024]{1,0:T(8,128)(2,1)}, u32[]{:S(2)}, u32[]{:S(2)}) %collective-permute-start.44) | collective-permute-done | bytes 524320 | tf_op jit(solution)/shard_map/ppermute | solution.py:818
  325.3 10.8 %ffn_backward.4 = (bf16[1024,1024]{1,0:T(8,128)(2,1)}, bf16[1024,1024]{1,0:T(8,128)(2,1)}, bf16[512,1024]{1,0:T(8,128)(2,1)S(1)}, bf16[512,1024]{1,0:T(8,128)(2,1)}, f32[1,1024]{1,0:T(1,128)S(1)}) custom-call(bf16[256,1024]{1,0:T(8,128)(2,1)S(1)} %copy-done.215, bf16[256,1024]{1,0:T(8,128)(2,1)} %collective-permute-done.44.refs_1_.refs_3_, ...), custom_call_target="tpu_custom_call" | custom-call | flops 4294967296 | bytes 10485760 | tf_op jit(solution)/shard_map/ffn_backward/pallas_call | solution.py:182
  341.7 10.0 %collective-permute-done.48.refs_1_.refs_8_ = bf16[256,1024]{1,0:T(8,128)(2,1)} collective-permute-done((bf16[256,1024]{1,0:T(8,128)(2,1)}, bf16[256,1024]{1,0:T(8,128)(2,1)}, u32[]{:S(2)}, u32[]{:S(2)}) %collective-permute-start.48) | collective-permute-done | bytes 524320 | tf_op jit(solution)/shard_map/ppermute | solution.py:818
  357.1 8.6 %collective-permute-done.52.refs_3_ = bf16[1024,256]{1,0:T(8,128)(2,1)} collective-permute-done((bf16[1024,256]{1,0:T(8,128)(2,1)S(1)}, bf16[1024,256]{1,0:T(8,128)(2,1)}, u32[]{:S(2)}, u32[]{:S(2)}) %collective-permute-start.52) | collective-permute-done | bytes 524320 | tf_op jit(solution)/shard_map/ppermute | solution.py:859
  370.1 11.1 %ffn_backward.5 = (bf16[1024,1024]{1,0:T(8,128)(2,1)}, bf16[1024,1024]{1,0:T(8,128)(2,1)}, bf16[512,1024]{1,0:T(8,128)(2,1)S(1)}, bf16[512,1024]{1,0:T(8,128)(2,1)}, f32[1,1024]{1,0:T(1,128)S(1)}) custom-call(bf16[256,1024]{1,0:T(8,128)(2,1)} %get-tuple-element.326.refs_0_.refs_7_, bf16[256,1024]{1,0:T(8,128)(2,1)} %collective-permute-done.48.refs_1_.refs_8_, ...), custom_call_target="tpu_custom_call" | custom-call | flops 4294967296 | bytes 10485760 | tf_op jit(solution)/shard_map/ffn_backward/pallas_call | solution.py:182
  391.8 6.7 collective-permute-done.61.refs_1_
  400.8 9.8 %weight_grad.4.refs_4_.refs_0_ = bf16[4,256,1024]{2,1,0:T(8,128)(2,1)} custom-call(s32[1]{0:T(128)} %bitcast.31.refs_0_, s32[4]{0:T(128)S(1)} %and_select_fusion.2.refs_1_, bf16[256,1024]{1,0:T(8,128)(2,1)S(1)} %copy-done.216, bf16[256,1024]{1,0:T(8,128)(2,1)} %collective-permute-done.44.refs_1_.refs_3_, ...), custom_call_target="tpu_custom_call" | custom-call | flops 4831838208 | bytes 9437184 | tf_op jit(solution)/shard_map/weight_grad/pallas_call | solution.py:182
  412.7 5.2 collective-permute-start.72
  421.4 9.3 %weight_grad.5.refs_5_.refs_0_ = bf16[4,256,1024]{2,1,0:T(8,128)(2,1)} custom-call(s32[1]{0:T(128)} %bitcast.31.refs_0_, s32[4]{0:T(128)S(1)} %and_select_fusion.2.refs_1_, bf16[1024,1024]{1,0:T(8,128)(2,1)S(1)} %copy-done.226, bf16[1024,1024]{1,0:T(8,128)(2,1)} %get-tuple-element.324.refs_3_, bf16[1024,1024]{1,0:T(8,128)(2,1)} %get-tuple-element.325.refs_4_, ...), custom_call_target="tpu_custom_call" | custom-call | flops 4831838208 | bytes 9437184 | tf_op jit(solution)/shard_map/weight_grad/pallas_call | solution.py:182
  433.3 16.5 %encoder_attention_back.2 = (bf16[1024,1024]{1,0:T(8,128)(2,1)}, bf16[1024,256]{1,0:T(8,128)(2,1)S(1)}, bf16[1024,256]{1,0:T(8,128)(2,1)S(1)}, bf16[1024,256]{1,...) custom-call(bf16[256,1024]{1,0:T(8,128)(2,1)} %get-tuple-element.358.refs_0_, ...), custom_call_target="tpu_custom_call" | custom-call | flops 5368709120 | bytes 6291456 | tf_op jit(solution)/shard_map/encoder_attention_back/pallas_call | solution.py:182
  465.6 2.8 sum_line.8
  470.6 4.4 collective-permute-done.69.refs_1_
  481.4 16.6 %encoder_attention_back.3 = (bf16[1024,1024]{1,0:T(8,128)(2,1)}, bf16[1024,256]{1,0:T(8,128)(2,1)S(1)}, bf16[1024,256]{1,0:T(8,128)(2,1)S(1)}, bf16[1024,256]{1,...) custom-call(bf16[256,1024]{1,0:T(8,128)(2,1)} %get-tuple-element.375.refs_0_, ...), custom_call_target="tpu_custom_call" | custom-call | flops 5368709120 | bytes 6291456 | tf_op jit(solution)/shard_map/encoder_attention_back/pallas_call | solution.py:182
  500.6 7.2 %weight_grad.6.refs_14_.refs_0_ = bf16[4,256,512]{2,1,0:T(8,128)(2,1)} custom-call(s32[1]{0:T(128)} %bitcast.31.refs_0_, s32[4]{0:T(128)S(1)} %copy-done.185, bf16[1024,1024]{1,0:T(8,128)(2,1)} %get-tuple-element.381.refs_2_.refs_4_, bf16[1024,256]{1,0:T(8,128)(2,1)S(1)} %copy-done.93, bf16[1024,1024]{1,0:T(8,128)(2,1)} %get-tuple-element.381.refs_2_.refs_4_, ...), custom_call_target="tpu_custom_call" | custom-call | flops 2415919104 | bytes 7077888 | tf_op jit(solution)/shard_map/weight_grad/pallas_call | solution.py:182
  507.9 7.1 weight_grad.7.refs_2_.refs_0_
  515.0 3.4 sum_line.10
  519.4 3.6 back_sum.7
  526.0 13.0 %collective-permute-done.68.refs_2_ = bf16[256,1024]{1,0:T(8,128)(2,1)S(1)} collective-permute-done((bf16[256,1024]{1,0:T(8,128)(2,1)S(1)}, bf16[256,1024]{1,0:T(8,128)(2,1)S(1)}, u32[]{:S(2)}, u32[]{:S(2)}) %collective-permute-start.68) | collective-permute-done | bytes 524320 | tf_op jit(solution)/shard_map/ppermute | solution.py:818
  539.0 4.3 collective-permute-start.82
  544.3 2.8 collective-permute-start.84
  555.3 12.7 %collective-permute-start.89 = (bf16[4,256,512]{2,1,0:T(8,128)(2,1)}, bf16[4,256,512]{2,1,0:T(8,128)(2,1)}, u32[]{:S(2)}, u32[]{:S(2)}) collective-permute-start(bf16[4,256,512]{2,1,0:T(8,128)(2,1)} %weight_grad.7.refs_2_.refs_0_), channel_id=1, source_target_pairs={{0,4},{12,8},{1,5},{13,9},{2,6},{14,10},{3,7},{15,11},{16,20},{28,... | collective-permute-start | bytes 3145736 | tf_op jit(solution)/shard_map/ppermute | solution.py:609
  574.1 11.7 %collective-permute-done.78.refs_2_ = bf16[256,1024]{1,0:T(8,128)(2,1)S(1)} collective-permute-done((bf16[256,1024]{1,0:T(8,128)(2,1)S(1)}, bf16[256,1024]{1,0:T(8,128)(2,1)S(1)}, u32[]{:S(2)}, u32[]{:S(2)}) %collective-permute-start.78) | collective-permute-done | bytes 524320 | tf_op jit(solution)/shard_map/ppermute | solution.py:818
  594.1 10.8 %collective-permute-done.89.refs_1_ = bf16[4,256,512]{2,1,0:T(8,128)(2,1)} collective-permute-done((bf16[4,256,512]{2,1,0:T(8,128)(2,1)}, bf16[4,256,512]{2,1,0:T(8,128)(2,1)}, u32[]{:S(2)}, u32[]{:S(2)}) %collective-permute-start.89) | collective-permute-done | bytes 1048608 | tf_op jit(solution)/shard_map/ppermute | solution.py:609
  612.7 10.5 %collective-permute-done.86.refs_4_ = bf16[2,256,1024]{2,1,0:T(8,128)(2,1)} collective-permute-done((bf16[2,256,1024]{2,1,0:T(8,128)(2,1)S(1)}, bf16[2,256,1024]{2,1,0:T(8,128)(2,1)}, u32[]{:S(2)}, u32[]{:S(2)}) %collective-permute-start.86) | collective-permute-done | bytes 1048608 | tf_op jit(solution)/shard_map/ppermute | solution.py:638
  626.9 4.2 unite_one.2.refs_2_
  640.7 5.0 collective-permute-done.92.refs_4_
  647.6 4.5 unite_one.3.refs_2_
  653.7 3.1 collective-permute-done.91.refs_1_
  656.9 9.8 %collective-permute-done.96.refs_1_ = bf16[2,256,512]{2,1,0:T(8,128)(2,1)} collective-permute-done((bf16[2,256,512]{2,1,0:T(8,128)(2,1)S(1)}, bf16[2,256,512]{2,1,0:T(8,128)(2,1)}, u32[]{:S(2)}, u32[]{:S(2)}) %collective-permute-start.96) | collective-permute-done | bytes 524320 | tf_op jit(solution)/shard_map/ppermute | solution.py:635
  672.4 5.0 collective-permute-start.100
  690.9 4.2 collective-permute-done.94.refs_5_
  695.1 8.1 %collective-permute-done.97.refs_9_ = bf16[2,256,512]{2,1,0:T(8,128)(2,1)S(1)} collective-permute-done((bf16[2,256,512]{2,1,0:T(8,128)(2,1)S(1)}, bf16[2,256,512]{2,1,0:T(8,128)(2,1)S(1)}, u32[]{:S(2)}, u32[]{:S(2)}) %collective-permute-start.97) | collective-permute-done | bytes 524320 | tf_op jit(solution)/shard_map/ppermute | solution.py:638
  703.2 5.1 unite.1
  (772 shorter events, 235.6 us)
Async XLA Ops:
  7.1 40.7 %collective-permute-start = (bf16[1024,256]{1,0:T(8,128)(2,1)}, bf16[1024,256]{1,0:T(8,128)(2,1)}, u32[]{:S(2)}, u32[]{:S(2)}) collective-permute-start(bf16[1024,256]{1,0:T(8,128)(2,1)} %get-tuple-element.220.refs_9_), channel_id=1, source_target_pairs={{0,16},{1,17},{2,18},{3,19},{4,20},{5,21},{6,22},{7,23},{8,24},{9,... | collective-permute-start | bytes 1572872 | tf_op jit(solution)/shard_map/ppermute | solution.py:855
  12.7 35.0 %collective-permute-start.1 = (bf16[1024,256]{1,0:T(8,128)(2,1)}, bf16[1024,256]{1,0:T(8,128)(2,1)}, u32[]{:S(2)}, u32[]{:S(2)}) collective-permute-start(bf16[1024,256]{1,0:T(8,128)(2,1)} %get-tuple-element.221), channel_id=1, source_target_pairs={{0,16},{1,17},{2,18},{3,19},{4,20},{5,21},{6,22},{7,23},{8,24},{9,... | collective-permute-start | bytes 1572872 | tf_op jit(solution)/shard_map/ppermute | solution.py:855
  14.8 32.9 %collective-permute-start.2 = (f32[1,256]{1,0:T(1,128)}, f32[1,256]{1,0:T(1,128)S(1)}, u32[]{:S(2)}, u32[]{:S(2)}) collective-permute-start(f32[1,256]{1,0:T(1,128)} %get-tuple-element.222), channel_id=1, source_target_pairs={{0,16},{1,17},{2,18},{3,19},{4,20},{5,21},{6,22},{7,23},{8,24},{9,... | collective-permute-start | bytes 3080 | tf_op jit(solution)/shard_map/ppermute | solution.py:855
  40.9 15.6 %collective-permute-start.3 = (bf16[512,1024]{1,0:T(8,128)(2,1)}, bf16[512,1024]{1,0:T(8,128)(2,1)}, u32[]{:S(2)}, u32[]{:S(2)}) collective-permute-start(bf16[512,1024]{1,0:T(8,128)(2,1)} %get-tuple-element.232), channel_id=1, source_target_pairs={{0,1},{1,0},{2,3},{3,2},{4,5},{5,4},{6,7},{7,6},{8,9},{9,8},{10,11... | collective-permute-start | bytes 3145736 | tf_op jit(solution)/shard_map/ppermute | solution.py:818
  58.6 14.4 %collective-permute-start.5 = (bf16[256,1024]{1,0:T(8,128)(2,1)S(1)}, bf16[256,1024]{1,0:T(8,128)(2,1)S(1)}, u32[]{:S(2)}, u32[]{:S(2)}) collective-permute-start(bf16[256,1024]{1,0:T(8,128)(2,1)S(1)} %get-tuple-element.237), channel_id=1, source_target_pairs={{0,2},{1,3},{2,0},{3,1},{4,6},{5,7},{6,4},{7,5},{8,10},{9,11},{10,... | collective-permute-start | bytes 1572872 | tf_op jit(solution)/shard_map/ppermute | solution.py:818
  72.3 18.2 %collective-permute-start.4 = (bf16[512,1024]{1,0:T(8,128)(2,1)}, bf16[512,1024]{1,0:T(8,128)(2,1)}, u32[]{:S(2)}, u32[]{:S(2)}) collective-permute-start(bf16[512,1024]{1,0:T(8,128)(2,1)} %get-tuple-element.235), channel_id=1, source_target_pairs={{0,1},{1,0},{2,3},{3,2},{4,5},{5,4},{6,7},{7,6},{8,9},{9,8},{10,11... | collective-permute-start | bytes 3145736 | tf_op jit(solution)/shard_map/ppermute | solution.py:818
  76.3 14.2 %collective-permute-start.9 = (bf16[256,1024]{1,0:T(8,128)(2,1)}, bf16[256,1024]{1,0:T(8,128)(2,1)}, u32[]{:S(2)}, u32[]{:S(2)}) collective-permute-start(bf16[256,1024]{1,0:T(8,128)(2,1)} %get-tuple-element.246.refs_0_), channel_id=1, source_target_pairs={{0,2},{1,3},{2,0},{3,1},{4,6},{5,7},{6,4},{7,5},{8,10},{9,11},{10,... | collective-permute-start | bytes 1572872 | tf_op jit(solution)/shard_map/ppermute | solution.py:818
  78.9 21.8 %collective-permute-start.10 = (bf16[256,1024]{1,0:T(8,128)(2,1)}, bf16[256,1024]{1,0:T(8,128)(2,1)S(1)}, u32[]{:S(2)}, u32[]{:S(2)}) collective-permute-start(bf16[256,1024]{1,0:T(8,128)(2,1)} %get-tuple-element.246.refs_0_), channel_id=1, source_target_pairs={{0,1},{1,0},{2,3},{3,2},{4,5},{5,4},{6,7},{7,6},{8,9},{9,8},{10,11... | collective-permute-start | bytes 1572872 | tf_op jit(solution)/shard_map/ppermute | solution.py:818
  111.5 24.5 %collective-permute-start.13 = (bf16[512,1024]{1,0:T(8,128)(2,1)S(1)}, bf16[512,1024]{1,0:T(8,128)(2,1)S(1)}, u32[]{:S(2)}, u32[]{:S(2)}) collective-permute-start(bf16[512,1024]{1,0:T(8,128)(2,1)S(1)} %get-tuple-element.252), channel_id=1, source_target_pairs={{0,1},{1,0},{2,3},{3,2},{4,5},{5,4},{6,7},{7,6},{8,9},{9,8},{10,11... | collective-permute-start | bytes 3145736 | tf_op jit(solution)/shard_map/ppermute | solution.py:818
  115.1 21.2 %collective-permute-start.16 = (bf16[256,1024]{1,0:T(8,128)(2,1)S(1)}, bf16[256,1024]{1,0:T(8,128)(2,1)S(1)}, u32[]{:S(2)}, u32[]{:S(2)}) collective-permute-start(bf16[256,1024]{1,0:T(8,128)(2,1)S(1)} %get-tuple-element.256.refs_0_), channel_id=1, source_target_pairs={{0,1},{1,0},{2,3},{3,2},{4,5},{5,4},{6,7},{7,6},{8,9},{9,8},{10,11... | collective-permute-start | bytes 1572872 | tf_op jit(solution)/shard_map/ppermute | solution.py:818
  146.5 15.9 %collective-permute-start.22 = (bf16[512,1024]{1,0:T(8,128)(2,1)S(1)}, bf16[512,1024]{1,0:T(8,128)(2,1)S(1)}, u32[]{:S(2)}, u32[]{:S(2)}) collective-permute-start(bf16[512,1024]{1,0:T(8,128)(2,1)S(1)} %get-tuple-element.262), channel_id=1, source_target_pairs={{0,1},{1,0},{2,3},{3,2},{4,5},{5,4},{6,7},{7,6},{8,9},{9,8},{10,11... | collective-permute-start | bytes 3145736 | tf_op jit(solution)/shard_map/ppermute | solution.py:818
  146.5 14.3 %collective-permute-start.14 = (bf16[256,1024]{1,0:T(8,128)(2,1)S(1)}, bf16[256,1024]{1,0:T(8,128)(2,1)S(1)}, u32[]{:S(2)}, u32[]{:S(2)}) collective-permute-start(bf16[256,1024]{1,0:T(8,128)(2,1)S(1)} %get-tuple-element.255), channel_id=1, source_target_pairs={{0,2},{1,3},{2,0},{3,1},{4,6},{5,7},{6,4},{7,5},{8,10},{9,11},{10,... | collective-permute-start | bytes 1572872 | tf_op jit(solution)/shard_map/ppermute | solution.py:818
  163.9 15.1 %collective-permute-start.18 = (bf16[256,1024]{1,0:T(8,128)(2,1)S(1)}, bf16[256,1024]{1,0:T(8,128)(2,1)S(1)}, u32[]{:S(2)}, u32[]{:S(2)}) collective-permute-start(bf16[256,1024]{1,0:T(8,128)(2,1)S(1)} %get-tuple-element.258), channel_id=1, source_target_pairs={{0,16},{1,17},{2,18},{3,19},{4,20},{5,21},{6,22},{7,23},{8,24},{9,... | collective-permute-start | bytes 1572872 | tf_op jit(solution)/shard_map/ppermute | solution.py:855
  179.0 14.2 %collective-permute-start.19 = (bf16[256,1024]{1,0:T(8,128)(2,1)S(1)}, bf16[256,1024]{1,0:T(8,128)(2,1)S(1)}, u32[]{:S(2)}, u32[]{:S(2)}) collective-permute-start(bf16[256,1024]{1,0:T(8,128)(2,1)S(1)} %collective-permute-done.18.refs_0_), channel_id=1, source_target_pairs={{0,2},{1,3},{2,0},{3,1},{4,6},{5,7},{6,4},{7,5},{8,10},{9,11},{10,... | collective-permute-start | bytes 1572872 | tf_op jit(solution)/shard_map/ppermute | solution.py:818
  193.2 14.2 %collective-permute-start.26 = (bf16[256,1024]{1,0:T(8,128)(2,1)S(1)}, bf16[256,1024]{1,0:T(8,128)(2,1)S(1)}, u32[]{:S(2)}, u32[]{:S(2)}) collective-permute-start(bf16[256,1024]{1,0:T(8,128)(2,1)S(1)} %collective-permute-done.24.refs_0_), channel_id=1, source_target_pairs={{0,1},{1,0},{2,3},{3,2},{4,5},{5,4},{6,7},{7,6},{8,9},{9,8},{10,11... | collective-permute-start | bytes 1572872 | tf_op jit(solution)/shard_map/ppermute | solution.py:818
  276.7 14.8 %collective-permute-start.40 = (bf16[256,1024]{1,0:T(8,128)(2,1)S(1)}, bf16[256,1024]{1,0:T(8,128)(2,1)S(1)}, u32[]{:S(2)}, u32[]{:S(2)}) collective-permute-start(bf16[256,1024]{1,0:T(8,128)(2,1)S(1)} %get-tuple-element.308), channel_id=1, source_target_pairs={{0,2},{1,3},{2,0},{3,1},{4,6},{5,7},{6,4},{7,5},{8,10},{9,11},{10,... | collective-permute-start | bytes 1572872 | tf_op jit(solution)/shard_map/ppermute | solution.py:818
  279.0 23.0 %collective-permute-start.39 = (bf16[256,1024]{1,0:T(8,128)(2,1)S(1)}, bf16[256,1024]{1,0:T(8,128)(2,1)S(1)}, u32[]{:S(2)}, u32[]{:S(2)}) collective-permute-start(bf16[256,1024]{1,0:T(8,128)(2,1)S(1)} %get-tuple-element.307), channel_id=1, source_target_pairs={{0,2},{1,3},{2,0},{3,1},{4,6},{5,7},{6,4},{7,5},{8,10},{9,11},{10,... | collective-permute-start | bytes 1572872 | tf_op jit(solution)/shard_map/ppermute | solution.py:818
  291.7 14.2 %collective-permute-start.42 = (bf16[256,1024]{1,0:T(8,128)(2,1)S(1)}, bf16[256,1024]{1,0:T(8,128)(2,1)S(1)}, u32[]{:S(2)}, u32[]{:S(2)}) collective-permute-start(bf16[256,1024]{1,0:T(8,128)(2,1)S(1)} %add_rows.12.refs_2_), channel_id=1, source_target_pairs={{16,0},{17,1},{18,2},{19,3},{20,4},{21,5},{22,6},{23,7},{24,8},{25... | collective-permute-start | bytes 1572872 | tf_op jit(solution)/shard_map/ppermute | solution.py:859
  309.5 14.7 %collective-permute-start.45 = (bf16[256,1024]{1,0:T(8,128)(2,1)S(1)}, bf16[256,1024]{1,0:T(8,128)(2,1)}, u32[]{:S(2)}, u32[]{:S(2)}) collective-permute-start(bf16[256,1024]{1,0:T(8,128)(2,1)S(1)} %get-tuple-element.319.refs_0_.refs_2_), channel_id=1, source_target_pairs={{0,1},{1,0},{2,3},{3,2},{4,5},{5,4},{6,7},{7,6},{8,9},{9,8},{10,11... | collective-permute-start | bytes 1572872 | tf_op jit(solution)/shard_map/ppermute | solution.py:818
  337.1 16.4 %collective-permute-start.53 = (bf16[512,1024]{1,0:T(8,128)(2,1)}, bf16[512,1024]{1,0:T(8,128)(2,1)}, u32[]{:S(2)}, u32[]{:S(2)}) collective-permute-start(bf16[512,1024]{1,0:T(8,128)(2,1)} %get-tuple-element.330), channel_id=1, source_target_pairs={{0,1},{1,0},{2,3},{3,2},{4,5},{5,4},{6,7},{7,6},{8,9},{9,8},{10,11... | collective-permute-start | bytes 3145736 | tf_op jit(solution)/shard_map/ppermute | solution.py:818
  337.1 14.7 %collective-permute-start.48 = (bf16[256,1024]{1,0:T(8,128)(2,1)}, bf16[256,1024]{1,0:T(8,128)(2,1)}, u32[]{:S(2)}, u32[]{:S(2)}) collective-permute-start(bf16[256,1024]{1,0:T(8,128)(2,1)} %get-tuple-element.326.refs_0_.refs_7_), channel_id=1, source_target_pairs={{0,2},{1,3},{2,0},{3,1},{4,6},{5,7},{6,4},{7,5},{8,10},{9,11},{10,... | collective-permute-start | bytes 1572872 | tf_op jit(solution)/shard_map/ppermute | solution.py:818
  338.1 19.0 %collective-permute-start.51 = (bf16[1024,256]{1,0:T(8,128)(2,1)}, bf16[1024,256]{1,0:T(8,128)(2,1)}, u32[]{:S(2)}, u32[]{:S(2)}) collective-permute-start(bf16[1024,256]{1,0:T(8,128)(2,1)} %get-tuple-element.321.refs_7_), channel_id=1, source_target_pairs={{16,0},{17,1},{18,2},{19,3},{20,4},{21,5},{22,6},{23,7},{24,8},{25... | collective-permute-start | bytes 1572872 | tf_op jit(solution)/shard_map/ppermute | solution.py:859
  339.4 26.2 %collective-permute-start.52 = (bf16[1024,256]{1,0:T(8,128)(2,1)S(1)}, bf16[1024,256]{1,0:T(8,128)(2,1)}, u32[]{:S(2)}, u32[]{:S(2)}) collective-permute-start(bf16[1024,256]{1,0:T(8,128)(2,1)S(1)} %copy-done.22), channel_id=1, source_target_pairs={{16,0},{17,1},{18,2},{19,3},{20,4},{21,5},{22,6},{23,7},{24,8},{25... | collective-permute-start | bytes 1572872 | tf_op jit(solution)/shard_map/ppermute | solution.py:859
  341.5 28.6 %collective-permute-start.49 = (bf16[256,1024]{1,0:T(8,128)(2,1)}, bf16[256,1024]{1,0:T(8,128)(2,1)}, u32[]{:S(2)}, u32[]{:S(2)}) collective-permute-start(bf16[256,1024]{1,0:T(8,128)(2,1)} %get-tuple-element.326.refs_0_.refs_7_), channel_id=1, source_target_pairs={{0,1},{1,0},{2,3},{3,2},{4,5},{5,4},{6,7},{7,6},{8,9},{9,8},{10,11... | collective-permute-start | bytes 1572872 | tf_op jit(solution)/shard_map/ppermute | solution.py:818
  351.8 18.3 %collective-permute-start.50 = (bf16[256,1024]{1,0:T(8,128)(2,1)}, bf16[256,1024]{1,0:T(8,128)(2,1)}, u32[]{:S(2)}, u32[]{:S(2)}) collective-permute-start(bf16[256,1024]{1,0:T(8,128)(2,1)} %collective-permute-done.48.refs_1_.refs_8_), channel_id=1, source_target_pairs={{0,1},{1,0},{2,3},{3,2},{4,5},{5,4},{6,7},{7,6},{8,9},{9,8},{10,11... | collective-permute-start | bytes 1572872 | tf_op jit(solution)/shard_map/ppermute | solution.py:818
  356.2 25.0 %collective-permute-start.58 = (bf16[256,1024]{1,0:T(8,128)(2,1)S(1)}, bf16[256,1024]{1,0:T(8,128)(2,1)S(1)}, u32[]{:S(2)}, u32[]{:S(2)}) collective-permute-start(bf16[256,1024]{1,0:T(8,128)(2,1)S(1)} %get-tuple-element.346), channel_id=1, source_target_pairs={{0,2},{1,3},{2,0},{3,1},{4,6},{5,7},{6,4},{7,5},{8,10},{9,11},{10,... | collective-permute-start | bytes 1572872 | tf_op jit(solution)/shard_map/ppermute | solution.py:818
  383.9 14.6 %collective-permute-start.61 = (bf16[256,1024]{1,0:T(8,128)(2,1)}, bf16[256,1024]{1,0:T(8,128)(2,1)}, u32[]{:S(2)}, u32[]{:S(2)}) collective-permute-start(bf16[256,1024]{1,0:T(8,128)(2,1)} %get-tuple-element.358.refs_0_), channel_id=1, source_target_pairs={{0,2},{1,3},{2,0},{3,1},{4,6},{5,7},{6,4},{7,5},{8,10},{9,11},{10,... | collective-permute-start | bytes 1572872 | tf_op jit(solution)/shard_map/ppermute | solution.py:818
  386.2 24.3 %collective-permute-start.54 = (bf16[256,512]{1,0:T(8,128)(2,1)}, bf16[256,512]{1,0:T(8,128)(2,1)S(1)}, u32[]{:S(2)}, u32[]{:S(2)}) collective-permute-start(bf16[256,512]{1,0:T(8,128)(2,1)} %copy-done.223), channel_id=1, source_target_pairs={{0,4},{4,8},{8,12},{12,0},{1,5},{5,9},{9,13},{13,1},{2,6},{6,10},{... | collective-permute-start | bytes 786440 | tf_op jit(solution)/shard_map/ppermute | solution.py:691
  387.9 24.0 %collective-permute-start.55 = (bf16[256,512]{1,0:T(8,128)(2,1)}, bf16[256,512]{1,0:T(8,128)(2,1)S(1)}, u32[]{:S(2)}, u32[]{:S(2)}) collective-permute-start(bf16[256,512]{1,0:T(8,128)(2,1)} %copy-done.222), channel_id=1, source_target_pairs={{0,8},{4,12},{8,0},{12,4},{1,9},{5,13},{9,1},{13,5},{2,10},{6,14},... | collective-permute-start | bytes 786440 | tf_op jit(solution)/shard_map/ppermute | solution.py:691
  390.5 22.2 %collective-permute-start.56 = (bf16[256,512]{1,0:T(8,128)(2,1)}, bf16[256,512]{1,0:T(8,128)(2,1)S(1)}, u32[]{:S(2)}, u32[]{:S(2)}) collective-permute-start(bf16[256,512]{1,0:T(8,128)(2,1)} %copy-done.221), channel_id=1, source_target_pairs={{0,12},{4,0},{8,4},{12,8},{1,13},{5,1},{9,5},{13,9},{2,14},{6,2},{... | collective-permute-start | bytes 786440 | tf_op jit(solution)/shard_map/ppermute | solution.py:691
  391.8 41.4 %collective-permute-start.62 = (bf16[256,1024]{1,0:T(8,128)(2,1)}, bf16[256,1024]{1,0:T(8,128)(2,1)S(1)}, u32[]{:S(2)}, u32[]{:S(2)}) collective-permute-start(bf16[256,1024]{1,0:T(8,128)(2,1)} %get-tuple-element.358.refs_0_), channel_id=1, source_target_pairs={{0,1},{1,0},{2,3},{3,2},{4,5},{5,4},{6,7},{7,6},{8,9},{9,8},{10,11... | collective-permute-start | bytes 1572872 | tf_op jit(solution)/shard_map/ppermute | solution.py:818
  398.5 34.7 %collective-permute-start.63 = (bf16[256,1024]{1,0:T(8,128)(2,1)}, bf16[256,1024]{1,0:T(8,128)(2,1)S(1)}, u32[]{:S(2)}, u32[]{:S(2)}) collective-permute-start(bf16[256,1024]{1,0:T(8,128)(2,1)} %collective-permute-done.61.refs_1_), channel_id=1, source_target_pairs={{0,1},{1,0},{2,3},{3,2},{4,5},{5,4},{6,7},{7,6},{8,9},{9,8},{10,11... | collective-permute-start | bytes 1572872 | tf_op jit(solution)/shard_map/ppermute | solution.py:818
  410.6 20.2 %collective-permute-start.47 = (bf16[128,1024]{1,0:T(8,128)(2,1)}, bf16[128,1024]{1,0:T(8,128)(2,1)S(1)}, u32[]{:S(2)}, u32[]{:S(2)}) collective-permute-start(bf16[128,1024]{1,0:T(8,128)(2,1)} %add_rows.14.refs_2_.refs_1_), channel_id=1, source_target_pairs={{0,2},{1,3},{2,0},{3,1},{4,6},{5,7},{6,4},{7,5},{8,10},{9,11},{10,... | collective-permute-start | bytes 786440 | tf_op jit(solution)/shard_map/ppermute | solution.py:818
  411.9 38.6 %collective-permute-start.60 = (bf16[256,1024]{1,0:T(8,128)(2,1)}, bf16[256,1024]{1,0:T(8,128)(2,1)S(1)}, u32[]{:S(2)}, u32[]{:S(2)}) collective-permute-start(bf16[256,1024]{1,0:T(8,128)(2,1)} %get-tuple-element.357), channel_id=1, source_target_pairs={{0,2},{1,3},{2,0},{3,1},{4,6},{5,7},{6,4},{7,5},{8,10},{9,11},{10,... | collective-permute-start | bytes 1572872 | tf_op jit(solution)/shard_map/ppermute | solution.py:818
  412.7 51.2 %collective-permute-start.72 = (bf16[4,256,1024]{2,1,0:T(8,128)(2,1)}, bf16[4,256,1024]{2,1,0:T(8,128)(2,1)}, u32[]{:S(2)}, u32[]{:S(2)}) collective-permute-start(bf16[4,256,1024]{2,1,0:T(8,128)(2,1)} %weight_grad.4.refs_4_.refs_0_), channel_id=1, source_target_pairs={{0,4},{12,8},{1,5},{13,9},{2,6},{14,10},{3,7},{15,11},{16,20},{28,... | collective-permute-start | bytes 6291464 | tf_op jit(solution)/shard_map/ppermute | solution.py:609
  433.2 19.0 %collective-permute-start.59 = (bf16[128,1024]{1,0:T(8,128)(2,1)S(1)}, bf16[128,1024]{1,0:T(8,128)(2,1)S(1)}, u32[]{:S(2)}, u32[]{:S(2)}) collective-permute-start(bf16[128,1024]{1,0:T(8,128)(2,1)S(1)} %get-tuple-element.351.refs_0_), channel_id=1, source_target_pairs={{0,1},{1,0},{2,3},{3,2},{4,5},{5,4},{6,7},{7,6},{8,9},{9,8},{10,11... | collective-permute-start | bytes 786440 | tf_op jit(solution)/shard_map/ppermute | solution.py:818
  458.1 56.9 %collective-permute-start.73 = (bf16[4,256,1024]{2,1,0:T(8,128)(2,1)}, bf16[4,256,1024]{2,1,0:T(8,128)(2,1)}, u32[]{:S(2)}, u32[]{:S(2)}) collective-permute-start(bf16[4,256,1024]{2,1,0:T(8,128)(2,1)} %weight_grad.5.refs_5_.refs_0_), channel_id=1, source_target_pairs={{0,4},{12,8},{1,5},{13,9},{2,6},{14,10},{3,7},{15,11},{16,20},{28,... | collective-permute-start | bytes 6291464 | tf_op jit(solution)/shard_map/ppermute | solution.py:609
  460.8 14.2 %collective-permute-start.69 = (bf16[256,1024]{1,0:T(8,128)(2,1)}, bf16[256,1024]{1,0:T(8,128)(2,1)}, u32[]{:S(2)}, u32[]{:S(2)}) collective-permute-start(bf16[256,1024]{1,0:T(8,128)(2,1)} %get-tuple-element.375.refs_0_), channel_id=1, source_target_pairs={{0,2},{1,3},{2,0},{3,1},{4,6},{5,7},{6,4},{7,5},{8,10},{9,11},{10,... | collective-permute-start | bytes 1572872 | tf_op jit(solution)/shard_map/ppermute | solution.py:818
  469.5 28.6 %collective-permute-start.74 = (bf16[2,256,1024]{2,1,0:T(8,128)(2,1)}, bf16[2,256,1024]{2,1,0:T(8,128)(2,1)S(1)}, u32[]{:S(2)}, u32[]{:S(2)}) collective-permute-start(bf16[2,256,1024]{2,1,0:T(8,128)(2,1)} %get-tuple-element.393), channel_id=1, source_target_pairs={{4,8},{8,4},{5,9},{9,5},{6,10},{10,6},{7,11},{11,7},{20,24},{24,20... | collective-permute-start | bytes 3145736 | tf_op jit(solution)/shard_map/ppermute | solution.py:624
  498.3 44.9 %collective-permute-start.76 = (bf16[2,256,1024]{2,1,0:T(8,128)(2,1)S(1)}, bf16[2,256,1024]{2,1,0:T(8,128)(2,1)S(1)}, u32[]{:S(2)}, u32[]{:S(2)}) collective-permute-start(bf16[2,256,1024]{2,1,0:T(8,128)(2,1)S(1)} %sum_line.9.refs_14_.refs_1_), channel_id=1, source_target_pairs={{4,8},{8,4},{5,9},{9,5},{6,10},{10,6},{7,11},{11,7},{20,24},{24,20... | collective-permute-start | bytes 3145736 | tf_op jit(solution)/shard_map/ppermute | solution.py:634
  499.2 44.1 %collective-permute-start.77 = (bf16[2,256,1024]{2,1,0:T(8,128)(2,1)S(1)}, bf16[2,256,1024]{2,1,0:T(8,128)(2,1)S(1)}, u32[]{:S(2)}, u32[]{:S(2)}) collective-permute-start(bf16[2,256,1024]{2,1,0:T(8,128)(2,1)S(1)} %sum_line.9.refs_14_.refs_1_), channel_id=1, source_target_pairs={{4,0},{8,12},{5,1},{9,13},{6,2},{10,14},{7,3},{11,15},{20,16},{24,... | collective-permute-start | bytes 3145736 | tf_op jit(solution)/shard_map/ppermute | solution.py:635
  523.0 28.4 %collective-permute-start.75 = (bf16[512,1024]{1,0:T(8,128)(2,1)}, bf16[512,1024]{1,0:T(8,128)(2,1)S(1)}, u32[]{:S(2)}, u32[]{:S(2)}) collective-permute-start(bf16[512,1024]{1,0:T(8,128)(2,1)} %get-tuple-element.399), channel_id=1, source_target_pairs={{0,1},{1,0},{2,3},{3,2},{4,5},{5,4},{6,7},{7,6},{8,9},{9,8},{10,11... | collective-permute-start | bytes 3145736 | tf_op jit(solution)/shard_map/ppermute | solution.py:818
  523.1 32.2 %collective-permute-start.79 = (bf16[2,256,1024]{2,1,0:T(8,128)(2,1)}, bf16[2,256,1024]{2,1,0:T(8,128)(2,1)}, u32[]{:S(2)}, u32[]{:S(2)}) collective-permute-start(bf16[2,256,1024]{2,1,0:T(8,128)(2,1)} %get-tuple-element.405), channel_id=1, source_target_pairs={{4,8},{8,4},{5,9},{9,5},{6,10},{10,6},{7,11},{11,7},{20,24},{24,20... | collective-permute-start | bytes 3145736 | tf_op jit(solution)/shard_map/ppermute | solution.py:624
  524.8 14.2 %collective-permute-start.68 = (bf16[256,1024]{1,0:T(8,128)(2,1)S(1)}, bf16[256,1024]{1,0:T(8,128)(2,1)S(1)}, u32[]{:S(2)}, u32[]{:S(2)}) collective-permute-start(bf16[256,1024]{1,0:T(8,128)(2,1)S(1)} %copy-done.218), channel_id=1, source_target_pairs={{0,2},{1,3},{2,0},{3,1},{4,6},{5,7},{6,4},{7,5},{8,10},{9,11},{10,... | collective-permute-start | bytes 1572872 | tf_op jit(solution)/shard_map/ppermute | solution.py:818
  539.0 31.7 %collective-permute-start.82 = (bf16[256,512]{1,0:T(8,128)(2,1)S(1)}, bf16[256,512]{1,0:T(8,128)(2,1)}, u32[]{:S(2)}, u32[]{:S(2)}) collective-permute-start(bf16[256,512]{1,0:T(8,128)(2,1)S(1)} %sum_chunks.1.refs_8_.refs_0_), channel_id=1, source_target_pairs={{0,4},{4,8},{8,12},{12,0},{1,5},{5,9},{9,13},{13,1},{2,6},{6,10},{... | collective-permute-start | bytes 786440 | tf_op jit(solution)/shard_map/ppermute | solution.py:691
  543.3 28.2 %collective-permute-start.83 = (bf16[256,512]{1,0:T(8,128)(2,1)S(1)}, bf16[256,512]{1,0:T(8,128)(2,1)}, u32[]{:S(2)}, u32[]{:S(2)}) collective-permute-start(bf16[256,512]{1,0:T(8,128)(2,1)S(1)} %sum_chunks.1.refs_8_.refs_0_), channel_id=1, source_target_pairs={{0,8},{4,12},{8,0},{12,4},{1,9},{5,13},{9,1},{13,5},{2,10},{6,14},... | collective-permute-start | bytes 786440 | tf_op jit(solution)/shard_map/ppermute | solution.py:691
  544.3 28.4 %collective-permute-start.84 = (bf16[256,512]{1,0:T(8,128)(2,1)S(1)}, bf16[256,512]{1,0:T(8,128)(2,1)}, u32[]{:S(2)}, u32[]{:S(2)}) collective-permute-start(bf16[256,512]{1,0:T(8,128)(2,1)S(1)} %sum_chunks.1.refs_8_.refs_0_), channel_id=1, source_target_pairs={{0,12},{4,0},{8,4},{12,8},{1,13},{5,1},{9,5},{13,9},{2,14},{6,2},{... | collective-permute-start | bytes 786440 | tf_op jit(solution)/shard_map/ppermute | solution.py:691
  551.4 39.2 %collective-permute-start.81 = (bf16[4,256,512]{2,1,0:T(8,128)(2,1)}, bf16[4,256,512]{2,1,0:T(8,128)(2,1)}, u32[]{:S(2)}, u32[]{:S(2)}) collective-permute-start(bf16[4,256,512]{2,1,0:T(8,128)(2,1)} %weight_grad.6.refs_14_.refs_0_), channel_id=1, source_target_pairs={{0,4},{12,8},{1,5},{13,9},{2,6},{14,10},{3,7},{15,11},{16,20},{28,... | collective-permute-start | bytes 3145736 | tf_op jit(solution)/shard_map/ppermute | solution.py:609
  555.3 49.6 %collective-permute-start.89 = (bf16[4,256,512]{2,1,0:T(8,128)(2,1)}, bf16[4,256,512]{2,1,0:T(8,128)(2,1)}, u32[]{:S(2)}, u32[]{:S(2)}) collective-permute-start(bf16[4,256,512]{2,1,0:T(8,128)(2,1)} %weight_grad.7.refs_2_.refs_0_), channel_id=1, source_target_pairs={{0,4},{12,8},{1,5},{13,9},{2,6},{14,10},{3,7},{15,11},{16,20},{28,... | collective-permute-start | bytes 3145736 | tf_op jit(solution)/shard_map/ppermute | solution.py:609
  570.7 36.8 %collective-permute-start.87 = (bf16[2,256,1024]{2,1,0:T(8,128)(2,1)S(1)}, bf16[2,256,1024]{2,1,0:T(8,128)(2,1)S(1)}, u32[]{:S(2)}, u32[]{:S(2)}) collective-permute-start(bf16[2,256,1024]{2,1,0:T(8,128)(2,1)S(1)} %sum_line.11.refs_5_.refs_1_), channel_id=1, source_target_pairs={{4,8},{8,4},{5,9},{9,5},{6,10},{10,6},{7,11},{11,7},{20,24},{24,20... | collective-permute-start | bytes 3145736 | tf_op jit(solution)/shard_map/ppermute | solution.py:634
  571.4 36.0 %collective-permute-start.88 = (bf16[2,256,1024]{2,1,0:T(8,128)(2,1)S(1)}, bf16[2,256,1024]{2,1,0:T(8,128)(2,1)}, u32[]{:S(2)}, u32[]{:S(2)}) collective-permute-start(bf16[2,256,1024]{2,1,0:T(8,128)(2,1)S(1)} %sum_line.11.refs_5_.refs_1_), channel_id=1, source_target_pairs={{4,0},{8,12},{5,1},{9,13},{6,2},{10,14},{7,3},{11,15},{20,16},{24,... | collective-permute-start | bytes 3145736 | tf_op jit(solution)/shard_map/ppermute | solution.py:635
  585.7 37.5 %collective-permute-start.86 = (bf16[2,256,1024]{2,1,0:T(8,128)(2,1)S(1)}, bf16[2,256,1024]{2,1,0:T(8,128)(2,1)}, u32[]{:S(2)}, u32[]{:S(2)}) collective-permute-start(bf16[2,256,1024]{2,1,0:T(8,128)(2,1)S(1)} %copy-done.5), channel_id=1, source_target_pairs={{4,0},{8,12},{5,1},{9,13},{6,2},{10,14},{7,3},{11,15},{20,16},{24,... | collective-permute-start | bytes 3145736 | tf_op jit(solution)/shard_map/ppermute | solution.py:638
  608.6 37.0 %collective-permute-start.92 = (bf16[2,256,1024]{2,1,0:T(8,128)(2,1)}, bf16[2,256,1024]{2,1,0:T(8,128)(2,1)}, u32[]{:S(2)}, u32[]{:S(2)}) collective-permute-start(bf16[2,256,1024]{2,1,0:T(8,128)(2,1)} %get-tuple-element.413.refs_5_.refs_2_), channel_id=1, source_target_pairs={{4,0},{8,12},{5,1},{9,13},{6,2},{10,14},{7,3},{11,15},{20,16},{24,... | collective-permute-start | bytes 3145736 | tf_op jit(solution)/shard_map/ppermute | solution.py:638
  609.9 21.2 %collective-permute-start.85 = (bf16[2,256,512]{2,1,0:T(8,128)(2,1)}, bf16[2,256,512]{2,1,0:T(8,128)(2,1)S(1)}, u32[]{:S(2)}, u32[]{:S(2)}) collective-permute-start(bf16[2,256,512]{2,1,0:T(8,128)(2,1)} %copy-done.220), channel_id=1, source_target_pairs={{4,8},{8,4},{5,9},{9,5},{6,10},{10,6},{7,11},{11,7},{20,24},{24,20... | collective-permute-start | bytes 1572872 | tf_op jit(solution)/shard_map/ppermute | solution.py:624
  610.6 26.8 %collective-permute-start.93 = (bf16[2,256,512]{2,1,0:T(8,128)(2,1)}, bf16[2,256,512]{2,1,0:T(8,128)(2,1)S(1)}, u32[]{:S(2)}, u32[]{:S(2)}) collective-permute-start(bf16[2,256,512]{2,1,0:T(8,128)(2,1)} %copy-done.219), channel_id=1, source_target_pairs={{4,8},{8,4},{5,9},{9,5},{6,10},{10,6},{7,11},{11,7},{20,24},{24,20... | collective-permute-start | bytes 1572872 | tf_op jit(solution)/shard_map/ppermute | solution.py:624
  611.3 27.0 %collective-permute-start.65 = (bf16[128,1024]{1,0:T(8,128)(2,1)S(1)}, bf16[128,1024]{1,0:T(8,128)(2,1)}, u32[]{:S(2)}, u32[]{:S(2)}) collective-permute-start(bf16[128,1024]{1,0:T(8,128)(2,1)S(1)} %copy-done.43), channel_id=1, source_target_pairs={{0,2},{1,3},{2,0},{3,1},{4,6},{5,7},{6,4},{7,5},{8,10},{9,11},{10,... | collective-permute-start | bytes 786440 | tf_op jit(solution)/shard_map/ppermute | solution.py:818
  635.3 17.0 %collective-permute-start.90 = (bf16[2,256,512]{2,1,0:T(8,128)(2,1)S(1)}, bf16[2,256,512]{2,1,0:T(8,128)(2,1)S(1)}, u32[]{:S(2)}, u32[]{:S(2)}) collective-permute-start(bf16[2,256,512]{2,1,0:T(8,128)(2,1)S(1)} %sum_line.14.refs_2_), channel_id=1, source_target_pairs={{4,8},{8,4},{5,9},{9,5},{6,10},{10,6},{7,11},{11,7},{20,24},{24,20... | collective-permute-start | bytes 1572872 | tf_op jit(solution)/shard_map/ppermute | solution.py:634
  636.1 20.8 %collective-permute-start.91 = (bf16[2,256,512]{2,1,0:T(8,128)(2,1)S(1)}, bf16[2,256,512]{2,1,0:T(8,128)(2,1)}, u32[]{:S(2)}, u32[]{:S(2)}) collective-permute-start(bf16[2,256,512]{2,1,0:T(8,128)(2,1)S(1)} %sum_line.14.refs_2_), channel_id=1, source_target_pairs={{4,0},{8,12},{5,1},{9,13},{6,2},{10,14},{7,3},{11,15},{20,16},{24,... | collective-permute-start | bytes 1572872 | tf_op jit(solution)/shard_map/ppermute | solution.py:635
  637.5 19.3 %collective-permute-start.95 = (bf16[2,256,512]{2,1,0:T(8,128)(2,1)S(1)}, bf16[2,256,512]{2,1,0:T(8,128)(2,1)S(1)}, u32[]{:S(2)}, u32[]{:S(2)}) collective-permute-start(bf16[2,256,512]{2,1,0:T(8,128)(2,1)S(1)} %sum_line.15.refs_5_.refs_6_), channel_id=1, source_target_pairs={{4,8},{8,4},{5,9},{9,5},{6,10},{10,6},{7,11},{11,7},{20,24},{24,20... | collective-permute-start | bytes 1572872 | tf_op jit(solution)/shard_map/ppermute | solution.py:634
  638.3 28.5 %collective-permute-start.96 = (bf16[2,256,512]{2,1,0:T(8,128)(2,1)S(1)}, bf16[2,256,512]{2,1,0:T(8,128)(2,1)}, u32[]{:S(2)}, u32[]{:S(2)}) collective-permute-start(bf16[2,256,512]{2,1,0:T(8,128)(2,1)S(1)} %sum_line.15.refs_5_.refs_6_), channel_id=1, source_target_pairs={{4,0},{8,12},{5,1},{9,13},{6,2},{10,14},{7,3},{11,15},{20,16},{24,... | collective-permute-start | bytes 1572872 | tf_op jit(solution)/shard_map/ppermute | solution.py:635
  645.6 21.1 %collective-permute-start.98 = (f32[1,256]{1,0:T(1,128)S(1)}, f32[1,256]{1,0:T(1,128)S(1)}, u32[]{:S(2)}, u32[]{:S(2)}) collective-permute-start(f32[1,256]{1,0:T(1,128)S(1)} %copy-done.225), channel_id=1, source_target_pairs={{16,0},{17,1},{18,2},{19,3},{20,4},{21,5},{22,6},{23,7},{24,8},{25... | collective-permute-start | bytes 3080 | tf_op jit(solution)/shard_map/ppermute | solution.py:859
  652.3 25.0 %collective-permute-start.66 = (bf16[2,2,16,1024]{3,2,1,0:T(8,128)(2,1)}, bf16[2,2,16,1024]{3,2,1,0:T(8,128)(2,1)}, u32[]{:S(2)}, u32[]{:S(2)}) collective-permute-start(bf16[2,2,16,1024]{3,2,1,0:T(8,128)(2,1)} %slice_bitcast_fusion.7), channel_id=1, source_target_pairs={{16,0},{17,1},{18,2},{19,3},{20,4},{21,5},{22,6},{23,7},{24,8},{25... | collective-permute-start | bytes 393224 | tf_op jit(solution)/shard_map/ppermute | solution.py:1324
  678.3 16.8 %collective-permute-start.94 = (bf16[2,256,512]{2,1,0:T(8,128)(2,1)S(1)}, bf16[2,256,512]{2,1,0:T(8,128)(2,1)S(1)}, u32[]{:S(2)}, u32[]{:S(2)}) collective-permute-start(bf16[2,256,512]{2,1,0:T(8,128)(2,1)S(1)} %copy-done.17), channel_id=1, source_target_pairs={{4,0},{8,12},{5,1},{9,13},{6,2},{10,14},{7,3},{11,15},{20,16},{24,... | collective-permute-start | bytes 1572872 | tf_op jit(solution)/shard_map/ppermute | solution.py:638
  679.7 23.5 %collective-permute-start.97 = (bf16[2,256,512]{2,1,0:T(8,128)(2,1)S(1)}, bf16[2,256,512]{2,1,0:T(8,128)(2,1)S(1)}, u32[]{:S(2)}, u32[]{:S(2)}) collective-permute-start(bf16[2,256,512]{2,1,0:T(8,128)(2,1)S(1)} %copy-done.20), channel_id=1, source_target_pairs={{4,0},{8,12},{5,1},{9,13},{6,2},{10,14},{7,3},{11,15},{20,16},{24,... | collective-permute-start | bytes 1572872 | tf_op jit(solution)/shard_map/ppermute | solution.py:638
  (282 other events, 2429.0 us)
